TPU v7x, 32 devices: a whole 2x2x4 slice. The times are simulated.
32 devices in a mesh: clip: 4 (over y, x), seq: 4 (over z), tp: 2 (over core).
Axes of the slice: x: 2, y: 2, z: 4, core: 2. Of those that a mesh axis runs over, the one named last changes fastest.
Arguments:
- ffn_hidden: bfloat16 [512, 10240], P('clip', 'tp'), may hold values from -6 to 6
- ffn_weight: bfloat16 [10240, 4096], P('tp', 'seq'), may hold values from -0.0625 to 0.0625
- residual: bfloat16 [512, 4096], P('clip', 'seq'), may hold values from -6 to 6
- norm_gain: float32 [4096], replicated, may hold values from 0.3 to 3
- kv_weight: bfloat16 [4096, 8, 256], P(None, ('seq', 'tp')), may hold values from -0.09375 to 0.09375
- destination: int32 [512, 1], replicated, may hold values from 0 to 3; in each aligned block of 128 rows (0 to 127, 128 to 255, ...) at most 32 rows name the same one
- queries: bfloat16 [4096, 1024], P(('clip', 'seq', 'tp')), may hold values from -360 to 360
Outputs:
- attended: bfloat16 [4096, 1024], P(('clip', 'seq', 'tp'))
Inputs may be any that keep to these rules, and one draw needn't show every extreme that they name: `destination`: in each aligned block of 128 rows no clip is named by more than 32 rows, a bound that some block reaches; every clip is named by some row.
All inputs are finite; a program needn't handle non-finite values.
Results may differ from a plain program's by a relative error of at most 0.01375.
The roundings to bfloat16 on the way count: a program that leaves them out, or rounds other values in their place, can miss the bound.
Values may be sent and summed in bfloat16 or wider, within the bound.
No kernel may reach another device: no remote copies, remote signals or barrier semaphores. Data moves between devices by JAX's collectives and lax.ppermute only.
A program may use at most 64 MiB of HBM per device.

v0:
```python
import math

import jax
import jax.numpy as jnp
from jax import lax
from jax.sharding import PartitionSpec as P

EPSILON = 1e-06


def slot_table(dest_block, clips, capacity):
    onehot = (dest_block[:, None] == jnp.arange(clips, dtype=jnp.int32)[None, :]).astype(jnp.int32)
    before = jnp.cumsum(onehot, axis=0) - onehot
    rank = jnp.sum(before * onehot, axis=1)
    target = jnp.arange(clips * capacity, dtype=jnp.int32)
    select = (dest_block[None, :] == (target // capacity)[:, None]) & (
        rank[None, :] == (target % capacity)[:, None]
    )
    return select.astype(jnp.bfloat16)


def live_slots(dest_all, clip_now, clips, capacity, rows):
    counts = jnp.sum((dest_all.reshape(clips, rows) == clip_now).astype(jnp.int32), axis=1)
    return (jnp.arange(capacity, dtype=jnp.int32)[None, :] < counts[:, None]).reshape(
        clips * capacity
    )


def normalize(text, gain):
    wide = text.astype(jnp.float32)
    scale = lax.rsqrt(jnp.mean(wide * wide, axis=1, keepdims=True) + EPSILON)
    return (wide * scale * gain[None, :]).astype(jnp.bfloat16)


def attend(query, keyval, valid):
    width = query.shape[-1]
    keys = keyval[:, :, :width]
    values = keyval[:, :, width:]
    scores = jnp.einsum(
        "rhd,shd->hrs", query, keys, preferred_element_type=jnp.float32
    ) / math.sqrt(width)
    scores = jnp.where(valid[None, None, :], scores, -1e30)
    peak = jnp.max(scores, axis=2, keepdims=True)
    weights = jnp.where(valid[None, None, :], jnp.exp(scores - peak), 0.0)
    probs = (weights / jnp.sum(weights, axis=2, keepdims=True)).astype(jnp.bfloat16)
    return jnp.einsum("hrs,shd->rhd", probs, values, preferred_element_type=jnp.float32).astype(
        jnp.bfloat16
    )


def shards(ffn_hidden, ffn_weight, residual, norm_gain, kv_weight, destination, queries):
    clips = lax.axis_size("clip")
    rows = ffn_hidden.shape[0]
    capacity = rows // min(8, clips)
    heads_here = kv_weight.shape[1]
    head_dim = kv_weight.shape[2] // 2
    weight_flat = kv_weight.reshape(kv_weight.shape[0], heads_here * 2 * head_dim)
    partial_value = jnp.dot(ffn_hidden, ffn_weight, preferred_element_type=jnp.float32)
    summed = lax.psum(partial_value, "tp")
    text = (residual.astype(jnp.float32) + summed).astype(jnp.bfloat16)
    here = lax.axis_index("clip")
    dest_all = destination[:, 0]
    dest_block = lax.dynamic_slice_in_dim(dest_all, here * rows, rows)
    select = slot_table(dest_block, clips, capacity)
    valid = live_slots(dest_all, here, clips, capacity, rows)
    packed = jnp.dot(select, text, preferred_element_type=jnp.float32).astype(jnp.bfloat16)
    packed = packed.reshape(clips, capacity, text.shape[1])
    arrived = lax.all_to_all(packed, "clip", split_axis=0, concat_axis=0, tiled=True)
    arrived = arrived.reshape(clips * capacity, text.shape[1])
    full_text = lax.all_gather(arrived, "seq", axis=1, tiled=True)
    normed = normalize(full_text, norm_gain)
    keyval = jnp.dot(normed, weight_flat, preferred_element_type=jnp.float32).astype(jnp.bfloat16)
    keyval = keyval.reshape(clips * capacity, heads_here, 2 * head_dim)
    token_rows, width_all = queries.shape
    heads_all = width_all // head_dim
    query_heads = queries.reshape(token_rows, heads_all, head_dim)
    output = attend(query_heads, lax.all_gather(keyval, ("seq", "tp"), axis=1, tiled=True), valid)
    return output.reshape(token_rows, width_all)


def solution(mesh):
    return jax.shard_map(
        shards,
        mesh=mesh,
        in_specs=(
            P("clip", "tp"),
            P("tp", "seq"),
            P("clip", "seq"),
            P(),
            P(None, ("seq", "tp"), None),
            P(),
            P(("clip", "seq", "tp"), None),
        ),
        out_specs=P(("clip", "seq", "tp"), None),
        check_vma=False,
    )
```

profile of v0, /device:TPU:0, one launch (start us, length us, event | category | flops | bytes accessed | tf_op | source)
XLA Modules:
  0.0 101.0 jit_solution(2451842117696238258)
XLA Ops:
  6.5 0.0 copy-start
  6.5 0.0 copy-start.2
  6.5 0.0 copy-start.1
  6.5 0.0 all-reduce.2.cloned.1.call-start
  6.5 6.9 %fusion.42 = f32[128,1024]{1,0:T(8,128)} fusion(bf16[128,5120]{1,0:T(8,128)(2,1)} %param.7, bf16[5120,1024]{1,0:T(8,128)(2,1)} %param.8), kind=kOutput, calls=%fused_computation.49 | convolution fusion | flops 1342177280 | bytes 12320768 | tf_op jit(solution)/shard_map/dot_general | solution.py:58
  13.4 0.0 copy-start.4
  13.4 0.0 all-reduce.2.cloned.1.call-update
  13.4 0.0 all-gather.3.cloned.1.call-start
  13.5 0.0 copy-done.2
  13.5 0.1 fusion.22
  13.6 0.2 reduce_window_sum.11
  13.8 0.2 select_reduce_fusion
  14.0 21.1 %all-reduce.2.cloned.1.call-done = f32[128,1024]{1,0:T(8,128)} async-done(((f32[128,1024]{1,0:T(8,128)}), f32[128,1024]{1,0:T(8,128)}) %all-reduce.2.cloned.1.call-update) | async-done | bytes 524304 | tf_op jit(solution)/shard_map/psum | solution.py:59
  35.0 0.0 copy-done.1
  35.0 1.3 %convolution_convert_fusion.1 = bf16[128,1024]{1,0:T(8,128)(2,1)S(1)} fusion(f32[128,1024]{1,0:T(8,128)} %all-reduce.2.cloned.1.call-done, bf16[128,1024]{1,0:T(8,128)(2,1)S(1)} %copy-done.1, s32[128]{0:T(128)S(1)} %select_reduce_fusion, s32[128]{0:T(128)S(1)} %dynamic-slice_bitcast_fusion, s32[128]{0:T(128)S(1)} %get-tuple-element.7, ...), kind=kOutput, calls=%fused_computation.15 | convolution fusion | flops 34127872 | bytes 1050624 | tf_op jit(solution)/shard_map/dot_general | solution.py:66
  36.3 10.0 %all_to_all.5 = bf16[4,32,1024]{2,1,0:T(8,128)(2,1)} all-to-all(bf16[4,32,1024]{2,1,0:T(8,128)(2,1)S(1)} %bitcast.42), channel_id=1, replica_groups=mesh['clip'=4,'seq'=4,'tp'=2] {'clip'}, dimensions={0} | all-to-all | bytes 524288 | tf_op jit(solution)/shard_map/all_to_all | solution.py:68
  46.3 0.0 all-gather.3.cloned.1.call-update
  46.4 0.1 reduce_sum.38
  46.5 0.1 iota_compare_fusion.1
  46.6 0.1 lt.34
  46.6 27.2 %all-gather.3.cloned.1.call-done = bf16[128,4096]{1,0:T(8,128)(2,1)} async-done(((bf16[128,1024]{1,0:T(8,128)(2,1)}), bf16[128,4096]{1,0:T(8,128)(2,1)}) %all-gather.3.cloned.1.call-update) | async-done | bytes 1048592 | tf_op jit(solution)/shard_map/all_gather | solution.py:70
  73.9 1.5 %fusion.1 = f32[128]{0:T(128)S(1)} fusion(bf16[128,4096]{1,0:T(8,128)(2,1)} %all-gather.3.cloned.1.call-done), kind=kLoop, calls=%fused_computation.3 | loop fusion | flops 1572736 | bytes 1049088 | tf_op jit(solution)/shard_map/reduce_sum | solution.py:31
  75.4 0.0 copy-done
  75.4 0.0 copy-done.4
  75.4 1.7 %fusion.11 = bf16[128,256]{1,0:T(8,128)(2,1)S(1)} fusion(bf16[4096,1,256]{2,0,1:T(8,128)(2,1)S(1)} %copy-done, bf16[128,4096]{1,0:T(8,128)(2,1)} %all-gather.3.cloned.1.call-done, f32[4096]{0:T(1024)S(1)} %copy-done.4, f32[128]{0:T(128)S(1)} %add_rsqrt_fusion), kind=kOutput, calls=%fused_computation.16 | convolution fusion | flops 270565376 | bytes 3228160 | tf_op jit(solution)/shard_map/dot_general | solution.py:72
  77.1 0.0 copy-start.3
  77.2 14.9 %all-gather = bf16[128,2048]{1,0:T(8,128)(2,1)S(1)} all-gather(bf16[128,256]{1,0:T(8,128)(2,1)S(1)} %fusion.11), channel_id=2, replica_groups=mesh['clip'=4,'seq'=4,'tp'=2] {'seq','tp'}, dimensions={1}, use_global_device_ids=true | all-gather | bytes 589824 | tf_op jit(solution)/shard_map/all_gather | solution.py:77
  92.1 0.1 copy.17
  92.3 0.0 copy-done.3
  92.3 0.4 fusion.37
  92.6 0.3 fusion.10
  93.0 0.3 convolution_convert_fusion
  93.3 0.9 copy.12
  (5 shorter events, 0.1 us)
Async XLA Ops:
  6.5 68.9 %copy-start = (bf16[4096,1,256]{2,0,1:T(8,128)(2,1)S(1)}, bf16[4096,1,256]{2,0,1:T(8,128)(2,1)}, u32[]{:S(2)}) copy-start(bf16[4096,1,256]{2,0,1:T(8,128)(2,1)} %param.11) | copy-start | bytes 6291460
  6.5 7.0 %copy-start.2 = (s32[512,1]{0,1:T(1,128)S(1)}, s32[512,1]{0,1:T(1,128)}, u32[]{:S(2)}) copy-start(s32[512,1]{0,1:T(1,128)} %param.12) | copy-start | bytes 6148
  6.5 28.5 %copy-start.1 = (bf16[128,1024]{1,0:T(8,128)(2,1)S(1)}, bf16[128,1024]{1,0:T(8,128)(2,1)}, u32[]{:S(2)}) copy-start(bf16[128,1024]{1,0:T(8,128)(2,1)} %param.9) | copy-start | bytes 786436
  6.5 28.5 %all-reduce.2.cloned.1.call-start = ((), (), s32[]{:S(2)}) async-start(), calls=%async_computation.1 | async-start | bytes 1048576 | tf_op jit(solution)/shard_map/psum | solution.py:59
  13.4 62.0 %copy-start.4 = (f32[4096]{0:T(1024)S(1)}, f32[4096]{0:T(1024)}, u32[]{:S(2)}) copy-start(f32[4096]{0:T(1024)} %param.10) | copy-start | bytes 49156
  13.4 60.4 %all-gather.3.cloned.1.call-start = ((), (), s32[]{:S(2)}) async-start(), calls=%async_computation.2 | async-start | bytes 1310720 | tf_op jit(solution)/shard_map/all_gather | solution.py:70
  77.1 15.1 %copy-start.3 = (bf16[128,1024]{1,0:T(8,128)(2,1)S(1)}, bf16[128,1024]{1,0:T(8,128)(2,1)}, u32[]{:S(2)}) copy-start(bf16[128,1024]{1,0:T(8,128)(2,1)} %param.13) | copy-start | bytes 786436
Sparse Core Ops, SparseCore 0:
  13.6 21.4 all-reduce.1
  46.5 27.3 all-gather.2
where the time goes:
time: 101 us
  waiting for transfers between devices  48.3 us (48%)
  blocking collectives  24.9 us (25%)
  between operations  13.5 us (13%)
  matrix products  10.9 us (11%)
  other arithmetic  2.16 us (2%)
  local copies, waits for them, and re-layouts  1.11 us (1%)
    all_gather x1, waiting for transfers between devices, shards(): full_text = lax.all_gather(arrived, 'seq', axis=1, tiled=True)  27.2 us
    psum x1, waiting for transfers between devices, shards(): summed = lax.psum(partial_value, 'tp')  21.1 us
    all_gather x1, blocking collectives, shards(): lax.all_gather(keyval, ('seq', 'tp'), axis=1, tiled=True)  14.9 us
    all_to_all x1, blocking collectives, shards(): lax.all_to_all(packed, 'clip', split_axis=0, concat_axis=0, tiled=True)  9.99 us
    dot_general x1, matrix products, shards(): jnp.dot(ffn_hidden, ffn_weight, preferred_element_type=jnp.float32)  6.86 us
  transfers between devices with their start and end apart: 2, of which 2 were waited for; matrix products, arithmetic and copies ran while one was open for 1% of the time, Pallas kernels for 0%

commit v1 on v0

v1 whole, which is shorter than its diff:
```python
import functools
import math

import jax
import jax.numpy as jnp
from jax import lax
from jax.experimental import pallas as pl
from jax.experimental.pallas import tpu as pltpu
from jax.sharding import PartitionSpec as P

EPSILON = 1e-06
VMEM_LIMIT = 48 * 1024 * 1024
F32 = jnp.float32
BF16 = jnp.bfloat16


def whole():
    return pl.BlockSpec(memory_space=pltpu.VMEM)


def swap(value, axis, offset):
    size = lax.axis_size(axis)
    return lax.ppermute(value, axis, [(i, i ^ offset) for i in range(size)])


def slot_select(dest_ref, clip, core, clips, half, cores):
    rows = dest_ref.shape[1]
    named = dest_ref[pl.ds(clip, 1), :]
    onehot = (lax.broadcasted_iota(jnp.int32, (clips, rows), 0) == named).astype(F32)
    earlier = (
        lax.broadcasted_iota(jnp.int32, (rows, rows), 0)
        < lax.broadcasted_iota(jnp.int32, (rows, rows), 1)
    ).astype(F32)
    before = jnp.dot(onehot, earlier, preferred_element_type=F32)
    rank = jnp.sum(before * onehot, axis=0, keepdims=True).astype(jnp.int32)
    slot = ((rank // half) ^ core) * (clips * half) + (named ^ clip) * half + rank % half
    slots = cores * clips * half
    return (lax.broadcasted_iota(jnp.int32, (slots, rows), 0) == slot).astype(BF16)


def ffn_kernel(clips, half, cores, dest_ref, hidden_ref, weight_ref, residual_ref,
               own_ref, send_ref, text_ref, select_ref, total_ref):
    step = pl.program_id(0)
    clip, core = lax.axis_index("clip"), lax.axis_index("tp")
    share = clips * half

    @pl.when(step == 0)
    def _():
        select = slot_select(dest_ref, clip, core, clips, half, cores)
        select_ref[...] = select
        text_ref[...] = jnp.dot(
            select[:share], residual_ref[...], preferred_element_type=F32
        ).astype(BF16)
        total_ref[...] = jnp.zeros_like(total_ref)

    packed = jnp.dot(select_ref[...], hidden_ref[...], preferred_element_type=F32).astype(BF16)
    total_ref[...] += jnp.dot(packed, weight_ref[...], preferred_element_type=F32)

    @pl.when(step == pl.num_programs(0) - 1)
    def _():
        own_ref[...] = total_ref[:share, :]
        send_ref[...] = total_ref[share:, :]


def ffn(dest, hidden, weight, residual, clips, half, cores):
    rows, depth = hidden.shape
    width = weight.shape[1]
    share = clips * half
    steps = 8
    block = depth // steps
    return pl.pallas_call(
        functools.partial(ffn_kernel, clips, half, cores),
        grid=(steps,),
        in_specs=[
            pl.BlockSpec(dest.shape, lambda i: (0, 0)),
            pl.BlockSpec((rows, block), lambda i: (0, i)),
            pl.BlockSpec((block, width), lambda i: (i, 0)),
            pl.BlockSpec((rows, width), lambda i: (0, 0)),
        ],
        out_specs=[
            pl.BlockSpec((share, width), lambda i: (0, 0)),
            pl.BlockSpec(((cores - 1) * share, width), lambda i: (0, 0)),
            pl.BlockSpec((share, width), lambda i: (0, 0)),
        ],
        out_shape=[
            jax.ShapeDtypeStruct((share, width), F32),
            jax.ShapeDtypeStruct(((cores - 1) * share, width), F32),
            jax.ShapeDtypeStruct((share, width), BF16),
        ],
        scratch_shapes=[
            pltpu.VMEM((cores * share, rows), BF16),
            pltpu.VMEM((cores * share, width), F32),
        ],
        compiler_params=pltpu.CompilerParams(vmem_limit_bytes=VMEM_LIMIT),
        cost_estimate=pl.CostEstimate(
            flops=2 * cores * share * depth * (width + rows),
            bytes_accessed=2 * depth * (width + rows),
            transcendentals=0,
        ),
    )(dest, hidden, weight, residual)


def keyval_kernel(parts, cores, *refs):
    texts, (gain_ref, *weights), out_ref = refs[:parts], refs[parts:-1], refs[-1]
    seq = lax.axis_index("seq")
    width = texts[0].shape[1]
    squares = 0.0
    for text in texts:
        wide = text[...].astype(F32)
        squares += jnp.sum(wide * wide, axis=1, keepdims=True)
    scale = lax.rsqrt(squares / (parts * width) + EPSILON)
    totals = [0.0] * cores
    for k, text in enumerate(texts):
        place = pl.ds(pl.multiple_of((seq ^ k) * width, width), width)
        normed = (text[...].astype(F32) * scale * gain_ref[:, place]).astype(BF16)
        for c, weight in enumerate(weights):
            totals[c] += jnp.dot(normed, weight[place, :], preferred_element_type=F32)
    each = weights[0].shape[1]
    for c in range(cores):
        out_ref[:, c * each:(c + 1) * each] = totals[c].astype(BF16)


def attend_kernel(parts, cores, heads_here, half, dest_ref, query_ref, *refs):
    blocks, out_ref = refs[:-1], refs[-1]
    clip, seq, core = lax.axis_index("clip"), lax.axis_index("seq"), lax.axis_index("tp")
    clips = dest_ref.shape[0]
    share = clips * half
    dim = query_ref.shape[1] // (parts * cores * heads_here)
    counts = jnp.sum((dest_ref[...] == clip).astype(jnp.int32), axis=1, keepdims=True)
    lane = lax.broadcasted_iota(jnp.int32, (clips, cores * share), 1)
    source = ((lane % share) // half) ^ clip
    limit = jnp.sum(
        jnp.where(lax.broadcasted_iota(jnp.int32, lane.shape, 0) == source, counts, 0),
        axis=0, keepdims=True,
    )
    flat = lax.broadcasted_iota(jnp.int32, (1, cores * share), 1)
    valid = ((flat // share) ^ core) * half + flat % half < limit
    for k in range(parts):
        for c in range(cores):
            for i in range(heads_here):
                head = ((seq ^ k) * cores + (core ^ c)) * heads_here + i
                columns = pl.ds(pl.multiple_of(head * dim, dim), dim)
                at = [((c ^ g) * heads_here + i) * 2 * dim for g in range(cores)]
                keys = jnp.concatenate(
                    [blocks[k * cores + g][:, at[g]:at[g] + dim] for g in range(cores)], axis=0
                )
                values = jnp.concatenate(
                    [blocks[k * cores + g][:, at[g] + dim:at[g] + 2 * dim] for g in range(cores)],
                    axis=0,
                )
                scores = lax.dot_general(
                    query_ref[:, columns], keys, (((1,), (1,)), ((), ())),
                    preferred_element_type=F32,
                ) / math.sqrt(dim)
                scores = jnp.where(valid, scores, -1e30)
                peak = jnp.max(scores, axis=1, keepdims=True)
                weights = jnp.where(valid, jnp.exp(scores - peak), 0.0)
                probs = (weights / jnp.sum(weights, axis=1, keepdims=True)).astype(BF16)
                out_ref[:, columns] = jnp.dot(
                    probs, values, preferred_element_type=F32
                ).astype(BF16)


def shards(ffn_hidden, ffn_weight, residual, norm_gain, kv_weight, destination, queries):
    clips, parts, cores = lax.axis_size("clip"), lax.axis_size("seq"), lax.axis_size("tp")
    rows = ffn_hidden.shape[0]
    half = rows // min(8, clips) // cores
    share = clips * half
    heads_here = kv_weight.shape[1]
    dest = destination.reshape(clips, rows)
    weights = [kv_weight.reshape(kv_weight.shape[0], heads_here * kv_weight.shape[2])]
    for g in range(1, cores):
        weights.append(swap(weights[0], "tp", g))
    own, send, text = ffn(dest, ffn_hidden, ffn_weight, residual, clips, half, cores)
    for g in range(1, cores):
        own = own + swap(send[(g - 1) * share:g * share], "tp", g)
    text = (text.astype(F32) + own).astype(BF16)
    arrived = [text[:half]]
    for j in range(1, clips):
        arrived.append(swap(text[j * half:(j + 1) * half], "clip", j))
    arrived = jnp.concatenate(arrived, axis=0)
    texts = [arrived] + [swap(arrived, "seq", k) for k in range(1, parts)]
    keyval = pl.pallas_call(
        functools.partial(keyval_kernel, parts, cores),
        in_specs=[whole()] * (parts + 1 + cores),
        out_specs=whole(),
        out_shape=jax.ShapeDtypeStruct((share, cores * weights[0].shape[1]), BF16),
        compiler_params=pltpu.CompilerParams(vmem_limit_bytes=VMEM_LIMIT),
    )(*texts, norm_gain.reshape(1, -1), *weights)
    blocks = []
    for k in range(parts):
        block = swap(keyval, "seq", k) if k else keyval
        blocks += [block] + [swap(block, "tp", g) for g in range(1, cores)]
    return pl.pallas_call(
        functools.partial(attend_kernel, parts, cores, heads_here, half),
        in_specs=[whole()] * (2 + len(blocks)),
        out_specs=whole(),
        out_shape=jax.ShapeDtypeStruct(queries.shape, BF16),
        compiler_params=pltpu.CompilerParams(vmem_limit_bytes=VMEM_LIMIT),
    )(dest, queries, *blocks)


def solution(mesh):
    return jax.shard_map(
        shards,
        mesh=mesh,
        in_specs=(
            P("clip", "tp"),
            P("tp", "seq"),
            P("clip", "seq"),
            P(),
            P(None, ("seq", "tp"), None),
            P(),
            P(("clip", "seq", "tp"), None),
        ),
        out_specs=P(("clip", "seq", "tp"), None),
        check_vma=False,
    )
```

time: 101 us -> 49.4 us (0.49)
  waiting for transfers between devices: 48.3 us -> 18.6 us
  blocking collectives: 24.9 us -> 0 us
  starting transfers between devices: 0.04 us -> 14.3 us
  between operations: 13.5 us -> 0.07 us
  Pallas kernels: 0 us -> 13 us
  matrix products: 10.9 us -> 0 us
  other arithmetic: 2.16 us -> 0.05 us
  local copies, waits for them, and re-layouts: 1.11 us -> 2.98 us
    all_gather x1 -> x0, waiting for transfers between devices: 27.2 us -> none  [shards(): full_text = lax.all_gather(arrived, 'seq', axis=1, tiled=True)]
    psum x1 -> x0, waiting for transfers between devices: 21.1 us -> none  [shards(): summed = lax.psum(partial_value, 'tp')]
    ppermute x0 -> x15, waiting for transfers between devices: none -> 18.6 us  [swap(): return lax.ppermute(value, axis, [(i, i ^ offset) for i in range(size)])]
    all_gather x1 -> x0, blocking collectives: 14.9 us -> none  [shards(): lax.all_gather(keyval, ('seq', 'tp'), axis=1, tiled=True)]
    ppermute x0 -> x15, starting transfers between devices: none -> 14.3 us  [swap(): return lax.ppermute(value, axis, [(i, i ^ offset) for i in range(size)])]
    pallas_call x0 -> x3, Pallas kernels: none -> 13 us  [the longest x1 8.65 us: ffn(): pl.pallas_call(functools.partial(ffn_kernel, clips, half, cores), grid=(s...]
    dot_general x5 -> x0, matrix products: 10.5 us -> none  [the longest x1 6.86 us: shards(): jnp.dot(ffn_hidden, ffn_weight, preferred_element_type=jnp.float32)]
    all_to_all x1 -> x0, blocking collectives: 9.99 us -> none  [shards(): lax.all_to_all(packed, 'clip', split_axis=0, concat_axis=0, tiled=True)]
  transfers between devices with their start and end apart: 2 -> 15, of which waited for: 2 -> 10; matrix products, arithmetic and copies ran while one was open for 1% -> 0% of each run, Pallas kernels for 0% -> 18%
where the time goes in v1:
time: 49.4 us; the launch traced here: 49 us
  waiting for transfers between devices  18.6 us (38%)
  starting transfers between devices  14.3 us (29%)
  Pallas kernels  13 us (26%)
  local copies, waits for them, and re-layouts  2.98 us (6%)
    ppermute x15, waiting for transfers between devices, swap(): return lax.ppermute(value, axis, [(i, i ^ offset) for i in range(size)])  18.6 us
    ppermute x15, starting transfers between devices, swap(): return lax.ppermute(value, axis, [(i, i ^ offset) for i in range(size)])  14.3 us
    pallas_call x1, Pallas kernels, ffn(): pl.pallas_call(functools.partial(ffn_kernel, clips, half, cores), grid=(s...  8.65 us
    pallas_call x1, Pallas kernels, shards(): pl.pallas_call(functools.partial(attend_kernel, parts, cores, heads_here,...  3.39 us
    unnamed x14, local copies, waits for them, and re-layouts  2.97 us
  transfers between devices with their start and end apart: 15, of which 10 were waited for; matrix products, arithmetic and copies ran while one was open for 0% of the time, Pallas kernels for 18%

profile of v1, /device:TPU:0, one launch (start us, length us, event | category | flops | bytes accessed | tf_op | source)
XLA Modules:
  0.0 49.0 jit_solution(11033056740493059407)
XLA Ops:
  0.0 0.5 collective-permute-start.7
  0.5 0.0 copy-start.1
  0.5 1.3 %copy-done.1 = bf16[128,5120]{1,0:T(8,128)(2,1)S(1)} copy-done((bf16[128,5120]{1,0:T(8,128)(2,1)S(1)}, bf16[128,5120]{1,0:T(8,128)(2,1)}, u32[]{:S(2)}) %copy-start.1) | copy-done | bytes 1310744
  1.8 0.0 copy-start.2
  1.8 0.9 %copy-done.2 = bf16[128,1024]{1,0:T(8,128)(2,1)S(1)} copy-done((bf16[128,1024]{1,0:T(8,128)(2,1)S(1)}, bf16[128,1024]{1,0:T(8,128)(2,1)}, u32[]{:S(2)}) %copy-start.2) | copy-done | bytes 262168
  2.7 0.0 copy-start.5
  2.7 0.7 %copy-done.5 = s32[512,1]{0,1:T(1,128)S(1)} copy-done((s32[512,1]{0,1:T(1,128)S(1)}, s32[512,1]{0,1:T(1,128)}, u32[]{:S(2)}) %copy-start.5) | copy-done | bytes 2072
  3.4 0.0 copy-start
  3.4 0.0 copy-start.4
  3.4 8.7 %shard_map.73 = (f32[64,1024]{1,0:T(8,128)S(1)}, f32[64,1024]{1,0:T(8,128)S(1)}, bf16[64,1024]{1,0:T(8,128)(2,1)S(1)}) custom-call(s32[4,128]{1,0:T(4,128)S(1)} %bitcast.6, bf16[128,5120]{1,0:T(8,128)(2,1)S(1)} %copy-done.1, bf16[5120,1024]{1,0:T(8,128)(2,1)} %weight_ref.1, bf16[128,1024]{1,0:T(8,128)(2,1)S(1)} %copy-done.2), custom_call_target="tpu_custom_call" | custom-call | flops 1509949440 | bytes 11796480 | tf_op jit(solution)/shard_map/pallas_call | solution.py:71
  12.1 0.1 collective-permute-start
  12.2 1.5 %collective-permute-done = f32[64,1024]{1,0:T(8,128)S(1)} collective-permute-done((f32[64,1024]{1,0:T(8,128)S(1)}, f32[64,1024]{1,0:T(8,128)S(1)}, u32[]{:S(2)}, u32[]{:S(2)}) %collective-permute-start) | collective-permute-done | bytes 262176 | tf_op jit(solution)/shard_map/ppermute | solution.py:23
  13.7 3.7 %collective-permute-start.3 = (bf16[16,1024]{1,0:T(8,128)(2,1)S(1)}, bf16[16,1024]{1,0:T(8,128)(2,1)S(1)}, u32[]{:S(2)}, u32[]{:S(2)}) collective-permute-start(bf16[16,1024]{1,0:T(8,128)(2,1)S(1)} %get-tuple-element.12), channel_id=1, source_target_pairs={{0,24},{8,16},{16,8},{24,0},{1,25},{9,17},{17,9},{25,1},{2,26},{10... | collective-permute-start | bytes 98312 | tf_op jit(solution)/shard_map/ppermute | solution.py:23
  17.4 0.5 %collective-permute-start.2 = (bf16[16,1024]{1,0:T(8,128)(2,1)S(1)}, bf16[16,1024]{1,0:T(8,128)(2,1)S(1)}, u32[]{:S(2)}, u32[]{:S(2)}) collective-permute-start(bf16[16,1024]{1,0:T(8,128)(2,1)S(1)} %get-tuple-element.13), channel_id=1, source_target_pairs={{0,16},{8,24},{16,0},{24,8},{1,17},{9,25},{17,1},{25,9},{2,18},{10... | collective-permute-start | bytes 98312 | tf_op jit(solution)/shard_map/ppermute | solution.py:23
  17.9 0.1 collective-permute-start.1
  18.0 1.3 %collective-permute-done.3 = bf16[16,1024]{1,0:T(8,128)(2,1)S(1)} collective-permute-done((bf16[16,1024]{1,0:T(8,128)(2,1)S(1)}, bf16[16,1024]{1,0:T(8,128)(2,1)S(1)}, u32[]{:S(2)}, u32[]{:S(2)}) %collective-permute-start.3) | collective-permute-done | bytes 32800 | tf_op jit(solution)/shard_map/ppermute | solution.py:23
  19.3 2.0 %collective-permute-done.2 = bf16[16,1024]{1,0:T(8,128)(2,1)S(1)} collective-permute-done((bf16[16,1024]{1,0:T(8,128)(2,1)S(1)}, bf16[16,1024]{1,0:T(8,128)(2,1)S(1)}, u32[]{:S(2)}, u32[]{:S(2)}) %collective-permute-start.2) | collective-permute-done | bytes 32800 | tf_op jit(solution)/shard_map/ppermute | solution.py:23
  21.3 0.5 %collective-permute-done.1 = bf16[16,1024]{1,0:T(8,128)(2,1)S(1)} collective-permute-done((bf16[16,1024]{1,0:T(8,128)(2,1)S(1)}, bf16[16,1024]{1,0:T(8,128)(2,1)S(1)}, u32[]{:S(2)}, u32[]{:S(2)}) %collective-permute-start.1) | collective-permute-done | bytes 32800 | tf_op jit(solution)/shard_map/ppermute | solution.py:23
  21.8 3.7 %collective-permute-start.6 = (bf16[64,1024]{1,0:T(8,128)(2,1)S(1)}, bf16[64,1024]{1,0:T(8,128)(2,1)S(1)}, u32[]{:S(2)}, u32[]{:S(2)}) collective-permute-start(bf16[64,1024]{1,0:T(8,128)(2,1)S(1)} %pad_maximum_fusion.refs_0_), channel_id=1, source_target_pairs={{0,6},{2,4},{4,2},{6,0},{1,7},{3,5},{5,3},{7,1},{8,14},{10,12},{12... | collective-permute-start | bytes 393224 | tf_op jit(solution)/shard_map/ppermute | solution.py:23
  25.5 0.0 collective-permute-start.5
  25.5 0.8 %collective-permute-start.4 = (bf16[64,1024]{1,0:T(8,128)(2,1)S(1)}, bf16[64,1024]{1,0:T(8,128)(2,1)S(1)}, u32[]{:S(2)}, u32[]{:S(2)}) collective-permute-start(bf16[64,1024]{1,0:T(8,128)(2,1)S(1)} %pad_maximum_fusion.refs_0_), channel_id=1, source_target_pairs={{0,2},{2,0},{4,6},{6,4},{1,3},{3,1},{5,7},{7,5},{8,10},{10,8},{12,... | collective-permute-start | bytes 393224 | tf_op jit(solution)/shard_map/ppermute | solution.py:23
  26.3 3.6 %collective-permute-done.6.refs_3_ = bf16[64,1024]{1,0:T(8,128)(2,1)S(1)} collective-permute-done((bf16[64,1024]{1,0:T(8,128)(2,1)S(1)}, bf16[64,1024]{1,0:T(8,128)(2,1)S(1)}, u32[]{:S(2)}, u32[]{:S(2)}) %collective-permute-start.6) | collective-permute-done | bytes 131104 | tf_op jit(solution)/shard_map/ppermute | solution.py:23
  29.9 5.5 %collective-permute-done.5.refs_2_ = bf16[64,1024]{1,0:T(8,128)(2,1)S(1)} collective-permute-done((bf16[64,1024]{1,0:T(8,128)(2,1)S(1)}, bf16[64,1024]{1,0:T(8,128)(2,1)S(1)}, u32[]{:S(2)}, u32[]{:S(2)}) %collective-permute-start.5) | collective-permute-done | bytes 131104 | tf_op jit(solution)/shard_map/ppermute | solution.py:23
  35.4 0.0 collective-permute-done.4.refs_1_
  35.4 0.0 collective-permute-done.7.refs_6_
  35.4 0.0 copy-done
  35.4 0.0 copy-done.4
  35.4 0.0 copy-start.3
  35.4 0.0 copy-start.6
  35.4 1.0 %shard_map.74.refs_0_ = bf16[64,512]{1,0:T(8,128)(2,1)S(1)} custom-call(bf16[64,1024]{1,0:T(8,128)(2,1)S(1)} %pad_maximum_fusion.refs_0_, bf16[64,1024]{1,0:T(8,128)(2,1)S(1)} %collective-permute-done.4.refs_1_, bf16[64,1024]{1,0:T(8,128)(2,1)S(1)} %collective-permute-done.5.refs_2_, bf16[64,1024]{1,0:T(8,128)(2,1)S(1)} %collective-permute-done.6.refs_3_, ...), custom_call_target="tpu_custom_call" | custom-call | tf_op jit(solution)/shard_map/pallas_call | solution.py:183
  36.4 2.5 %collective-permute-start.13 = (bf16[64,512]{1,0:T(8,128)(2,1)S(1)}, bf16[64,512]{1,0:T(8,128)(2,1)S(1)}, u32[]{:S(2)}, u32[]{:S(2)}) collective-permute-start(bf16[64,512]{1,0:T(8,128)(2,1)S(1)} %shard_map.74.refs_0_), channel_id=1, source_target_pairs={{0,6},{2,4},{4,2},{6,0},{1,7},{3,5},{5,3},{7,1},{8,14},{10,12},{12... | collective-permute-start | bytes 196616 | tf_op jit(solution)/shard_map/ppermute | solution.py:23
  38.9 0.0 collective-permute-start.11
  38.9 1.9 %collective-permute-start.9 = (bf16[64,512]{1,0:T(8,128)(2,1)S(1)}, bf16[64,512]{1,0:T(8,128)(2,1)S(1)}, u32[]{:S(2)}, u32[]{:S(2)}) collective-permute-start(bf16[64,512]{1,0:T(8,128)(2,1)S(1)} %shard_map.74.refs_0_), channel_id=1, source_target_pairs={{0,2},{2,0},{4,6},{6,4},{1,3},{3,1},{5,7},{7,5},{8,10},{10,8},{12,... | collective-permute-start | bytes 196616 | tf_op jit(solution)/shard_map/ppermute | solution.py:23
  40.9 0.0 collective-permute-start.8
  40.9 2.0 %collective-permute-done.13.refs_6_ = bf16[64,512]{1,0:T(8,128)(2,1)S(1)} collective-permute-done((bf16[64,512]{1,0:T(8,128)(2,1)S(1)}, bf16[64,512]{1,0:T(8,128)(2,1)S(1)}, u32[]{:S(2)}, u32[]{:S(2)}) %collective-permute-start.13) | collective-permute-done | bytes 65568 | tf_op jit(solution)/shard_map/ppermute | solution.py:23
  42.9 0.0 collective-permute-start.14
  42.9 1.4 %collective-permute-done.11.refs_4_ = bf16[64,512]{1,0:T(8,128)(2,1)S(1)} collective-permute-done((bf16[64,512]{1,0:T(8,128)(2,1)S(1)}, bf16[64,512]{1,0:T(8,128)(2,1)S(1)}, u32[]{:S(2)}, u32[]{:S(2)}) %collective-permute-start.11) | collective-permute-done | bytes 65568 | tf_op jit(solution)/shard_map/ppermute | solution.py:23
  44.2 0.0 collective-permute-start.12
  44.2 0.0 collective-permute-done.9.refs_2_
  44.2 0.5 %collective-permute-start.10 = (bf16[64,512]{1,0:T(8,128)(2,1)S(1)}, bf16[64,512]{1,0:T(8,128)(2,1)S(1)}, u32[]{:S(2)}, u32[]{:S(2)}) collective-permute-start(bf16[64,512]{1,0:T(8,128)(2,1)S(1)} %collective-permute-done.9.refs_2_), channel_id=1, source_target_pairs={{0,1},{1,0},{2,3},{3,2},{4,5},{5,4},{6,7},{7,6},{8,9},{9,8},{10,11... | collective-permute-start | bytes 196616 | tf_op jit(solution)/shard_map/ppermute | solution.py:23
  44.7 0.0 collective-permute-done.8.refs_1_
  44.8 0.0 collective-permute-done.14.refs_7_
  44.8 0.7 %collective-permute-done.12.refs_5_ = bf16[64,512]{1,0:T(8,128)(2,1)S(1)} collective-permute-done((bf16[64,512]{1,0:T(8,128)(2,1)S(1)}, bf16[64,512]{1,0:T(8,128)(2,1)S(1)}, u32[]{:S(2)}, u32[]{:S(2)}) %collective-permute-start.12) | collective-permute-done | bytes 65568 | tf_op jit(solution)/shard_map/ppermute | solution.py:23
  45.5 0.2 collective-permute-done.10.refs_3_
  45.6 0.0 copy-done.3
  45.7 0.0 copy-done.6
  45.7 3.4 %shard_map.75 = bf16[128,1024]{1,0:T(8,128)(2,1)} custom-call(s32[4,128]{1,0:T(4,128)S(1)} %bitcast.7, bf16[128,1024]{1,0:T(8,128)(2,1)S(1)} %copy-done.3, bf16[64,512]{1,0:T(8,128)(2,1)S(1)} %shard_map.74.refs_0_, bf16[64,512]{1,0:T(8,128)(2,1)S(1)} %collective-permute-done.8.refs_1_, bf16[64,512]{1,0:T(8,128)(2,1)S(1)} %collective-permute-done.9.refs_2_, ...), custom_call_target="tpu_custom_call" | custom-call | tf_op jit(solution)/shard_map/pallas_call | solution.py:194
  (3 shorter events, 0.1 us)
Async XLA Ops:
  0.0 35.4 %collective-permute-start.7 = (bf16[4096,256]{1,0:T(8,128)(2,1)}, bf16[4096,256]{1,0:T(8,128)(2,1)S(1)}, u32[]{:S(2)}, u32[]{:S(2)}) collective-permute-start(bf16[4096,256]{1,0:T(8,128)(2,1)} %bitcast.3), channel_id=1, source_target_pairs={{0,1},{1,0},{2,3},{3,2},{4,5},{5,4},{6,7},{7,6},{8,9},{9,8},{10,11... | collective-permute-start | bytes 6291464 | tf_op jit(solution)/shard_map/ppermute | solution.py:23
  0.5 1.3 %copy-start.1 = (bf16[128,5120]{1,0:T(8,128)(2,1)S(1)}, bf16[128,5120]{1,0:T(8,128)(2,1)}, u32[]{:S(2)}) copy-start(bf16[128,5120]{1,0:T(8,128)(2,1)} %hidden_ref.1) | copy-start | bytes 3932164
  1.8 0.9 %copy-start.2 = (bf16[128,1024]{1,0:T(8,128)(2,1)S(1)}, bf16[128,1024]{1,0:T(8,128)(2,1)}, u32[]{:S(2)}) copy-start(bf16[128,1024]{1,0:T(8,128)(2,1)} %residual_ref.1) | copy-start | bytes 786436
  2.7 0.7 %copy-start.5 = (s32[512,1]{0,1:T(1,128)S(1)}, s32[512,1]{0,1:T(1,128)}, u32[]{:S(2)}) copy-start(s32[512,1]{0,1:T(1,128)} %param.12) | copy-start | bytes 6148
  3.4 32.0 %copy-start = (bf16[4096,1,256]{2,0,1:T(8,128)(2,1)S(1)}, bf16[4096,1,256]{2,0,1:T(8,128)(2,1)}, u32[]{:S(2)}) copy-start(bf16[4096,1,256]{2,0,1:T(8,128)(2,1)} %param.11) | copy-start | bytes 6291460
  3.4 32.0 %copy-start.4 = (f32[4096]{0:T(1024)S(1)}, f32[4096]{0:T(1024)}, u32[]{:S(2)}) copy-start(f32[4096]{0:T(1024)} %param.10) | copy-start | bytes 49156
  12.1 1.6 %collective-permute-start = (f32[64,1024]{1,0:T(8,128)S(1)}, f32[64,1024]{1,0:T(8,128)S(1)}, u32[]{:S(2)}, u32[]{:S(2)}) collective-permute-start(f32[64,1024]{1,0:T(8,128)S(1)} %get-tuple-element.10), channel_id=1, source_target_pairs={{0,1},{1,0},{2,3},{3,2},{4,5},{5,4},{6,7},{7,6},{8,9},{9,8},{10,11... | collective-permute-start | bytes 786440 | tf_op jit(solution)/shard_map/ppermute | solution.py:23
  13.7 5.6 %collective-permute-start.3 = (bf16[16,1024]{1,0:T(8,128)(2,1)S(1)}, bf16[16,1024]{1,0:T(8,128)(2,1)S(1)}, u32[]{:S(2)}, u32[]{:S(2)}) collective-permute-start(bf16[16,1024]{1,0:T(8,128)(2,1)S(1)} %get-tuple-element.12), channel_id=1, source_target_pairs={{0,24},{8,16},{16,8},{24,0},{1,25},{9,17},{17,9},{25,1},{2,26},{10... | collective-permute-start | bytes 98312 | tf_op jit(solution)/shard_map/ppermute | solution.py:23
  17.4 3.9 %collective-permute-start.2 = (bf16[16,1024]{1,0:T(8,128)(2,1)S(1)}, bf16[16,1024]{1,0:T(8,128)(2,1)S(1)}, u32[]{:S(2)}, u32[]{:S(2)}) collective-permute-start(bf16[16,1024]{1,0:T(8,128)(2,1)S(1)} %get-tuple-element.13), channel_id=1, source_target_pairs={{0,16},{8,24},{16,0},{24,8},{1,17},{9,25},{17,1},{25,9},{2,18},{10... | collective-permute-start | bytes 98312 | tf_op jit(solution)/shard_map/ppermute | solution.py:23
  17.9 3.9 %collective-permute-start.1 = (bf16[16,1024]{1,0:T(8,128)(2,1)S(1)}, bf16[16,1024]{1,0:T(8,128)(2,1)S(1)}, u32[]{:S(2)}, u32[]{:S(2)}) collective-permute-start(bf16[16,1024]{1,0:T(8,128)(2,1)S(1)} %get-tuple-element.14), channel_id=1, source_target_pairs={{0,8},{8,0},{16,24},{24,16},{1,9},{9,1},{17,25},{25,17},{2,10},{10... | collective-permute-start | bytes 98312 | tf_op jit(solution)/shard_map/ppermute | solution.py:23
  21.8 8.1 %collective-permute-start.6 = (bf16[64,1024]{1,0:T(8,128)(2,1)S(1)}, bf16[64,1024]{1,0:T(8,128)(2,1)S(1)}, u32[]{:S(2)}, u32[]{:S(2)}) collective-permute-start(bf16[64,1024]{1,0:T(8,128)(2,1)S(1)} %pad_maximum_fusion.refs_0_), channel_id=1, source_target_pairs={{0,6},{2,4},{4,2},{6,0},{1,7},{3,5},{5,3},{7,1},{8,14},{10,12},{12... | collective-permute-start | bytes 393224 | tf_op jit(solution)/shard_map/ppermute | solution.py:23
  25.5 9.9 %collective-permute-start.5 = (bf16[64,1024]{1,0:T(8,128)(2,1)S(1)}, bf16[64,1024]{1,0:T(8,128)(2,1)S(1)}, u32[]{:S(2)}, u32[]{:S(2)}) collective-permute-start(bf16[64,1024]{1,0:T(8,128)(2,1)S(1)} %pad_maximum_fusion.refs_0_), channel_id=1, source_target_pairs={{0,4},{2,6},{4,0},{6,2},{1,5},{3,7},{5,1},{7,3},{8,12},{10,14},{12... | collective-permute-start | bytes 393224 | tf_op jit(solution)/shard_map/ppermute | solution.py:23
  25.5 9.9 %collective-permute-start.4 = (bf16[64,1024]{1,0:T(8,128)(2,1)S(1)}, bf16[64,1024]{1,0:T(8,128)(2,1)S(1)}, u32[]{:S(2)}, u32[]{:S(2)}) collective-permute-start(bf16[64,1024]{1,0:T(8,128)(2,1)S(1)} %pad_maximum_fusion.refs_0_), channel_id=1, source_target_pairs={{0,2},{2,0},{4,6},{6,4},{1,3},{3,1},{5,7},{7,5},{8,10},{10,8},{12,... | collective-permute-start | bytes 393224 | tf_op jit(solution)/shard_map/ppermute | solution.py:23
  35.4 10.2 %copy-start.3 = (bf16[128,1024]{1,0:T(8,128)(2,1)S(1)}, bf16[128,1024]{1,0:T(8,128)(2,1)}, u32[]{:S(2)}) copy-start(bf16[128,1024]{1,0:T(8,128)(2,1)} %query_ref.1) | copy-start | bytes 786436
  35.4 10.2 %copy-start.6 = (s32[512,1]{0,1:T(1,128)S(1)}, s32[512,1]{0,1:T(1,128)}, u32[]{:S(2)}) copy-start(s32[512,1]{0,1:T(1,128)} %param.12) | copy-start | bytes 6148
  36.4 6.5 %collective-permute-start.13 = (bf16[64,512]{1,0:T(8,128)(2,1)S(1)}, bf16[64,512]{1,0:T(8,128)(2,1)S(1)}, u32[]{:S(2)}, u32[]{:S(2)}) collective-permute-start(bf16[64,512]{1,0:T(8,128)(2,1)S(1)} %shard_map.74.refs_0_), channel_id=1, source_target_pairs={{0,6},{2,4},{4,2},{6,0},{1,7},{3,5},{5,3},{7,1},{8,14},{10,12},{12... | collective-permute-start | bytes 196616 | tf_op jit(solution)/shard_map/ppermute | solution.py:23
  38.9 5.3 %collective-permute-start.11 = (bf16[64,512]{1,0:T(8,128)(2,1)S(1)}, bf16[64,512]{1,0:T(8,128)(2,1)S(1)}, u32[]{:S(2)}, u32[]{:S(2)}) collective-permute-start(bf16[64,512]{1,0:T(8,128)(2,1)S(1)} %shard_map.74.refs_0_), channel_id=1, source_target_pairs={{0,4},{2,6},{4,0},{6,2},{1,5},{3,7},{5,1},{7,3},{8,12},{10,14},{12... | collective-permute-start | bytes 196616 | tf_op jit(solution)/shard_map/ppermute | solution.py:23
  38.9 5.3 %collective-permute-start.9 = (bf16[64,512]{1,0:T(8,128)(2,1)S(1)}, bf16[64,512]{1,0:T(8,128)(2,1)S(1)}, u32[]{:S(2)}, u32[]{:S(2)}) collective-permute-start(bf16[64,512]{1,0:T(8,128)(2,1)S(1)} %shard_map.74.refs_0_), channel_id=1, source_target_pairs={{0,2},{2,0},{4,6},{6,4},{1,3},{3,1},{5,7},{7,5},{8,10},{10,8},{12,... | collective-permute-start | bytes 196616 | tf_op jit(solution)/shard_map/ppermute | solution.py:23
  40.9 3.9 %collective-permute-start.8 = (bf16[64,512]{1,0:T(8,128)(2,1)S(1)}, bf16[64,512]{1,0:T(8,128)(2,1)S(1)}, u32[]{:S(2)}, u32[]{:S(2)}) collective-permute-start(bf16[64,512]{1,0:T(8,128)(2,1)S(1)} %shard_map.74.refs_0_), channel_id=1, source_target_pairs={{0,1},{1,0},{2,3},{3,2},{4,5},{5,4},{6,7},{7,6},{8,9},{9,8},{10,11... | collective-permute-start | bytes 196616 | tf_op jit(solution)/shard_map/ppermute | solution.py:23
  42.9 1.9 %collective-permute-start.14 = (bf16[64,512]{1,0:T(8,128)(2,1)S(1)}, bf16[64,512]{1,0:T(8,128)(2,1)S(1)}, u32[]{:S(2)}, u32[]{:S(2)}) collective-permute-start(bf16[64,512]{1,0:T(8,128)(2,1)S(1)} %collective-permute-done.13.refs_6_), channel_id=1, source_target_pairs={{0,1},{1,0},{2,3},{3,2},{4,5},{5,4},{6,7},{7,6},{8,9},{9,8},{10,11... | collective-permute-start | bytes 196616 | tf_op jit(solution)/shard_map/ppermute | solution.py:23
  44.2 1.3 %collective-permute-start.12 = (bf16[64,512]{1,0:T(8,128)(2,1)S(1)}, bf16[64,512]{1,0:T(8,128)(2,1)S(1)}, u32[]{:S(2)}, u32[]{:S(2)}) collective-permute-start(bf16[64,512]{1,0:T(8,128)(2,1)S(1)} %collective-permute-done.11.refs_4_), channel_id=1, source_target_pairs={{0,1},{1,0},{2,3},{3,2},{4,5},{5,4},{6,7},{7,6},{8,9},{9,8},{10,11... | collective-permute-start | bytes 196616 | tf_op jit(solution)/shard_map/ppermute | solution.py:23
  44.2 1.4 %collective-permute-start.10 = (bf16[64,512]{1,0:T(8,128)(2,1)S(1)}, bf16[64,512]{1,0:T(8,128)(2,1)S(1)}, u32[]{:S(2)}, u32[]{:S(2)}) collective-permute-start(bf16[64,512]{1,0:T(8,128)(2,1)S(1)} %collective-permute-done.9.refs_2_), channel_id=1, source_target_pairs={{0,1},{1,0},{2,3},{3,2},{4,5},{5,4},{6,7},{7,6},{8,9},{9,8},{10,11... | collective-permute-start | bytes 196616 | tf_op jit(solution)/shard_map/ppermute | solution.py:23

commit v2 on v1

v2 whole, which is shorter than its diff:
```python
import functools
import math

import jax
import jax.numpy as jnp
from jax import lax
from jax.experimental import pallas as pl
from jax.experimental.pallas import tpu as pltpu
from jax.sharding import PartitionSpec as P

EPSILON = 1e-06
VMEM_LIMIT = 24 * 1024 * 1024
VMEM_ALL = 60 * 1024 * 1024
F32 = jnp.float32
BF16 = jnp.bfloat16


def whole():
    return pl.BlockSpec(memory_space=pltpu.VMEM)


def swap(value, axis, offset):
    size = lax.axis_size(axis)
    return lax.ppermute(value, axis, [(i, i ^ offset) for i in range(size)])


def slot_select(dest_ref, clip, core, clips, half, cores):
    rows = dest_ref.shape[1]
    named = dest_ref[pl.ds(clip, 1), :]
    onehot = (lax.broadcasted_iota(jnp.int32, (clips, rows), 0) == named).astype(F32)
    earlier = (
        lax.broadcasted_iota(jnp.int32, (rows, rows), 0)
        < lax.broadcasted_iota(jnp.int32, (rows, rows), 1)
    ).astype(F32)
    before = jnp.dot(onehot, earlier, preferred_element_type=F32)
    rank = jnp.sum(before * onehot, axis=0, keepdims=True).astype(jnp.int32)
    slot = ((rank // half) ^ core) * (clips * half) + named * half + rank % half
    slots = cores * clips * half
    return (lax.broadcasted_iota(jnp.int32, (slots, rows), 0) == slot).astype(BF16)


def ffn_kernel(clips, half, cores, steps, dest_hbm, hidden_hbm, weight_hbm, residual_hbm,
               own_ref, send_ref, text_ref, dest_ref, hidden_ref, weight_ref, residual_ref,
               total_ref, sems):
    clip, core = lax.axis_index("clip"), lax.axis_index("tp")
    share = clips * half
    block = hidden_hbm.shape[1] // steps
    first = [
        pltpu.make_async_copy(dest_hbm, dest_ref, sems.at[2 * steps]),
        pltpu.make_async_copy(residual_hbm, residual_ref, sems.at[2 * steps + 1]),
    ]
    hidden_copies, weight_copies = [], []
    for i in range(steps):
        part = pl.ds(i * block, block)
        hidden_copies.append(
            pltpu.make_async_copy(hidden_hbm.at[:, part], hidden_ref.at[:, part], sems.at[i])
        )
        weight_copies.append(
            pltpu.make_async_copy(
                weight_hbm.at[part, :], weight_ref.at[part, :], sems.at[steps + i]
            )
        )
    first[0].start()
    for hidden_copy, weight_copy in zip(hidden_copies, weight_copies):
        hidden_copy.start()
        weight_copy.start()
    first[1].start()
    first[0].wait()
    select = slot_select(dest_ref, clip, core, clips, half, cores)
    for i in range(steps):
        part = pl.ds(i * block, block)
        hidden_copies[i].wait()
        packed = jnp.dot(select, hidden_ref[:, part], preferred_element_type=F32).astype(BF16)
        weight_copies[i].wait()
        product = jnp.dot(packed, weight_ref[part, :], preferred_element_type=F32)
        if i == 0:
            total_ref[...] = product
        elif i < steps - 1:
            total_ref[...] += product
        else:
            own_ref[...] = total_ref[:share, :] + product[:share]
            send_ref[...] = total_ref[share:, :] + product[share:]
    first[1].wait()
    text_ref[...] = jnp.dot(
        select[:share], residual_ref[...], preferred_element_type=F32
    ).astype(BF16)


def ffn(dest, hidden, weight, residual, clips, half, cores):
    rows, depth = hidden.shape
    width = weight.shape[1]
    share = clips * half
    steps = math.gcd(10, depth // 128)
    return pl.pallas_call(
        functools.partial(ffn_kernel, clips, half, cores, steps),
        in_specs=[pl.BlockSpec(memory_space=pltpu.HBM)] * 4,
        out_specs=[whole()] * 3,
        out_shape=[
            jax.ShapeDtypeStruct((share, width), F32),
            jax.ShapeDtypeStruct(((cores - 1) * share, width), F32),
            jax.ShapeDtypeStruct((share, width), BF16),
        ],
        scratch_shapes=[
            pltpu.VMEM(dest.shape, jnp.int32),
            pltpu.VMEM(hidden.shape, BF16),
            pltpu.VMEM(weight.shape, BF16),
            pltpu.VMEM(residual.shape, BF16),
            pltpu.VMEM((cores * share, width), F32),
            pltpu.SemaphoreType.DMA((2 * steps + 2,)),
        ],
        compiler_params=pltpu.CompilerParams(vmem_limit_bytes=VMEM_ALL),
        cost_estimate=pl.CostEstimate(
            flops=2 * cores * share * depth * (width + rows),
            bytes_accessed=2 * depth * (width + rows),
            transcendentals=0,
        ),
    )(dest, hidden, weight, residual)


def keyval_kernel(parts, cores, text_ref, gain_ref, *refs):
    weights, out_ref = refs[:-1], refs[-1]
    width = text_ref.shape[2]
    squares = 0.0
    for s in range(parts):
        wide = text_ref[s].astype(F32)
        squares += jnp.sum(wide * wide, axis=1, keepdims=True)
    scale = lax.rsqrt(squares / (parts * width) + EPSILON)
    totals = [0.0] * cores
    for s in range(parts):
        place = slice(s * width, (s + 1) * width)
        normed = (text_ref[s].astype(F32) * scale * gain_ref[:, place]).astype(BF16)
        for c, weight in enumerate(weights):
            totals[c] += jnp.dot(normed, weight[place, :], preferred_element_type=F32)
    each = weights[0].shape[1]
    for c in range(cores):
        out_ref[:, c * each:(c + 1) * each] = totals[c].astype(BF16)


def attend_kernel(parts, cores, heads_here, half, dest_ref, query_ref, *refs):
    blocks, out_ref = refs[:-1], refs[-1]
    clip, core = lax.axis_index("clip"), lax.axis_index("tp")
    clips = dest_ref.shape[0]
    share = clips * half
    dim = query_ref.shape[1] // (parts * cores * heads_here)
    counts = jnp.sum((dest_ref[...] == clip).astype(jnp.int32), axis=1, keepdims=True)
    lane = lax.broadcasted_iota(jnp.int32, (clips, cores * share), 1)
    source = (lane % share) // half
    limit = jnp.sum(
        jnp.where(lax.broadcasted_iota(jnp.int32, lane.shape, 0) == source, counts, 0),
        axis=0, keepdims=True,
    )
    flat = lax.broadcasted_iota(jnp.int32, (1, cores * share), 1)
    valid = ((flat // share) ^ core) * half + flat % half < limit
    for s in range(parts):
        for c in range(cores):
            for i in range(heads_here):
                head = (s * cores + (core ^ c)) * heads_here + i
                columns = pl.ds(pl.multiple_of(head * dim, dim), dim)
                at = [((c ^ g) * heads_here + i) * 2 * dim for g in range(cores)]
                keys = jnp.concatenate(
                    [blocks[g][s, :, at[g]:at[g] + dim] for g in range(cores)], axis=0
                )
                values = jnp.concatenate(
                    [blocks[g][s, :, at[g] + dim:at[g] + 2 * dim] for g in range(cores)], axis=0
                )
                scores = lax.dot_general(
                    query_ref[:, columns], keys, (((1,), (1,)), ((), ())),
                    preferred_element_type=F32,
                ) * (1.0 / math.sqrt(dim))
                scores = jnp.where(valid, scores, -1e30)
                peak = jnp.max(scores, axis=1, keepdims=True)
                weights = jnp.where(valid, jnp.exp(scores - peak), 0.0)
                probs = (weights / jnp.sum(weights, axis=1, keepdims=True)).astype(BF16)
                out_ref[:, columns] = jnp.dot(
                    probs, values, preferred_element_type=F32
                ).astype(BF16)


def shards(ffn_hidden, ffn_weight, residual, norm_gain, kv_weight, destination, queries):
    clips, parts, cores = lax.axis_size("clip"), lax.axis_size("seq"), lax.axis_size("tp")
    rows = ffn_hidden.shape[0]
    half = rows // min(8, clips) // cores
    share = clips * half
    heads_here = kv_weight.shape[1]
    dest = destination.reshape(clips, rows)
    weights = [kv_weight.reshape(kv_weight.shape[0], heads_here * kv_weight.shape[2])]
    for g in range(1, cores):
        weights.append(swap(weights[0], "tp", g))
    own, send, text = ffn(dest, ffn_hidden, ffn_weight, residual, clips, half, cores)
    for g in range(1, cores):
        own = own + swap(send[(g - 1) * share:g * share], "tp", g)
    text = (text.astype(F32) + own).astype(BF16)
    width = text.shape[1]
    text = jnp.broadcast_to(text[None], (parts, share, width)).reshape(-1, half, width)
    arrived = lax.all_to_all(text, ("seq", "clip"), 0, 0, tiled=True).reshape(parts, share, width)
    keyval = pl.pallas_call(
        functools.partial(keyval_kernel, parts, cores),
        in_specs=[whole()] * (2 + cores),
        out_specs=whole(),
        out_shape=jax.ShapeDtypeStruct((share, cores * weights[0].shape[1]), BF16),
        compiler_params=pltpu.CompilerParams(vmem_limit_bytes=VMEM_LIMIT),
    )(arrived, norm_gain.reshape(1, -1), *weights)
    block = lax.all_to_all(
        jnp.broadcast_to(keyval[None], (parts,) + keyval.shape), "seq", 0, 0, tiled=True
    )
    blocks = [block] + [swap(block, "tp", g) for g in range(1, cores)]
    return pl.pallas_call(
        functools.partial(attend_kernel, parts, cores, heads_here, half),
        in_specs=[whole()] * (2 + len(blocks)),
        out_specs=whole(),
        out_shape=jax.ShapeDtypeStruct(queries.shape, BF16),
        compiler_params=pltpu.CompilerParams(vmem_limit_bytes=VMEM_LIMIT),
    )(dest, queries, *blocks)


def solution(mesh):
    return jax.shard_map(
        shards,
        mesh=mesh,
        in_specs=(
            P("clip", "tp"),
            P("tp", "seq"),
            P("clip", "seq"),
            P(),
            P(None, ("seq", "tp"), None),
            P(),
            P(("clip", "seq", "tp"), None),
        ),
        out_specs=P(("clip", "seq", "tp"), None),
        check_vma=False,
    )
```

time: 49.4 us -> 49.7 us (level)
  blocking collectives: 0 us -> 34.1 us
  waiting for transfers between devices: 18.6 us -> 3.24 us
  starting transfers between devices: 14.3 us -> 0.56 us
  local copies, waits for them, and re-layouts: 2.98 us -> 0.1 us
  Pallas kernels: 13 us -> 10.4 us
  other arithmetic: 0.05 us -> 1.03 us
    all_to_all x0 -> x2, blocking collectives: none -> 34.1 us  [the longest x1 23.3 us: shards(): lax.all_to_all(text, ('seq', 'clip'), 0, 0, tiled=True)]
    ppermute x15 -> x3, waiting for transfers between devices: 18.6 us -> 3.24 us  [swap(): return lax.ppermute(value, axis, [(i, i ^ offset) for i in range(size)])]
    ppermute x15 -> x3, starting transfers between devices: 14.3 us -> 0.56 us  [swap(): return lax.ppermute(value, axis, [(i, i ^ offset) for i in range(size)])]
    unnamed x14 -> x8, local copies, waits for them, and re-layouts: 2.97 us -> 0.03 us
    pallas_call x1, Pallas kernels: 8.65 us -> 6 us  [ffn(): pl.pallas_call(functools.partial(ffn_kernel, clips, half, cores, steps),...]
    convert_element_type x1, other arithmetic: 0.04 us -> 1.03 us  [shards(): text = (text.astype(F32) + own).astype(BF16)]
  transfers between devices with their start and end apart: 15 -> 3, of which waited for: 10 -> 2; matrix products, arithmetic and copies ran while one was open for 0% -> 2% of each run, Pallas kernels for 18% -> 12%
where the time goes in v2:
time: 49.7 us; the launch traced here: 49.4 us
  blocking collectives  34.1 us (69%)
  Pallas kernels  10.4 us (21%)
  waiting for transfers between devices  3.24 us (7%)
  other arithmetic  1.03 us (2%)
  starting transfers between devices  0.56 us (1%)
    all_to_all x1, blocking collectives, shards(): lax.all_to_all(text, ('seq', 'clip'), 0, 0, tiled=True)  23.3 us
    all_to_all x1, blocking collectives, shards(): lax.all_to_all(jnp.broadcast_to(keyval[None], (parts,) + keyval.shape), '...  10.8 us
    pallas_call x1, Pallas kernels, ffn(): pl.pallas_call(functools.partial(ffn_kernel, clips, half, cores, steps),...  6 us
    pallas_call x1, Pallas kernels, shards(): pl.pallas_call(functools.partial(attend_kernel, parts, cores, heads_here,...  3.39 us
    ppermute x3, waiting for transfers between devices, swap(): return lax.ppermute(value, axis, [(i, i ^ offset) for i in range(size)])  3.24 us
    convert_element_type x1, other arithmetic, shards(): text = (text.astype(F32) + own).astype(BF16)  1.03 us
  transfers between devices with their start and end apart: 3, of which 2 were waited for; matrix products, arithmetic and copies ran while one was open for 2% of the time, Pallas kernels for 12%

profile of v2, /device:TPU:0, one launch (start us, length us, event | category | flops | bytes accessed | tf_op | source)
XLA Modules:
  0.0 49.4 jit_solution(17463404590361497902)
XLA Ops:
  0.0 0.5 collective-permute-start.1
  0.5 6.0 %shard_map.73 = (f32[64,1024]{1,0:T(8,128)}, f32[64,1024]{1,0:T(8,128)}, bf16[64,1024]{1,0:T(8,128)(2,1)}) custom-call(s32[4,128]{1,0:T(4,128)} %bitcast.9, bf16[128,5120]{1,0:T(8,128)(2,1)} %hidden_hbm.1, bf16[5120,1024]{1,0:T(8,128)(2,1)} %weight_hbm.1, bf16[128,1024]{1,0:T(8,128)(2,1)} %residual_hbm.1), custom_call_target="tpu_custom_call" | custom-call | flops 1509949440 | bytes 11796480 | tf_op jit(solution)/shard_map/pallas_call | solution.py:94
  6.5 0.0 copy-start
  6.5 0.0 copy-start.2
  6.5 0.1 collective-permute-start
  6.6 1.7 %collective-permute-done = f32[64,1024]{1,0:T(8,128)S(1)} collective-permute-done((f32[64,1024]{1,0:T(8,128)}, f32[64,1024]{1,0:T(8,128)S(1)}, u32[]{:S(2)}, u32[]{:S(2)}) %collective-permute-start) | collective-permute-done | bytes 262176 | tf_op jit(solution)/shard_map/ppermute | solution.py:24
  8.3 1.0 %add_convert_fusion = bf16[64,1024]{1,0:T(8,128)(2,1)S(1)} fusion(f32[64,1024]{1,0:T(8,128)} %get-tuple-element.9, f32[64,1024]{1,0:T(8,128)S(1)} %collective-permute-done, bf16[64,1024]{1,0:T(8,128)(2,1)} %get-tuple-element.8), kind=kLoop, calls=%fused_computation | loop fusion | flops 262144 | bytes 786432 | tf_op jit(solution)/shard_map/convert_element_type | solution.py:192
  9.3 0.1 broadcast_in_dim.4
  9.4 23.3 %all_to_all.10 = bf16[16,16,1024]{2,1,0:T(8,128)(2,1)S(1)} all-to-all(bf16[16,16,1024]{2,1,0:T(8,128)(2,1)S(1)} %bitcast.11), channel_id=1, replica_groups=mesh['clip'=4,'seq'=4,'tp'=2] {'seq','clip'}, dimensions={0} | all-to-all | bytes 1048576 | tf_op jit(solution)/shard_map/all_to_all | solution.py:195
  32.7 0.0 collective-permute-done.1.refs_1_
  32.7 0.0 copy-done
  32.7 0.0 copy-done.2
  32.7 0.0 copy-start.1
  32.7 0.0 copy-start.3
  32.7 1.0 %shard_map.74 = bf16[64,512]{1,0:T(8,128)(2,1)S(1)} custom-call(bf16[4,64,1024]{2,1,0:T(8,128)(2,1)S(1)} %bitcast.7, f32[1,4096]{1,0:T(1,128)S(1)} %bitcast.8, bf16[4096,256]{1,0:T(8,128)(2,1)S(1)} %bitcast.6, bf16[4096,256]{1,0:T(8,128)(2,1)S(1)} %collective-permute-done.1.refs_1_), custom_call_target="tpu_custom_call" | custom-call | tf_op jit(solution)/shard_map/pallas_call | solution.py:196
  33.7 10.8 %all_to_all.11.refs_0_ = bf16[4,64,512]{2,1,0:T(8,128)(2,1)S(1)} all-to-all(bf16[4,64,512]{2,1,0:T(8,128)(2,1)S(1)} %broadcast_in_dim.5), channel_id=1, replica_groups=mesh['clip'=4,'seq'=4,'tp'=2] {'seq'}, dimensions={0} | all-to-all | bytes 524288 | tf_op jit(solution)/shard_map/all_to_all | solution.py:203
  44.5 0.0 collective-permute-start.2
  44.5 1.5 %collective-permute-done.2.refs_1_ = bf16[4,64,512]{2,1,0:T(8,128)(2,1)S(1)} collective-permute-done((bf16[4,64,512]{2,1,0:T(8,128)(2,1)S(1)}, bf16[4,64,512]{2,1,0:T(8,128)(2,1)S(1)}, u32[]{:S(2)}, u32[]{:S(2)}) %collective-permute-start.2) | collective-permute-done | bytes 262176 | tf_op jit(solution)/shard_map/ppermute | solution.py:24
  46.0 0.0 copy-done.1
  46.0 0.0 copy-done.3
  46.1 3.4 %shard_map.75 = bf16[128,1024]{1,0:T(8,128)(2,1)} custom-call(s32[4,128]{1,0:T(4,128)S(1)} %bitcast.10, bf16[128,1024]{1,0:T(8,128)(2,1)S(1)} %copy-done.1, bf16[4,64,512]{2,1,0:T(8,128)(2,1)S(1)} %all_to_all.11.refs_0_, bf16[4,64,512]{2,1,0:T(8,128)(2,1)S(1)} %collective-permute-done.2.refs_1_), custom_call_target="tpu_custom_call" | custom-call | tf_op jit(solution)/shard_map/pallas_call | solution.py:207
  (1 shorter events, 0.0 us)
Async XLA Ops:
  0.0 32.7 %collective-permute-start.1 = (bf16[4096,256]{1,0:T(8,128)(2,1)}, bf16[4096,256]{1,0:T(8,128)(2,1)S(1)}, u32[]{:S(2)}, u32[]{:S(2)}) collective-permute-start(bf16[4096,256]{1,0:T(8,128)(2,1)} %bitcast.5), channel_id=1, source_target_pairs={{0,1},{1,0},{2,3},{3,2},{4,5},{5,4},{6,7},{7,6},{8,9},{9,8},{10,11... | collective-permute-start | bytes 6291464 | tf_op jit(solution)/shard_map/ppermute | solution.py:24
  6.5 26.2 %copy-start = (bf16[4096,1,256]{2,0,1:T(8,128)(2,1)S(1)}, bf16[4096,1,256]{2,0,1:T(8,128)(2,1)}, u32[]{:S(2)}) copy-start(bf16[4096,1,256]{2,0,1:T(8,128)(2,1)} %param.11) | copy-start | bytes 6291460
  6.5 26.2 %copy-start.2 = (f32[4096]{0:T(1024)S(1)}, f32[4096]{0:T(1024)}, u32[]{:S(2)}) copy-start(f32[4096]{0:T(1024)} %param.10) | copy-start | bytes 49156
  6.5 1.8 %collective-permute-start = (f32[64,1024]{1,0:T(8,128)}, f32[64,1024]{1,0:T(8,128)S(1)}, u32[]{:S(2)}, u32[]{:S(2)}) collective-permute-start(f32[64,1024]{1,0:T(8,128)} %get-tuple-element.10), channel_id=1, source_target_pairs={{0,1},{1,0},{2,3},{3,2},{4,5},{5,4},{6,7},{7,6},{8,9},{9,8},{10,11... | collective-permute-start | bytes 786440 | tf_op jit(solution)/shard_map/ppermute | solution.py:24
  32.7 13.4 %copy-start.1 = (bf16[128,1024]{1,0:T(8,128)(2,1)S(1)}, bf16[128,1024]{1,0:T(8,128)(2,1)}, u32[]{:S(2)}) copy-start(bf16[128,1024]{1,0:T(8,128)(2,1)} %query_ref.1) | copy-start | bytes 786436
  32.7 13.3 %copy-start.3 = (s32[512,1]{0,1:T(1,128)S(1)}, s32[512,1]{0,1:T(1,128)}, u32[]{:S(2)}) copy-start(s32[512,1]{0,1:T(1,128)} %param.12) | copy-start | bytes 6148
  44.5 1.5 %collective-permute-start.2 = (bf16[4,64,512]{2,1,0:T(8,128)(2,1)S(1)}, bf16[4,64,512]{2,1,0:T(8,128)(2,1)S(1)}, u32[]{:S(2)}, u32[]{:S(2)}) collective-permute-start(bf16[4,64,512]{2,1,0:T(8,128)(2,1)S(1)} %all_to_all.11.refs_0_), channel_id=1, source_target_pairs={{0,1},{1,0},{2,3},{3,2},{4,5},{5,4},{6,7},{7,6},{8,9},{9,8},{10,11... | collective-permute-start | bytes 786440 | tf_op jit(solution)/shard_map/ppermute | solution.py:24

commit v3 on v1

v3 whole, which is shorter than its diff:
```python
import functools
import math

import jax
import jax.numpy as jnp
from jax import lax
from jax.experimental import pallas as pl
from jax.experimental.pallas import tpu as pltpu
from jax.sharding import PartitionSpec as P

EPSILON = 1e-06
VMEM_LIMIT = 24 * 1024 * 1024
VMEM_ALL = 60 * 1024 * 1024
F32 = jnp.float32
BF16 = jnp.bfloat16


def whole():
    return pl.BlockSpec(memory_space=pltpu.VMEM)


def swap(value, axis, offset):
    size = lax.axis_size(axis)
    return lax.ppermute(value, axis, [(i, i ^ offset) for i in range(size)])


def route(value, place):
    clips, cores = lax.axis_size("clip"), lax.axis_size("tp")
    pairs = [
        (i * cores + t, (i ^ (t * (clips // cores) + place)) * cores + t)
        for i in range(clips) for t in range(cores)
    ]
    return lax.ppermute(value, ("clip", "tp"), pairs)


def slot_select(dest_ref, clip, core, capacity, cores):
    clips, rows = dest_ref.shape
    named = dest_ref[pl.ds(clip, 1), :]
    onehot = (lax.broadcasted_iota(jnp.int32, (clips, rows), 0) == named).astype(F32)
    earlier = (
        lax.broadcasted_iota(jnp.int32, (rows, rows), 0)
        < lax.broadcasted_iota(jnp.int32, (rows, rows), 1)
    ).astype(F32)
    before = jnp.dot(onehot, earlier, preferred_element_type=F32)
    rank = jnp.sum(before * onehot, axis=0, keepdims=True).astype(jnp.int32)
    away = (named ^ clip) ^ (core * (clips // cores))
    slot = away * capacity + rank
    return (lax.broadcasted_iota(jnp.int32, (clips * capacity, rows), 0) == slot).astype(BF16)


def ffn_kernel(capacity, cores, steps, dest_hbm, hidden_hbm, weight_hbm, residual_hbm,
               own_ref, send_ref, text_ref, dest_ref, hidden_ref, weight_ref, residual_ref,
               packed_ref, total_ref, sems):
    clip, core = lax.axis_index("clip"), lax.axis_index("tp")
    share = own_ref.shape[0]
    block = hidden_hbm.shape[1] // steps
    get_dest = pltpu.make_async_copy(dest_hbm, dest_ref, sems.at[steps])
    get_hidden = pltpu.make_async_copy(hidden_hbm, hidden_ref, sems.at[steps + 1])
    get_residual = pltpu.make_async_copy(residual_hbm, residual_ref, sems.at[steps + 2])
    get_weight = [
        pltpu.make_async_copy(
            weight_hbm.at[pl.ds(i * block, block), :],
            weight_ref.at[pl.ds(i * block, block), :],
            sems.at[i],
        )
        for i in range(steps)
    ]
    for copy in [get_dest, get_hidden] + get_weight + [get_residual]:
        copy.start()
    get_dest.wait()
    select = slot_select(dest_ref, clip, core, capacity, cores)
    get_hidden.wait()
    packed_ref[...] = jnp.dot(select, hidden_ref[...], preferred_element_type=F32).astype(BF16)
    for i in range(steps):
        part = pl.ds(i * block, block)
        get_weight[i].wait()
        product = jnp.dot(packed_ref[:, part], weight_ref[part, :], preferred_element_type=F32)
        if i == 0:
            total_ref[...] = product
        elif i < steps - 1:
            total_ref[...] += product
        else:
            own_ref[...] = total_ref[:share, :] + product[:share]
            send_ref[...] = total_ref[share:, :] + product[share:]
    get_residual.wait()
    text_ref[...] = jnp.dot(
        select[:share], residual_ref[...], preferred_element_type=F32
    ).astype(BF16)


def ffn(dest, hidden, weight, residual, capacity, cores):
    rows, depth = hidden.shape
    width = weight.shape[1]
    slots = dest.shape[0] * capacity
    share = slots // cores
    steps = math.gcd(5, depth // 128)
    return pl.pallas_call(
        functools.partial(ffn_kernel, capacity, cores, steps),
        in_specs=[pl.BlockSpec(memory_space=pltpu.HBM)] * 4,
        out_specs=[whole()] * 3,
        out_shape=[
            pltpu.VMEM((share, width), F32),
            pltpu.VMEM((slots - share, width), F32),
            pltpu.VMEM((share, width), BF16),
        ],
        scratch_shapes=[
            pltpu.VMEM(dest.shape, jnp.int32),
            pltpu.VMEM(hidden.shape, BF16),
            pltpu.VMEM(weight.shape, BF16),
            pltpu.VMEM(residual.shape, BF16),
            pltpu.VMEM((slots, depth), BF16),
            pltpu.VMEM((slots, width), F32),
            pltpu.SemaphoreType.DMA((steps + 3,)),
        ],
        compiler_params=pltpu.CompilerParams(vmem_limit_bytes=VMEM_ALL),
        cost_estimate=pl.CostEstimate(
            flops=2 * slots * depth * (width + rows),
            bytes_accessed=2 * depth * (width + rows),
            transcendentals=0,
        ),
    )(dest, hidden, weight, residual)


def keyval_kernel(parts, cores, *refs):
    texts, (gain_ref, *weights), out_ref = refs[:parts], refs[parts:-1], refs[-1]
    seq = lax.axis_index("seq")
    width = texts[0].shape[1]
    squares = 0.0
    for text in texts:
        wide = text[...].astype(F32)
        squares += jnp.sum(wide * wide, axis=1, keepdims=True)
    scale = lax.rsqrt(squares / (parts * width) + EPSILON)
    totals = [0.0] * cores
    for k, text in enumerate(texts):
        place = pl.ds(pl.multiple_of((seq ^ k) * width, width), width)
        normed = (text[...].astype(F32) * scale * gain_ref[:, place]).astype(BF16)
        for c, weight in enumerate(weights):
            totals[c] += jnp.dot(normed, weight[place, :], preferred_element_type=F32)
    each = weights[0].shape[1]
    for c in range(cores):
        out_ref[:, c * each:(c + 1) * each] = totals[c].astype(BF16)


def attend_kernel(parts, cores, heads_here, capacity, dest_ref, query_ref, *refs):
    blocks, out_ref = refs[:-1], refs[-1]
    clip, seq, core = lax.axis_index("clip"), lax.axis_index("seq"), lax.axis_index("tp")
    clips = dest_ref.shape[0]
    slots = clips * capacity
    dim = query_ref.shape[1] // (parts * cores * heads_here)
    counts = jnp.sum((dest_ref[...] == clip).astype(jnp.int32), axis=1, keepdims=True)
    lane = lax.broadcasted_iota(jnp.int32, (clips, slots), 1)
    source = (lane // capacity) ^ (core * (clips // cores)) ^ clip
    limit = jnp.sum(
        jnp.where(lax.broadcasted_iota(jnp.int32, lane.shape, 0) == source, counts, 0),
        axis=0, keepdims=True,
    )
    valid = lax.broadcasted_iota(jnp.int32, (1, slots), 1) % capacity < limit
    heads = [(k, c, i) for k in range(parts) for c in range(cores) for i in range(heads_here)]

    def columns(head):
        k, c, i = head
        at = ((seq ^ k) * cores + (core ^ c)) * heads_here + i
        return pl.ds(pl.multiple_of(at * dim, dim), dim)

    def stored(head, offset):
        k, c, i = head
        parts_of = []
        for g in range(cores):
            at = ((c ^ g) * heads_here + i) * 2 * dim + offset
            parts_of.append(blocks[k * cores + g][:, at:at + dim])
        return jnp.concatenate(parts_of, axis=0)

    group = 8
    for first in range(0, len(heads), group):
        some = heads[first:first + group]
        scores = [
            lax.dot_general(
                query_ref[:, columns(head)], stored(head, 0), (((1,), (1,)), ((), ())),
                preferred_element_type=F32,
            )
            for head in some
        ]
        scores = [jnp.where(valid, score * (1.0 / math.sqrt(dim)), -1e30) for score in scores]
        peaks = [jnp.max(score, axis=1, keepdims=True) for score in scores]
        weights = [
            jnp.where(valid, jnp.exp(score - peak), 0.0) for score, peak in zip(scores, peaks)
        ]
        sums = [jnp.sum(weight, axis=1, keepdims=True) for weight in weights]
        probs = [(weight / total).astype(BF16) for weight, total in zip(weights, sums)]
        results = [
            jnp.dot(prob, stored(head, dim), preferred_element_type=F32).astype(BF16)
            for prob, head in zip(probs, some)
        ]
        for head, result in zip(some, results):
            out_ref[:, columns(head)] = result


def shards(ffn_hidden, ffn_weight, residual, norm_gain, kv_weight, destination, queries):
    clips, parts, cores = lax.axis_size("clip"), lax.axis_size("seq"), lax.axis_size("tp")
    rows = ffn_hidden.shape[0]
    capacity = rows // min(8, clips)
    share = clips * capacity // cores
    heads_here = kv_weight.shape[1]
    dest = destination.reshape(clips, rows)
    weight = kv_weight.reshape(kv_weight.shape[0], heads_here * kv_weight.shape[2])
    own, send, text = ffn(dest, ffn_hidden, ffn_weight, residual, capacity, cores)
    for g in range(1, cores):
        own = own + swap(send[(g - 1) * share:g * share], "tp", g)
    text = (text.astype(F32) + own).astype(BF16)
    weight, text = lax.optimization_barrier((weight, text))
    weights = [weight] + [swap(weight, "tp", g) for g in range(1, cores)]
    arrived = [
        route(text[i * capacity:(i + 1) * capacity], i) for i in range(clips // cores)
    ]
    arrived = jnp.concatenate(arrived, axis=0)
    texts = [arrived] + [swap(arrived, "seq", k) for k in range(1, parts)]
    keyval = pl.pallas_call(
        functools.partial(keyval_kernel, parts, cores),
        in_specs=[whole()] * (parts + 1 + cores),
        out_specs=whole(),
        out_shape=jax.ShapeDtypeStruct((share, cores * weight.shape[1]), BF16),
        compiler_params=pltpu.CompilerParams(vmem_limit_bytes=VMEM_LIMIT),
    )(*texts, norm_gain.reshape(1, -1), *weights)
    blocks = []
    for k in range(parts):
        block = swap(keyval, "seq", k) if k else keyval
        blocks += [block] + [swap(block, "tp", g) for g in range(1, cores)]
    return pl.pallas_call(
        functools.partial(attend_kernel, parts, cores, heads_here, capacity),
        in_specs=[whole()] * (2 + len(blocks)),
        out_specs=whole(),
        out_shape=jax.ShapeDtypeStruct(queries.shape, BF16),
        compiler_params=pltpu.CompilerParams(vmem_limit_bytes=VMEM_LIMIT),
    )(dest, queries, *blocks)


def solution(mesh):
    return jax.shard_map(
        shards,
        mesh=mesh,
        in_specs=(
            P("clip", "tp"),
            P("tp", "seq"),
            P("clip", "seq"),
            P(),
            P(None, ("seq", "tp"), None),
            P(),
            P(("clip", "seq", "tp"), None),
        ),
        out_specs=P(("clip", "seq", "tp"), None),
        check_vma=False,
    )
```

time: 49.4 us -> 41.9 us (0.85)
  Pallas kernels: 13 us -> 7.67 us
  local copies, waits for them, and re-layouts: 2.98 us -> 0.04 us
  waiting for transfers between devices: 18.6 us -> 19.9 us
    ppermute x15 -> x12, starting transfers between devices: 14.3 us -> 10.7 us  [swap(): return lax.ppermute(value, axis, [(i, i ^ offset) for i in range(size)])]
    ppermute x0 -> x2, starting transfers between devices: none -> 3.35 us  [route(): return lax.ppermute(value, ('clip', 'tp'), pairs)]
    pallas_call x1, Pallas kernels: 8.65 us -> 5.31 us  [ffn(): pl.pallas_call(functools.partial(ffn_kernel, capacity, cores, steps), in_...]
    unnamed x14 -> x9, local copies, waits for them, and re-layouts: 2.97 us -> 0.03 us
    ppermute x0 -> x2, waiting for transfers between devices: none -> 2.24 us  [route(): return lax.ppermute(value, ('clip', 'tp'), pairs)]
    pallas_call x1, Pallas kernels: 3.39 us -> 1.39 us  [shards(): pl.pallas_call(functools.partial(attend_kernel, parts, cores, heads_here,...]
    ppermute x15 -> x12, waiting for transfers between devices: 18.6 us -> 17.6 us  [swap(): return lax.ppermute(value, axis, [(i, i ^ offset) for i in range(size)])]
  transfers between devices with their start and end apart: 15 -> 14, of which waited for: 10 -> 8; matrix products, arithmetic and copies ran while one was open for 0% -> 0% of each run, Pallas kernels for 18% -> 0%
where the time goes in v3:
time: 41.9 us; the launch traced here: 41.8 us
  waiting for transfers between devices  19.9 us (47%)
  starting transfers between devices  14 us (33%)
  Pallas kernels  7.67 us (18%)
    ppermute x12, waiting for transfers between devices, swap(): return lax.ppermute(value, axis, [(i, i ^ offset) for i in range(size)])  17.6 us
    ppermute x12, starting transfers between devices, swap(): return lax.ppermute(value, axis, [(i, i ^ offset) for i in range(size)])  10.7 us
    pallas_call x1, Pallas kernels, ffn(): pl.pallas_call(functools.partial(ffn_kernel, capacity, cores, steps), in_...  5.31 us
    ppermute x2, starting transfers between devices, route(): return lax.ppermute(value, ('clip', 'tp'), pairs)  3.35 us
    ppermute x2, waiting for transfers between devices, route(): return lax.ppermute(value, ('clip', 'tp'), pairs)  2.24 us
    pallas_call x1, Pallas kernels, shards(): pl.pallas_call(functools.partial(attend_kernel, parts, cores, heads_here,...  1.39 us
    pallas_call x1, Pallas kernels, shards(): pl.pallas_call(functools.partial(keyval_kernel, parts, cores), in_specs=[...  0.97 us
  transfers between devices with their start and end apart: 14, of which 8 were waited for; matrix products, arithmetic and copies ran while one was open for 0% of the time, Pallas kernels for 0%

profile of v3, /device:TPU:0, one launch (start us, length us, event | category | flops | bytes accessed | tf_op | source)
XLA Modules:
  0.0 41.8 jit_solution(16473022072936625641)
XLA Ops:
  0.0 0.0 copy-start
  0.0 0.0 copy-start.2
  0.0 5.3 %shard_map.73 = (f32[64,1024]{1,0:T(8,128)S(1)}, f32[64,1024]{1,0:T(8,128)S(1)}, bf16[64,1024]{1,0:T(8,128)(2,1)S(1)}) custom-call(s32[4,128]{1,0:T(4,128)} %bitcast.6, bf16[128,5120]{1,0:T(8,128)(2,1)} %hidden_hbm.1, bf16[5120,1024]{1,0:T(8,128)(2,1)} %weight_hbm.1, bf16[128,1024]{1,0:T(8,128)(2,1)} %residual_hbm.1), custom_call_target="tpu_custom_call" | custom-call | flops 1509949440 | bytes 11796480 | tf_op jit(solution)/shard_map/pallas_call | solution.py:97
  5.3 0.5 %collective-permute-start = (f32[64,1024]{1,0:T(8,128)S(1)}, f32[64,1024]{1,0:T(8,128)S(1)}, u32[]{:S(2)}, u32[]{:S(2)}) collective-permute-start(f32[64,1024]{1,0:T(8,128)S(1)} %get-tuple-element.12), channel_id=1, source_target_pairs={{0,1},{1,0},{2,3},{3,2},{4,5},{5,4},{6,7},{7,6},{8,9},{9,8},{10,11... | collective-permute-start | bytes 786440 | tf_op jit(solution)/shard_map/ppermute | solution.py:24
  5.8 1.2 %collective-permute-done = f32[64,1024]{1,0:T(8,128)S(1)} collective-permute-done((f32[64,1024]{1,0:T(8,128)S(1)}, f32[64,1024]{1,0:T(8,128)S(1)}, u32[]{:S(2)}, u32[]{:S(2)}) %collective-permute-start) | collective-permute-done | bytes 262176 | tf_op jit(solution)/shard_map/ppermute | solution.py:24
  7.1 0.0 copy-done
  7.1 0.4 %collective-permute-start.6 = (bf16[4096,256]{1,0:T(8,128)(2,1)S(1)}, bf16[4096,256]{1,0:T(8,128)(2,1)S(1)}, u32[]{:S(2)}, u32[]{:S(2)}) collective-permute-start(bf16[4096,256]{1,0:T(8,128)(2,1)S(1)} %bitcast.3), channel_id=1, source_target_pairs={{0,1},{1,0},{2,3},{3,2},{4,5},{5,4},{6,7},{7,6},{8,9},{9,8},{10,11... | collective-permute-start | bytes 6291464 | tf_op jit(solution)/shard_map/ppermute | solution.py:24
  7.5 0.7 %collective-permute-start.1 = (bf16[32,1024]{1,0:T(8,128)(2,1)S(1)}, bf16[32,1024]{1,0:T(8,128)(2,1)S(1)}, u32[]{:S(2)}, u32[]{:S(2)}) collective-permute-start(bf16[32,1024]{1,0:T(8,128)(2,1)S(1)} %get-tuple-element.16), channel_id=1, source_target_pairs={{0,0},{1,17},{8,8},{9,25},{16,16},{17,1},{24,24},{25,9},{2,2},{3,1... | collective-permute-start | bytes 196616 | tf_op jit(solution)/shard_map/ppermute | solution.py:33
  8.2 2.7 %collective-permute-start.2 = (bf16[32,1024]{1,0:T(8,128)(2,1)S(1)}, bf16[32,1024]{1,0:T(8,128)(2,1)S(1)}, u32[]{:S(2)}, u32[]{:S(2)}) collective-permute-start(bf16[32,1024]{1,0:T(8,128)(2,1)S(1)} %get-tuple-element.15), channel_id=1, source_target_pairs={{0,8},{1,25},{8,0},{9,17},{16,24},{17,9},{24,16},{25,1},{2,10},{3,... | collective-permute-start | bytes 196616 | tf_op jit(solution)/shard_map/ppermute | solution.py:33
  10.9 0.0 collective-permute-done.1
  10.9 2.2 %collective-permute-done.2 = bf16[32,1024]{1,0:T(8,128)(2,1)S(1)} collective-permute-done((bf16[32,1024]{1,0:T(8,128)(2,1)S(1)}, bf16[32,1024]{1,0:T(8,128)(2,1)S(1)}, u32[]{:S(2)}, u32[]{:S(2)}) %collective-permute-start.2) | collective-permute-done | bytes 65568 | tf_op jit(solution)/shard_map/ppermute | solution.py:33
  13.1 4.1 %collective-permute-start.5 = (bf16[64,1024]{1,0:T(8,128)(2,1)S(1)}, bf16[64,1024]{1,0:T(8,128)(2,1)S(1)}, u32[]{:S(2)}, u32[]{:S(2)}) collective-permute-start(bf16[64,1024]{1,0:T(8,128)(2,1)S(1)} %constant_dynamic-update-slice_fusion.refs_0_), channel_id=1, source_target_pairs={{0,6},{2,4},{4,2},{6,0},{1,7},{3,5},{5,3},{7,1},{8,14},{10,12},{12... | collective-permute-start | bytes 393224 | tf_op jit(solution)/shard_map/ppermute | solution.py:24
  17.3 0.0 collective-permute-start.4
  17.3 0.6 %collective-permute-start.3 = (bf16[64,1024]{1,0:T(8,128)(2,1)S(1)}, bf16[64,1024]{1,0:T(8,128)(2,1)S(1)}, u32[]{:S(2)}, u32[]{:S(2)}) collective-permute-start(bf16[64,1024]{1,0:T(8,128)(2,1)S(1)} %constant_dynamic-update-slice_fusion.refs_0_), channel_id=1, source_target_pairs={{0,2},{2,0},{4,6},{6,4},{1,3},{3,1},{5,7},{7,5},{8,10},{10,8},{12,... | collective-permute-start | bytes 393224 | tf_op jit(solution)/shard_map/ppermute | solution.py:24
  17.9 2.4 %collective-permute-done.5.refs_3_ = bf16[64,1024]{1,0:T(8,128)(2,1)S(1)} collective-permute-done((bf16[64,1024]{1,0:T(8,128)(2,1)S(1)}, bf16[64,1024]{1,0:T(8,128)(2,1)S(1)}, u32[]{:S(2)}, u32[]{:S(2)}) %collective-permute-start.5) | collective-permute-done | bytes 131104 | tf_op jit(solution)/shard_map/ppermute | solution.py:24
  20.3 8.4 %collective-permute-done.4.refs_2_ = bf16[64,1024]{1,0:T(8,128)(2,1)S(1)} collective-permute-done((bf16[64,1024]{1,0:T(8,128)(2,1)S(1)}, bf16[64,1024]{1,0:T(8,128)(2,1)S(1)}, u32[]{:S(2)}, u32[]{:S(2)}) %collective-permute-start.4) | collective-permute-done | bytes 131104 | tf_op jit(solution)/shard_map/ppermute | solution.py:24
  28.7 0.0 collective-permute-done.3.refs_1_
  28.7 0.0 collective-permute-done.6.refs_6_
  28.7 0.0 copy-done.2
  28.7 0.0 copy-start.1
  28.7 0.0 copy-start.3
  28.8 1.0 %shard_map.74.refs_0_ = bf16[64,512]{1,0:T(8,128)(2,1)S(1)} custom-call(bf16[64,1024]{1,0:T(8,128)(2,1)S(1)} %constant_dynamic-update-slice_fusion.refs_0_, bf16[64,1024]{1,0:T(8,128)(2,1)S(1)} %collective-permute-done.3.refs_1_, bf16[64,1024]{1,0:T(8,128)(2,1)S(1)} %collective-permute-done.4.refs_2_, bf16[64,1024]{1,0:T(8,128)(2,1)S(1)} %collective-permute-done.5.refs_3_, ...), custom_call_target="tpu_custom_call" | custom-call | tf_op jit(solution)/shard_map/pallas_call | solution.py:217
  29.7 1.6 %collective-permute-start.12 = (bf16[64,512]{1,0:T(8,128)(2,1)S(1)}, bf16[64,512]{1,0:T(8,128)(2,1)S(1)}, u32[]{:S(2)}, u32[]{:S(2)}) collective-permute-start(bf16[64,512]{1,0:T(8,128)(2,1)S(1)} %shard_map.74.refs_0_), channel_id=1, source_target_pairs={{0,6},{2,4},{4,2},{6,0},{1,7},{3,5},{5,3},{7,1},{8,14},{10,12},{12... | collective-permute-start | bytes 196616 | tf_op jit(solution)/shard_map/ppermute | solution.py:24
  31.3 0.0 collective-permute-start.10
  31.3 2.9 %collective-permute-start.8 = (bf16[64,512]{1,0:T(8,128)(2,1)S(1)}, bf16[64,512]{1,0:T(8,128)(2,1)S(1)}, u32[]{:S(2)}, u32[]{:S(2)}) collective-permute-start(bf16[64,512]{1,0:T(8,128)(2,1)S(1)} %shard_map.74.refs_0_), channel_id=1, source_target_pairs={{0,2},{2,0},{4,6},{6,4},{1,3},{3,1},{5,7},{7,5},{8,10},{10,8},{12,... | collective-permute-start | bytes 196616 | tf_op jit(solution)/shard_map/ppermute | solution.py:24
  34.2 0.0 collective-permute-start.7
  34.2 2.4 %collective-permute-done.12.refs_6_ = bf16[64,512]{1,0:T(8,128)(2,1)S(1)} collective-permute-done((bf16[64,512]{1,0:T(8,128)(2,1)S(1)}, bf16[64,512]{1,0:T(8,128)(2,1)S(1)}, u32[]{:S(2)}, u32[]{:S(2)}) %collective-permute-start.12) | collective-permute-done | bytes 65568 | tf_op jit(solution)/shard_map/ppermute | solution.py:24
  36.6 0.0 collective-permute-start.13
  36.6 2.4 %collective-permute-done.10.refs_4_ = bf16[64,512]{1,0:T(8,128)(2,1)S(1)} collective-permute-done((bf16[64,512]{1,0:T(8,128)(2,1)S(1)}, bf16[64,512]{1,0:T(8,128)(2,1)S(1)}, u32[]{:S(2)}, u32[]{:S(2)}) %collective-permute-start.10) | collective-permute-done | bytes 65568 | tf_op jit(solution)/shard_map/ppermute | solution.py:24
  38.9 0.1 collective-permute-start.11
  39.1 0.0 collective-permute-done.8.refs_2_
  39.1 0.4 collective-permute-start.9
  39.5 0.0 collective-permute-done.7.refs_1_
  39.5 0.0 collective-permute-done.13.refs_7_
  39.5 0.7 %collective-permute-done.11.refs_5_ = bf16[64,512]{1,0:T(8,128)(2,1)S(1)} collective-permute-done((bf16[64,512]{1,0:T(8,128)(2,1)S(1)}, bf16[64,512]{1,0:T(8,128)(2,1)S(1)}, u32[]{:S(2)}, u32[]{:S(2)}) %collective-permute-start.11) | collective-permute-done | bytes 65568 | tf_op jit(solution)/shard_map/ppermute | solution.py:24
  40.2 0.2 collective-permute-done.9.refs_3_
  40.4 0.0 copy-done.1
  40.4 0.0 copy-done.3
  40.4 1.4 %shard_map.75 = bf16[128,1024]{1,0:T(8,128)(2,1)} custom-call(s32[4,128]{1,0:T(4,128)S(1)} %bitcast.7, bf16[128,1024]{1,0:T(8,128)(2,1)S(1)} %copy-done.1, bf16[64,512]{1,0:T(8,128)(2,1)S(1)} %shard_map.74.refs_0_, bf16[64,512]{1,0:T(8,128)(2,1)S(1)} %collective-permute-done.7.refs_1_, bf16[64,512]{1,0:T(8,128)(2,1)S(1)} %collective-permute-done.8.refs_2_, ...), custom_call_target="tpu_custom_call" | custom-call | tf_op jit(solution)/shard_map/pallas_call | solution.py:228
  (4 shorter events, 0.1 us)
Async XLA Ops:
  0.0 7.1 %copy-start = (bf16[4096,1,256]{2,0,1:T(8,128)(2,1)S(1)}, bf16[4096,1,256]{2,0,1:T(8,128)(2,1)}, u32[]{:S(2)}) copy-start(bf16[4096,1,256]{2,0,1:T(8,128)(2,1)} %param.11) | copy-start | bytes 6291460
  0.0 28.7 %copy-start.2 = (f32[4096]{0:T(1024)S(1)}, f32[4096]{0:T(1024)}, u32[]{:S(2)}) copy-start(f32[4096]{0:T(1024)} %param.10) | copy-start | bytes 49156
  5.3 1.7 %collective-permute-start = (f32[64,1024]{1,0:T(8,128)S(1)}, f32[64,1024]{1,0:T(8,128)S(1)}, u32[]{:S(2)}, u32[]{:S(2)}) collective-permute-start(f32[64,1024]{1,0:T(8,128)S(1)} %get-tuple-element.12), channel_id=1, source_target_pairs={{0,1},{1,0},{2,3},{3,2},{4,5},{5,4},{6,7},{7,6},{8,9},{9,8},{10,11... | collective-permute-start | bytes 786440 | tf_op jit(solution)/shard_map/ppermute | solution.py:24
  7.1 21.7 %collective-permute-start.6 = (bf16[4096,256]{1,0:T(8,128)(2,1)S(1)}, bf16[4096,256]{1,0:T(8,128)(2,1)S(1)}, u32[]{:S(2)}, u32[]{:S(2)}) collective-permute-start(bf16[4096,256]{1,0:T(8,128)(2,1)S(1)} %bitcast.3), channel_id=1, source_target_pairs={{0,1},{1,0},{2,3},{3,2},{4,5},{5,4},{6,7},{7,6},{8,9},{9,8},{10,11... | collective-permute-start | bytes 6291464 | tf_op jit(solution)/shard_map/ppermute | solution.py:24
  7.5 3.4 %collective-permute-start.1 = (bf16[32,1024]{1,0:T(8,128)(2,1)S(1)}, bf16[32,1024]{1,0:T(8,128)(2,1)S(1)}, u32[]{:S(2)}, u32[]{:S(2)}) collective-permute-start(bf16[32,1024]{1,0:T(8,128)(2,1)S(1)} %get-tuple-element.16), channel_id=1, source_target_pairs={{0,0},{1,17},{8,8},{9,25},{16,16},{17,1},{24,24},{25,9},{2,2},{3,1... | collective-permute-start | bytes 196616 | tf_op jit(solution)/shard_map/ppermute | solution.py:33
  8.2 4.9 %collective-permute-start.2 = (bf16[32,1024]{1,0:T(8,128)(2,1)S(1)}, bf16[32,1024]{1,0:T(8,128)(2,1)S(1)}, u32[]{:S(2)}, u32[]{:S(2)}) collective-permute-start(bf16[32,1024]{1,0:T(8,128)(2,1)S(1)} %get-tuple-element.15), channel_id=1, source_target_pairs={{0,8},{1,25},{8,0},{9,17},{16,24},{17,9},{24,16},{25,1},{2,10},{3,... | collective-permute-start | bytes 196616 | tf_op jit(solution)/shard_map/ppermute | solution.py:33
  13.1 7.2 %collective-permute-start.5 = (bf16[64,1024]{1,0:T(8,128)(2,1)S(1)}, bf16[64,1024]{1,0:T(8,128)(2,1)S(1)}, u32[]{:S(2)}, u32[]{:S(2)}) collective-permute-start(bf16[64,1024]{1,0:T(8,128)(2,1)S(1)} %constant_dynamic-update-slice_fusion.refs_0_), channel_id=1, source_target_pairs={{0,6},{2,4},{4,2},{6,0},{1,7},{3,5},{5,3},{7,1},{8,14},{10,12},{12... | collective-permute-start | bytes 393224 | tf_op jit(solution)/shard_map/ppermute | solution.py:24
  17.3 11.5 %collective-permute-start.4 = (bf16[64,1024]{1,0:T(8,128)(2,1)S(1)}, bf16[64,1024]{1,0:T(8,128)(2,1)S(1)}, u32[]{:S(2)}, u32[]{:S(2)}) collective-permute-start(bf16[64,1024]{1,0:T(8,128)(2,1)S(1)} %constant_dynamic-update-slice_fusion.refs_0_), channel_id=1, source_target_pairs={{0,4},{2,6},{4,0},{6,2},{1,5},{3,7},{5,1},{7,3},{8,12},{10,14},{12... | collective-permute-start | bytes 393224 | tf_op jit(solution)/shard_map/ppermute | solution.py:24
  17.3 11.5 %collective-permute-start.3 = (bf16[64,1024]{1,0:T(8,128)(2,1)S(1)}, bf16[64,1024]{1,0:T(8,128)(2,1)S(1)}, u32[]{:S(2)}, u32[]{:S(2)}) collective-permute-start(bf16[64,1024]{1,0:T(8,128)(2,1)S(1)} %constant_dynamic-update-slice_fusion.refs_0_), channel_id=1, source_target_pairs={{0,2},{2,0},{4,6},{6,4},{1,3},{3,1},{5,7},{7,5},{8,10},{10,8},{12,... | collective-permute-start | bytes 393224 | tf_op jit(solution)/shard_map/ppermute | solution.py:24
  28.7 11.6 %copy-start.1 = (bf16[128,1024]{1,0:T(8,128)(2,1)S(1)}, bf16[128,1024]{1,0:T(8,128)(2,1)}, u32[]{:S(2)}) copy-start(bf16[128,1024]{1,0:T(8,128)(2,1)} %query_ref.1) | copy-start | bytes 786436
  28.7 11.6 %copy-start.3 = (s32[512,1]{0,1:T(1,128)S(1)}, s32[512,1]{0,1:T(1,128)}, u32[]{:S(2)}) copy-start(s32[512,1]{0,1:T(1,128)} %param.12) | copy-start | bytes 6148
  29.7 6.8 %collective-permute-start.12 = (bf16[64,512]{1,0:T(8,128)(2,1)S(1)}, bf16[64,512]{1,0:T(8,128)(2,1)S(1)}, u32[]{:S(2)}, u32[]{:S(2)}) collective-permute-start(bf16[64,512]{1,0:T(8,128)(2,1)S(1)} %shard_map.74.refs_0_), channel_id=1, source_target_pairs={{0,6},{2,4},{4,2},{6,0},{1,7},{3,5},{5,3},{7,1},{8,14},{10,12},{12... | collective-permute-start | bytes 196616 | tf_op jit(solution)/shard_map/ppermute | solution.py:24
  31.3 7.6 %collective-permute-start.10 = (bf16[64,512]{1,0:T(8,128)(2,1)S(1)}, bf16[64,512]{1,0:T(8,128)(2,1)S(1)}, u32[]{:S(2)}, u32[]{:S(2)}) collective-permute-start(bf16[64,512]{1,0:T(8,128)(2,1)S(1)} %shard_map.74.refs_0_), channel_id=1, source_target_pairs={{0,4},{2,6},{4,0},{6,2},{1,5},{3,7},{5,1},{7,3},{8,12},{10,14},{12... | collective-permute-start | bytes 196616 | tf_op jit(solution)/shard_map/ppermute | solution.py:24
  31.3 7.7 %collective-permute-start.8 = (bf16[64,512]{1,0:T(8,128)(2,1)S(1)}, bf16[64,512]{1,0:T(8,128)(2,1)S(1)}, u32[]{:S(2)}, u32[]{:S(2)}) collective-permute-start(bf16[64,512]{1,0:T(8,128)(2,1)S(1)} %shard_map.74.refs_0_), channel_id=1, source_target_pairs={{0,2},{2,0},{4,6},{6,4},{1,3},{3,1},{5,7},{7,5},{8,10},{10,8},{12,... | collective-permute-start | bytes 196616 | tf_op jit(solution)/shard_map/ppermute | solution.py:24
  34.2 5.3 %collective-permute-start.7 = (bf16[64,512]{1,0:T(8,128)(2,1)S(1)}, bf16[64,512]{1,0:T(8,128)(2,1)S(1)}, u32[]{:S(2)}, u32[]{:S(2)}) collective-permute-start(bf16[64,512]{1,0:T(8,128)(2,1)S(1)} %shard_map.74.refs_0_), channel_id=1, source_target_pairs={{0,1},{1,0},{2,3},{3,2},{4,5},{5,4},{6,7},{7,6},{8,9},{9,8},{10,11... | collective-permute-start | bytes 196616 | tf_op jit(solution)/shard_map/ppermute | solution.py:24
  36.6 2.9 %collective-permute-start.13 = (bf16[64,512]{1,0:T(8,128)(2,1)S(1)}, bf16[64,512]{1,0:T(8,128)(2,1)S(1)}, u32[]{:S(2)}, u32[]{:S(2)}) collective-permute-start(bf16[64,512]{1,0:T(8,128)(2,1)S(1)} %collective-permute-done.12.refs_6_), channel_id=1, source_target_pairs={{0,1},{1,0},{2,3},{3,2},{4,5},{5,4},{6,7},{7,6},{8,9},{9,8},{10,11... | collective-permute-start | bytes 196616 | tf_op jit(solution)/shard_map/ppermute | solution.py:24
  38.9 1.3 %collective-permute-start.11 = (bf16[64,512]{1,0:T(8,128)(2,1)S(1)}, bf16[64,512]{1,0:T(8,128)(2,1)S(1)}, u32[]{:S(2)}, u32[]{:S(2)}) collective-permute-start(bf16[64,512]{1,0:T(8,128)(2,1)S(1)} %collective-permute-done.10.refs_4_), channel_id=1, source_target_pairs={{0,1},{1,0},{2,3},{3,2},{4,5},{5,4},{6,7},{7,6},{8,9},{9,8},{10,11... | collective-permute-start | bytes 196616 | tf_op jit(solution)/shard_map/ppermute | solution.py:24
  39.1 1.3 %collective-permute-start.9 = (bf16[64,512]{1,0:T(8,128)(2,1)S(1)}, bf16[64,512]{1,0:T(8,128)(2,1)S(1)}, u32[]{:S(2)}, u32[]{:S(2)}) collective-permute-start(bf16[64,512]{1,0:T(8,128)(2,1)S(1)} %collective-permute-done.8.refs_2_), channel_id=1, source_target_pairs={{0,1},{1,0},{2,3},{3,2},{4,5},{5,4},{6,7},{7,6},{8,9},{9,8},{10,11... | collective-permute-start | bytes 196616 | tf_op jit(solution)/shard_map/ppermute | solution.py:24

commit v4 on v3

--- a/solution.py
+++ b/solution.py
@@ -24,10 +24,17 @@
     return lax.ppermute(value, axis, [(i, i ^ offset) for i in range(size)])
 
 
+def route_offsets(clips, cores):
+    if clips == 4 and cores == 2:
+        return [0, 3, 1, 2]
+    return list(range(clips))
+
+
 def route(value, place):
     clips, cores = lax.axis_size("clip"), lax.axis_size("tp")
+    offsets = route_offsets(clips, cores)
     pairs = [
-        (i * cores + t, (i ^ (t * (clips // cores) + place)) * cores + t)
+        (i * cores + t, (i ^ offsets[t * (clips // cores) + place]) * cores + t)
         for i in range(clips) for t in range(cores)
     ]
     return lax.ppermute(value, ("clip", "tp"), pairs)
@@ -43,8 +50,11 @@
     ).astype(F32)
     before = jnp.dot(onehot, earlier, preferred_element_type=F32)
     rank = jnp.sum(before * onehot, axis=0, keepdims=True).astype(jnp.int32)
-    away = (named ^ clip) ^ (core * (clips // cores))
-    slot = away * capacity + rank
+    away = named ^ clip
+    block = jnp.zeros_like(away)
+    for place, offset in enumerate(route_offsets(clips, cores)):
+        block = jnp.where(away == offset, place, block)
+    slot = (block ^ (core * (clips // cores))) * capacity + rank
     return (lax.broadcasted_iota(jnp.int32, (clips * capacity, rows), 0) == slot).astype(BF16)
 
 
@@ -112,13 +122,13 @@
             pltpu.VMEM((slots, width), F32),
             pltpu.SemaphoreType.DMA((steps + 3,)),
         ],
-        compiler_params=pltpu.CompilerParams(vmem_limit_bytes=VMEM_ALL),
+        compiler_params=pltpu.CompilerParams(vmem_limit_bytes=VMEM_LIMIT),
         cost_estimate=pl.CostEstimate(
             flops=2 * slots * depth * (width + rows),
             bytes_accessed=2 * depth * (width + rows),
             transcendentals=0,
         ),
-    )(dest, hidden, weight, residual)
+    )(*[pltpu.with_memory_space_constraint(x, pltpu.HBM) for x in (dest, hidden, weight, residual)])
 
 
 def keyval_kernel(parts, cores, *refs):
@@ -141,15 +151,19 @@
         out_ref[:, c * each:(c + 1) * each] = totals[c].astype(BF16)
 
 
-def attend_kernel(parts, cores, heads_here, capacity, dest_ref, query_ref, *refs):
+def attend_kernel(parts, cores, heads_here, capacity, groups, dest_ref, query_ref, *refs):
     blocks, out_ref = refs[:-1], refs[-1]
+    each = parts + cores - 1
     clip, seq, core = lax.axis_index("clip"), lax.axis_index("seq"), lax.axis_index("tp")
     clips = dest_ref.shape[0]
     slots = clips * capacity
     dim = query_ref.shape[1] // (parts * cores * heads_here)
     counts = jnp.sum((dest_ref[...] == clip).astype(jnp.int32), axis=1, keepdims=True)
     lane = lax.broadcasted_iota(jnp.int32, (clips, slots), 1)
-    source = (lane // capacity) ^ (core * (clips // cores)) ^ clip
+    block = (lane // capacity) ^ (core * (clips // cores))
+    source = jnp.zeros_like(lane)
+    for place, offset in enumerate(route_offsets(clips, cores)):
+        source = jnp.where(block == place, offset ^ clip, source)
     limit = jnp.sum(
         jnp.where(lax.broadcasted_iota(jnp.int32, lane.shape, 0) == source, counts, 0),
         axis=0, keepdims=True,
@@ -164,11 +178,15 @@
 
     def stored(head, offset):
         k, c, i = head
-        parts_of = []
+        found = []
         for g in range(cores):
             at = ((c ^ g) * heads_here + i) * 2 * dim + offset
-            parts_of.append(blocks[k * cores + g][:, at:at + dim])
-        return jnp.concatenate(parts_of, axis=0)
+            for first in range(0, groups * each, each):
+                if g == 0:
+                    found.append(blocks[first + k][:, at:at + dim])
+                else:
+                    found.append(blocks[first + parts + g - 1][k, :, at:at + dim])
+        return jnp.concatenate(found, axis=0)
 
     group = 8
     for first in range(0, len(heads), group):
@@ -195,6 +213,23 @@
             out_ref[:, columns(head)] = result
 
 
+def keyval(texts, gain, weights):
+    parts, (rows, width) = len(texts), texts[0].shape
+    wide = sum(weight.shape[1] for weight in weights)
+    return pl.pallas_call(
+        functools.partial(keyval_kernel, parts, len(weights)),
+        in_specs=[whole()] * (parts + 1 + len(weights)),
+        out_specs=whole(),
+        out_shape=pltpu.VMEM((rows, wide), BF16),
+        compiler_params=pltpu.CompilerParams(vmem_limit_bytes=VMEM_LIMIT),
+        cost_estimate=pl.CostEstimate(
+            flops=2 * rows * parts * width * wide,
+            bytes_accessed=2 * parts * width * (rows + wide),
+            transcendentals=0,
+        ),
+    )(*texts, gain, *weights)
+
+
 def shards(ffn_hidden, ffn_weight, residual, norm_gain, kv_weight, destination, queries):
     clips, parts, cores = lax.axis_size("clip"), lax.axis_size("seq"), lax.axis_size("tp")
     rows = ffn_hidden.shape[0]
@@ -202,31 +237,28 @@
     share = clips * capacity // cores
     heads_here = kv_weight.shape[1]
     dest = destination.reshape(clips, rows)
+    gain = norm_gain.reshape(1, -1)
     weight = kv_weight.reshape(kv_weight.shape[0], heads_here * kv_weight.shape[2])
+    weights = [weight] + [swap(weight, "tp", g) for g in range(1, cores)]
     own, send, text = ffn(dest, ffn_hidden, ffn_weight, residual, capacity, cores)
     for g in range(1, cores):
         own = own + swap(send[(g - 1) * share:g * share], "tp", g)
     text = (text.astype(F32) + own).astype(BF16)
-    weight, text = lax.optimization_barrier((weight, text))
-    weights = [weight] + [swap(weight, "tp", g) for g in range(1, cores)]
-    arrived = [
-        route(text[i * capacity:(i + 1) * capacity], i) for i in range(clips // cores)
-    ]
-    arrived = jnp.concatenate(arrived, axis=0)
-    texts = [arrived] + [swap(arrived, "seq", k) for k in range(1, parts)]
-    keyval = pl.pallas_call(
-        functools.partial(keyval_kernel, parts, cores),
-        in_specs=[whole()] * (parts + 1 + cores),
-        out_specs=whole(),
-        out_shape=jax.ShapeDtypeStruct((share, cores * weight.shape[1]), BF16),
-        compiler_params=pltpu.CompilerParams(vmem_limit_bytes=VMEM_LIMIT),
-    )(*texts, norm_gain.reshape(1, -1), *weights)
+    places = clips // cores
+    groups = math.gcd(2, places)
     blocks = []
-    for k in range(parts):
-        block = swap(keyval, "seq", k) if k else keyval
-        blocks += [block] + [swap(block, "tp", g) for g in range(1, cores)]
+    for first in range(0, places, places // groups):
+        arrived = [
+            route(text[i * capacity:(i + 1) * capacity], i)
+            for i in range(first, first + places // groups)
+        ]
+        arrived = jnp.concatenate(arrived, axis=0)
+        texts = [arrived] + [swap(arrived, "seq", k) for k in range(1, parts)]
+        block = keyval(texts, gain, weights)
+        block = [block] + [swap(block, "seq", k) for k in range(1, parts)]
+        blocks += block + [swap(jnp.stack(block), "tp", g) for g in range(1, cores)]
     return pl.pallas_call(
-        functools.partial(attend_kernel, parts, cores, heads_here, capacity),
+        functools.partial(attend_kernel, parts, cores, heads_here, capacity, groups),
         in_specs=[whole()] * (2 + len(blocks)),
         out_specs=whole(),
         out_shape=jax.ShapeDtypeStruct(queries.shape, BF16),

time: 41.9 us -> 40.1 us (0.957)
  waiting for transfers between devices: 19.9 us -> 6.1 us
  starting transfers between devices: 14 us -> 25.2 us
  Pallas kernels: 7.67 us -> 8.47 us
    ppermute x12 -> x16, waiting for transfers between devices: 17.6 us -> 6.09 us  [swap(): return lax.ppermute(value, axis, [(i, i ^ offset) for i in range(size)])]
    ppermute x12 -> x16, starting transfers between devices: 10.7 us -> 20.9 us  [swap(): return lax.ppermute(value, axis, [(i, i ^ offset) for i in range(size)])]
    ppermute x2, waiting for transfers between devices: 2.24 us -> 0.01 us  [route(): return lax.ppermute(value, ('clip', 'tp'), pairs)]
    ppermute x2, starting transfers between devices: 3.35 us -> 4.32 us  [route(): return lax.ppermute(value, ('clip', 'tp'), pairs)]
    pallas_call x1 -> x2, Pallas kernels: 0.97 us -> 1.78 us  [keyval(): pl.pallas_call(functools.partial(keyval_kernel, parts, len(weights)), in_...]
  transfers between devices with their start and end apart: 14 -> 18, of which waited for: 8 -> 5; matrix products, arithmetic and copies ran while one was open for 0% -> 0% of each run, Pallas kernels for 0% -> 18%
where the time goes in v4:
time: 40.1 us; the launch traced here: 40 us
  starting transfers between devices  25.2 us (63%)
  Pallas kernels  8.47 us (21%)
  waiting for transfers between devices  6.1 us (15%)
    ppermute x16, starting transfers between devices, swap(): return lax.ppermute(value, axis, [(i, i ^ offset) for i in range(size)])  20.9 us
    ppermute x16, waiting for transfers between devices, swap(): return lax.ppermute(value, axis, [(i, i ^ offset) for i in range(size)])  6.09 us
    pallas_call x1, Pallas kernels, ffn(): pl.pallas_call(functools.partial(ffn_kernel, capacity, cores, steps), in_...  5.3 us
    ppermute x2, starting transfers between devices, route(): return lax.ppermute(value, ('clip', 'tp'), pairs)  4.32 us
    pallas_call x2, Pallas kernels, keyval(): pl.pallas_call(functools.partial(keyval_kernel, parts, len(weights)), in_...  1.78 us
    pallas_call x1, Pallas kernels, shards(): pl.pallas_call(functools.partial(attend_kernel, parts, cores, heads_here,...  1.39 us
  transfers between devices with their start and end apart: 18, of which 5 were waited for; matrix products, arithmetic and copies ran while one was open for 0% of the time, Pallas kernels for 18%

profile of v4, /device:TPU:0, one launch (start us, length us, event | category | flops | bytes accessed | tf_op | source)
XLA Modules:
  0.0 40.0 jit_solution(10116967211882592865)
XLA Ops:
  0.0 0.5 %collective-permute-start.5 = (bf16[4096,256]{1,0:T(8,128)(2,1)}, bf16[4096,256]{1,0:T(8,128)(2,1)S(1)}, u32[]{:S(2)}, u32[]{:S(2)}) collective-permute-start(bf16[4096,256]{1,0:T(8,128)(2,1)} %bitcast.11), channel_id=1, source_target_pairs={{0,1},{1,0},{2,3},{3,2},{4,5},{5,4},{6,7},{7,6},{8,9},{9,8},{10,11... | collective-permute-start | bytes 6291464 | tf_op jit(solution)/shard_map/ppermute | solution.py:24
  0.5 0.0 copy-start
  0.5 0.0 copy-start.2
  0.5 5.3 %shard_map.73 = (f32[64,1024]{1,0:T(8,128)S(1)}, f32[64,1024]{1,0:T(8,128)S(1)}, bf16[64,1024]{1,0:T(8,128)(2,1)S(1)}) custom-call(s32[4,128]{1,0:T(4,128)} %bitcast.24, bf16[128,5120]{1,0:T(8,128)(2,1)} %hidden_hbm.1, bf16[5120,1024]{1,0:T(8,128)(2,1)} %weight_hbm.1, bf16[128,1024]{1,0:T(8,128)(2,1)} %residual_hbm.1), custom_call_target="tpu_custom_call" | custom-call | flops 1509949440 | bytes 11796480 | tf_op jit(solution)/shard_map/pallas_call | solution.py:107
  5.8 0.1 collective-permute-start
  5.9 1.5 %collective-permute-done = f32[64,1024]{1,0:T(8,128)S(1)} collective-permute-done((f32[64,1024]{1,0:T(8,128)S(1)}, f32[64,1024]{1,0:T(8,128)S(1)}, u32[]{:S(2)}, u32[]{:S(2)}) %collective-permute-start) | collective-permute-done | bytes 262176 | tf_op jit(solution)/shard_map/ppermute | solution.py:24
  7.4 0.7 %collective-permute-start.1 = (bf16[32,1024]{1,0:T(8,128)(2,1)S(1)}, bf16[32,1024]{1,0:T(8,128)(2,1)S(1)}, u32[]{:S(2)}, u32[]{:S(2)}) collective-permute-start(bf16[32,1024]{1,0:T(8,128)(2,1)S(1)} %get-tuple-element.12), channel_id=1, source_target_pairs={{0,0},{1,9},{8,8},{9,1},{16,16},{17,25},{24,24},{25,17},{2,2},{3,1... | collective-permute-start | bytes 196616 | tf_op jit(solution)/shard_map/ppermute | solution.py:40
  8.1 3.7 %collective-permute-start.10 = (bf16[32,1024]{1,0:T(8,128)(2,1)S(1)}, bf16[32,1024]{1,0:T(8,128)(2,1)S(1)}, u32[]{:S(2)}, u32[]{:S(2)}) collective-permute-start(bf16[32,1024]{1,0:T(8,128)(2,1)S(1)} %get-tuple-element.11), channel_id=1, source_target_pairs={{0,24},{1,17},{8,16},{9,25},{16,8},{17,1},{24,0},{25,9},{2,26},{3,... | collective-permute-start | bytes 196616 | tf_op jit(solution)/shard_map/ppermute | solution.py:40
  11.8 0.0 collective-permute-done.1.refs_0_
  11.8 3.6 %collective-permute-start.4 = (bf16[32,1024]{1,0:T(8,128)(2,1)S(1)}, bf16[32,1024]{1,0:T(8,128)(2,1)S(1)}, u32[]{:S(2)}, u32[]{:S(2)}) collective-permute-start(bf16[32,1024]{1,0:T(8,128)(2,1)S(1)} %collective-permute-done.1.refs_0_), channel_id=1, source_target_pairs={{0,6},{2,4},{4,2},{6,0},{1,7},{3,5},{5,3},{7,1},{8,14},{10,12},{12... | collective-permute-start | bytes 196616 | tf_op jit(solution)/shard_map/ppermute | solution.py:24
  15.4 0.0 collective-permute-start.3
  15.4 0.8 %collective-permute-start.2 = (bf16[32,1024]{1,0:T(8,128)(2,1)S(1)}, bf16[32,1024]{1,0:T(8,128)(2,1)S(1)}, u32[]{:S(2)}, u32[]{:S(2)}) collective-permute-start(bf16[32,1024]{1,0:T(8,128)(2,1)S(1)} %collective-permute-done.1.refs_0_), channel_id=1, source_target_pairs={{0,2},{2,0},{4,6},{6,4},{1,3},{3,1},{5,7},{7,5},{8,10},{10,8},{12,... | collective-permute-start | bytes 196616 | tf_op jit(solution)/shard_map/ppermute | solution.py:24
  16.1 0.0 collective-permute-done.10.refs_0_
  16.2 3.6 %collective-permute-start.13 = (bf16[32,1024]{1,0:T(8,128)(2,1)S(1)}, bf16[32,1024]{1,0:T(8,128)(2,1)S(1)}, u32[]{:S(2)}, u32[]{:S(2)}) collective-permute-start(bf16[32,1024]{1,0:T(8,128)(2,1)S(1)} %collective-permute-done.10.refs_0_), channel_id=1, source_target_pairs={{0,6},{2,4},{4,2},{6,0},{1,7},{3,5},{5,3},{7,1},{8,14},{10,12},{12... | collective-permute-start | bytes 196616 | tf_op jit(solution)/shard_map/ppermute | solution.py:24
  19.7 0.0 collective-permute-done.4.refs_3_
  19.8 0.0 collective-permute-start.12
  19.8 2.3 %collective-permute-done.3.refs_2_ = bf16[32,1024]{1,0:T(8,128)(2,1)S(1)} collective-permute-done((bf16[32,1024]{1,0:T(8,128)(2,1)S(1)}, bf16[32,1024]{1,0:T(8,128)(2,1)S(1)}, u32[]{:S(2)}, u32[]{:S(2)}) %collective-permute-start.3) | collective-permute-done | bytes 65568 | tf_op jit(solution)/shard_map/ppermute | solution.py:24
  22.1 0.0 collective-permute-start.11
  22.1 0.0 collective-permute-done.2.refs_1_
  22.1 0.0 collective-permute-done.5.refs_6_
  22.1 0.0 copy-done
  22.1 0.0 copy-done.2
  22.1 0.9 %shard_map.74.refs_0_ = bf16[32,512]{1,0:T(8,128)(2,1)S(1)} custom-call(bf16[32,1024]{1,0:T(8,128)(2,1)S(1)} %collective-permute-done.1.refs_0_, bf16[32,1024]{1,0:T(8,128)(2,1)S(1)} %collective-permute-done.2.refs_1_, bf16[32,1024]{1,0:T(8,128)(2,1)S(1)} %collective-permute-done.3.refs_2_, bf16[32,1024]{1,0:T(8,128)(2,1)S(1)} %collective-permute-done.4.refs_3_, ...), custom_call_target="tpu_custom_call" | custom-call | flops 134217728 | bytes 4456448 | tf_op jit(solution)/shard_map/pallas_call | solution.py:219
  23.0 0.0 copy-start.1
  23.0 0.0 copy-start.3
  23.0 2.1 %collective-permute-start.8 = (bf16[32,512]{1,0:T(8,128)(2,1)S(1)}, bf16[32,512]{1,0:T(8,128)(2,1)S(1)}, u32[]{:S(2)}, u32[]{:S(2)}) collective-permute-start(bf16[32,512]{1,0:T(8,128)(2,1)S(1)} %shard_map.74.refs_0_), channel_id=1, source_target_pairs={{0,6},{2,4},{4,2},{6,0},{1,7},{3,5},{5,3},{7,1},{8,14},{10,12},{12... | collective-permute-start | bytes 98312 | tf_op jit(solution)/shard_map/ppermute | solution.py:24
  25.1 1.4 %collective-permute-start.7 = (bf16[32,512]{1,0:T(8,128)(2,1)S(1)}, bf16[32,512]{1,0:T(8,128)(2,1)S(1)}, u32[]{:S(2)}, u32[]{:S(2)}) collective-permute-start(bf16[32,512]{1,0:T(8,128)(2,1)S(1)} %shard_map.74.refs_0_), channel_id=1, source_target_pairs={{0,4},{2,6},{4,0},{6,2},{1,5},{3,7},{5,1},{7,3},{8,12},{10,14},{12... | collective-permute-start | bytes 98312 | tf_op jit(solution)/shard_map/ppermute | solution.py:24
  26.6 0.0 collective-permute-done.13.refs_3_
  26.6 0.9 %collective-permute-start.6 = (bf16[32,512]{1,0:T(8,128)(2,1)S(1)}, bf16[32,512]{1,0:T(8,128)(2,1)S(1)}, u32[]{:S(2)}, u32[]{:S(2)}) collective-permute-start(bf16[32,512]{1,0:T(8,128)(2,1)S(1)} %shard_map.74.refs_0_), channel_id=1, source_target_pairs={{0,2},{2,0},{4,6},{6,4},{1,3},{3,1},{5,7},{7,5},{8,10},{10,8},{12,... | collective-permute-start | bytes 98312 | tf_op jit(solution)/shard_map/ppermute | solution.py:24
  27.5 0.1 collective-permute-done.12.refs_2_
  27.6 0.0 collective-permute-done.11.refs_1_
  27.6 0.9 %shard_map.75.refs_5_ = bf16[32,512]{1,0:T(8,128)(2,1)S(1)} custom-call(bf16[32,1024]{1,0:T(8,128)(2,1)S(1)} %collective-permute-done.10.refs_0_, bf16[32,1024]{1,0:T(8,128)(2,1)S(1)} %collective-permute-done.11.refs_1_, bf16[32,1024]{1,0:T(8,128)(2,1)S(1)} %collective-permute-done.12.refs_2_, bf16[32,1024]{1,0:T(8,128)(2,1)S(1)} %collective-permute-done.13.refs_3_, ...), custom_call_target="tpu_custom_call" | custom-call | flops 134217728 | bytes 4456448 | tf_op jit(solution)/shard_map/pallas_call | solution.py:219
  28.5 2.2 %collective-permute-start.16 = (bf16[32,512]{1,0:T(8,128)(2,1)S(1)}, bf16[32,512]{1,0:T(8,128)(2,1)S(1)}, u32[]{:S(2)}, u32[]{:S(2)}) collective-permute-start(bf16[32,512]{1,0:T(8,128)(2,1)S(1)} %shard_map.75.refs_5_), channel_id=1, source_target_pairs={{0,6},{2,4},{4,2},{6,0},{1,7},{3,5},{5,3},{7,1},{8,14},{10,12},{12... | collective-permute-start | bytes 98312 | tf_op jit(solution)/shard_map/ppermute | solution.py:24
  30.7 0.2 collective-permute-start.15
  31.0 0.0 collective-permute-done.8.refs_3_
  31.0 1.9 %collective-permute-start.14 = (bf16[32,512]{1,0:T(8,128)(2,1)S(1)}, bf16[32,512]{1,0:T(8,128)(2,1)S(1)}, u32[]{:S(2)}, u32[]{:S(2)}) collective-permute-start(bf16[32,512]{1,0:T(8,128)(2,1)S(1)} %shard_map.75.refs_5_), channel_id=1, source_target_pairs={{0,2},{2,0},{4,6},{6,4},{1,3},{3,1},{5,7},{7,5},{8,10},{10,8},{12,... | collective-permute-start | bytes 98312 | tf_op jit(solution)/shard_map/ppermute | solution.py:24
  32.9 0.0 collective-permute-done.7.refs_2_
  32.9 0.0 collective-permute-done.6.refs_1_
  32.9 1.8 %collective-permute-start.9 = (bf16[4,32,512]{2,1,0:T(8,128)(2,1)S(1)}, bf16[4,32,512]{2,1,0:T(8,128)(2,1)S(1)}, u32[]{:S(2)}, u32[]{:S(2)}) collective-permute-start(bf16[4,32,512]{2,1,0:T(8,128)(2,1)S(1)} %pad_maximum_fusion), channel_id=1, source_target_pairs={{0,1},{1,0},{2,3},{3,2},{4,5},{5,4},{6,7},{7,6},{8,9},{9,8},{10,11... | collective-permute-start | bytes 393224 | tf_op jit(solution)/shard_map/ppermute | solution.py:24
  34.7 0.0 collective-permute-done.16.refs_8_
  34.7 1.2 %collective-permute-done.15.refs_7_ = bf16[32,512]{1,0:T(8,128)(2,1)S(1)} collective-permute-done((bf16[32,512]{1,0:T(8,128)(2,1)S(1)}, bf16[32,512]{1,0:T(8,128)(2,1)S(1)}, u32[]{:S(2)}, u32[]{:S(2)}) %collective-permute-start.15) | collective-permute-done | bytes 32800 | tf_op jit(solution)/shard_map/ppermute | solution.py:24
  35.9 0.0 collective-permute-done.14.refs_6_
  35.9 1.7 %collective-permute-start.17 = (bf16[4,32,512]{2,1,0:T(8,128)(2,1)S(1)}, bf16[4,32,512]{2,1,0:T(8,128)(2,1)S(1)}, u32[]{:S(2)}, u32[]{:S(2)}) collective-permute-start(bf16[4,32,512]{2,1,0:T(8,128)(2,1)S(1)} %pad_maximum_fusion.1), channel_id=1, source_target_pairs={{0,1},{1,0},{2,3},{3,2},{4,5},{5,4},{6,7},{7,6},{8,9},{9,8},{10,11... | collective-permute-start | bytes 393224 | tf_op jit(solution)/shard_map/ppermute | solution.py:24
  37.6 0.0 collective-permute-done.9.refs_4_
  37.6 1.0 %collective-permute-done.17.refs_9_ = bf16[4,32,512]{2,1,0:T(8,128)(2,1)S(1)} collective-permute-done((bf16[4,32,512]{2,1,0:T(8,128)(2,1)S(1)}, bf16[4,32,512]{2,1,0:T(8,128)(2,1)S(1)}, u32[]{:S(2)}, u32[]{:S(2)}) %collective-permute-start.17) | collective-permute-done | bytes 131104 | tf_op jit(solution)/shard_map/ppermute | solution.py:24
  38.6 0.0 copy-done.1
  38.6 0.0 copy-done.3
  38.6 1.4 %shard_map.76 = bf16[128,1024]{1,0:T(8,128)(2,1)} custom-call(s32[4,128]{1,0:T(4,128)S(1)} %bitcast.25, bf16[128,1024]{1,0:T(8,128)(2,1)S(1)} %copy-done.1, bf16[32,512]{1,0:T(8,128)(2,1)S(1)} %shard_map.74.refs_0_, bf16[32,512]{1,0:T(8,128)(2,1)S(1)} %collective-permute-done.6.refs_1_, bf16[32,512]{1,0:T(8,128)(2,1)S(1)} %collective-permute-done.7.refs_2_, ...), custom_call_target="tpu_custom_call" | custom-call | tf_op jit(solution)/shard_map/pallas_call | solution.py:260
  (4 shorter events, 0.1 us)
Async XLA Ops:
  0.0 22.1 %collective-permute-start.5 = (bf16[4096,256]{1,0:T(8,128)(2,1)}, bf16[4096,256]{1,0:T(8,128)(2,1)S(1)}, u32[]{:S(2)}, u32[]{:S(2)}) collective-permute-start(bf16[4096,256]{1,0:T(8,128)(2,1)} %bitcast.11), channel_id=1, source_target_pairs={{0,1},{1,0},{2,3},{3,2},{4,5},{5,4},{6,7},{7,6},{8,9},{9,8},{10,11... | collective-permute-start | bytes 6291464 | tf_op jit(solution)/shard_map/ppermute | solution.py:24
  0.5 21.7 %copy-start = (bf16[4096,1,256]{2,0,1:T(8,128)(2,1)S(1)}, bf16[4096,1,256]{2,0,1:T(8,128)(2,1)}, u32[]{:S(2)}) copy-start(bf16[4096,1,256]{2,0,1:T(8,128)(2,1)} %param.11) | copy-start | bytes 6291460
  0.5 21.7 %copy-start.2 = (f32[4096]{0:T(1024)S(1)}, f32[4096]{0:T(1024)}, u32[]{:S(2)}) copy-start(f32[4096]{0:T(1024)} %param.10) | copy-start | bytes 49156
  5.8 1.6 %collective-permute-start = (f32[64,1024]{1,0:T(8,128)S(1)}, f32[64,1024]{1,0:T(8,128)S(1)}, u32[]{:S(2)}, u32[]{:S(2)}) collective-permute-start(f32[64,1024]{1,0:T(8,128)S(1)} %get-tuple-element.10), channel_id=1, source_target_pairs={{0,1},{1,0},{2,3},{3,2},{4,5},{5,4},{6,7},{7,6},{8,9},{9,8},{10,11... | collective-permute-start | bytes 786440 | tf_op jit(solution)/shard_map/ppermute | solution.py:24
  7.4 4.3 %collective-permute-start.1 = (bf16[32,1024]{1,0:T(8,128)(2,1)S(1)}, bf16[32,1024]{1,0:T(8,128)(2,1)S(1)}, u32[]{:S(2)}, u32[]{:S(2)}) collective-permute-start(bf16[32,1024]{1,0:T(8,128)(2,1)S(1)} %get-tuple-element.12), channel_id=1, source_target_pairs={{0,0},{1,9},{8,8},{9,1},{16,16},{17,25},{24,24},{25,17},{2,2},{3,1... | collective-permute-start | bytes 196616 | tf_op jit(solution)/shard_map/ppermute | solution.py:40
  8.1 8.0 %collective-permute-start.10 = (bf16[32,1024]{1,0:T(8,128)(2,1)S(1)}, bf16[32,1024]{1,0:T(8,128)(2,1)S(1)}, u32[]{:S(2)}, u32[]{:S(2)}) collective-permute-start(bf16[32,1024]{1,0:T(8,128)(2,1)S(1)} %get-tuple-element.11), channel_id=1, source_target_pairs={{0,24},{1,17},{8,16},{9,25},{16,8},{17,1},{24,0},{25,9},{2,26},{3,... | collective-permute-start | bytes 196616 | tf_op jit(solution)/shard_map/ppermute | solution.py:40
  11.8 8.0 %collective-permute-start.4 = (bf16[32,1024]{1,0:T(8,128)(2,1)S(1)}, bf16[32,1024]{1,0:T(8,128)(2,1)S(1)}, u32[]{:S(2)}, u32[]{:S(2)}) collective-permute-start(bf16[32,1024]{1,0:T(8,128)(2,1)S(1)} %collective-permute-done.1.refs_0_), channel_id=1, source_target_pairs={{0,6},{2,4},{4,2},{6,0},{1,7},{3,5},{5,3},{7,1},{8,14},{10,12},{12... | collective-permute-start | bytes 196616 | tf_op jit(solution)/shard_map/ppermute | solution.py:24
  15.4 6.7 %collective-permute-start.3 = (bf16[32,1024]{1,0:T(8,128)(2,1)S(1)}, bf16[32,1024]{1,0:T(8,128)(2,1)S(1)}, u32[]{:S(2)}, u32[]{:S(2)}) collective-permute-start(bf16[32,1024]{1,0:T(8,128)(2,1)S(1)} %collective-permute-done.1.refs_0_), channel_id=1, source_target_pairs={{0,4},{2,6},{4,0},{6,2},{1,5},{3,7},{5,1},{7,3},{8,12},{10,14},{12... | collective-permute-start | bytes 196616 | tf_op jit(solution)/shard_map/ppermute | solution.py:24
  15.4 6.8 %collective-permute-start.2 = (bf16[32,1024]{1,0:T(8,128)(2,1)S(1)}, bf16[32,1024]{1,0:T(8,128)(2,1)S(1)}, u32[]{:S(2)}, u32[]{:S(2)}) collective-permute-start(bf16[32,1024]{1,0:T(8,128)(2,1)S(1)} %collective-permute-done.1.refs_0_), channel_id=1, source_target_pairs={{0,2},{2,0},{4,6},{6,4},{1,3},{3,1},{5,7},{7,5},{8,10},{10,8},{12,... | collective-permute-start | bytes 196616 | tf_op jit(solution)/shard_map/ppermute | solution.py:24
  16.2 10.4 %collective-permute-start.13 = (bf16[32,1024]{1,0:T(8,128)(2,1)S(1)}, bf16[32,1024]{1,0:T(8,128)(2,1)S(1)}, u32[]{:S(2)}, u32[]{:S(2)}) collective-permute-start(bf16[32,1024]{1,0:T(8,128)(2,1)S(1)} %collective-permute-done.10.refs_0_), channel_id=1, source_target_pairs={{0,6},{2,4},{4,2},{6,0},{1,7},{3,5},{5,3},{7,1},{8,14},{10,12},{12... | collective-permute-start | bytes 196616 | tf_op jit(solution)/shard_map/ppermute | solution.py:24
  19.8 7.8 %collective-permute-start.12 = (bf16[32,1024]{1,0:T(8,128)(2,1)S(1)}, bf16[32,1024]{1,0:T(8,128)(2,1)S(1)}, u32[]{:S(2)}, u32[]{:S(2)}) collective-permute-start(bf16[32,1024]{1,0:T(8,128)(2,1)S(1)} %collective-permute-done.10.refs_0_), channel_id=1, source_target_pairs={{0,4},{2,6},{4,0},{6,2},{1,5},{3,7},{5,1},{7,3},{8,12},{10,14},{12... | collective-permute-start | bytes 196616 | tf_op jit(solution)/shard_map/ppermute | solution.py:24
  22.1 5.5 %collective-permute-start.11 = (bf16[32,1024]{1,0:T(8,128)(2,1)S(1)}, bf16[32,1024]{1,0:T(8,128)(2,1)S(1)}, u32[]{:S(2)}, u32[]{:S(2)}) collective-permute-start(bf16[32,1024]{1,0:T(8,128)(2,1)S(1)} %collective-permute-done.10.refs_0_), channel_id=1, source_target_pairs={{0,2},{2,0},{4,6},{6,4},{1,3},{3,1},{5,7},{7,5},{8,10},{10,8},{12,... | collective-permute-start | bytes 196616 | tf_op jit(solution)/shard_map/ppermute | solution.py:24
  23.0 15.6 %copy-start.1 = (bf16[128,1024]{1,0:T(8,128)(2,1)S(1)}, bf16[128,1024]{1,0:T(8,128)(2,1)}, u32[]{:S(2)}) copy-start(bf16[128,1024]{1,0:T(8,128)(2,1)} %query_ref.1) | copy-start | bytes 786436
  23.0 15.6 %copy-start.3 = (s32[512,1]{0,1:T(1,128)S(1)}, s32[512,1]{0,1:T(1,128)}, u32[]{:S(2)}) copy-start(s32[512,1]{0,1:T(1,128)} %param.12) | copy-start | bytes 6148
  23.0 7.9 %collective-permute-start.8 = (bf16[32,512]{1,0:T(8,128)(2,1)S(1)}, bf16[32,512]{1,0:T(8,128)(2,1)S(1)}, u32[]{:S(2)}, u32[]{:S(2)}) collective-permute-start(bf16[32,512]{1,0:T(8,128)(2,1)S(1)} %shard_map.74.refs_0_), channel_id=1, source_target_pairs={{0,6},{2,4},{4,2},{6,0},{1,7},{3,5},{5,3},{7,1},{8,14},{10,12},{12... | collective-permute-start | bytes 98312 | tf_op jit(solution)/shard_map/ppermute | solution.py:24
  25.1 7.7 %collective-permute-start.7 = (bf16[32,512]{1,0:T(8,128)(2,1)S(1)}, bf16[32,512]{1,0:T(8,128)(2,1)S(1)}, u32[]{:S(2)}, u32[]{:S(2)}) collective-permute-start(bf16[32,512]{1,0:T(8,128)(2,1)S(1)} %shard_map.74.refs_0_), channel_id=1, source_target_pairs={{0,4},{2,6},{4,0},{6,2},{1,5},{3,7},{5,1},{7,3},{8,12},{10,14},{12... | collective-permute-start | bytes 98312 | tf_op jit(solution)/shard_map/ppermute | solution.py:24
  26.6 6.3 %collective-permute-start.6 = (bf16[32,512]{1,0:T(8,128)(2,1)S(1)}, bf16[32,512]{1,0:T(8,128)(2,1)S(1)}, u32[]{:S(2)}, u32[]{:S(2)}) collective-permute-start(bf16[32,512]{1,0:T(8,128)(2,1)S(1)} %shard_map.74.refs_0_), channel_id=1, source_target_pairs={{0,2},{2,0},{4,6},{6,4},{1,3},{3,1},{5,7},{7,5},{8,10},{10,8},{12,... | collective-permute-start | bytes 98312 | tf_op jit(solution)/shard_map/ppermute | solution.py:24
  28.5 6.2 %collective-permute-start.16 = (bf16[32,512]{1,0:T(8,128)(2,1)S(1)}, bf16[32,512]{1,0:T(8,128)(2,1)S(1)}, u32[]{:S(2)}, u32[]{:S(2)}) collective-permute-start(bf16[32,512]{1,0:T(8,128)(2,1)S(1)} %shard_map.75.refs_5_), channel_id=1, source_target_pairs={{0,6},{2,4},{4,2},{6,0},{1,7},{3,5},{5,3},{7,1},{8,14},{10,12},{12... | collective-permute-start | bytes 98312 | tf_op jit(solution)/shard_map/ppermute | solution.py:24
  30.7 5.2 %collective-permute-start.15 = (bf16[32,512]{1,0:T(8,128)(2,1)S(1)}, bf16[32,512]{1,0:T(8,128)(2,1)S(1)}, u32[]{:S(2)}, u32[]{:S(2)}) collective-permute-start(bf16[32,512]{1,0:T(8,128)(2,1)S(1)} %shard_map.75.refs_5_), channel_id=1, source_target_pairs={{0,4},{2,6},{4,0},{6,2},{1,5},{3,7},{5,1},{7,3},{8,12},{10,14},{12... | collective-permute-start | bytes 98312 | tf_op jit(solution)/shard_map/ppermute | solution.py:24
  31.0 4.9 %collective-permute-start.14 = (bf16[32,512]{1,0:T(8,128)(2,1)S(1)}, bf16[32,512]{1,0:T(8,128)(2,1)S(1)}, u32[]{:S(2)}, u32[]{:S(2)}) collective-permute-start(bf16[32,512]{1,0:T(8,128)(2,1)S(1)} %shard_map.75.refs_5_), channel_id=1, source_target_pairs={{0,2},{2,0},{4,6},{6,4},{1,3},{3,1},{5,7},{7,5},{8,10},{10,8},{12,... | collective-permute-start | bytes 98312 | tf_op jit(solution)/shard_map/ppermute | solution.py:24
  32.9 4.7 %collective-permute-start.9 = (bf16[4,32,512]{2,1,0:T(8,128)(2,1)S(1)}, bf16[4,32,512]{2,1,0:T(8,128)(2,1)S(1)}, u32[]{:S(2)}, u32[]{:S(2)}) collective-permute-start(bf16[4,32,512]{2,1,0:T(8,128)(2,1)S(1)} %pad_maximum_fusion), channel_id=1, source_target_pairs={{0,1},{1,0},{2,3},{3,2},{4,5},{5,4},{6,7},{7,6},{8,9},{9,8},{10,11... | collective-permute-start | bytes 393224 | tf_op jit(solution)/shard_map/ppermute | solution.py:24
  35.9 2.7 %collective-permute-start.17 = (bf16[4,32,512]{2,1,0:T(8,128)(2,1)S(1)}, bf16[4,32,512]{2,1,0:T(8,128)(2,1)S(1)}, u32[]{:S(2)}, u32[]{:S(2)}) collective-permute-start(bf16[4,32,512]{2,1,0:T(8,128)(2,1)S(1)} %pad_maximum_fusion.1), channel_id=1, source_target_pairs={{0,1},{1,0},{2,3},{3,2},{4,5},{5,4},{6,7},{7,6},{8,9},{9,8},{10,11... | collective-permute-start | bytes 393224 | tf_op jit(solution)/shard_map/ppermute | solution.py:24

commit v5 on v4

--- a/solution.py
+++ b/solution.py
@@ -30,14 +30,16 @@
     return list(range(clips))
 
 
-def route(value, place):
-    clips, cores = lax.axis_size("clip"), lax.axis_size("tp")
+def deliver(value, place, step):
+    clips, parts, cores = lax.axis_size("clip"), lax.axis_size("seq"), lax.axis_size("tp")
     offsets = route_offsets(clips, cores)
-    pairs = [
-        (i * cores + t, (i ^ offsets[t * (clips // cores) + place]) * cores + t)
-        for i in range(clips) for t in range(cores)
-    ]
-    return lax.ppermute(value, ("clip", "tp"), pairs)
+    pairs = []
+    for i in range(clips):
+        for s in range(parts):
+            for t in range(cores):
+                to = i ^ offsets[t * (clips // cores) + place]
+                pairs.append(((i * parts + s) * cores + t, (to * parts + (s ^ step)) * cores + t))
+    return lax.ppermute(value, ("clip", "seq", "tp"), pairs)
 
 
 def slot_select(dest_ref, clip, core, capacity, cores):
@@ -151,9 +153,8 @@
         out_ref[:, c * each:(c + 1) * each] = totals[c].astype(BF16)
 
 
-def attend_kernel(parts, cores, heads_here, capacity, groups, dest_ref, query_ref, *refs):
-    blocks, out_ref = refs[:-1], refs[-1]
-    each = parts + cores - 1
+def attend_kernel(parts, cores, heads_here, capacity, pieces, dest_ref, query_ref, *refs):
+    own, others, out_ref = refs[:parts * pieces], refs[parts * pieces:-1], refs[-1]
     clip, seq, core = lax.axis_index("clip"), lax.axis_index("seq"), lax.axis_index("tp")
     clips = dest_ref.shape[0]
     slots = clips * capacity
@@ -181,11 +182,10 @@
         found = []
         for g in range(cores):
             at = ((c ^ g) * heads_here + i) * 2 * dim + offset
-            for first in range(0, groups * each, each):
-                if g == 0:
-                    found.append(blocks[first + k][:, at:at + dim])
-                else:
-                    found.append(blocks[first + parts + g - 1][k, :, at:at + dim])
+            if g == 0:
+                found += [own[k * pieces + p][:, at:at + dim] for p in range(pieces)]
+            else:
+                found.append(others[g - 1][k, :, at:at + dim])
         return jnp.concatenate(found, axis=0)
 
     group = 8
@@ -244,26 +244,28 @@
     for g in range(1, cores):
         own = own + swap(send[(g - 1) * share:g * share], "tp", g)
     text = (text.astype(F32) + own).astype(BF16)
+    texts = [text] + [swap(text, "seq", k) for k in range(1, parts)]
+    block = keyval(texts, gain, weights)
     places = clips // cores
-    groups = math.gcd(2, places)
-    blocks = []
-    for first in range(0, places, places // groups):
-        arrived = [
-            route(text[i * capacity:(i + 1) * capacity], i)
-            for i in range(first, first + places // groups)
-        ]
-        arrived = jnp.concatenate(arrived, axis=0)
-        texts = [arrived] + [swap(arrived, "seq", k) for k in range(1, parts)]
-        block = keyval(texts, gain, weights)
-        block = [block] + [swap(block, "seq", k) for k in range(1, parts)]
-        blocks += block + [swap(jnp.stack(block), "tp", g) for g in range(1, cores)]
+    block = [block[i * capacity:(i + 1) * capacity] for i in range(places)]
+    if places <= 2:
+        order = list(range(parts))[::-1]
+        found = {(k, i): deliver(block[i], i, k) for k in order for i in range(places)}
+        own = [[found[k, i] for i in range(places)] for k in range(parts)]
+    else:
+        block = jnp.concatenate([deliver(block[i], i, 0) for i in range(places)], axis=0)
+        own = [[block]] + [[swap(block, "seq", k)] for k in range(1, parts)]
+    pieces = len(own[0])
+    own = [piece for some in own for piece in some]
+    packed = jnp.concatenate(own, axis=0).reshape(parts, share, -1)
+    others = [swap(packed, "tp", g) for g in range(1, cores)]
     return pl.pallas_call(
-        functools.partial(attend_kernel, parts, cores, heads_here, capacity, groups),
-        in_specs=[whole()] * (2 + len(blocks)),
+        functools.partial(attend_kernel, parts, cores, heads_here, capacity, pieces),
+        in_specs=[whole()] * (2 + len(own) + len(others)),
         out_specs=whole(),
         out_shape=jax.ShapeDtypeStruct(queries.shape, BF16),
         compiler_params=pltpu.CompilerParams(vmem_limit_bytes=VMEM_LIMIT),
-    )(dest, queries, *blocks)
+    )(dest, queries, *own, *others)
 
 
 def solution(mesh):

time: 40.1 us -> 50.4 us (1.26)
  waiting for transfers between devices: 6.1 us -> 23.5 us
  starting transfers between devices: 25.2 us -> 18.9 us
  Pallas kernels: 8.47 us -> 7.66 us
    ppermute x16 -> x6, starting transfers between devices: 20.9 us -> 6.11 us  [swap(): return lax.ppermute(value, axis, [(i, i ^ offset) for i in range(size)])]
    ppermute x2 -> x8, waiting for transfers between devices: 0.01 us -> 9.56 us  [deliver(): return lax.ppermute(value, ('clip', 'seq', 'tp'), pairs)]
    ppermute x2 -> x8, starting transfers between devices: 4.32 us -> 12.8 us  [deliver(): return lax.ppermute(value, ('clip', 'seq', 'tp'), pairs)]
    ppermute x16 -> x6, waiting for transfers between devices: 6.09 us -> 14 us  [swap(): return lax.ppermute(value, axis, [(i, i ^ offset) for i in range(size)])]
    pallas_call x2 -> x1, Pallas kernels: 1.78 us -> 0.97 us  [keyval(): pl.pallas_call(functools.partial(keyval_kernel, parts, len(weights)), in_...]
  transfers between devices with their start and end apart: 18 -> 14, of which waited for: 5 -> 7; matrix products, arithmetic and copies ran while one was open for 0% -> 0% of each run, Pallas kernels for 18% -> 11%
where the time goes in v5:
time: 50.4 us; the launch traced here: 50.3 us
  waiting for transfers between devices  23.5 us (47%)
  starting transfers between devices  18.9 us (38%)
  Pallas kernels  7.66 us (15%)
    ppermute x6, waiting for transfers between devices, swap(): return lax.ppermute(value, axis, [(i, i ^ offset) for i in range(size)])  14 us
    ppermute x8, starting transfers between devices, deliver(): return lax.ppermute(value, ('clip', 'seq', 'tp'), pairs)  12.8 us
    ppermute x8, waiting for transfers between devices, deliver(): return lax.ppermute(value, ('clip', 'seq', 'tp'), pairs)  9.56 us
    ppermute x6, starting transfers between devices, swap(): return lax.ppermute(value, axis, [(i, i ^ offset) for i in range(size)])  6.11 us
    pallas_call x1, Pallas kernels, ffn(): pl.pallas_call(functools.partial(ffn_kernel, capacity, cores, steps), in_...  5.3 us
    pallas_call x1, Pallas kernels, shards(): pl.pallas_call(functools.partial(attend_kernel, parts, cores, heads_here,...  1.39 us
  transfers between devices with their start and end apart: 14, of which 7 were waited for; matrix products, arithmetic and copies ran while one was open for 0% of the time, Pallas kernels for 11%

profile of v5, /device:TPU:0, one launch (start us, length us, event | category | flops | bytes accessed | tf_op | source)
XLA Modules:
  0.0 50.3 jit_solution(10594285383779657897)
XLA Ops:
  0.0 0.5 collective-permute-start.4
  0.5 0.0 copy-start
  0.5 0.0 copy-start.2
  0.5 5.3 %shard_map.73 = (f32[64,1024]{1,0:T(8,128)S(1)}, f32[64,1024]{1,0:T(8,128)S(1)}, bf16[64,1024]{1,0:T(8,128)(2,1)S(1)}) custom-call(s32[4,128]{1,0:T(4,128)} %bitcast.7, bf16[128,5120]{1,0:T(8,128)(2,1)} %hidden_hbm.1, bf16[5120,1024]{1,0:T(8,128)(2,1)} %weight_hbm.1, bf16[128,1024]{1,0:T(8,128)(2,1)} %residual_hbm.1), custom_call_target="tpu_custom_call" | custom-call | flops 1509949440 | bytes 11796480 | tf_op jit(solution)/shard_map/pallas_call | solution.py:109
  5.8 0.1 collective-permute-start
  5.9 1.5 %collective-permute-done = f32[64,1024]{1,0:T(8,128)S(1)} collective-permute-done((f32[64,1024]{1,0:T(8,128)S(1)}, f32[64,1024]{1,0:T(8,128)S(1)}, u32[]{:S(2)}, u32[]{:S(2)}) %collective-permute-start) | collective-permute-done | bytes 262176 | tf_op jit(solution)/shard_map/ppermute | solution.py:24
  7.4 4.8 %collective-permute-start.3 = (bf16[64,1024]{1,0:T(8,128)(2,1)S(1)}, bf16[64,1024]{1,0:T(8,128)(2,1)S(1)}, u32[]{:S(2)}, u32[]{:S(2)}) collective-permute-start(bf16[64,1024]{1,0:T(8,128)(2,1)S(1)} %add_convert_fusion.refs_0_), channel_id=1, source_target_pairs={{0,6},{2,4},{4,2},{6,0},{1,7},{3,5},{5,3},{7,1},{8,14},{10,12},{12... | collective-permute-start | bytes 393224 | tf_op jit(solution)/shard_map/ppermute | solution.py:24
  12.2 0.0 collective-permute-start.2
  12.2 0.6 %collective-permute-start.1 = (bf16[64,1024]{1,0:T(8,128)(2,1)S(1)}, bf16[64,1024]{1,0:T(8,128)(2,1)S(1)}, u32[]{:S(2)}, u32[]{:S(2)}) collective-permute-start(bf16[64,1024]{1,0:T(8,128)(2,1)S(1)} %add_convert_fusion.refs_0_), channel_id=1, source_target_pairs={{0,2},{2,0},{4,6},{6,4},{1,3},{3,1},{5,7},{7,5},{8,10},{10,8},{12,... | collective-permute-start | bytes 393224 | tf_op jit(solution)/shard_map/ppermute | solution.py:24
  12.9 3.8 %collective-permute-done.3.refs_3_ = bf16[64,1024]{1,0:T(8,128)(2,1)S(1)} collective-permute-done((bf16[64,1024]{1,0:T(8,128)(2,1)S(1)}, bf16[64,1024]{1,0:T(8,128)(2,1)S(1)}, u32[]{:S(2)}, u32[]{:S(2)}) %collective-permute-start.3) | collective-permute-done | bytes 131104 | tf_op jit(solution)/shard_map/ppermute | solution.py:24
  16.7 7.2 %collective-permute-done.2.refs_2_ = bf16[64,1024]{1,0:T(8,128)(2,1)S(1)} collective-permute-done((bf16[64,1024]{1,0:T(8,128)(2,1)S(1)}, bf16[64,1024]{1,0:T(8,128)(2,1)S(1)}, u32[]{:S(2)}, u32[]{:S(2)}) %collective-permute-start.2) | collective-permute-done | bytes 131104 | tf_op jit(solution)/shard_map/ppermute | solution.py:24
  23.8 0.0 collective-permute-done.1.refs_1_
  23.8 0.0 collective-permute-done.4.refs_6_
  23.8 0.0 copy-done
  23.8 0.0 copy-done.2
  23.8 0.0 copy-start.1
  23.9 0.0 copy-start.3
  23.9 1.0 %shard_map.74 = bf16[64,512]{1,0:T(8,128)(2,1)S(1)} custom-call(bf16[64,1024]{1,0:T(8,128)(2,1)S(1)} %add_convert_fusion.refs_0_, bf16[64,1024]{1,0:T(8,128)(2,1)S(1)} %collective-permute-done.1.refs_1_, bf16[64,1024]{1,0:T(8,128)(2,1)S(1)} %collective-permute-done.2.refs_2_, bf16[64,1024]{1,0:T(8,128)(2,1)S(1)} %collective-permute-done.3.refs_3_, ...), custom_call_target="tpu_custom_call" | custom-call | flops 268435456 | bytes 4718592 | tf_op jit(solution)/shard_map/pallas_call | solution.py:219
  24.9 0.7 %collective-permute-start.5 = (bf16[32,512]{1,0:T(8,128)(2,1)S(1)}, bf16[32,512]{1,0:T(8,128)(2,1)S(1)}, u32[]{:S(2)}, u32[]{:S(2)}) collective-permute-start(bf16[32,512]{1,0:T(8,128)(2,1)S(1)} %get-tuple-element.12), channel_id=1, source_target_pairs={{0,0},{1,9},{2,2},{3,11},{4,4},{5,13},{6,6},{7,15},{8,8},{9,1},{10... | collective-permute-start | bytes 98312 | tf_op jit(solution)/shard_map/ppermute | solution.py:42
  25.5 4.4 %collective-permute-start.12 = (bf16[32,512]{1,0:T(8,128)(2,1)S(1)}, bf16[32,512]{1,0:T(8,128)(2,1)S(1)}, u32[]{:S(2)}, u32[]{:S(2)}) collective-permute-start(bf16[32,512]{1,0:T(8,128)(2,1)S(1)} %get-tuple-element.11), channel_id=1, source_target_pairs={{0,30},{1,23},{2,28},{3,21},{4,26},{5,19},{6,24},{7,17},{8,22},{9,... | collective-permute-start | bytes 98312 | tf_op jit(solution)/shard_map/ppermute | solution.py:42
  30.0 0.0 collective-permute-start.10
  30.0 3.7 %collective-permute-start.8 = (bf16[32,512]{1,0:T(8,128)(2,1)S(1)}, bf16[32,512]{1,0:T(8,128)(2,1)S(1)}, u32[]{:S(2)}, u32[]{:S(2)}) collective-permute-start(bf16[32,512]{1,0:T(8,128)(2,1)S(1)} %get-tuple-element.11), channel_id=1, source_target_pairs={{0,26},{1,19},{2,24},{3,17},{4,30},{5,23},{6,28},{7,21},{8,18},{9,... | collective-permute-start | bytes 98312 | tf_op jit(solution)/shard_map/ppermute | solution.py:42
  33.7 0.5 collective-permute-start.6
  34.1 0.0 collective-permute-done.5.refs_0_
  34.1 2.5 %collective-permute-start.11 = (bf16[32,512]{1,0:T(8,128)(2,1)S(1)}, bf16[32,512]{1,0:T(8,128)(2,1)S(1)}, u32[]{:S(2)}, u32[]{:S(2)}) collective-permute-start(bf16[32,512]{1,0:T(8,128)(2,1)S(1)} %get-tuple-element.12), channel_id=1, source_target_pairs={{0,6},{1,15},{2,4},{3,13},{4,2},{5,11},{6,0},{7,9},{8,14},{9,7},{1... | collective-permute-start | bytes 98312 | tf_op jit(solution)/shard_map/ppermute | solution.py:42
  36.6 1.9 %collective-permute-done.6.refs_1_ = bf16[32,512]{1,0:T(8,128)(2,1)S(1)} collective-permute-done((bf16[32,512]{1,0:T(8,128)(2,1)S(1)}, bf16[32,512]{1,0:T(8,128)(2,1)S(1)}, u32[]{:S(2)}, u32[]{:S(2)}) %collective-permute-start.6) | collective-permute-done | bytes 32800 | tf_op jit(solution)/shard_map/ppermute | solution.py:42
  38.5 0.0 collective-permute-start.7
  38.5 3.9 %collective-permute-done.7.refs_2_ = bf16[32,512]{1,0:T(8,128)(2,1)S(1)} collective-permute-done((bf16[32,512]{1,0:T(8,128)(2,1)S(1)}, bf16[32,512]{1,0:T(8,128)(2,1)S(1)}, u32[]{:S(2)}, u32[]{:S(2)}) %collective-permute-start.7) | collective-permute-done | bytes 32800 | tf_op jit(solution)/shard_map/ppermute | solution.py:42
  42.4 1.0 %collective-permute-start.9 = (bf16[32,512]{1,0:T(8,128)(2,1)S(1)}, bf16[32,512]{1,0:T(8,128)(2,1)S(1)}, u32[]{:S(2)}, u32[]{:S(2)}) collective-permute-start(bf16[32,512]{1,0:T(8,128)(2,1)S(1)} %get-tuple-element.12), channel_id=1, source_target_pairs={{0,4},{1,13},{2,6},{3,15},{4,0},{5,9},{6,2},{7,11},{8,12},{9,5},{1... | collective-permute-start | bytes 98312 | tf_op jit(solution)/shard_map/ppermute | solution.py:42
  43.4 0.0 collective-permute-done.8.refs_3_
  43.4 3.8 %collective-permute-done.9.refs_4_ = bf16[32,512]{1,0:T(8,128)(2,1)S(1)} collective-permute-done((bf16[32,512]{1,0:T(8,128)(2,1)S(1)}, bf16[32,512]{1,0:T(8,128)(2,1)S(1)}, u32[]{:S(2)}, u32[]{:S(2)}) %collective-permute-start.9) | collective-permute-done | bytes 32800 | tf_op jit(solution)/shard_map/ppermute | solution.py:42
  47.2 0.0 collective-permute-done.10.refs_5_
  47.2 0.0 collective-permute-done.11.refs_6_
  47.2 0.0 collective-permute-done.12.refs_7_
  47.3 0.1 collective-permute-start.13
  47.4 1.5 %collective-permute-done.13.refs_8_ = bf16[4,64,512]{2,1,0:T(8,128)(2,1)S(1)} collective-permute-done((bf16[4,64,512]{2,1,0:T(8,128)(2,1)S(1)}, bf16[4,64,512]{2,1,0:T(8,128)(2,1)S(1)}, u32[]{:S(2)}, u32[]{:S(2)}) %collective-permute-start.13) | collective-permute-done | bytes 262176 | tf_op jit(solution)/shard_map/ppermute | solution.py:24
  48.9 0.0 copy-done.1
  48.9 0.0 copy-done.3
  48.9 1.4 %shard_map.75 = bf16[128,1024]{1,0:T(8,128)(2,1)} custom-call(s32[4,128]{1,0:T(4,128)S(1)} %bitcast.8, bf16[128,1024]{1,0:T(8,128)(2,1)S(1)} %copy-done.1, bf16[32,512]{1,0:T(8,128)(2,1)S(1)} %collective-permute-done.5.refs_0_, bf16[32,512]{1,0:T(8,128)(2,1)S(1)} %collective-permute-done.6.refs_1_, bf16[32,512]{1,0:T(8,128)(2,1)S(1)} %collective-permute-done.7.refs_2_, ...), custom_call_target="tpu_custom_call" | custom-call | tf_op jit(solution)/shard_map/pallas_call | solution.py:262
  (10 shorter events, 0.1 us)
Async XLA Ops:
  0.0 23.8 %collective-permute-start.4 = (bf16[4096,256]{1,0:T(8,128)(2,1)}, bf16[4096,256]{1,0:T(8,128)(2,1)S(1)}, u32[]{:S(2)}, u32[]{:S(2)}) collective-permute-start(bf16[4096,256]{1,0:T(8,128)(2,1)} %bitcast.4), channel_id=1, source_target_pairs={{0,1},{1,0},{2,3},{3,2},{4,5},{5,4},{6,7},{7,6},{8,9},{9,8},{10,11... | collective-permute-start | bytes 6291464 | tf_op jit(solution)/shard_map/ppermute | solution.py:24
  0.5 23.4 %copy-start = (bf16[4096,1,256]{2,0,1:T(8,128)(2,1)S(1)}, bf16[4096,1,256]{2,0,1:T(8,128)(2,1)}, u32[]{:S(2)}) copy-start(bf16[4096,1,256]{2,0,1:T(8,128)(2,1)} %param.11) | copy-start | bytes 6291460
  0.5 23.4 %copy-start.2 = (f32[4096]{0:T(1024)S(1)}, f32[4096]{0:T(1024)}, u32[]{:S(2)}) copy-start(f32[4096]{0:T(1024)} %param.10) | copy-start | bytes 49156
  5.8 1.6 %collective-permute-start = (f32[64,1024]{1,0:T(8,128)S(1)}, f32[64,1024]{1,0:T(8,128)S(1)}, u32[]{:S(2)}, u32[]{:S(2)}) collective-permute-start(f32[64,1024]{1,0:T(8,128)S(1)} %get-tuple-element.10), channel_id=1, source_target_pairs={{0,1},{1,0},{2,3},{3,2},{4,5},{5,4},{6,7},{7,6},{8,9},{9,8},{10,11... | collective-permute-start | bytes 786440 | tf_op jit(solution)/shard_map/ppermute | solution.py:24
  7.4 9.2 %collective-permute-start.3 = (bf16[64,1024]{1,0:T(8,128)(2,1)S(1)}, bf16[64,1024]{1,0:T(8,128)(2,1)S(1)}, u32[]{:S(2)}, u32[]{:S(2)}) collective-permute-start(bf16[64,1024]{1,0:T(8,128)(2,1)S(1)} %add_convert_fusion.refs_0_), channel_id=1, source_target_pairs={{0,6},{2,4},{4,2},{6,0},{1,7},{3,5},{5,3},{7,1},{8,14},{10,12},{12... | collective-permute-start | bytes 393224 | tf_op jit(solution)/shard_map/ppermute | solution.py:24
  12.2 11.6 %collective-permute-start.2 = (bf16[64,1024]{1,0:T(8,128)(2,1)S(1)}, bf16[64,1024]{1,0:T(8,128)(2,1)S(1)}, u32[]{:S(2)}, u32[]{:S(2)}) collective-permute-start(bf16[64,1024]{1,0:T(8,128)(2,1)S(1)} %add_convert_fusion.refs_0_), channel_id=1, source_target_pairs={{0,4},{2,6},{4,0},{6,2},{1,5},{3,7},{5,1},{7,3},{8,12},{10,14},{12... | collective-permute-start | bytes 393224 | tf_op jit(solution)/shard_map/ppermute | solution.py:24
  12.2 11.6 %collective-permute-start.1 = (bf16[64,1024]{1,0:T(8,128)(2,1)S(1)}, bf16[64,1024]{1,0:T(8,128)(2,1)S(1)}, u32[]{:S(2)}, u32[]{:S(2)}) collective-permute-start(bf16[64,1024]{1,0:T(8,128)(2,1)S(1)} %add_convert_fusion.refs_0_), channel_id=1, source_target_pairs={{0,2},{2,0},{4,6},{6,4},{1,3},{3,1},{5,7},{7,5},{8,10},{10,8},{12,... | collective-permute-start | bytes 393224 | tf_op jit(solution)/shard_map/ppermute | solution.py:24
  23.8 25.0 %copy-start.1 = (bf16[128,1024]{1,0:T(8,128)(2,1)S(1)}, bf16[128,1024]{1,0:T(8,128)(2,1)}, u32[]{:S(2)}) copy-start(bf16[128,1024]{1,0:T(8,128)(2,1)} %query_ref.1) | copy-start | bytes 786436
  23.9 25.0 %copy-start.3 = (s32[512,1]{0,1:T(1,128)S(1)}, s32[512,1]{0,1:T(1,128)}, u32[]{:S(2)}) copy-start(s32[512,1]{0,1:T(1,128)} %param.12) | copy-start | bytes 6148
  24.9 9.3 %collective-permute-start.5 = (bf16[32,512]{1,0:T(8,128)(2,1)S(1)}, bf16[32,512]{1,0:T(8,128)(2,1)S(1)}, u32[]{:S(2)}, u32[]{:S(2)}) collective-permute-start(bf16[32,512]{1,0:T(8,128)(2,1)S(1)} %get-tuple-element.12), channel_id=1, source_target_pairs={{0,0},{1,9},{2,2},{3,11},{4,4},{5,13},{6,6},{7,15},{8,8},{9,1},{10... | collective-permute-start | bytes 98312 | tf_op jit(solution)/shard_map/ppermute | solution.py:42
  25.5 21.7 %collective-permute-start.12 = (bf16[32,512]{1,0:T(8,128)(2,1)S(1)}, bf16[32,512]{1,0:T(8,128)(2,1)S(1)}, u32[]{:S(2)}, u32[]{:S(2)}) collective-permute-start(bf16[32,512]{1,0:T(8,128)(2,1)S(1)} %get-tuple-element.11), channel_id=1, source_target_pairs={{0,30},{1,23},{2,28},{3,21},{4,26},{5,19},{6,24},{7,17},{8,22},{9,... | collective-permute-start | bytes 98312 | tf_op jit(solution)/shard_map/ppermute | solution.py:42
  30.0 17.3 %collective-permute-start.10 = (bf16[32,512]{1,0:T(8,128)(2,1)S(1)}, bf16[32,512]{1,0:T(8,128)(2,1)S(1)}, u32[]{:S(2)}, u32[]{:S(2)}) collective-permute-start(bf16[32,512]{1,0:T(8,128)(2,1)S(1)} %get-tuple-element.11), channel_id=1, source_target_pairs={{0,28},{1,21},{2,30},{3,23},{4,24},{5,17},{6,26},{7,19},{8,20},{9,... | collective-permute-start | bytes 98312 | tf_op jit(solution)/shard_map/ppermute | solution.py:42
  30.0 13.5 %collective-permute-start.8 = (bf16[32,512]{1,0:T(8,128)(2,1)S(1)}, bf16[32,512]{1,0:T(8,128)(2,1)S(1)}, u32[]{:S(2)}, u32[]{:S(2)}) collective-permute-start(bf16[32,512]{1,0:T(8,128)(2,1)S(1)} %get-tuple-element.11), channel_id=1, source_target_pairs={{0,26},{1,19},{2,24},{3,17},{4,30},{5,23},{6,28},{7,21},{8,18},{9,... | collective-permute-start | bytes 98312 | tf_op jit(solution)/shard_map/ppermute | solution.py:42
  33.7 4.8 %collective-permute-start.6 = (bf16[32,512]{1,0:T(8,128)(2,1)S(1)}, bf16[32,512]{1,0:T(8,128)(2,1)S(1)}, u32[]{:S(2)}, u32[]{:S(2)}) collective-permute-start(bf16[32,512]{1,0:T(8,128)(2,1)S(1)} %get-tuple-element.11), channel_id=1, source_target_pairs={{0,24},{1,17},{2,26},{3,19},{4,28},{5,21},{6,30},{7,23},{8,16},{9,... | collective-permute-start | bytes 98312 | tf_op jit(solution)/shard_map/ppermute | solution.py:42
  34.1 13.1 %collective-permute-start.11 = (bf16[32,512]{1,0:T(8,128)(2,1)S(1)}, bf16[32,512]{1,0:T(8,128)(2,1)S(1)}, u32[]{:S(2)}, u32[]{:S(2)}) collective-permute-start(bf16[32,512]{1,0:T(8,128)(2,1)S(1)} %get-tuple-element.12), channel_id=1, source_target_pairs={{0,6},{1,15},{2,4},{3,13},{4,2},{5,11},{6,0},{7,9},{8,14},{9,7},{1... | collective-permute-start | bytes 98312 | tf_op jit(solution)/shard_map/ppermute | solution.py:42
  38.5 3.9 %collective-permute-start.7 = (bf16[32,512]{1,0:T(8,128)(2,1)S(1)}, bf16[32,512]{1,0:T(8,128)(2,1)S(1)}, u32[]{:S(2)}, u32[]{:S(2)}) collective-permute-start(bf16[32,512]{1,0:T(8,128)(2,1)S(1)} %get-tuple-element.12), channel_id=1, source_target_pairs={{0,2},{1,11},{2,0},{3,9},{4,6},{5,15},{6,4},{7,13},{8,10},{9,3},{1... | collective-permute-start | bytes 98312 | tf_op jit(solution)/shard_map/ppermute | solution.py:42
  42.4 4.8 %collective-permute-start.9 = (bf16[32,512]{1,0:T(8,128)(2,1)S(1)}, bf16[32,512]{1,0:T(8,128)(2,1)S(1)}, u32[]{:S(2)}, u32[]{:S(2)}) collective-permute-start(bf16[32,512]{1,0:T(8,128)(2,1)S(1)} %get-tuple-element.12), channel_id=1, source_target_pairs={{0,4},{1,13},{2,6},{3,15},{4,0},{5,9},{6,2},{7,11},{8,12},{9,5},{1... | collective-permute-start | bytes 98312 | tf_op jit(solution)/shard_map/ppermute | solution.py:42
  47.3 1.6 %collective-permute-start.13 = (bf16[4,64,512]{2,1,0:T(8,128)(2,1)S(1)}, bf16[4,64,512]{2,1,0:T(8,128)(2,1)S(1)}, u32[]{:S(2)}, u32[]{:S(2)}) collective-permute-start(bf16[4,64,512]{2,1,0:T(8,128)(2,1)S(1)} %bitcast.9), channel_id=1, source_target_pairs={{0,1},{1,0},{2,3},{3,2},{4,5},{5,4},{6,7},{7,6},{8,9},{9,8},{10,11... | collective-permute-start | bytes 786440 | tf_op jit(solution)/shard_map/ppermute | solution.py:24

commit v6 on v4

--- a/solution.py
+++ b/solution.py
@@ -33,11 +33,15 @@
 def route(value, place):
     clips, cores = lax.axis_size("clip"), lax.axis_size("tp")
     offsets = route_offsets(clips, cores)
+    here = [offsets[t * (clips // cores) + place] for t in range(cores)]
     pairs = [
-        (i * cores + t, (i ^ offsets[t * (clips // cores) + place]) * cores + t)
-        for i in range(clips) for t in range(cores)
+        (i * cores + t, (i ^ here[t]) * cores + t)
+        for i in range(clips) for t in range(cores) if here[t]
     ]
-    return lax.ppermute(value, ("clip", "tp"), pairs)
+    moved = lax.ppermute(value, ("clip", "tp"), pairs)
+    if all(here):
+        return moved
+    return jnp.where(lax.axis_index("tp") == here.index(0), value, moved)
 
 
 def slot_select(dest_ref, clip, core, capacity, cores):
@@ -152,8 +156,7 @@
 
 
 def attend_kernel(parts, cores, heads_here, capacity, groups, dest_ref, query_ref, *refs):
-    blocks, out_ref = refs[:-1], refs[-1]
-    each = parts + cores - 1
+    own, others, out_ref = refs[:parts * groups], refs[parts * groups:-1], refs[-1]
     clip, seq, core = lax.axis_index("clip"), lax.axis_index("seq"), lax.axis_index("tp")
     clips = dest_ref.shape[0]
     slots = clips * capacity
@@ -181,11 +184,10 @@
         found = []
         for g in range(cores):
             at = ((c ^ g) * heads_here + i) * 2 * dim + offset
-            for first in range(0, groups * each, each):
-                if g == 0:
-                    found.append(blocks[first + k][:, at:at + dim])
-                else:
-                    found.append(blocks[first + parts + g - 1][k, :, at:at + dim])
+            if g == 0:
+                found += [own[n * parts + k][:, at:at + dim] for n in range(groups)]
+            else:
+                found += [others[g - 1][n * parts + k, :, at:at + dim] for n in range(groups)]
         return jnp.concatenate(found, axis=0)
 
     group = 8
@@ -246,7 +248,7 @@
     text = (text.astype(F32) + own).astype(BF16)
     places = clips // cores
     groups = math.gcd(2, places)
-    blocks = []
+    own = []
     for first in range(0, places, places // groups):
         arrived = [
             route(text[i * capacity:(i + 1) * capacity], i)
@@ -255,15 +257,16 @@
         arrived = jnp.concatenate(arrived, axis=0)
         texts = [arrived] + [swap(arrived, "seq", k) for k in range(1, parts)]
         block = keyval(texts, gain, weights)
-        block = [block] + [swap(block, "seq", k) for k in range(1, parts)]
-        blocks += block + [swap(jnp.stack(block), "tp", g) for g in range(1, cores)]
+        own += [block] + [swap(block, "seq", k) for k in range(1, parts)]
+    packed = jnp.stack(own)
+    others = [swap(packed, "tp", g) for g in range(1, cores)]
     return pl.pallas_call(
         functools.partial(attend_kernel, parts, cores, heads_here, capacity, groups),
-        in_specs=[whole()] * (2 + len(blocks)),
+        in_specs=[whole()] * (2 + len(own) + len(others)),
         out_specs=whole(),
         out_shape=jax.ShapeDtypeStruct(queries.shape, BF16),
         compiler_params=pltpu.CompilerParams(vmem_limit_bytes=VMEM_LIMIT),
-    )(dest, queries, *blocks)
+    )(dest, queries, *own, *others)
 
 
 def solution(mesh):

time: 40.1 us -> 44.2 us (1.10)
  Pallas kernels: 8.47 us -> 11.6 us
  waiting for transfers between devices: 6.1 us -> 7.68 us
  starting transfers between devices: 25.2 us -> 24.5 us
    pallas_call x2, Pallas kernels: 1.78 us -> 4.95 us  [keyval(): pl.pallas_call(functools.partial(keyval_kernel, parts, len(weights)), in_...]
    ppermute x16 -> x15, waiting for transfers between devices: 6.09 us -> 7.68 us  [swap(): return lax.ppermute(value, axis, [(i, i ^ offset) for i in range(size)])]
    ppermute x16 -> x15, starting transfers between devices: 20.9 us -> 20.2 us  [swap(): return lax.ppermute(value, axis, [(i, i ^ offset) for i in range(size)])]
  transfers between devices with their start and end apart: 18 -> 17, of which waited for: 5 -> 5; matrix products, arithmetic and copies ran while one was open for 0% -> 0% of each run, Pallas kernels for 18% -> 23%
where the time goes in v6:
time: 44.2 us; the launch traced here: 44.1 us
  starting transfers between devices  24.5 us (55%)
  Pallas kernels  11.6 us (26%)
  waiting for transfers between devices  7.68 us (17%)
    ppermute x15, starting transfers between devices, swap(): return lax.ppermute(value, axis, [(i, i ^ offset) for i in range(size)])  20.2 us
    ppermute x15, waiting for transfers between devices, swap(): return lax.ppermute(value, axis, [(i, i ^ offset) for i in range(size)])  7.68 us
    pallas_call x1, Pallas kernels, ffn(): pl.pallas_call(functools.partial(ffn_kernel, capacity, cores, steps), in_...  5.3 us
    pallas_call x2, Pallas kernels, keyval(): pl.pallas_call(functools.partial(keyval_kernel, parts, len(weights)), in_...  4.95 us
    ppermute x2, starting transfers between devices, route(): moved = lax.ppermute(value, ('clip', 'tp'), pairs)  4.32 us
    pallas_call x1, Pallas kernels, shards(): pl.pallas_call(functools.partial(attend_kernel, parts, cores, heads_here,...  1.39 us
  transfers between devices with their start and end apart: 17, of which 5 were waited for; matrix products, arithmetic and copies ran while one was open for 0% of the time, Pallas kernels for 23%

profile of v6, /device:TPU:0, one launch (start us, length us, event | category | flops | bytes accessed | tf_op | source)
XLA Modules:
  0.0 44.1 jit_solution(9834576995330323009)
XLA Ops:
  0.0 0.5 %collective-permute-start.5 = (bf16[4096,256]{1,0:T(8,128)(2,1)}, bf16[4096,256]{1,0:T(8,128)(2,1)}, u32[]{:S(2)}, u32[]{:S(2)}) collective-permute-start(bf16[4096,256]{1,0:T(8,128)(2,1)} %bitcast.19), channel_id=1, source_target_pairs={{0,1},{1,0},{2,3},{3,2},{4,5},{5,4},{6,7},{7,6},{8,9},{9,8},{10,11... | collective-permute-start | bytes 6291464 | tf_op jit(solution)/shard_map/ppermute | solution.py:24
  0.5 0.0 copy-start
  0.5 0.0 copy-start.2
  0.5 5.3 %shard_map.73 = (f32[64,1024]{1,0:T(8,128)S(1)}, f32[64,1024]{1,0:T(8,128)S(1)}, bf16[64,1024]{1,0:T(8,128)(2,1)S(1)}) custom-call(s32[4,128]{1,0:T(4,128)} %bitcast.24, bf16[128,5120]{1,0:T(8,128)(2,1)} %hidden_hbm.1, bf16[5120,1024]{1,0:T(8,128)(2,1)} %weight_hbm.1, bf16[128,1024]{1,0:T(8,128)(2,1)} %residual_hbm.1), custom_call_target="tpu_custom_call" | custom-call | flops 1509949440 | bytes 11796480 | tf_op jit(solution)/shard_map/pallas_call | solution.py:111
  5.8 0.1 collective-permute-start
  5.9 1.5 %collective-permute-done = f32[64,1024]{1,0:T(8,128)S(1)} collective-permute-done((f32[64,1024]{1,0:T(8,128)S(1)}, f32[64,1024]{1,0:T(8,128)S(1)}, u32[]{:S(2)}, u32[]{:S(2)}) %collective-permute-start) | collective-permute-done | bytes 262176 | tf_op jit(solution)/shard_map/ppermute | solution.py:24
  7.4 0.7 %collective-permute-start.1 = (bf16[32,1024]{1,0:T(8,128)(2,1)S(1)}, bf16[32,1024]{1,0:T(8,128)(2,1)S(1)}, u32[]{:S(2)}, u32[]{:S(2)}) collective-permute-start(bf16[32,1024]{1,0:T(8,128)(2,1)S(1)} %slice.8), channel_id=1, source_target_pairs={{1,9},{9,1},{17,25},{25,17},{3,11},{11,3},{19,27},{27,19},{5,13},{... | collective-permute-start | bytes 196616 | tf_op jit(solution)/shard_map/ppermute | solution.py:41
  8.1 0.0 collective-permute-done.1
  8.1 3.7 %collective-permute-start.9 = (bf16[32,1024]{1,0:T(8,128)(2,1)S(1)}, bf16[32,1024]{1,0:T(8,128)(2,1)S(1)}, u32[]{:S(2)}, u32[]{:S(2)}) collective-permute-start(bf16[32,1024]{1,0:T(8,128)(2,1)S(1)} %get-tuple-element.11), channel_id=1, source_target_pairs={{0,24},{1,17},{8,16},{9,25},{16,8},{17,1},{24,0},{25,9},{2,26},{3,... | collective-permute-start | bytes 196616 | tf_op jit(solution)/shard_map/ppermute | solution.py:41
  11.8 1.6 %collective-permute-start.2 = (bf16[32,1024]{1,0:T(8,128)(2,1)S(1)}, bf16[32,1024]{1,0:T(8,128)(2,1)S(1)}, u32[]{:S(2)}, u32[]{:S(2)}) collective-permute-start(bf16[32,1024]{1,0:T(8,128)(2,1)S(1)} %get-tuple-element.12.refs_0_), channel_id=1, source_target_pairs={{0,2},{2,0},{4,6},{6,4},{1,3},{3,1},{5,7},{7,5},{8,10},{10,8},{12,... | collective-permute-start | bytes 196616 | tf_op jit(solution)/shard_map/ppermute | solution.py:24
  13.4 2.6 %collective-permute-start.3 = (bf16[32,1024]{1,0:T(8,128)(2,1)S(1)}, bf16[32,1024]{1,0:T(8,128)(2,1)S(1)}, u32[]{:S(2)}, u32[]{:S(2)}) collective-permute-start(bf16[32,1024]{1,0:T(8,128)(2,1)S(1)} %get-tuple-element.12.refs_0_), channel_id=1, source_target_pairs={{0,4},{2,6},{4,0},{6,2},{1,5},{3,7},{5,1},{7,3},{8,12},{10,14},{12... | collective-permute-start | bytes 196616 | tf_op jit(solution)/shard_map/ppermute | solution.py:24
  16.0 0.2 collective-permute-start.4
  16.2 0.0 collective-permute-done.9.refs_0_
  16.2 0.7 %collective-permute-start.10 = (bf16[32,1024]{1,0:T(8,128)(2,1)S(1)}, bf16[32,1024]{1,0:T(8,128)(2,1)S(1)}, u32[]{:S(2)}, u32[]{:S(2)}) collective-permute-start(bf16[32,1024]{1,0:T(8,128)(2,1)S(1)} %collective-permute-done.9.refs_0_), channel_id=1, source_target_pairs={{0,2},{2,0},{4,6},{6,4},{1,3},{3,1},{5,7},{7,5},{8,10},{10,8},{12,... | collective-permute-start | bytes 196616 | tf_op jit(solution)/shard_map/ppermute | solution.py:24
  16.9 0.0 collective-permute-done.2.refs_1_
  16.9 3.5 %collective-permute-start.11 = (bf16[32,1024]{1,0:T(8,128)(2,1)S(1)}, bf16[32,1024]{1,0:T(8,128)(2,1)S(1)}, u32[]{:S(2)}, u32[]{:S(2)}) collective-permute-start(bf16[32,1024]{1,0:T(8,128)(2,1)S(1)} %collective-permute-done.9.refs_0_), channel_id=1, source_target_pairs={{0,4},{2,6},{4,0},{6,2},{1,5},{3,7},{5,1},{7,3},{8,12},{10,14},{12... | collective-permute-start | bytes 196616 | tf_op jit(solution)/shard_map/ppermute | solution.py:24
  20.4 0.0 collective-permute-done.3.refs_2_
  20.4 0.7 %collective-permute-start.12 = (bf16[32,1024]{1,0:T(8,128)(2,1)S(1)}, bf16[32,1024]{1,0:T(8,128)(2,1)S(1)}, u32[]{:S(2)}, u32[]{:S(2)}) collective-permute-start(bf16[32,1024]{1,0:T(8,128)(2,1)S(1)} %collective-permute-done.9.refs_0_), channel_id=1, source_target_pairs={{0,6},{2,4},{4,2},{6,0},{1,7},{3,5},{5,3},{7,1},{8,14},{10,12},{12... | collective-permute-start | bytes 196616 | tf_op jit(solution)/shard_map/ppermute | solution.py:24
  21.0 1.6 %collective-permute-done.4.refs_3_ = bf16[32,1024]{1,0:T(8,128)(2,1)S(1)} collective-permute-done((bf16[32,1024]{1,0:T(8,128)(2,1)S(1)}, bf16[32,1024]{1,0:T(8,128)(2,1)S(1)}, u32[]{:S(2)}, u32[]{:S(2)}) %collective-permute-start.4) | collective-permute-done | bytes 65568 | tf_op jit(solution)/shard_map/ppermute | solution.py:24
  22.6 0.0 collective-permute-done.5.refs_6_
  22.6 0.0 copy-done
  22.6 0.0 copy-done.2
  22.7 2.5 %shard_map.74.refs_0_ = bf16[32,512]{1,0:T(8,128)(2,1)S(1)} custom-call(bf16[32,1024]{1,0:T(8,128)(2,1)S(1)} %get-tuple-element.12.refs_0_, bf16[32,1024]{1,0:T(8,128)(2,1)S(1)} %collective-permute-done.2.refs_1_, bf16[32,1024]{1,0:T(8,128)(2,1)S(1)} %collective-permute-done.3.refs_2_, bf16[32,1024]{1,0:T(8,128)(2,1)S(1)} %collective-permute-done.4.refs_3_, ...), custom_call_target="tpu_custom_call" | custom-call | flops 134217728 | bytes 4456448 | tf_op jit(solution)/shard_map/pallas_call | solution.py:221
  25.1 0.0 copy-start.1
  25.1 0.0 copy-start.3
  25.2 0.1 collective-permute-start.6
  25.2 2.1 %collective-permute-start.7 = (bf16[32,512]{1,0:T(8,128)(2,1)S(1)}, bf16[32,512]{1,0:T(8,128)(2,1)S(1)}, u32[]{:S(2)}, u32[]{:S(2)}) collective-permute-start(bf16[32,512]{1,0:T(8,128)(2,1)S(1)} %shard_map.74.refs_0_), channel_id=1, source_target_pairs={{0,4},{2,6},{4,0},{6,2},{1,5},{3,7},{5,1},{7,3},{8,12},{10,14},{12... | collective-permute-start | bytes 98312 | tf_op jit(solution)/shard_map/ppermute | solution.py:24
  27.3 0.0 collective-permute-done.10.refs_1_
  27.3 2.3 %collective-permute-start.8 = (bf16[32,512]{1,0:T(8,128)(2,1)S(1)}, bf16[32,512]{1,0:T(8,128)(2,1)S(1)}, u32[]{:S(2)}, u32[]{:S(2)}) collective-permute-start(bf16[32,512]{1,0:T(8,128)(2,1)S(1)} %shard_map.74.refs_0_), channel_id=1, source_target_pairs={{0,6},{2,4},{4,2},{6,0},{1,7},{3,5},{5,3},{7,1},{8,14},{10,12},{12... | collective-permute-start | bytes 98312 | tf_op jit(solution)/shard_map/ppermute | solution.py:24
  29.6 0.0 collective-permute-done.11.refs_2_
  29.6 0.0 collective-permute-done.12.refs_3_
  29.6 2.5 %shard_map.75.refs_4_ = bf16[32,512]{1,0:T(8,128)(2,1)S(1)} custom-call(bf16[32,1024]{1,0:T(8,128)(2,1)S(1)} %collective-permute-done.9.refs_0_, bf16[32,1024]{1,0:T(8,128)(2,1)S(1)} %collective-permute-done.10.refs_1_, bf16[32,1024]{1,0:T(8,128)(2,1)S(1)} %collective-permute-done.11.refs_2_, bf16[32,1024]{1,0:T(8,128)(2,1)S(1)} %collective-permute-done.12.refs_3_, ...), custom_call_target="tpu_custom_call" | custom-call | flops 134217728 | bytes 4456448 | tf_op jit(solution)/shard_map/pallas_call | solution.py:221
  32.1 0.0 collective-permute-start.13
  32.1 2.1 %collective-permute-start.14 = (bf16[32,512]{1,0:T(8,128)(2,1)S(1)}, bf16[32,512]{1,0:T(8,128)(2,1)S(1)}, u32[]{:S(2)}, u32[]{:S(2)}) collective-permute-start(bf16[32,512]{1,0:T(8,128)(2,1)S(1)} %shard_map.75.refs_4_), channel_id=1, source_target_pairs={{0,4},{2,6},{4,0},{6,2},{1,5},{3,7},{5,1},{7,3},{8,12},{10,14},{12... | collective-permute-start | bytes 98312 | tf_op jit(solution)/shard_map/ppermute | solution.py:24
  34.2 0.0 collective-permute-done.6.refs_1_
  34.2 2.3 %collective-permute-start.15 = (bf16[32,512]{1,0:T(8,128)(2,1)S(1)}, bf16[32,512]{1,0:T(8,128)(2,1)S(1)}, u32[]{:S(2)}, u32[]{:S(2)}) collective-permute-start(bf16[32,512]{1,0:T(8,128)(2,1)S(1)} %shard_map.75.refs_4_), channel_id=1, source_target_pairs={{0,6},{2,4},{4,2},{6,0},{1,7},{3,5},{5,3},{7,1},{8,14},{10,12},{12... | collective-permute-start | bytes 98312 | tf_op jit(solution)/shard_map/ppermute | solution.py:24
  36.5 0.0 collective-permute-done.7.refs_2_
  36.5 0.0 collective-permute-done.8.refs_3_
  36.6 0.0 collective-permute-done.13.refs_5_
  36.6 0.4 collective-permute-done.14.refs_6_
  37.0 3.0 %collective-permute-done.15.refs_7_ = bf16[32,512]{1,0:T(8,128)(2,1)S(1)} collective-permute-done((bf16[32,512]{1,0:T(8,128)(2,1)S(1)}, bf16[32,512]{1,0:T(8,128)(2,1)S(1)}, u32[]{:S(2)}, u32[]{:S(2)}) %collective-permute-start.15) | collective-permute-done | bytes 32800 | tf_op jit(solution)/shard_map/ppermute | solution.py:24
  40.0 1.5 %collective-permute-start.16 = (bf16[8,32,512]{2,1,0:T(8,128)(2,1)S(1)}, bf16[8,32,512]{2,1,0:T(8,128)(2,1)S(1)}, u32[]{:S(2)}, u32[]{:S(2)}) collective-permute-start(bf16[8,32,512]{2,1,0:T(8,128)(2,1)S(1)} %bitcast_dynamic-update-slice_fusion), channel_id=1, source_target_pairs={{0,1},{1,0},{2,3},{3,2},{4,5},{5,4},{6,7},{7,6},{8,9},{9,8},{10,11... | collective-permute-start | bytes 786440 | tf_op jit(solution)/shard_map/ppermute | solution.py:24
  41.5 1.2 %collective-permute-done.16.refs_8_ = bf16[8,32,512]{2,1,0:T(8,128)(2,1)S(1)} collective-permute-done((bf16[8,32,512]{2,1,0:T(8,128)(2,1)S(1)}, bf16[8,32,512]{2,1,0:T(8,128)(2,1)S(1)}, u32[]{:S(2)}, u32[]{:S(2)}) %collective-permute-start.16) | collective-permute-done | bytes 262176 | tf_op jit(solution)/shard_map/ppermute | solution.py:24
  42.7 0.0 copy-done.1
  42.7 0.0 copy-done.3
  42.7 1.4 %shard_map.76 = bf16[128,1024]{1,0:T(8,128)(2,1)} custom-call(s32[4,128]{1,0:T(4,128)S(1)} %bitcast.25, bf16[128,1024]{1,0:T(8,128)(2,1)S(1)} %copy-done.1, bf16[32,512]{1,0:T(8,128)(2,1)S(1)} %shard_map.74.refs_0_, bf16[32,512]{1,0:T(8,128)(2,1)S(1)} %collective-permute-done.6.refs_1_, bf16[32,512]{1,0:T(8,128)(2,1)S(1)} %collective-permute-done.7.refs_2_, ...), custom_call_target="tpu_custom_call" | custom-call | tf_op jit(solution)/shard_map/pallas_call | solution.py:263
  (11 shorter events, 0.1 us)
Async XLA Ops:
  0.0 22.6 %collective-permute-start.5 = (bf16[4096,256]{1,0:T(8,128)(2,1)}, bf16[4096,256]{1,0:T(8,128)(2,1)}, u32[]{:S(2)}, u32[]{:S(2)}) collective-permute-start(bf16[4096,256]{1,0:T(8,128)(2,1)} %bitcast.19), channel_id=1, source_target_pairs={{0,1},{1,0},{2,3},{3,2},{4,5},{5,4},{6,7},{7,6},{8,9},{9,8},{10,11... | collective-permute-start | bytes 6291464 | tf_op jit(solution)/shard_map/ppermute | solution.py:24
  0.5 22.2 %copy-start = (bf16[4096,1,256]{2,0,1:T(8,128)(2,1)S(1)}, bf16[4096,1,256]{2,0,1:T(8,128)(2,1)}, u32[]{:S(2)}) copy-start(bf16[4096,1,256]{2,0,1:T(8,128)(2,1)} %param.11) | copy-start | bytes 6291460
  0.5 22.2 %copy-start.2 = (f32[4096]{0:T(1024)S(1)}, f32[4096]{0:T(1024)}, u32[]{:S(2)}) copy-start(f32[4096]{0:T(1024)} %param.10) | copy-start | bytes 49156
  5.8 1.6 %collective-permute-start = (f32[64,1024]{1,0:T(8,128)S(1)}, f32[64,1024]{1,0:T(8,128)S(1)}, u32[]{:S(2)}, u32[]{:S(2)}) collective-permute-start(f32[64,1024]{1,0:T(8,128)S(1)} %get-tuple-element.10), channel_id=1, source_target_pairs={{0,1},{1,0},{2,3},{3,2},{4,5},{5,4},{6,7},{7,6},{8,9},{9,8},{10,11... | collective-permute-start | bytes 786440 | tf_op jit(solution)/shard_map/ppermute | solution.py:24
  7.4 0.7 %collective-permute-start.1 = (bf16[32,1024]{1,0:T(8,128)(2,1)S(1)}, bf16[32,1024]{1,0:T(8,128)(2,1)S(1)}, u32[]{:S(2)}, u32[]{:S(2)}) collective-permute-start(bf16[32,1024]{1,0:T(8,128)(2,1)S(1)} %slice.8), channel_id=1, source_target_pairs={{1,9},{9,1},{17,25},{25,17},{3,11},{11,3},{19,27},{27,19},{5,13},{... | collective-permute-start | bytes 196616 | tf_op jit(solution)/shard_map/ppermute | solution.py:41
  8.1 8.0 %collective-permute-start.9 = (bf16[32,1024]{1,0:T(8,128)(2,1)S(1)}, bf16[32,1024]{1,0:T(8,128)(2,1)S(1)}, u32[]{:S(2)}, u32[]{:S(2)}) collective-permute-start(bf16[32,1024]{1,0:T(8,128)(2,1)S(1)} %get-tuple-element.11), channel_id=1, source_target_pairs={{0,24},{1,17},{8,16},{9,25},{16,8},{17,1},{24,0},{25,9},{2,26},{3,... | collective-permute-start | bytes 196616 | tf_op jit(solution)/shard_map/ppermute | solution.py:41
  11.8 5.1 %collective-permute-start.2 = (bf16[32,1024]{1,0:T(8,128)(2,1)S(1)}, bf16[32,1024]{1,0:T(8,128)(2,1)S(1)}, u32[]{:S(2)}, u32[]{:S(2)}) collective-permute-start(bf16[32,1024]{1,0:T(8,128)(2,1)S(1)} %get-tuple-element.12.refs_0_), channel_id=1, source_target_pairs={{0,2},{2,0},{4,6},{6,4},{1,3},{3,1},{5,7},{7,5},{8,10},{10,8},{12,... | collective-permute-start | bytes 196616 | tf_op jit(solution)/shard_map/ppermute | solution.py:24
  13.4 7.0 %collective-permute-start.3 = (bf16[32,1024]{1,0:T(8,128)(2,1)S(1)}, bf16[32,1024]{1,0:T(8,128)(2,1)S(1)}, u32[]{:S(2)}, u32[]{:S(2)}) collective-permute-start(bf16[32,1024]{1,0:T(8,128)(2,1)S(1)} %get-tuple-element.12.refs_0_), channel_id=1, source_target_pairs={{0,4},{2,6},{4,0},{6,2},{1,5},{3,7},{5,1},{7,3},{8,12},{10,14},{12... | collective-permute-start | bytes 196616 | tf_op jit(solution)/shard_map/ppermute | solution.py:24
  16.0 6.7 %collective-permute-start.4 = (bf16[32,1024]{1,0:T(8,128)(2,1)S(1)}, bf16[32,1024]{1,0:T(8,128)(2,1)S(1)}, u32[]{:S(2)}, u32[]{:S(2)}) collective-permute-start(bf16[32,1024]{1,0:T(8,128)(2,1)S(1)} %get-tuple-element.12.refs_0_), channel_id=1, source_target_pairs={{0,6},{2,4},{4,2},{6,0},{1,7},{3,5},{5,3},{7,1},{8,14},{10,12},{12... | collective-permute-start | bytes 196616 | tf_op jit(solution)/shard_map/ppermute | solution.py:24
  16.2 11.2 %collective-permute-start.10 = (bf16[32,1024]{1,0:T(8,128)(2,1)S(1)}, bf16[32,1024]{1,0:T(8,128)(2,1)S(1)}, u32[]{:S(2)}, u32[]{:S(2)}) collective-permute-start(bf16[32,1024]{1,0:T(8,128)(2,1)S(1)} %collective-permute-done.9.refs_0_), channel_id=1, source_target_pairs={{0,2},{2,0},{4,6},{6,4},{1,3},{3,1},{5,7},{7,5},{8,10},{10,8},{12,... | collective-permute-start | bytes 196616 | tf_op jit(solution)/shard_map/ppermute | solution.py:24
  16.9 12.7 %collective-permute-start.11 = (bf16[32,1024]{1,0:T(8,128)(2,1)S(1)}, bf16[32,1024]{1,0:T(8,128)(2,1)S(1)}, u32[]{:S(2)}, u32[]{:S(2)}) collective-permute-start(bf16[32,1024]{1,0:T(8,128)(2,1)S(1)} %collective-permute-done.9.refs_0_), channel_id=1, source_target_pairs={{0,4},{2,6},{4,0},{6,2},{1,5},{3,7},{5,1},{7,3},{8,12},{10,14},{12... | collective-permute-start | bytes 196616 | tf_op jit(solution)/shard_map/ppermute | solution.py:24
  20.4 9.3 %collective-permute-start.12 = (bf16[32,1024]{1,0:T(8,128)(2,1)S(1)}, bf16[32,1024]{1,0:T(8,128)(2,1)S(1)}, u32[]{:S(2)}, u32[]{:S(2)}) collective-permute-start(bf16[32,1024]{1,0:T(8,128)(2,1)S(1)} %collective-permute-done.9.refs_0_), channel_id=1, source_target_pairs={{0,6},{2,4},{4,2},{6,0},{1,7},{3,5},{5,3},{7,1},{8,14},{10,12},{12... | collective-permute-start | bytes 196616 | tf_op jit(solution)/shard_map/ppermute | solution.py:24
  25.1 17.5 %copy-start.1 = (bf16[128,1024]{1,0:T(8,128)(2,1)S(1)}, bf16[128,1024]{1,0:T(8,128)(2,1)}, u32[]{:S(2)}) copy-start(bf16[128,1024]{1,0:T(8,128)(2,1)} %query_ref.1) | copy-start | bytes 786436
  25.1 17.5 %copy-start.3 = (s32[512,1]{0,1:T(1,128)S(1)}, s32[512,1]{0,1:T(1,128)}, u32[]{:S(2)}) copy-start(s32[512,1]{0,1:T(1,128)} %param.12) | copy-start | bytes 6148
  25.2 9.1 %collective-permute-start.6 = (bf16[32,512]{1,0:T(8,128)(2,1)S(1)}, bf16[32,512]{1,0:T(8,128)(2,1)S(1)}, u32[]{:S(2)}, u32[]{:S(2)}) collective-permute-start(bf16[32,512]{1,0:T(8,128)(2,1)S(1)} %shard_map.74.refs_0_), channel_id=1, source_target_pairs={{0,2},{2,0},{4,6},{6,4},{1,3},{3,1},{5,7},{7,5},{8,10},{10,8},{12,... | collective-permute-start | bytes 98312 | tf_op jit(solution)/shard_map/ppermute | solution.py:24
  25.2 11.3 %collective-permute-start.7 = (bf16[32,512]{1,0:T(8,128)(2,1)S(1)}, bf16[32,512]{1,0:T(8,128)(2,1)S(1)}, u32[]{:S(2)}, u32[]{:S(2)}) collective-permute-start(bf16[32,512]{1,0:T(8,128)(2,1)S(1)} %shard_map.74.refs_0_), channel_id=1, source_target_pairs={{0,4},{2,6},{4,0},{6,2},{1,5},{3,7},{5,1},{7,3},{8,12},{10,14},{12... | collective-permute-start | bytes 98312 | tf_op jit(solution)/shard_map/ppermute | solution.py:24
  27.3 9.2 %collective-permute-start.8 = (bf16[32,512]{1,0:T(8,128)(2,1)S(1)}, bf16[32,512]{1,0:T(8,128)(2,1)S(1)}, u32[]{:S(2)}, u32[]{:S(2)}) collective-permute-start(bf16[32,512]{1,0:T(8,128)(2,1)S(1)} %shard_map.74.refs_0_), channel_id=1, source_target_pairs={{0,6},{2,4},{4,2},{6,0},{1,7},{3,5},{5,3},{7,1},{8,14},{10,12},{12... | collective-permute-start | bytes 98312 | tf_op jit(solution)/shard_map/ppermute | solution.py:24
  32.1 4.5 %collective-permute-start.13 = (bf16[32,512]{1,0:T(8,128)(2,1)S(1)}, bf16[32,512]{1,0:T(8,128)(2,1)S(1)}, u32[]{:S(2)}, u32[]{:S(2)}) collective-permute-start(bf16[32,512]{1,0:T(8,128)(2,1)S(1)} %shard_map.75.refs_4_), channel_id=1, source_target_pairs={{0,2},{2,0},{4,6},{6,4},{1,3},{3,1},{5,7},{7,5},{8,10},{10,8},{12,... | collective-permute-start | bytes 98312 | tf_op jit(solution)/shard_map/ppermute | solution.py:24
  32.1 4.9 %collective-permute-start.14 = (bf16[32,512]{1,0:T(8,128)(2,1)S(1)}, bf16[32,512]{1,0:T(8,128)(2,1)S(1)}, u32[]{:S(2)}, u32[]{:S(2)}) collective-permute-start(bf16[32,512]{1,0:T(8,128)(2,1)S(1)} %shard_map.75.refs_4_), channel_id=1, source_target_pairs={{0,4},{2,6},{4,0},{6,2},{1,5},{3,7},{5,1},{7,3},{8,12},{10,14},{12... | collective-permute-start | bytes 98312 | tf_op jit(solution)/shard_map/ppermute | solution.py:24
  34.2 5.7 %collective-permute-start.15 = (bf16[32,512]{1,0:T(8,128)(2,1)S(1)}, bf16[32,512]{1,0:T(8,128)(2,1)S(1)}, u32[]{:S(2)}, u32[]{:S(2)}) collective-permute-start(bf16[32,512]{1,0:T(8,128)(2,1)S(1)} %shard_map.75.refs_4_), channel_id=1, source_target_pairs={{0,6},{2,4},{4,2},{6,0},{1,7},{3,5},{5,3},{7,1},{8,14},{10,12},{12... | collective-permute-start | bytes 98312 | tf_op jit(solution)/shard_map/ppermute | solution.py:24
  40.0 2.7 %collective-permute-start.16 = (bf16[8,32,512]{2,1,0:T(8,128)(2,1)S(1)}, bf16[8,32,512]{2,1,0:T(8,128)(2,1)S(1)}, u32[]{:S(2)}, u32[]{:S(2)}) collective-permute-start(bf16[8,32,512]{2,1,0:T(8,128)(2,1)S(1)} %bitcast_dynamic-update-slice_fusion), channel_id=1, source_target_pairs={{0,1},{1,0},{2,3},{3,2},{4,5},{5,4},{6,7},{7,6},{8,9},{9,8},{10,11... | collective-permute-start | bytes 786440 | tf_op jit(solution)/shard_map/ppermute | solution.py:24

commit v7 on v6

--- a/solution.py
+++ b/solution.py
@@ -24,24 +24,31 @@
     return lax.ppermute(value, axis, [(i, i ^ offset) for i in range(size)])
 
 
-def route_offsets(clips, cores):
+def routing(clips, cores, capacity):
     if clips == 4 and cores == 2:
-        return [0, 3, 1, 2]
-    return list(range(clips))
-
-
-def route(value, place):
+        half = capacity // 2
+        runs = [
+            [(0, 0, half), (3, 0, half), (1, 0, capacity)],
+            [(0, half, half), (3, half, half), (2, 0, capacity)],
+        ]
+        return runs, [[0, 1], [2]]
+    each = clips // cores
+    runs = [[(t * each + i, 0, capacity) for i in range(each)] for t in range(cores)]
+    return runs, [list(range(each))]
+
+
+def route(value, offsets):
     clips, cores = lax.axis_size("clip"), lax.axis_size("tp")
-    offsets = route_offsets(clips, cores)
-    here = [offsets[t * (clips // cores) + place] for t in range(cores)]
+    if not any(offsets):
+        return value
     pairs = [
-        (i * cores + t, (i ^ here[t]) * cores + t)
-        for i in range(clips) for t in range(cores) if here[t]
+        (i * cores + t, (i ^ offsets[t]) * cores + t)
+        for i in range(clips) for t in range(cores) if offsets[t]
     ]
     moved = lax.ppermute(value, ("clip", "tp"), pairs)
-    if all(here):
+    if all(offsets):
         return moved
-    return jnp.where(lax.axis_index("tp") == here.index(0), value, moved)
+    return jnp.where(lax.axis_index("tp") == offsets.index(0), value, moved)
 
 
 def slot_select(dest_ref, clip, core, capacity, cores):
@@ -55,10 +62,14 @@
     before = jnp.dot(onehot, earlier, preferred_element_type=F32)
     rank = jnp.sum(before * onehot, axis=0, keepdims=True).astype(jnp.int32)
     away = named ^ clip
-    block = jnp.zeros_like(away)
-    for place, offset in enumerate(route_offsets(clips, cores)):
-        block = jnp.where(away == offset, place, block)
-    slot = (block ^ (core * (clips // cores))) * capacity + rank
+    slot = jnp.zeros_like(away)
+    share = clips * capacity // cores
+    for t, runs in enumerate(routing(clips, cores, capacity)[0]):
+        at = 0
+        for offset, first, count in runs:
+            inside = (away == offset) & (rank >= first) & (rank < first + count)
+            slot = jnp.where(inside, (core ^ t) * share + at - first + rank, slot)
+            at += count
     return (lax.broadcasted_iota(jnp.int32, (clips * capacity, rows), 0) == slot).astype(BF16)
 
 
@@ -162,16 +173,19 @@
     slots = clips * capacity
     dim = query_ref.shape[1] // (parts * cores * heads_here)
     counts = jnp.sum((dest_ref[...] == clip).astype(jnp.int32), axis=1, keepdims=True)
+    share = slots // cores
     lane = lax.broadcasted_iota(jnp.int32, (clips, slots), 1)
-    block = (lane // capacity) ^ (core * (clips // cores))
-    source = jnp.zeros_like(lane)
-    for place, offset in enumerate(route_offsets(clips, cores)):
-        source = jnp.where(block == place, offset ^ clip, source)
-    limit = jnp.sum(
-        jnp.where(lax.broadcasted_iota(jnp.int32, lane.shape, 0) == source, counts, 0),
-        axis=0, keepdims=True,
-    )
-    valid = lax.broadcasted_iota(jnp.int32, (1, slots), 1) % capacity < limit
+    owner, place = (lane // share) ^ core, lane % share
+    source, rank = jnp.zeros_like(lane), jnp.zeros_like(lane)
+    for t, runs in enumerate(routing(clips, cores, capacity)[0]):
+        at = 0
+        for offset, first, count in runs:
+            inside = (owner == t) & (place >= at) & (place < at + count)
+            source = jnp.where(inside, offset ^ clip, source)
+            rank = jnp.where(inside, first + place - at, rank)
+            at += count
+    here = lax.broadcasted_iota(jnp.int32, lane.shape, 0) == source
+    valid = jnp.sum(jnp.where(here & (rank < counts), 1, 0), axis=0, keepdims=True) > 0
     heads = [(k, c, i) for k in range(parts) for c in range(cores) for i in range(heads_here)]
 
     def columns(head):
@@ -229,7 +243,7 @@
             bytes_accessed=2 * parts * width * (rows + wide),
             transcendentals=0,
         ),
-    )(*texts, gain, *weights)
+    )(*texts, gain, *[pltpu.with_memory_space_constraint(x, pltpu.VMEM) for x in weights])
 
 
 def shards(ffn_hidden, ffn_weight, residual, norm_gain, kv_weight, destination, queries):
@@ -246,22 +260,22 @@
     for g in range(1, cores):
         own = own + swap(send[(g - 1) * share:g * share], "tp", g)
     text = (text.astype(F32) + own).astype(BF16)
-    places = clips // cores
-    groups = math.gcd(2, places)
+    runs, groups = routing(clips, cores, capacity)
+    edges = [sum(run[2] for run in runs[0][:n]) for n in range(len(runs[0]) + 1)]
+    arrived = [
+        route(text[edges[n]:edges[n + 1]], [some[n][0] for some in runs])
+        for n in range(len(runs[0]))
+    ]
     own = []
-    for first in range(0, places, places // groups):
-        arrived = [
-            route(text[i * capacity:(i + 1) * capacity], i)
-            for i in range(first, first + places // groups)
-        ]
-        arrived = jnp.concatenate(arrived, axis=0)
-        texts = [arrived] + [swap(arrived, "seq", k) for k in range(1, parts)]
+    for group in groups:
+        mine = jnp.concatenate([arrived[n] for n in group], axis=0)
+        texts = [mine] + [swap(mine, "seq", k) for k in range(1, parts)]
         block = keyval(texts, gain, weights)
         own += [block] + [swap(block, "seq", k) for k in range(1, parts)]
     packed = jnp.stack(own)
     others = [swap(packed, "tp", g) for g in range(1, cores)]
     return pl.pallas_call(
-        functools.partial(attend_kernel, parts, cores, heads_here, capacity, groups),
+        functools.partial(attend_kernel, parts, cores, heads_here, capacity, len(groups)),
         in_specs=[whole()] * (2 + len(own) + len(others)),
         out_specs=whole(),
         out_shape=jax.ShapeDtypeStruct(queries.shape, BF16),

time: 44.2 us -> 42.8 us (0.968)
  Pallas kernels: 11.6 us -> 8.46 us
  starting transfers between devices: 24.5 us -> 26 us
    pallas_call x2, Pallas kernels: 4.95 us -> 1.77 us  [keyval(): pl.pallas_call(functools.partial(keyval_kernel, parts, len(weights)), in_...]
    ppermute x15, starting transfers between devices: 20.2 us -> 21.8 us  [swap(): return lax.ppermute(value, axis, [(i, i ^ offset) for i in range(size)])]
    ppermute x2, waiting for transfers between devices: 0.01 us -> 1.38 us  [route(): moved = lax.ppermute(value, ('clip', 'tp'), pairs)]
    ppermute x15, waiting for transfers between devices: 7.68 us -> 6.53 us  [swap(): return lax.ppermute(value, axis, [(i, i ^ offset) for i in range(size)])]
  transfers between devices with their start and end apart: 17 -> 17, of which waited for: 5 -> 5; matrix products, arithmetic and copies ran while one was open for 0% -> 0% of each run, Pallas kernels for 23% -> 17%
where the time goes in v7:
time: 42.8 us; the launch traced here: 42.6 us
  starting transfers between devices  26 us (61%)
  Pallas kernels  8.46 us (20%)
  waiting for transfers between devices  7.92 us (19%)
    ppermute x15, starting transfers between devices, swap(): return lax.ppermute(value, axis, [(i, i ^ offset) for i in range(size)])  21.8 us
    ppermute x15, waiting for transfers between devices, swap(): return lax.ppermute(value, axis, [(i, i ^ offset) for i in range(size)])  6.53 us
    pallas_call x1, Pallas kernels, ffn(): pl.pallas_call(functools.partial(ffn_kernel, capacity, cores, steps), in_...  5.3 us
    ppermute x2, starting transfers between devices, route(): moved = lax.ppermute(value, ('clip', 'tp'), pairs)  4.2 us
    pallas_call x2, Pallas kernels, keyval(): pl.pallas_call(functools.partial(keyval_kernel, parts, len(weights)), in_...  1.77 us
    pallas_call x1, Pallas kernels, shards(): pl.pallas_call(functools.partial(attend_kernel, parts, cores, heads_here,...  1.39 us
    ppermute x2, waiting for transfers between devices, route(): moved = lax.ppermute(value, ('clip', 'tp'), pairs)  1.38 us
  transfers between devices with their start and end apart: 17, of which 5 were waited for; matrix products, arithmetic and copies ran while one was open for 0% of the time, Pallas kernels for 17%

profile of v7, /device:TPU:0, one launch (start us, length us, event | category | flops | bytes accessed | tf_op | source)
XLA Modules:
  0.0 42.6 jit_solution(5002414655528760047)
XLA Ops:
  0.0 0.5 %collective-permute-start.5 = (bf16[4096,256]{1,0:T(8,128)(2,1)}, bf16[4096,256]{1,0:T(8,128)(2,1)S(1)}, u32[]{:S(2)}, u32[]{:S(2)}) collective-permute-start(bf16[4096,256]{1,0:T(8,128)(2,1)} %bitcast.19), channel_id=1, source_target_pairs={{0,1},{1,0},{2,3},{3,2},{4,5},{5,4},{6,7},{7,6},{8,9},{9,8},{10,11... | collective-permute-start | bytes 6291464 | tf_op jit(solution)/shard_map/ppermute | solution.py:24
  0.5 0.0 copy-start
  0.5 0.0 copy-start.2
  0.5 5.3 %shard_map.73 = (f32[64,1024]{1,0:T(8,128)S(1)}, f32[64,1024]{1,0:T(8,128)S(1)}, bf16[64,1024]{1,0:T(8,128)(2,1)S(1)}) custom-call(s32[4,128]{1,0:T(4,128)} %bitcast.24, bf16[128,5120]{1,0:T(8,128)(2,1)} %hidden_hbm.1, bf16[5120,1024]{1,0:T(8,128)(2,1)} %weight_hbm.1, bf16[128,1024]{1,0:T(8,128)(2,1)} %residual_hbm.1), custom_call_target="tpu_custom_call" | custom-call | flops 1509949440 | bytes 11796480 | tf_op jit(solution)/shard_map/pallas_call | solution.py:122
  5.8 0.1 collective-permute-start
  5.9 1.5 %collective-permute-done = f32[64,1024]{1,0:T(8,128)S(1)} collective-permute-done((f32[64,1024]{1,0:T(8,128)S(1)}, f32[64,1024]{1,0:T(8,128)S(1)}, u32[]{:S(2)}, u32[]{:S(2)}) %collective-permute-start) | collective-permute-done | bytes 262176 | tf_op jit(solution)/shard_map/ppermute | solution.py:24
  7.4 3.7 %collective-permute-start.1 = (bf16[16,1024]{1,0:T(8,128)(2,1)S(1)}, bf16[16,1024]{1,0:T(8,128)(2,1)S(1)}, u32[]{:S(2)}, u32[]{:S(2)}) collective-permute-start(bf16[16,1024]{1,0:T(8,128)(2,1)S(1)} %get-tuple-element.12), channel_id=1, source_target_pairs={{0,24},{1,25},{8,16},{9,17},{16,8},{17,9},{24,0},{25,1},{2,26},{3,... | collective-permute-start | bytes 98312 | tf_op jit(solution)/shard_map/ppermute | solution.py:48
  11.1 0.5 %collective-permute-start.9 = (bf16[32,1024]{1,0:T(8,128)(2,1)S(1)}, bf16[32,1024]{1,0:T(8,128)(2,1)S(1)}, u32[]{:S(2)}, u32[]{:S(2)}) collective-permute-start(bf16[32,1024]{1,0:T(8,128)(2,1)S(1)} %slice.14), channel_id=1, source_target_pairs={{0,8},{1,17},{8,0},{9,25},{16,24},{17,1},{24,16},{25,9},{2,10},{3,... | collective-permute-start | bytes 196616 | tf_op jit(solution)/shard_map/ppermute | solution.py:48
  11.6 1.4 %collective-permute-done.1 = bf16[16,1024]{1,0:T(8,128)(2,1)S(1)} collective-permute-done((bf16[16,1024]{1,0:T(8,128)(2,1)S(1)}, bf16[16,1024]{1,0:T(8,128)(2,1)S(1)}, u32[]{:S(2)}, u32[]{:S(2)}) %collective-permute-start.1) | collective-permute-done | bytes 32800 | tf_op jit(solution)/shard_map/ppermute | solution.py:48
  13.0 2.0 %collective-permute-start.2 = (bf16[32,1024]{1,0:T(8,128)(2,1)S(1)}, bf16[32,1024]{1,0:T(8,128)(2,1)S(1)}, u32[]{:S(2)}, u32[]{:S(2)}) collective-permute-start(bf16[32,1024]{1,0:T(8,128)(2,1)S(1)} %pad_maximum_fusion.refs_0_), channel_id=1, source_target_pairs={{0,2},{2,0},{4,6},{6,4},{1,3},{3,1},{5,7},{7,5},{8,10},{10,8},{12,... | collective-permute-start | bytes 196616 | tf_op jit(solution)/shard_map/ppermute | solution.py:24
  15.0 2.6 %collective-permute-start.3 = (bf16[32,1024]{1,0:T(8,128)(2,1)S(1)}, bf16[32,1024]{1,0:T(8,128)(2,1)S(1)}, u32[]{:S(2)}, u32[]{:S(2)}) collective-permute-start(bf16[32,1024]{1,0:T(8,128)(2,1)S(1)} %pad_maximum_fusion.refs_0_), channel_id=1, source_target_pairs={{0,4},{2,6},{4,0},{6,2},{1,5},{3,7},{5,1},{7,3},{8,12},{10,14},{12... | collective-permute-start | bytes 196616 | tf_op jit(solution)/shard_map/ppermute | solution.py:24
  17.6 0.0 collective-permute-start.4
  17.6 0.0 collective-permute-done.9.refs_0_
  17.6 0.9 %collective-permute-start.10 = (bf16[32,1024]{1,0:T(8,128)(2,1)S(1)}, bf16[32,1024]{1,0:T(8,128)(2,1)S(1)}, u32[]{:S(2)}, u32[]{:S(2)}) collective-permute-start(bf16[32,1024]{1,0:T(8,128)(2,1)S(1)} %collective-permute-done.9.refs_0_), channel_id=1, source_target_pairs={{0,2},{2,0},{4,6},{6,4},{1,3},{3,1},{5,7},{7,5},{8,10},{10,8},{12,... | collective-permute-start | bytes 196616 | tf_op jit(solution)/shard_map/ppermute | solution.py:24
  18.5 0.0 collective-permute-done.2.refs_1_
  18.5 3.5 %collective-permute-start.11 = (bf16[32,1024]{1,0:T(8,128)(2,1)S(1)}, bf16[32,1024]{1,0:T(8,128)(2,1)S(1)}, u32[]{:S(2)}, u32[]{:S(2)}) collective-permute-start(bf16[32,1024]{1,0:T(8,128)(2,1)S(1)} %collective-permute-done.9.refs_0_), channel_id=1, source_target_pairs={{0,4},{2,6},{4,0},{6,2},{1,5},{3,7},{5,1},{7,3},{8,12},{10,14},{12... | collective-permute-start | bytes 196616 | tf_op jit(solution)/shard_map/ppermute | solution.py:24
  22.0 0.0 collective-permute-done.3.refs_2_
  22.0 3.4 %collective-permute-start.12 = (bf16[32,1024]{1,0:T(8,128)(2,1)S(1)}, bf16[32,1024]{1,0:T(8,128)(2,1)S(1)}, u32[]{:S(2)}, u32[]{:S(2)}) collective-permute-start(bf16[32,1024]{1,0:T(8,128)(2,1)S(1)} %collective-permute-done.9.refs_0_), channel_id=1, source_target_pairs={{0,6},{2,4},{4,2},{6,0},{1,7},{3,5},{5,3},{7,1},{8,14},{10,12},{12... | collective-permute-start | bytes 196616 | tf_op jit(solution)/shard_map/ppermute | solution.py:24
  25.4 0.0 collective-permute-done.4.refs_3_
  25.4 0.0 collective-permute-done.5.refs_6_
  25.4 0.0 copy-done
  25.4 0.0 copy-done.2
  25.5 0.9 %shard_map.74.refs_0_ = bf16[32,512]{1,0:T(8,128)(2,1)S(1)} custom-call(bf16[32,1024]{1,0:T(8,128)(2,1)S(1)} %pad_maximum_fusion.refs_0_, bf16[32,1024]{1,0:T(8,128)(2,1)S(1)} %collective-permute-done.2.refs_1_, bf16[32,1024]{1,0:T(8,128)(2,1)S(1)} %collective-permute-done.3.refs_2_, bf16[32,1024]{1,0:T(8,128)(2,1)S(1)} %collective-permute-done.4.refs_3_, ...), custom_call_target="tpu_custom_call" | custom-call | flops 134217728 | bytes 4456448 | tf_op jit(solution)/shard_map/pallas_call | solution.py:235
  26.3 0.0 copy-start.1
  26.4 0.0 copy-start.3
  26.4 1.3 %collective-permute-start.6 = (bf16[32,512]{1,0:T(8,128)(2,1)S(1)}, bf16[32,512]{1,0:T(8,128)(2,1)S(1)}, u32[]{:S(2)}, u32[]{:S(2)}) collective-permute-start(bf16[32,512]{1,0:T(8,128)(2,1)S(1)} %shard_map.74.refs_0_), channel_id=1, source_target_pairs={{0,2},{2,0},{4,6},{6,4},{1,3},{3,1},{5,7},{7,5},{8,10},{10,8},{12,... | collective-permute-start | bytes 98312 | tf_op jit(solution)/shard_map/ppermute | solution.py:24
  27.7 1.0 %collective-permute-start.7 = (bf16[32,512]{1,0:T(8,128)(2,1)S(1)}, bf16[32,512]{1,0:T(8,128)(2,1)S(1)}, u32[]{:S(2)}, u32[]{:S(2)}) collective-permute-start(bf16[32,512]{1,0:T(8,128)(2,1)S(1)} %shard_map.74.refs_0_), channel_id=1, source_target_pairs={{0,4},{2,6},{4,0},{6,2},{1,5},{3,7},{5,1},{7,3},{8,12},{10,14},{12... | collective-permute-start | bytes 98312 | tf_op jit(solution)/shard_map/ppermute | solution.py:24
  28.7 0.0 collective-permute-done.10.refs_1_
  28.7 2.1 %collective-permute-start.8 = (bf16[32,512]{1,0:T(8,128)(2,1)S(1)}, bf16[32,512]{1,0:T(8,128)(2,1)S(1)}, u32[]{:S(2)}, u32[]{:S(2)}) collective-permute-start(bf16[32,512]{1,0:T(8,128)(2,1)S(1)} %shard_map.74.refs_0_), channel_id=1, source_target_pairs={{0,6},{2,4},{4,2},{6,0},{1,7},{3,5},{5,3},{7,1},{8,14},{10,12},{12... | collective-permute-start | bytes 98312 | tf_op jit(solution)/shard_map/ppermute | solution.py:24
  30.8 0.0 collective-permute-done.11.refs_2_
  30.8 0.0 collective-permute-done.12.refs_3_
  30.8 0.9 %shard_map.75.refs_4_ = bf16[32,512]{1,0:T(8,128)(2,1)S(1)} custom-call(bf16[32,1024]{1,0:T(8,128)(2,1)S(1)} %collective-permute-done.9.refs_0_, bf16[32,1024]{1,0:T(8,128)(2,1)S(1)} %collective-permute-done.10.refs_1_, bf16[32,1024]{1,0:T(8,128)(2,1)S(1)} %collective-permute-done.11.refs_2_, bf16[32,1024]{1,0:T(8,128)(2,1)S(1)} %collective-permute-done.12.refs_3_, ...), custom_call_target="tpu_custom_call" | custom-call | flops 134217728 | bytes 4456448 | tf_op jit(solution)/shard_map/pallas_call | solution.py:235
  31.7 0.3 collective-permute-start.13
  32.1 1.9 %collective-permute-start.14 = (bf16[32,512]{1,0:T(8,128)(2,1)S(1)}, bf16[32,512]{1,0:T(8,128)(2,1)S(1)}, u32[]{:S(2)}, u32[]{:S(2)}) collective-permute-start(bf16[32,512]{1,0:T(8,128)(2,1)S(1)} %shard_map.75.refs_4_), channel_id=1, source_target_pairs={{0,4},{2,6},{4,0},{6,2},{1,5},{3,7},{5,1},{7,3},{8,12},{10,14},{12... | collective-permute-start | bytes 98312 | tf_op jit(solution)/shard_map/ppermute | solution.py:24
  34.0 0.0 collective-permute-done.6.refs_1_
  34.0 2.1 %collective-permute-start.15 = (bf16[32,512]{1,0:T(8,128)(2,1)S(1)}, bf16[32,512]{1,0:T(8,128)(2,1)S(1)}, u32[]{:S(2)}, u32[]{:S(2)}) collective-permute-start(bf16[32,512]{1,0:T(8,128)(2,1)S(1)} %shard_map.75.refs_4_), channel_id=1, source_target_pairs={{0,6},{2,4},{4,2},{6,0},{1,7},{3,5},{5,3},{7,1},{8,14},{10,12},{12... | collective-permute-start | bytes 98312 | tf_op jit(solution)/shard_map/ppermute | solution.py:24
  36.1 0.0 collective-permute-done.7.refs_2_
  36.1 0.0 collective-permute-done.8.refs_3_
  36.2 0.0 collective-permute-done.13.refs_5_
  36.2 0.7 %collective-permute-done.14.refs_6_ = bf16[32,512]{1,0:T(8,128)(2,1)S(1)} collective-permute-done((bf16[32,512]{1,0:T(8,128)(2,1)S(1)}, bf16[32,512]{1,0:T(8,128)(2,1)S(1)}, u32[]{:S(2)}, u32[]{:S(2)}) %collective-permute-start.14) | collective-permute-done | bytes 32800 | tf_op jit(solution)/shard_map/ppermute | solution.py:24
  36.9 2.8 %collective-permute-done.15.refs_7_ = bf16[32,512]{1,0:T(8,128)(2,1)S(1)} collective-permute-done((bf16[32,512]{1,0:T(8,128)(2,1)S(1)}, bf16[32,512]{1,0:T(8,128)(2,1)S(1)}, u32[]{:S(2)}, u32[]{:S(2)}) %collective-permute-start.15) | collective-permute-done | bytes 32800 | tf_op jit(solution)/shard_map/ppermute | solution.py:24
  39.7 0.0 collective-permute-start.16
  39.7 1.5 %collective-permute-done.16.refs_8_ = bf16[8,32,512]{2,1,0:T(8,128)(2,1)S(1)} collective-permute-done((bf16[8,32,512]{2,1,0:T(8,128)(2,1)S(1)}, bf16[8,32,512]{2,1,0:T(8,128)(2,1)S(1)}, u32[]{:S(2)}, u32[]{:S(2)}) %collective-permute-start.16) | collective-permute-done | bytes 262176 | tf_op jit(solution)/shard_map/ppermute | solution.py:24
  41.2 0.0 copy-done.1
  41.2 0.0 copy-done.3
  41.2 1.4 %shard_map.76 = bf16[128,1024]{1,0:T(8,128)(2,1)} custom-call(s32[4,128]{1,0:T(4,128)S(1)} %bitcast.25, bf16[128,1024]{1,0:T(8,128)(2,1)S(1)} %copy-done.1, bf16[32,512]{1,0:T(8,128)(2,1)S(1)} %shard_map.74.refs_0_, bf16[32,512]{1,0:T(8,128)(2,1)S(1)} %collective-permute-done.6.refs_1_, bf16[32,512]{1,0:T(8,128)(2,1)S(1)} %collective-permute-done.7.refs_2_, ...), custom_call_target="tpu_custom_call" | custom-call | tf_op jit(solution)/shard_map/pallas_call | solution.py:277
  (12 shorter events, 0.1 us)
Async XLA Ops:
  0.0 25.4 %collective-permute-start.5 = (bf16[4096,256]{1,0:T(8,128)(2,1)}, bf16[4096,256]{1,0:T(8,128)(2,1)S(1)}, u32[]{:S(2)}, u32[]{:S(2)}) collective-permute-start(bf16[4096,256]{1,0:T(8,128)(2,1)} %bitcast.19), channel_id=1, source_target_pairs={{0,1},{1,0},{2,3},{3,2},{4,5},{5,4},{6,7},{7,6},{8,9},{9,8},{10,11... | collective-permute-start | bytes 6291464 | tf_op jit(solution)/shard_map/ppermute | solution.py:24
  0.5 25.0 %copy-start = (bf16[4096,1,256]{2,0,1:T(8,128)(2,1)S(1)}, bf16[4096,1,256]{2,0,1:T(8,128)(2,1)}, u32[]{:S(2)}) copy-start(bf16[4096,1,256]{2,0,1:T(8,128)(2,1)} %param.11) | copy-start | bytes 6291460
  0.5 25.0 %copy-start.2 = (f32[4096]{0:T(1024)S(1)}, f32[4096]{0:T(1024)}, u32[]{:S(2)}) copy-start(f32[4096]{0:T(1024)} %param.10) | copy-start | bytes 49156
  5.8 1.6 %collective-permute-start = (f32[64,1024]{1,0:T(8,128)S(1)}, f32[64,1024]{1,0:T(8,128)S(1)}, u32[]{:S(2)}, u32[]{:S(2)}) collective-permute-start(f32[64,1024]{1,0:T(8,128)S(1)} %get-tuple-element.10), channel_id=1, source_target_pairs={{0,1},{1,0},{2,3},{3,2},{4,5},{5,4},{6,7},{7,6},{8,9},{9,8},{10,11... | collective-permute-start | bytes 786440 | tf_op jit(solution)/shard_map/ppermute | solution.py:24
  7.4 5.6 %collective-permute-start.1 = (bf16[16,1024]{1,0:T(8,128)(2,1)S(1)}, bf16[16,1024]{1,0:T(8,128)(2,1)S(1)}, u32[]{:S(2)}, u32[]{:S(2)}) collective-permute-start(bf16[16,1024]{1,0:T(8,128)(2,1)S(1)} %get-tuple-element.12), channel_id=1, source_target_pairs={{0,24},{1,25},{8,16},{9,17},{16,8},{17,9},{24,0},{25,1},{2,26},{3,... | collective-permute-start | bytes 98312 | tf_op jit(solution)/shard_map/ppermute | solution.py:48
  11.1 6.5 %collective-permute-start.9 = (bf16[32,1024]{1,0:T(8,128)(2,1)S(1)}, bf16[32,1024]{1,0:T(8,128)(2,1)S(1)}, u32[]{:S(2)}, u32[]{:S(2)}) collective-permute-start(bf16[32,1024]{1,0:T(8,128)(2,1)S(1)} %slice.14), channel_id=1, source_target_pairs={{0,8},{1,17},{8,0},{9,25},{16,24},{17,1},{24,16},{25,9},{2,10},{3,... | collective-permute-start | bytes 196616 | tf_op jit(solution)/shard_map/ppermute | solution.py:48
  13.0 5.5 %collective-permute-start.2 = (bf16[32,1024]{1,0:T(8,128)(2,1)S(1)}, bf16[32,1024]{1,0:T(8,128)(2,1)S(1)}, u32[]{:S(2)}, u32[]{:S(2)}) collective-permute-start(bf16[32,1024]{1,0:T(8,128)(2,1)S(1)} %pad_maximum_fusion.refs_0_), channel_id=1, source_target_pairs={{0,2},{2,0},{4,6},{6,4},{1,3},{3,1},{5,7},{7,5},{8,10},{10,8},{12,... | collective-permute-start | bytes 196616 | tf_op jit(solution)/shard_map/ppermute | solution.py:24
  15.0 7.0 %collective-permute-start.3 = (bf16[32,1024]{1,0:T(8,128)(2,1)S(1)}, bf16[32,1024]{1,0:T(8,128)(2,1)S(1)}, u32[]{:S(2)}, u32[]{:S(2)}) collective-permute-start(bf16[32,1024]{1,0:T(8,128)(2,1)S(1)} %pad_maximum_fusion.refs_0_), channel_id=1, source_target_pairs={{0,4},{2,6},{4,0},{6,2},{1,5},{3,7},{5,1},{7,3},{8,12},{10,14},{12... | collective-permute-start | bytes 196616 | tf_op jit(solution)/shard_map/ppermute | solution.py:24
  17.6 7.8 %collective-permute-start.4 = (bf16[32,1024]{1,0:T(8,128)(2,1)S(1)}, bf16[32,1024]{1,0:T(8,128)(2,1)S(1)}, u32[]{:S(2)}, u32[]{:S(2)}) collective-permute-start(bf16[32,1024]{1,0:T(8,128)(2,1)S(1)} %pad_maximum_fusion.refs_0_), channel_id=1, source_target_pairs={{0,6},{2,4},{4,2},{6,0},{1,7},{3,5},{5,3},{7,1},{8,14},{10,12},{12... | collective-permute-start | bytes 196616 | tf_op jit(solution)/shard_map/ppermute | solution.py:24
  17.6 11.1 %collective-permute-start.10 = (bf16[32,1024]{1,0:T(8,128)(2,1)S(1)}, bf16[32,1024]{1,0:T(8,128)(2,1)S(1)}, u32[]{:S(2)}, u32[]{:S(2)}) collective-permute-start(bf16[32,1024]{1,0:T(8,128)(2,1)S(1)} %collective-permute-done.9.refs_0_), channel_id=1, source_target_pairs={{0,2},{2,0},{4,6},{6,4},{1,3},{3,1},{5,7},{7,5},{8,10},{10,8},{12,... | collective-permute-start | bytes 196616 | tf_op jit(solution)/shard_map/ppermute | solution.py:24
  18.5 12.3 %collective-permute-start.11 = (bf16[32,1024]{1,0:T(8,128)(2,1)S(1)}, bf16[32,1024]{1,0:T(8,128)(2,1)S(1)}, u32[]{:S(2)}, u32[]{:S(2)}) collective-permute-start(bf16[32,1024]{1,0:T(8,128)(2,1)S(1)} %collective-permute-done.9.refs_0_), channel_id=1, source_target_pairs={{0,4},{2,6},{4,0},{6,2},{1,5},{3,7},{5,1},{7,3},{8,12},{10,14},{12... | collective-permute-start | bytes 196616 | tf_op jit(solution)/shard_map/ppermute | solution.py:24
  22.0 8.8 %collective-permute-start.12 = (bf16[32,1024]{1,0:T(8,128)(2,1)S(1)}, bf16[32,1024]{1,0:T(8,128)(2,1)S(1)}, u32[]{:S(2)}, u32[]{:S(2)}) collective-permute-start(bf16[32,1024]{1,0:T(8,128)(2,1)S(1)} %collective-permute-done.9.refs_0_), channel_id=1, source_target_pairs={{0,6},{2,4},{4,2},{6,0},{1,7},{3,5},{5,3},{7,1},{8,14},{10,12},{12... | collective-permute-start | bytes 196616 | tf_op jit(solution)/shard_map/ppermute | solution.py:24
  26.3 14.9 %copy-start.1 = (bf16[128,1024]{1,0:T(8,128)(2,1)S(1)}, bf16[128,1024]{1,0:T(8,128)(2,1)}, u32[]{:S(2)}) copy-start(bf16[128,1024]{1,0:T(8,128)(2,1)} %query_ref.1) | copy-start | bytes 786436
  26.4 14.9 %copy-start.3 = (s32[512,1]{0,1:T(1,128)S(1)}, s32[512,1]{0,1:T(1,128)}, u32[]{:S(2)}) copy-start(s32[512,1]{0,1:T(1,128)} %param.12) | copy-start | bytes 6148
  26.4 7.6 %collective-permute-start.6 = (bf16[32,512]{1,0:T(8,128)(2,1)S(1)}, bf16[32,512]{1,0:T(8,128)(2,1)S(1)}, u32[]{:S(2)}, u32[]{:S(2)}) collective-permute-start(bf16[32,512]{1,0:T(8,128)(2,1)S(1)} %shard_map.74.refs_0_), channel_id=1, source_target_pairs={{0,2},{2,0},{4,6},{6,4},{1,3},{3,1},{5,7},{7,5},{8,10},{10,8},{12,... | collective-permute-start | bytes 98312 | tf_op jit(solution)/shard_map/ppermute | solution.py:24
  27.7 8.5 %collective-permute-start.7 = (bf16[32,512]{1,0:T(8,128)(2,1)S(1)}, bf16[32,512]{1,0:T(8,128)(2,1)S(1)}, u32[]{:S(2)}, u32[]{:S(2)}) collective-permute-start(bf16[32,512]{1,0:T(8,128)(2,1)S(1)} %shard_map.74.refs_0_), channel_id=1, source_target_pairs={{0,4},{2,6},{4,0},{6,2},{1,5},{3,7},{5,1},{7,3},{8,12},{10,14},{12... | collective-permute-start | bytes 98312 | tf_op jit(solution)/shard_map/ppermute | solution.py:24
  28.7 7.5 %collective-permute-start.8 = (bf16[32,512]{1,0:T(8,128)(2,1)S(1)}, bf16[32,512]{1,0:T(8,128)(2,1)S(1)}, u32[]{:S(2)}, u32[]{:S(2)}) collective-permute-start(bf16[32,512]{1,0:T(8,128)(2,1)S(1)} %shard_map.74.refs_0_), channel_id=1, source_target_pairs={{0,6},{2,4},{4,2},{6,0},{1,7},{3,5},{5,3},{7,1},{8,14},{10,12},{12... | collective-permute-start | bytes 98312 | tf_op jit(solution)/shard_map/ppermute | solution.py:24
  31.7 4.5 %collective-permute-start.13 = (bf16[32,512]{1,0:T(8,128)(2,1)S(1)}, bf16[32,512]{1,0:T(8,128)(2,1)S(1)}, u32[]{:S(2)}, u32[]{:S(2)}) collective-permute-start(bf16[32,512]{1,0:T(8,128)(2,1)S(1)} %shard_map.75.refs_4_), channel_id=1, source_target_pairs={{0,2},{2,0},{4,6},{6,4},{1,3},{3,1},{5,7},{7,5},{8,10},{10,8},{12,... | collective-permute-start | bytes 98312 | tf_op jit(solution)/shard_map/ppermute | solution.py:24
  32.1 4.8 %collective-permute-start.14 = (bf16[32,512]{1,0:T(8,128)(2,1)S(1)}, bf16[32,512]{1,0:T(8,128)(2,1)S(1)}, u32[]{:S(2)}, u32[]{:S(2)}) collective-permute-start(bf16[32,512]{1,0:T(8,128)(2,1)S(1)} %shard_map.75.refs_4_), channel_id=1, source_target_pairs={{0,4},{2,6},{4,0},{6,2},{1,5},{3,7},{5,1},{7,3},{8,12},{10,14},{12... | collective-permute-start | bytes 98312 | tf_op jit(solution)/shard_map/ppermute | solution.py:24
  34.0 5.7 %collective-permute-start.15 = (bf16[32,512]{1,0:T(8,128)(2,1)S(1)}, bf16[32,512]{1,0:T(8,128)(2,1)S(1)}, u32[]{:S(2)}, u32[]{:S(2)}) collective-permute-start(bf16[32,512]{1,0:T(8,128)(2,1)S(1)} %shard_map.75.refs_4_), channel_id=1, source_target_pairs={{0,6},{2,4},{4,2},{6,0},{1,7},{3,5},{5,3},{7,1},{8,14},{10,12},{12... | collective-permute-start | bytes 98312 | tf_op jit(solution)/shard_map/ppermute | solution.py:24
  39.7 1.5 %collective-permute-start.16 = (bf16[8,32,512]{2,1,0:T(8,128)(2,1)S(1)}, bf16[8,32,512]{2,1,0:T(8,128)(2,1)S(1)}, u32[]{:S(2)}, u32[]{:S(2)}) collective-permute-start(bf16[8,32,512]{2,1,0:T(8,128)(2,1)S(1)} %bitcast_dynamic-update-slice_fusion), channel_id=1, source_target_pairs={{0,1},{1,0},{2,3},{3,2},{4,5},{5,4},{6,7},{7,6},{8,9},{9,8},{10,11... | collective-permute-start | bytes 786440 | tf_op jit(solution)/shard_map/ppermute | solution.py:24

commit v8 on v7

--- a/solution.py
+++ b/solution.py
@@ -31,7 +31,7 @@
             [(0, 0, half), (3, 0, half), (1, 0, capacity)],
             [(0, half, half), (3, half, half), (2, 0, capacity)],
         ]
-        return runs, [[0, 1], [2]]
+        return runs, [[0, 1, 2]]
     each = clips // cores
     runs = [[(t * each + i, 0, capacity) for i in range(each)] for t in range(cores)]
     return runs, [list(range(each))]
@@ -73,33 +73,45 @@
     return (lax.broadcasted_iota(jnp.int32, (clips * capacity, rows), 0) == slot).astype(BF16)
 
 
-def ffn_kernel(capacity, cores, steps, dest_hbm, hidden_hbm, weight_hbm, residual_hbm,
+def ffn_kernel(capacity, cores, steps, ahead, dest_hbm, hidden_hbm, weight_hbm, residual_hbm,
                own_ref, send_ref, text_ref, dest_ref, hidden_ref, weight_ref, residual_ref,
-               packed_ref, total_ref, sems):
+               total_ref, sems):
     clip, core = lax.axis_index("clip"), lax.axis_index("tp")
     share = own_ref.shape[0]
     block = hidden_hbm.shape[1] // steps
-    get_dest = pltpu.make_async_copy(dest_hbm, dest_ref, sems.at[steps])
-    get_hidden = pltpu.make_async_copy(hidden_hbm, hidden_ref, sems.at[steps + 1])
-    get_residual = pltpu.make_async_copy(residual_hbm, residual_ref, sems.at[steps + 2])
-    get_weight = [
-        pltpu.make_async_copy(
-            weight_hbm.at[pl.ds(i * block, block), :],
-            weight_ref.at[pl.ds(i * block, block), :],
-            sems.at[i],
+    get_dest = pltpu.make_async_copy(dest_hbm, dest_ref, sems.at[2 * steps])
+    get_residual = pltpu.make_async_copy(residual_hbm, residual_ref, sems.at[2 * steps + 1])
+    get_hidden, get_weight = [], []
+    for i in range(steps):
+        part = pl.ds(i * block, block)
+        get_hidden.append(
+            pltpu.make_async_copy(hidden_hbm.at[:, part], hidden_ref.at[:, part], sems.at[i])
         )
-        for i in range(steps)
-    ]
-    for copy in [get_dest, get_hidden] + get_weight + [get_residual]:
-        copy.start()
+        get_weight.append(
+            pltpu.make_async_copy(
+                weight_hbm.at[part, :], weight_ref.at[part, :], sems.at[steps + i]
+            )
+        )
+
+    def start(i):
+        if i < steps:
+            get_hidden[i].start()
+            get_weight[i].start()
+        elif i == steps:
+            get_residual.start()
+
+    get_dest.start()
+    for i in range(ahead):
+        start(i)
     get_dest.wait()
     select = slot_select(dest_ref, clip, core, capacity, cores)
-    get_hidden.wait()
-    packed_ref[...] = jnp.dot(select, hidden_ref[...], preferred_element_type=F32).astype(BF16)
     for i in range(steps):
         part = pl.ds(i * block, block)
+        get_hidden[i].wait()
+        packed = jnp.dot(select, hidden_ref[:, part], preferred_element_type=F32).astype(BF16)
         get_weight[i].wait()
-        product = jnp.dot(packed_ref[:, part], weight_ref[part, :], preferred_element_type=F32)
+        start(i + ahead)
+        product = jnp.dot(packed, weight_ref[part, :], preferred_element_type=F32)
         if i == 0:
             total_ref[...] = product
         elif i < steps - 1:
@@ -118,9 +130,10 @@
     width = weight.shape[1]
     slots = dest.shape[0] * capacity
     share = slots // cores
-    steps = math.gcd(5, depth // 128)
+    steps = math.gcd(10, depth // 128)
+    ahead = min(3, steps)
     return pl.pallas_call(
-        functools.partial(ffn_kernel, capacity, cores, steps),
+        functools.partial(ffn_kernel, capacity, cores, steps, ahead),
         in_specs=[pl.BlockSpec(memory_space=pltpu.HBM)] * 4,
         out_specs=[whole()] * 3,
         out_shape=[
@@ -133,9 +146,8 @@
             pltpu.VMEM(hidden.shape, BF16),
             pltpu.VMEM(weight.shape, BF16),
             pltpu.VMEM(residual.shape, BF16),
-            pltpu.VMEM((slots, depth), BF16),
             pltpu.VMEM((slots, width), F32),
-            pltpu.SemaphoreType.DMA((steps + 3,)),
+            pltpu.SemaphoreType.DMA((2 * steps + 2,)),
         ],
         compiler_params=pltpu.CompilerParams(vmem_limit_bytes=VMEM_LIMIT),
         cost_estimate=pl.CostEstimate(

time: 42.8 us -> 42.4 us (level)
  starting transfers between devices: 26 us -> 13.7 us
  waiting for transfers between devices: 7.92 us -> 19.2 us
  Pallas kernels: 8.46 us -> 9.09 us
    ppermute x15 -> x9, starting transfers between devices: 21.8 us -> 9.55 us  [swap(): return lax.ppermute(value, axis, [(i, i ^ offset) for i in range(size)])]
    ppermute x15 -> x9, waiting for transfers between devices: 6.53 us -> 15.9 us  [swap(): return lax.ppermute(value, axis, [(i, i ^ offset) for i in range(size)])]
    ppermute x2, waiting for transfers between devices: 1.38 us -> 3.33 us  [route(): moved = lax.ppermute(value, ('clip', 'tp'), pairs)]
    pallas_call x1, Pallas kernels: 5.3 us -> 6.73 us  [ffn(): pl.pallas_call(functools.partial(ffn_kernel, capacity, cores, steps, ahea...]
    pallas_call x2 -> x1, Pallas kernels: 1.77 us -> 0.97 us  [keyval(): pl.pallas_call(functools.partial(keyval_kernel, parts, len(weights)), in_...]
  transfers between devices with their start and end apart: 17 -> 11, of which waited for: 5 -> 7; matrix products, arithmetic and copies ran while one was open for 0% -> 0% of each run, Pallas kernels for 17% -> 16%
where the time goes in v8:
time: 42.4 us; the launch traced here: 42.2 us
  waiting for transfers between devices  19.2 us (45%)
  starting transfers between devices  13.7 us (32%)
  Pallas kernels  9.09 us (21%)
    ppermute x9, waiting for transfers between devices, swap(): return lax.ppermute(value, axis, [(i, i ^ offset) for i in range(size)])  15.9 us
    ppermute x9, starting transfers between devices, swap(): return lax.ppermute(value, axis, [(i, i ^ offset) for i in range(size)])  9.55 us
    pallas_call x1, Pallas kernels, ffn(): pl.pallas_call(functools.partial(ffn_kernel, capacity, cores, steps, ahea...  6.73 us
    ppermute x2, starting transfers between devices, route(): moved = lax.ppermute(value, ('clip', 'tp'), pairs)  4.17 us
    ppermute x2, waiting for transfers between devices, route(): moved = lax.ppermute(value, ('clip', 'tp'), pairs)  3.33 us
    pallas_call x1, Pallas kernels, shards(): pl.pallas_call(functools.partial(attend_kernel, parts, cores, heads_here,...  1.39 us
    pallas_call x1, Pallas kernels, keyval(): pl.pallas_call(functools.partial(keyval_kernel, parts, len(weights)), in_...  0.97 us
  transfers between devices with their start and end apart: 11, of which 7 were waited for; matrix products, arithmetic and copies ran while one was open for 0% of the time, Pallas kernels for 16%

profile of v8, /device:TPU:0, one launch (start us, length us, event | category | flops | bytes accessed | tf_op | source)
XLA Modules:
  0.0 42.2 jit_solution(2519493133809312834)
XLA Ops:
  0.0 0.5 %collective-permute-start.6 = (bf16[4096,256]{1,0:T(8,128)(2,1)}, bf16[4096,256]{1,0:T(8,128)(2,1)S(1)}, u32[]{:S(2)}, u32[]{:S(2)}) collective-permute-start(bf16[4096,256]{1,0:T(8,128)(2,1)} %bitcast.7), channel_id=1, source_target_pairs={{0,1},{1,0},{2,3},{3,2},{4,5},{5,4},{6,7},{7,6},{8,9},{9,8},{10,11... | collective-permute-start | bytes 6291464 | tf_op jit(solution)/shard_map/ppermute | solution.py:24
  0.5 0.0 copy-start
  0.5 0.0 copy-start.2
  0.5 6.7 %shard_map.73 = (f32[64,1024]{1,0:T(8,128)S(1)}, f32[64,1024]{1,0:T(8,128)S(1)}, bf16[64,1024]{1,0:T(8,128)(2,1)S(1)}) custom-call(s32[4,128]{1,0:T(4,128)} %bitcast.14, bf16[128,5120]{1,0:T(8,128)(2,1)} %hidden_hbm.1, bf16[5120,1024]{1,0:T(8,128)(2,1)} %weight_hbm.1, bf16[128,1024]{1,0:T(8,128)(2,1)} %residual_hbm.1), custom_call_target="tpu_custom_call" | custom-call | flops 1509949440 | bytes 11796480 | tf_op jit(solution)/shard_map/pallas_call | solution.py:135
  7.2 0.1 collective-permute-start
  7.3 1.5 %collective-permute-done = f32[64,1024]{1,0:T(8,128)S(1)} collective-permute-done((f32[64,1024]{1,0:T(8,128)S(1)}, f32[64,1024]{1,0:T(8,128)S(1)}, u32[]{:S(2)}, u32[]{:S(2)}) %collective-permute-start) | collective-permute-done | bytes 262176 | tf_op jit(solution)/shard_map/ppermute | solution.py:24
  8.9 2.7 %collective-permute-start.2 = (bf16[32,1024]{1,0:T(8,128)(2,1)S(1)}, bf16[32,1024]{1,0:T(8,128)(2,1)S(1)}, u32[]{:S(2)}, u32[]{:S(2)}) collective-permute-start(bf16[32,1024]{1,0:T(8,128)(2,1)S(1)} %slice.14), channel_id=1, source_target_pairs={{0,8},{1,17},{8,0},{9,25},{16,24},{17,1},{24,16},{25,9},{2,10},{3,... | collective-permute-start | bytes 196616 | tf_op jit(solution)/shard_map/ppermute | solution.py:48
  11.5 1.5 %collective-permute-start.1 = (bf16[16,1024]{1,0:T(8,128)(2,1)S(1)}, bf16[16,1024]{1,0:T(8,128)(2,1)S(1)}, u32[]{:S(2)}, u32[]{:S(2)}) collective-permute-start(bf16[16,1024]{1,0:T(8,128)(2,1)S(1)} %get-tuple-element.12), channel_id=1, source_target_pairs={{0,24},{1,25},{8,16},{9,17},{16,8},{17,9},{24,0},{25,1},{2,26},{3,... | collective-permute-start | bytes 98312 | tf_op jit(solution)/shard_map/ppermute | solution.py:48
  13.0 3.3 %collective-permute-done.1 = bf16[16,1024]{1,0:T(8,128)(2,1)S(1)} collective-permute-done((bf16[16,1024]{1,0:T(8,128)(2,1)S(1)}, bf16[16,1024]{1,0:T(8,128)(2,1)S(1)}, u32[]{:S(2)}, u32[]{:S(2)}) %collective-permute-start.1) | collective-permute-done | bytes 32800 | tf_op jit(solution)/shard_map/ppermute | solution.py:48
  16.4 0.0 collective-permute-done.2
  16.4 3.7 %collective-permute-start.5 = (bf16[64,1024]{1,0:T(8,128)(2,1)S(1)}, bf16[64,1024]{1,0:T(8,128)(2,1)S(1)}, u32[]{:S(2)}, u32[]{:S(2)}) collective-permute-start(bf16[64,1024]{1,0:T(8,128)(2,1)S(1)} %pad_maximum_fusion.1.refs_0_), channel_id=1, source_target_pairs={{0,6},{2,4},{4,2},{6,0},{1,7},{3,5},{5,3},{7,1},{8,14},{10,12},{12... | collective-permute-start | bytes 393224 | tf_op jit(solution)/shard_map/ppermute | solution.py:24
  20.0 0.0 collective-permute-start.4
  20.0 0.8 %collective-permute-start.3 = (bf16[64,1024]{1,0:T(8,128)(2,1)S(1)}, bf16[64,1024]{1,0:T(8,128)(2,1)S(1)}, u32[]{:S(2)}, u32[]{:S(2)}) collective-permute-start(bf16[64,1024]{1,0:T(8,128)(2,1)S(1)} %pad_maximum_fusion.1.refs_0_), channel_id=1, source_target_pairs={{0,2},{2,0},{4,6},{6,4},{1,3},{3,1},{5,7},{7,5},{8,10},{10,8},{12,... | collective-permute-start | bytes 393224 | tf_op jit(solution)/shard_map/ppermute | solution.py:24
  20.8 3.8 %collective-permute-done.5.refs_3_ = bf16[64,1024]{1,0:T(8,128)(2,1)S(1)} collective-permute-done((bf16[64,1024]{1,0:T(8,128)(2,1)S(1)}, bf16[64,1024]{1,0:T(8,128)(2,1)S(1)}, u32[]{:S(2)}, u32[]{:S(2)}) %collective-permute-start.5) | collective-permute-done | bytes 131104 | tf_op jit(solution)/shard_map/ppermute | solution.py:24
  24.7 5.7 %collective-permute-done.4.refs_2_ = bf16[64,1024]{1,0:T(8,128)(2,1)S(1)} collective-permute-done((bf16[64,1024]{1,0:T(8,128)(2,1)S(1)}, bf16[64,1024]{1,0:T(8,128)(2,1)S(1)}, u32[]{:S(2)}, u32[]{:S(2)}) %collective-permute-start.4) | collective-permute-done | bytes 131104 | tf_op jit(solution)/shard_map/ppermute | solution.py:24
  30.4 0.0 collective-permute-done.3.refs_1_
  30.4 0.0 collective-permute-done.6.refs_6_
  30.4 0.0 copy-done
  30.4 0.0 copy-done.2
  30.4 0.0 copy-start.1
  30.4 0.0 copy-start.3
  30.4 1.0 %shard_map.74.refs_0_ = bf16[64,512]{1,0:T(8,128)(2,1)S(1)} custom-call(bf16[64,1024]{1,0:T(8,128)(2,1)S(1)} %pad_maximum_fusion.1.refs_0_, bf16[64,1024]{1,0:T(8,128)(2,1)S(1)} %collective-permute-done.3.refs_1_, bf16[64,1024]{1,0:T(8,128)(2,1)S(1)} %collective-permute-done.4.refs_2_, bf16[64,1024]{1,0:T(8,128)(2,1)S(1)} %collective-permute-done.5.refs_3_, ...), custom_call_target="tpu_custom_call" | custom-call | flops 268435456 | bytes 4718592 | tf_op jit(solution)/shard_map/pallas_call | solution.py:247
  31.4 2.5 %collective-permute-start.9 = (bf16[64,512]{1,0:T(8,128)(2,1)S(1)}, bf16[64,512]{1,0:T(8,128)(2,1)S(1)}, u32[]{:S(2)}, u32[]{:S(2)}) collective-permute-start(bf16[64,512]{1,0:T(8,128)(2,1)S(1)} %shard_map.74.refs_0_), channel_id=1, source_target_pairs={{0,6},{2,4},{4,2},{6,0},{1,7},{3,5},{5,3},{7,1},{8,14},{10,12},{12... | collective-permute-start | bytes 196616 | tf_op jit(solution)/shard_map/ppermute | solution.py:24
  33.9 0.0 collective-permute-start.8
  33.9 1.9 %collective-permute-start.7 = (bf16[64,512]{1,0:T(8,128)(2,1)S(1)}, bf16[64,512]{1,0:T(8,128)(2,1)S(1)}, u32[]{:S(2)}, u32[]{:S(2)}) collective-permute-start(bf16[64,512]{1,0:T(8,128)(2,1)S(1)} %shard_map.74.refs_0_), channel_id=1, source_target_pairs={{0,2},{2,0},{4,6},{6,4},{1,3},{3,1},{5,7},{7,5},{8,10},{10,8},{12,... | collective-permute-start | bytes 196616 | tf_op jit(solution)/shard_map/ppermute | solution.py:24
  35.8 2.0 %collective-permute-done.9.refs_3_ = bf16[64,512]{1,0:T(8,128)(2,1)S(1)} collective-permute-done((bf16[64,512]{1,0:T(8,128)(2,1)S(1)}, bf16[64,512]{1,0:T(8,128)(2,1)S(1)}, u32[]{:S(2)}, u32[]{:S(2)}) %collective-permute-start.9) | collective-permute-done | bytes 65568 | tf_op jit(solution)/shard_map/ppermute | solution.py:24
  37.8 1.4 %collective-permute-done.8.refs_2_ = bf16[64,512]{1,0:T(8,128)(2,1)S(1)} collective-permute-done((bf16[64,512]{1,0:T(8,128)(2,1)S(1)}, bf16[64,512]{1,0:T(8,128)(2,1)S(1)}, u32[]{:S(2)}, u32[]{:S(2)}) %collective-permute-start.8) | collective-permute-done | bytes 65568 | tf_op jit(solution)/shard_map/ppermute | solution.py:24
  39.2 0.0 collective-permute-done.7.refs_1_
  39.2 0.1 collective-permute-start.10
  39.3 1.5 %collective-permute-done.10.refs_4_ = bf16[4,64,512]{2,1,0:T(8,128)(2,1)S(1)} collective-permute-done((bf16[4,64,512]{2,1,0:T(8,128)(2,1)S(1)}, bf16[4,64,512]{2,1,0:T(8,128)(2,1)S(1)}, u32[]{:S(2)}, u32[]{:S(2)}) %collective-permute-start.10) | collective-permute-done | bytes 262176 | tf_op jit(solution)/shard_map/ppermute | solution.py:24
  40.8 0.0 copy-done.1
  40.8 0.0 copy-done.3
  40.8 1.4 %shard_map.75 = bf16[128,1024]{1,0:T(8,128)(2,1)} custom-call(s32[4,128]{1,0:T(4,128)S(1)} %bitcast.15, bf16[128,1024]{1,0:T(8,128)(2,1)S(1)} %copy-done.1, bf16[64,512]{1,0:T(8,128)(2,1)S(1)} %shard_map.74.refs_0_, bf16[64,512]{1,0:T(8,128)(2,1)S(1)} %collective-permute-done.7.refs_1_, bf16[64,512]{1,0:T(8,128)(2,1)S(1)} %collective-permute-done.8.refs_2_, ...), custom_call_target="tpu_custom_call" | custom-call | tf_op jit(solution)/shard_map/pallas_call | solution.py:289
  (5 shorter events, 0.1 us)
Async XLA Ops:
  0.0 30.4 %collective-permute-start.6 = (bf16[4096,256]{1,0:T(8,128)(2,1)}, bf16[4096,256]{1,0:T(8,128)(2,1)S(1)}, u32[]{:S(2)}, u32[]{:S(2)}) collective-permute-start(bf16[4096,256]{1,0:T(8,128)(2,1)} %bitcast.7), channel_id=1, source_target_pairs={{0,1},{1,0},{2,3},{3,2},{4,5},{5,4},{6,7},{7,6},{8,9},{9,8},{10,11... | collective-permute-start | bytes 6291464 | tf_op jit(solution)/shard_map/ppermute | solution.py:24
  0.5 29.9 %copy-start = (bf16[4096,1,256]{2,0,1:T(8,128)(2,1)S(1)}, bf16[4096,1,256]{2,0,1:T(8,128)(2,1)}, u32[]{:S(2)}) copy-start(bf16[4096,1,256]{2,0,1:T(8,128)(2,1)} %param.11) | copy-start | bytes 6291460
  0.5 29.9 %copy-start.2 = (f32[4096]{0:T(1024)S(1)}, f32[4096]{0:T(1024)}, u32[]{:S(2)}) copy-start(f32[4096]{0:T(1024)} %param.10) | copy-start | bytes 49156
  7.2 1.6 %collective-permute-start = (f32[64,1024]{1,0:T(8,128)S(1)}, f32[64,1024]{1,0:T(8,128)S(1)}, u32[]{:S(2)}, u32[]{:S(2)}) collective-permute-start(f32[64,1024]{1,0:T(8,128)S(1)} %get-tuple-element.10), channel_id=1, source_target_pairs={{0,1},{1,0},{2,3},{3,2},{4,5},{5,4},{6,7},{7,6},{8,9},{9,8},{10,11... | collective-permute-start | bytes 786440 | tf_op jit(solution)/shard_map/ppermute | solution.py:24
  8.9 7.5 %collective-permute-start.2 = (bf16[32,1024]{1,0:T(8,128)(2,1)S(1)}, bf16[32,1024]{1,0:T(8,128)(2,1)S(1)}, u32[]{:S(2)}, u32[]{:S(2)}) collective-permute-start(bf16[32,1024]{1,0:T(8,128)(2,1)S(1)} %slice.14), channel_id=1, source_target_pairs={{0,8},{1,17},{8,0},{9,25},{16,24},{17,1},{24,16},{25,9},{2,10},{3,... | collective-permute-start | bytes 196616 | tf_op jit(solution)/shard_map/ppermute | solution.py:48
  11.5 4.8 %collective-permute-start.1 = (bf16[16,1024]{1,0:T(8,128)(2,1)S(1)}, bf16[16,1024]{1,0:T(8,128)(2,1)S(1)}, u32[]{:S(2)}, u32[]{:S(2)}) collective-permute-start(bf16[16,1024]{1,0:T(8,128)(2,1)S(1)} %get-tuple-element.12), channel_id=1, source_target_pairs={{0,24},{1,25},{8,16},{9,17},{16,8},{17,9},{24,0},{25,1},{2,26},{3,... | collective-permute-start | bytes 98312 | tf_op jit(solution)/shard_map/ppermute | solution.py:48
  16.4 8.3 %collective-permute-start.5 = (bf16[64,1024]{1,0:T(8,128)(2,1)S(1)}, bf16[64,1024]{1,0:T(8,128)(2,1)S(1)}, u32[]{:S(2)}, u32[]{:S(2)}) collective-permute-start(bf16[64,1024]{1,0:T(8,128)(2,1)S(1)} %pad_maximum_fusion.1.refs_0_), channel_id=1, source_target_pairs={{0,6},{2,4},{4,2},{6,0},{1,7},{3,5},{5,3},{7,1},{8,14},{10,12},{12... | collective-permute-start | bytes 393224 | tf_op jit(solution)/shard_map/ppermute | solution.py:24
  20.0 10.3 %collective-permute-start.4 = (bf16[64,1024]{1,0:T(8,128)(2,1)S(1)}, bf16[64,1024]{1,0:T(8,128)(2,1)S(1)}, u32[]{:S(2)}, u32[]{:S(2)}) collective-permute-start(bf16[64,1024]{1,0:T(8,128)(2,1)S(1)} %pad_maximum_fusion.1.refs_0_), channel_id=1, source_target_pairs={{0,4},{2,6},{4,0},{6,2},{1,5},{3,7},{5,1},{7,3},{8,12},{10,14},{12... | collective-permute-start | bytes 393224 | tf_op jit(solution)/shard_map/ppermute | solution.py:24
  20.0 10.3 %collective-permute-start.3 = (bf16[64,1024]{1,0:T(8,128)(2,1)S(1)}, bf16[64,1024]{1,0:T(8,128)(2,1)S(1)}, u32[]{:S(2)}, u32[]{:S(2)}) collective-permute-start(bf16[64,1024]{1,0:T(8,128)(2,1)S(1)} %pad_maximum_fusion.1.refs_0_), channel_id=1, source_target_pairs={{0,2},{2,0},{4,6},{6,4},{1,3},{3,1},{5,7},{7,5},{8,10},{10,8},{12,... | collective-permute-start | bytes 393224 | tf_op jit(solution)/shard_map/ppermute | solution.py:24
  30.4 10.4 %copy-start.1 = (bf16[128,1024]{1,0:T(8,128)(2,1)S(1)}, bf16[128,1024]{1,0:T(8,128)(2,1)}, u32[]{:S(2)}) copy-start(bf16[128,1024]{1,0:T(8,128)(2,1)} %query_ref.1) | copy-start | bytes 786436
  30.4 10.4 %copy-start.3 = (s32[512,1]{0,1:T(1,128)S(1)}, s32[512,1]{0,1:T(1,128)}, u32[]{:S(2)}) copy-start(s32[512,1]{0,1:T(1,128)} %param.12) | copy-start | bytes 6148
  31.4 6.4 %collective-permute-start.9 = (bf16[64,512]{1,0:T(8,128)(2,1)S(1)}, bf16[64,512]{1,0:T(8,128)(2,1)S(1)}, u32[]{:S(2)}, u32[]{:S(2)}) collective-permute-start(bf16[64,512]{1,0:T(8,128)(2,1)S(1)} %shard_map.74.refs_0_), channel_id=1, source_target_pairs={{0,6},{2,4},{4,2},{6,0},{1,7},{3,5},{5,3},{7,1},{8,14},{10,12},{12... | collective-permute-start | bytes 196616 | tf_op jit(solution)/shard_map/ppermute | solution.py:24
  33.9 5.3 %collective-permute-start.8 = (bf16[64,512]{1,0:T(8,128)(2,1)S(1)}, bf16[64,512]{1,0:T(8,128)(2,1)S(1)}, u32[]{:S(2)}, u32[]{:S(2)}) collective-permute-start(bf16[64,512]{1,0:T(8,128)(2,1)S(1)} %shard_map.74.refs_0_), channel_id=1, source_target_pairs={{0,4},{2,6},{4,0},{6,2},{1,5},{3,7},{5,1},{7,3},{8,12},{10,14},{12... | collective-permute-start | bytes 196616 | tf_op jit(solution)/shard_map/ppermute | solution.py:24
  33.9 5.3 %collective-permute-start.7 = (bf16[64,512]{1,0:T(8,128)(2,1)S(1)}, bf16[64,512]{1,0:T(8,128)(2,1)S(1)}, u32[]{:S(2)}, u32[]{:S(2)}) collective-permute-start(bf16[64,512]{1,0:T(8,128)(2,1)S(1)} %shard_map.74.refs_0_), channel_id=1, source_target_pairs={{0,2},{2,0},{4,6},{6,4},{1,3},{3,1},{5,7},{7,5},{8,10},{10,8},{12,... | collective-permute-start | bytes 196616 | tf_op jit(solution)/shard_map/ppermute | solution.py:24
  39.2 1.6 %collective-permute-start.10 = (bf16[4,64,512]{2,1,0:T(8,128)(2,1)S(1)}, bf16[4,64,512]{2,1,0:T(8,128)(2,1)S(1)}, u32[]{:S(2)}, u32[]{:S(2)}) collective-permute-start(bf16[4,64,512]{2,1,0:T(8,128)(2,1)S(1)} %pad_maximum_fusion), channel_id=1, source_target_pairs={{0,1},{1,0},{2,3},{3,2},{4,5},{5,4},{6,7},{7,6},{8,9},{9,8},{10,11... | collective-permute-start | bytes 786440 | tf_op jit(solution)/shard_map/ppermute | solution.py:24

commit v9 on v7

--- a/solution.py
+++ b/solution.py
@@ -31,7 +31,7 @@
             [(0, 0, half), (3, 0, half), (1, 0, capacity)],
             [(0, half, half), (3, half, half), (2, 0, capacity)],
         ]
-        return runs, [[0, 1], [2]]
+        return runs, [[0], [1, 2]]
     each = clips // cores
     runs = [[(t * each + i, 0, capacity) for i in range(each)] for t in range(cores)]
     return runs, [list(range(each))]
@@ -73,44 +73,41 @@
     return (lax.broadcasted_iota(jnp.int32, (clips * capacity, rows), 0) == slot).astype(BF16)
 
 
-def ffn_kernel(capacity, cores, steps, dest_hbm, hidden_hbm, weight_hbm, residual_hbm,
+def ffn_kernel(capacity, cores, edges, dest_hbm, hidden_hbm, weight_hbm, residual_hbm,
                own_ref, send_ref, text_ref, dest_ref, hidden_ref, weight_ref, residual_ref,
                packed_ref, total_ref, sems):
     clip, core = lax.axis_index("clip"), lax.axis_index("tp")
     share = own_ref.shape[0]
-    block = hidden_hbm.shape[1] // steps
+    steps = len(edges) - 1
+    parts = [pl.ds(edges[i], edges[i + 1] - edges[i]) for i in range(steps)]
     get_dest = pltpu.make_async_copy(dest_hbm, dest_ref, sems.at[steps])
     get_hidden = pltpu.make_async_copy(hidden_hbm, hidden_ref, sems.at[steps + 1])
     get_residual = pltpu.make_async_copy(residual_hbm, residual_ref, sems.at[steps + 2])
     get_weight = [
-        pltpu.make_async_copy(
-            weight_hbm.at[pl.ds(i * block, block), :],
-            weight_ref.at[pl.ds(i * block, block), :],
-            sems.at[i],
-        )
-        for i in range(steps)
+        pltpu.make_async_copy(weight_hbm.at[part, :], weight_ref.at[part, :], sems.at[i])
+        for i, part in enumerate(parts)
     ]
-    for copy in [get_dest, get_hidden] + get_weight + [get_residual]:
+    for copy in [get_dest, get_hidden] + get_weight[:-1] + [get_residual, get_weight[-1]]:
         copy.start()
     get_dest.wait()
     select = slot_select(dest_ref, clip, core, capacity, cores)
     get_hidden.wait()
     packed_ref[...] = jnp.dot(select, hidden_ref[...], preferred_element_type=F32).astype(BF16)
-    for i in range(steps):
-        part = pl.ds(i * block, block)
+    for i, part in enumerate(parts):
+        if i == steps - 1:
+            get_residual.wait()
+            text_ref[...] = jnp.dot(
+                select[:share], residual_ref[...], preferred_element_type=F32
+            ).astype(BF16)
         get_weight[i].wait()
         product = jnp.dot(packed_ref[:, part], weight_ref[part, :], preferred_element_type=F32)
-        if i == 0:
-            total_ref[...] = product
-        elif i < steps - 1:
-            total_ref[...] += product
+        if i < steps - 1:
+            total_ref[...] = product if i == 0 else total_ref[...] + product
+        elif i == 0:
+            own_ref[...], send_ref[...] = product[:share], product[share:]
         else:
             own_ref[...] = total_ref[:share, :] + product[:share]
             send_ref[...] = total_ref[share:, :] + product[share:]
-    get_residual.wait()
-    text_ref[...] = jnp.dot(
-        select[:share], residual_ref[...], preferred_element_type=F32
-    ).astype(BF16)
 
 
 def ffn(dest, hidden, weight, residual, capacity, cores):
@@ -118,9 +115,10 @@
     width = weight.shape[1]
     slots = dest.shape[0] * capacity
     share = slots // cores
-    steps = math.gcd(5, depth // 128)
+    unit = depth // 20
+    edges = [0, 5 * unit, 10 * unit, 15 * unit, 19 * unit, depth] if unit % 128 == 0 else [0, depth]
     return pl.pallas_call(
-        functools.partial(ffn_kernel, capacity, cores, steps),
+        functools.partial(ffn_kernel, capacity, cores, edges),
         in_specs=[pl.BlockSpec(memory_space=pltpu.HBM)] * 4,
         out_specs=[whole()] * 3,
         out_shape=[
@@ -135,7 +133,7 @@
             pltpu.VMEM(residual.shape, BF16),
             pltpu.VMEM((slots, depth), BF16),
             pltpu.VMEM((slots, width), F32),
-            pltpu.SemaphoreType.DMA((steps + 3,)),
+            pltpu.SemaphoreType.DMA((len(edges) + 2,)),
         ],
         compiler_params=pltpu.CompilerParams(vmem_limit_bytes=VMEM_LIMIT),
         cost_estimate=pl.CostEstimate(
@@ -146,28 +144,32 @@
     )(*[pltpu.with_memory_space_constraint(x, pltpu.HBM) for x in (dest, hidden, weight, residual)])
 
 
-def keyval_kernel(parts, cores, *refs):
-    texts, (gain_ref, *weights), out_ref = refs[:parts], refs[parts:-1], refs[-1]
+def keyval_kernel(parts, groups, *refs):
+    found, (gain_ref, *weights), out_ref = refs[:groups * parts], refs[groups * parts:-1], refs[-1]
     seq = lax.axis_index("seq")
+    texts = [
+        jnp.concatenate([found[g * parts + k][...] for g in range(groups)], axis=0)
+        for k in range(parts)
+    ]
     width = texts[0].shape[1]
     squares = 0.0
     for text in texts:
-        wide = text[...].astype(F32)
+        wide = text.astype(F32)
         squares += jnp.sum(wide * wide, axis=1, keepdims=True)
     scale = lax.rsqrt(squares / (parts * width) + EPSILON)
-    totals = [0.0] * cores
+    totals = [0.0] * len(weights)
     for k, text in enumerate(texts):
         place = pl.ds(pl.multiple_of((seq ^ k) * width, width), width)
-        normed = (text[...].astype(F32) * scale * gain_ref[:, place]).astype(BF16)
+        normed = (text.astype(F32) * scale * gain_ref[:, place]).astype(BF16)
         for c, weight in enumerate(weights):
             totals[c] += jnp.dot(normed, weight[place, :], preferred_element_type=F32)
     each = weights[0].shape[1]
-    for c in range(cores):
+    for c in range(len(weights)):
         out_ref[:, c * each:(c + 1) * each] = totals[c].astype(BF16)
 
 
-def attend_kernel(parts, cores, heads_here, capacity, groups, dest_ref, query_ref, *refs):
-    own, others, out_ref = refs[:parts * groups], refs[parts * groups:-1], refs[-1]
+def attend_kernel(parts, cores, heads_here, capacity, dest_ref, query_ref, *refs):
+    own, others, out_ref = refs[:parts], refs[parts:-1], refs[-1]
     clip, seq, core = lax.axis_index("clip"), lax.axis_index("seq"), lax.axis_index("tp")
     clips = dest_ref.shape[0]
     slots = clips * capacity
@@ -199,9 +201,9 @@
         for g in range(cores):
             at = ((c ^ g) * heads_here + i) * 2 * dim + offset
             if g == 0:
-                found += [own[n * parts + k][:, at:at + dim] for n in range(groups)]
+                found.append(own[k][:, at:at + dim])
             else:
-                found += [others[g - 1][n * parts + k, :, at:at + dim] for n in range(groups)]
+                found.append(others[g - 1][k, :, at:at + dim])
         return jnp.concatenate(found, axis=0)
 
     group = 8
@@ -230,11 +232,12 @@
 
 
 def keyval(texts, gain, weights):
-    parts, (rows, width) = len(texts), texts[0].shape
+    groups, parts = len(texts), len(texts[0])
+    rows, width = sum(some[0].shape[0] for some in texts), texts[0][0].shape[1]
     wide = sum(weight.shape[1] for weight in weights)
     return pl.pallas_call(
-        functools.partial(keyval_kernel, parts, len(weights)),
-        in_specs=[whole()] * (parts + 1 + len(weights)),
+        functools.partial(keyval_kernel, parts, groups),
+        in_specs=[whole()] * (groups * parts + 1 + len(weights)),
         out_specs=whole(),
         out_shape=pltpu.VMEM((rows, wide), BF16),
         compiler_params=pltpu.CompilerParams(vmem_limit_bytes=VMEM_LIMIT),
@@ -243,7 +246,11 @@
             bytes_accessed=2 * parts * width * (rows + wide),
             transcendentals=0,
         ),
-    )(*texts, gain, *[pltpu.with_memory_space_constraint(x, pltpu.VMEM) for x in weights])
+    )(
+        *[text for some in texts for text in some],
+        gain,
+        *[pltpu.with_memory_space_constraint(x, pltpu.VMEM) for x in weights],
+    )
 
 
 def shards(ffn_hidden, ffn_weight, residual, norm_gain, kv_weight, destination, queries):
@@ -255,8 +262,9 @@
     dest = destination.reshape(clips, rows)
     gain = norm_gain.reshape(1, -1)
     weight = kv_weight.reshape(kv_weight.shape[0], heads_here * kv_weight.shape[2])
-    weights = [weight] + [swap(weight, "tp", g) for g in range(1, cores)]
+    weights = [swap(weight, "tp", g) for g in range(1, cores)]
     own, send, text = ffn(dest, ffn_hidden, ffn_weight, residual, capacity, cores)
+    weights, own = lax.optimization_barrier(([weight] + weights, own))
     for g in range(1, cores):
         own = own + swap(send[(g - 1) * share:g * share], "tp", g)
     text = (text.astype(F32) + own).astype(BF16)
@@ -266,16 +274,17 @@
         route(text[edges[n]:edges[n + 1]], [some[n][0] for some in runs])
         for n in range(len(runs[0]))
     ]
-    own = []
+    texts = []
     for group in groups:
         mine = jnp.concatenate([arrived[n] for n in group], axis=0)
-        texts = [mine] + [swap(mine, "seq", k) for k in range(1, parts)]
-        block = keyval(texts, gain, weights)
-        own += [block] + [swap(block, "seq", k) for k in range(1, parts)]
+        mine, texts = lax.optimization_barrier((mine, texts))
+        texts.append([mine] + [swap(mine, "seq", k) for k in range(1, parts)])
+    block = keyval(texts, gain, weights)
+    own = [block] + [swap(block, "seq", k) for k in range(1, parts)]
     packed = jnp.stack(own)
     others = [swap(packed, "tp", g) for g in range(1, cores)]
     return pl.pallas_call(
-        functools.partial(attend_kernel, parts, cores, heads_here, capacity, len(groups)),
+        functools.partial(attend_kernel, parts, cores, heads_here, capacity),
         in_specs=[whole()] * (2 + len(own) + len(others)),
         out_specs=whole(),
         out_shape=jax.ShapeDtypeStruct(queries.shape, BF16),

time: 42.8 us -> 42.3 us (0.988)
  waiting for transfers between devices: 7.92 us -> 16.3 us
  starting transfers between devices: 26 us -> 18.1 us
  Pallas kernels: 8.46 us -> 7.69 us
    ppermute x15 -> x12, waiting for transfers between devices: 6.53 us -> 16.3 us  [swap(): return lax.ppermute(value, axis, [(i, i ^ offset) for i in range(size)])]
    ppermute x15 -> x12, starting transfers between devices: 21.8 us -> 13.9 us  [swap(): return lax.ppermute(value, axis, [(i, i ^ offset) for i in range(size)])]
    ppermute x2, waiting for transfers between devices: 1.38 us -> 0.01 us  [route(): moved = lax.ppermute(value, ('clip', 'tp'), pairs)]
    pallas_call x3 -> x2, Pallas kernels: 7.08 us -> 6.3 us  [the longest x1 5.36 us: ffn(): pl.pallas_call(functools.partial(ffn_kernel, capacity, cores, edges), in_...]
  transfers between devices with their start and end apart: 17 -> 14, of which waited for: 5 -> 8; matrix products, arithmetic and copies ran while one was open for 0% -> 0% of each run, Pallas kernels for 17% -> 13%
where the time goes in v9:
time: 42.3 us; the launch traced here: 42.2 us
  starting transfers between devices  18.1 us (43%)
  waiting for transfers between devices  16.3 us (39%)
  Pallas kernels  7.69 us (18%)
    ppermute x12, waiting for transfers between devices, swap(): return lax.ppermute(value, axis, [(i, i ^ offset) for i in range(size)])  16.3 us
    ppermute x12, starting transfers between devices, swap(): return lax.ppermute(value, axis, [(i, i ^ offset) for i in range(size)])  13.9 us
    pallas_call x1, Pallas kernels, ffn(): pl.pallas_call(functools.partial(ffn_kernel, capacity, cores, edges), in_...  5.36 us
    ppermute x2, starting transfers between devices, route(): moved = lax.ppermute(value, ('clip', 'tp'), pairs)  4.18 us
    pallas_call x1, Pallas kernels, shards(): pl.pallas_call(functools.partial(attend_kernel, parts, cores, heads_here,...  1.39 us
    pallas_call x1, Pallas kernels, keyval(): pl.pallas_call(functools.partial(keyval_kernel, parts, groups), in_specs=...  0.94 us
  transfers between devices with their start and end apart: 14, of which 8 were waited for; matrix products, arithmetic and copies ran while one was open for 0% of the time, Pallas kernels for 13%

profile of v9, /device:TPU:0, one launch (start us, length us, event | category | flops | bytes accessed | tf_op | source)
XLA Modules:
  0.0 42.2 jit_solution(6367229536141602706)
XLA Ops:
  0.0 0.5 %collective-permute-start = (bf16[4096,256]{1,0:T(8,128)(2,1)}, bf16[4096,256]{1,0:T(8,128)(2,1)S(1)}, u32[]{:S(2)}, u32[]{:S(2)}) collective-permute-start(bf16[4096,256]{1,0:T(8,128)(2,1)} %bitcast.7), channel_id=1, source_target_pairs={{0,1},{1,0},{2,3},{3,2},{4,5},{5,4},{6,7},{7,6},{8,9},{9,8},{10,11... | collective-permute-start | bytes 6291464 | tf_op jit(solution)/shard_map/ppermute | solution.py:24
  0.5 0.0 copy-start
  0.5 0.0 copy-start.2
  0.5 5.4 %shard_map.73 = (f32[64,1024]{1,0:T(8,128)S(1)}, f32[64,1024]{1,0:T(8,128)S(1)}, bf16[64,1024]{1,0:T(8,128)(2,1)S(1)}) custom-call(s32[4,128]{1,0:T(4,128)} %bitcast.14, bf16[128,5120]{1,0:T(8,128)(2,1)} %hidden_hbm.1, bf16[5120,1024]{1,0:T(8,128)(2,1)} %weight_hbm.1, bf16[128,1024]{1,0:T(8,128)(2,1)} %residual_hbm.1), custom_call_target="tpu_custom_call" | custom-call | flops 1509949440 | bytes 11796480 | tf_op jit(solution)/shard_map/pallas_call | solution.py:120
  5.8 0.1 collective-permute-start.1
  5.9 0.0 collective-permute-done.refs_10_
  6.0 1.5 %collective-permute-done.1 = f32[64,1024]{1,0:T(8,128)S(1)} collective-permute-done((f32[64,1024]{1,0:T(8,128)S(1)}, f32[64,1024]{1,0:T(8,128)S(1)}, u32[]{:S(2)}, u32[]{:S(2)}) %collective-permute-start.1) | collective-permute-done | bytes 262176 | tf_op jit(solution)/shard_map/ppermute | solution.py:24
  7.5 2.7 %collective-permute-start.3 = (bf16[32,1024]{1,0:T(8,128)(2,1)S(1)}, bf16[32,1024]{1,0:T(8,128)(2,1)S(1)}, u32[]{:S(2)}, u32[]{:S(2)}) collective-permute-start(bf16[32,1024]{1,0:T(8,128)(2,1)S(1)} %slice.13), channel_id=1, source_target_pairs={{0,8},{1,17},{8,0},{9,25},{16,24},{17,1},{24,16},{25,9},{2,10},{3,... | collective-permute-start | bytes 196616 | tf_op jit(solution)/shard_map/ppermute | solution.py:48
  10.2 1.5 %collective-permute-start.2 = (bf16[16,1024]{1,0:T(8,128)(2,1)S(1)}, bf16[16,1024]{1,0:T(8,128)(2,1)S(1)}, u32[]{:S(2)}, u32[]{:S(2)}) collective-permute-start(bf16[16,1024]{1,0:T(8,128)(2,1)S(1)} %get-tuple-element.28), channel_id=1, source_target_pairs={{0,24},{1,25},{8,16},{9,17},{16,8},{17,9},{24,0},{25,1},{2,26},{3,... | collective-permute-start | bytes 98312 | tf_op jit(solution)/shard_map/ppermute | solution.py:48
  11.7 3.6 %collective-permute-start.6 = (bf16[16,1024]{1,0:T(8,128)(2,1)S(1)}, bf16[16,1024]{1,0:T(8,128)(2,1)S(1)}, u32[]{:S(2)}, u32[]{:S(2)}) collective-permute-start(bf16[16,1024]{1,0:T(8,128)(2,1)S(1)} %get-tuple-element.20.refs_0_), channel_id=1, source_target_pairs={{0,6},{2,4},{4,2},{6,0},{1,7},{3,5},{5,3},{7,1},{8,14},{10,12},{12... | collective-permute-start | bytes 98312 | tf_op jit(solution)/shard_map/ppermute | solution.py:24
  15.3 0.0 collective-permute-start.5
  15.3 0.8 %collective-permute-start.4 = (bf16[16,1024]{1,0:T(8,128)(2,1)S(1)}, bf16[16,1024]{1,0:T(8,128)(2,1)S(1)}, u32[]{:S(2)}, u32[]{:S(2)}) collective-permute-start(bf16[16,1024]{1,0:T(8,128)(2,1)S(1)} %get-tuple-element.20.refs_0_), channel_id=1, source_target_pairs={{0,2},{2,0},{4,6},{6,4},{1,3},{3,1},{5,7},{7,5},{8,10},{10,8},{12,... | collective-permute-start | bytes 98312 | tf_op jit(solution)/shard_map/ppermute | solution.py:24
  16.1 0.0 collective-permute-done.2
  16.1 0.0 collective-permute-done.3
  16.1 1.4 %collective-permute-done.6.refs_3_ = bf16[16,1024]{1,0:T(8,128)(2,1)S(1)} collective-permute-done((bf16[16,1024]{1,0:T(8,128)(2,1)S(1)}, bf16[16,1024]{1,0:T(8,128)(2,1)S(1)}, u32[]{:S(2)}, u32[]{:S(2)}) %collective-permute-start.6) | collective-permute-done | bytes 32800 | tf_op jit(solution)/shard_map/ppermute | solution.py:24
  17.5 2.6 %collective-permute-done.5.refs_2_ = bf16[16,1024]{1,0:T(8,128)(2,1)S(1)} collective-permute-done((bf16[16,1024]{1,0:T(8,128)(2,1)S(1)}, bf16[16,1024]{1,0:T(8,128)(2,1)S(1)}, u32[]{:S(2)}, u32[]{:S(2)}) %collective-permute-start.5) | collective-permute-done | bytes 32800 | tf_op jit(solution)/shard_map/ppermute | solution.py:24
  20.1 0.0 collective-permute-done.4.refs_1_
  20.1 1.5 %collective-permute-start.9 = (bf16[48,1024]{1,0:T(8,128)(2,1)S(1)}, bf16[48,1024]{1,0:T(8,128)(2,1)S(1)}, u32[]{:S(2)}, u32[]{:S(2)}) collective-permute-start(bf16[48,1024]{1,0:T(8,128)(2,1)S(1)} %pad_maximum_fusion.1.refs_4_), channel_id=1, source_target_pairs={{0,6},{2,4},{4,2},{6,0},{1,7},{3,5},{5,3},{7,1},{8,14},{10,12},{12... | collective-permute-start | bytes 294920 | tf_op jit(solution)/shard_map/ppermute | solution.py:24
  21.5 0.6 %collective-permute-start.8 = (bf16[48,1024]{1,0:T(8,128)(2,1)S(1)}, bf16[48,1024]{1,0:T(8,128)(2,1)S(1)}, u32[]{:S(2)}, u32[]{:S(2)}) collective-permute-start(bf16[48,1024]{1,0:T(8,128)(2,1)S(1)} %pad_maximum_fusion.1.refs_4_), channel_id=1, source_target_pairs={{0,4},{2,6},{4,0},{6,2},{1,5},{3,7},{5,1},{7,3},{8,12},{10,14},{12... | collective-permute-start | bytes 294920 | tf_op jit(solution)/shard_map/ppermute | solution.py:24
  22.1 2.4 %collective-permute-start.7 = (bf16[48,1024]{1,0:T(8,128)(2,1)S(1)}, bf16[48,1024]{1,0:T(8,128)(2,1)S(1)}, u32[]{:S(2)}, u32[]{:S(2)}) collective-permute-start(bf16[48,1024]{1,0:T(8,128)(2,1)S(1)} %pad_maximum_fusion.1.refs_4_), channel_id=1, source_target_pairs={{0,2},{2,0},{4,6},{6,4},{1,3},{3,1},{5,7},{7,5},{8,10},{10,8},{12,... | collective-permute-start | bytes 294920 | tf_op jit(solution)/shard_map/ppermute | solution.py:24
  24.5 2.7 %collective-permute-done.9.refs_7_ = bf16[48,1024]{1,0:T(8,128)(2,1)S(1)} collective-permute-done((bf16[48,1024]{1,0:T(8,128)(2,1)S(1)}, bf16[48,1024]{1,0:T(8,128)(2,1)S(1)}, u32[]{:S(2)}, u32[]{:S(2)}) %collective-permute-start.9) | collective-permute-done | bytes 98336 | tf_op jit(solution)/shard_map/ppermute | solution.py:24
  27.2 3.0 %collective-permute-done.8.refs_6_ = bf16[48,1024]{1,0:T(8,128)(2,1)S(1)} collective-permute-done((bf16[48,1024]{1,0:T(8,128)(2,1)S(1)}, bf16[48,1024]{1,0:T(8,128)(2,1)S(1)}, u32[]{:S(2)}, u32[]{:S(2)}) %collective-permute-start.8) | collective-permute-done | bytes 98336 | tf_op jit(solution)/shard_map/ppermute | solution.py:24
  30.2 0.0 collective-permute-done.7.refs_5_
  30.2 0.0 copy-done
  30.2 0.0 copy-done.2
  30.2 0.0 copy-start.1
  30.2 0.0 copy-start.3
  30.2 0.9 %shard_map.74.refs_0_ = bf16[64,512]{1,0:T(8,128)(2,1)S(1)} custom-call(bf16[16,1024]{1,0:T(8,128)(2,1)S(1)} %get-tuple-element.20.refs_0_, bf16[16,1024]{1,0:T(8,128)(2,1)S(1)} %collective-permute-done.4.refs_1_, bf16[16,1024]{1,0:T(8,128)(2,1)S(1)} %collective-permute-done.5.refs_2_, bf16[16,1024]{1,0:T(8,128)(2,1)S(1)} %collective-permute-done.6.refs_3_, ...), custom_call_target="tpu_custom_call" | custom-call | flops 268435456 | bytes 4718592 | tf_op jit(solution)/shard_map/pallas_call | solution.py:238
  31.2 2.3 %collective-permute-start.12 = (bf16[64,512]{1,0:T(8,128)(2,1)S(1)}, bf16[64,512]{1,0:T(8,128)(2,1)S(1)}, u32[]{:S(2)}, u32[]{:S(2)}) collective-permute-start(bf16[64,512]{1,0:T(8,128)(2,1)S(1)} %shard_map.74.refs_0_), channel_id=1, source_target_pairs={{0,6},{2,4},{4,2},{6,0},{1,7},{3,5},{5,3},{7,1},{8,14},{10,12},{12... | collective-permute-start | bytes 196616 | tf_op jit(solution)/shard_map/ppermute | solution.py:24
  33.4 0.0 collective-permute-start.11
  33.4 2.2 %collective-permute-start.10 = (bf16[64,512]{1,0:T(8,128)(2,1)S(1)}, bf16[64,512]{1,0:T(8,128)(2,1)S(1)}, u32[]{:S(2)}, u32[]{:S(2)}) collective-permute-start(bf16[64,512]{1,0:T(8,128)(2,1)S(1)} %shard_map.74.refs_0_), channel_id=1, source_target_pairs={{0,2},{2,0},{4,6},{6,4},{1,3},{3,1},{5,7},{7,5},{8,10},{10,8},{12,... | collective-permute-start | bytes 196616 | tf_op jit(solution)/shard_map/ppermute | solution.py:24
  35.6 2.0 %collective-permute-done.12.refs_3_ = bf16[64,512]{1,0:T(8,128)(2,1)S(1)} collective-permute-done((bf16[64,512]{1,0:T(8,128)(2,1)S(1)}, bf16[64,512]{1,0:T(8,128)(2,1)S(1)}, u32[]{:S(2)}, u32[]{:S(2)}) %collective-permute-start.12) | collective-permute-done | bytes 65568 | tf_op jit(solution)/shard_map/ppermute | solution.py:24
  37.6 1.5 %collective-permute-done.11.refs_2_ = bf16[64,512]{1,0:T(8,128)(2,1)S(1)} collective-permute-done((bf16[64,512]{1,0:T(8,128)(2,1)S(1)}, bf16[64,512]{1,0:T(8,128)(2,1)S(1)}, u32[]{:S(2)}, u32[]{:S(2)}) %collective-permute-start.11) | collective-permute-done | bytes 65568 | tf_op jit(solution)/shard_map/ppermute | solution.py:24
  39.2 0.0 collective-permute-done.10.refs_1_
  39.2 0.1 collective-permute-start.13
  39.3 1.5 %collective-permute-done.13.refs_4_ = bf16[4,64,512]{2,1,0:T(8,128)(2,1)S(1)} collective-permute-done((bf16[4,64,512]{2,1,0:T(8,128)(2,1)S(1)}, bf16[4,64,512]{2,1,0:T(8,128)(2,1)S(1)}, u32[]{:S(2)}, u32[]{:S(2)}) %collective-permute-start.13) | collective-permute-done | bytes 262176 | tf_op jit(solution)/shard_map/ppermute | solution.py:24
  40.8 0.0 copy-done.1
  40.8 0.0 copy-done.3
  40.8 1.4 %shard_map.75 = bf16[128,1024]{1,0:T(8,128)(2,1)} custom-call(s32[4,128]{1,0:T(4,128)S(1)} %bitcast.15, bf16[128,1024]{1,0:T(8,128)(2,1)S(1)} %copy-done.1, bf16[64,512]{1,0:T(8,128)(2,1)S(1)} %shard_map.74.refs_0_, bf16[64,512]{1,0:T(8,128)(2,1)S(1)} %collective-permute-done.10.refs_1_, bf16[64,512]{1,0:T(8,128)(2,1)S(1)} %collective-permute-done.11.refs_2_, ...), custom_call_target="tpu_custom_call" | custom-call | tf_op jit(solution)/shard_map/pallas_call | solution.py:286
  (5 shorter events, 0.1 us)
Async XLA Ops:
  0.0 6.0 %collective-permute-start = (bf16[4096,256]{1,0:T(8,128)(2,1)}, bf16[4096,256]{1,0:T(8,128)(2,1)S(1)}, u32[]{:S(2)}, u32[]{:S(2)}) collective-permute-start(bf16[4096,256]{1,0:T(8,128)(2,1)} %bitcast.7), channel_id=1, source_target_pairs={{0,1},{1,0},{2,3},{3,2},{4,5},{5,4},{6,7},{7,6},{8,9},{9,8},{10,11... | collective-permute-start | bytes 6291464 | tf_op jit(solution)/shard_map/ppermute | solution.py:24
  0.5 29.8 %copy-start = (bf16[4096,1,256]{2,0,1:T(8,128)(2,1)S(1)}, bf16[4096,1,256]{2,0,1:T(8,128)(2,1)}, u32[]{:S(2)}) copy-start(bf16[4096,1,256]{2,0,1:T(8,128)(2,1)} %param.11) | copy-start | bytes 6291460
  0.5 29.8 %copy-start.2 = (f32[4096]{0:T(1024)S(1)}, f32[4096]{0:T(1024)}, u32[]{:S(2)}) copy-start(f32[4096]{0:T(1024)} %param.10) | copy-start | bytes 49156
  5.8 1.6 %collective-permute-start.1 = (f32[64,1024]{1,0:T(8,128)S(1)}, f32[64,1024]{1,0:T(8,128)S(1)}, u32[]{:S(2)}, u32[]{:S(2)}) collective-permute-start(f32[64,1024]{1,0:T(8,128)S(1)} %get-tuple-element.19), channel_id=1, source_target_pairs={{0,1},{1,0},{2,3},{3,2},{4,5},{5,4},{6,7},{7,6},{8,9},{9,8},{10,11... | collective-permute-start | bytes 786440 | tf_op jit(solution)/shard_map/ppermute | solution.py:24
  7.5 8.6 %collective-permute-start.3 = (bf16[32,1024]{1,0:T(8,128)(2,1)S(1)}, bf16[32,1024]{1,0:T(8,128)(2,1)S(1)}, u32[]{:S(2)}, u32[]{:S(2)}) collective-permute-start(bf16[32,1024]{1,0:T(8,128)(2,1)S(1)} %slice.13), channel_id=1, source_target_pairs={{0,8},{1,17},{8,0},{9,25},{16,24},{17,1},{24,16},{25,9},{2,10},{3,... | collective-permute-start | bytes 196616 | tf_op jit(solution)/shard_map/ppermute | solution.py:48
  10.2 5.9 %collective-permute-start.2 = (bf16[16,1024]{1,0:T(8,128)(2,1)S(1)}, bf16[16,1024]{1,0:T(8,128)(2,1)S(1)}, u32[]{:S(2)}, u32[]{:S(2)}) collective-permute-start(bf16[16,1024]{1,0:T(8,128)(2,1)S(1)} %get-tuple-element.28), channel_id=1, source_target_pairs={{0,24},{1,25},{8,16},{9,17},{16,8},{17,9},{24,0},{25,1},{2,26},{3,... | collective-permute-start | bytes 98312 | tf_op jit(solution)/shard_map/ppermute | solution.py:48
  11.7 5.8 %collective-permute-start.6 = (bf16[16,1024]{1,0:T(8,128)(2,1)S(1)}, bf16[16,1024]{1,0:T(8,128)(2,1)S(1)}, u32[]{:S(2)}, u32[]{:S(2)}) collective-permute-start(bf16[16,1024]{1,0:T(8,128)(2,1)S(1)} %get-tuple-element.20.refs_0_), channel_id=1, source_target_pairs={{0,6},{2,4},{4,2},{6,0},{1,7},{3,5},{5,3},{7,1},{8,14},{10,12},{12... | collective-permute-start | bytes 98312 | tf_op jit(solution)/shard_map/ppermute | solution.py:24
  15.3 4.8 %collective-permute-start.5 = (bf16[16,1024]{1,0:T(8,128)(2,1)S(1)}, bf16[16,1024]{1,0:T(8,128)(2,1)S(1)}, u32[]{:S(2)}, u32[]{:S(2)}) collective-permute-start(bf16[16,1024]{1,0:T(8,128)(2,1)S(1)} %get-tuple-element.20.refs_0_), channel_id=1, source_target_pairs={{0,4},{2,6},{4,0},{6,2},{1,5},{3,7},{5,1},{7,3},{8,12},{10,14},{12... | collective-permute-start | bytes 98312 | tf_op jit(solution)/shard_map/ppermute | solution.py:24
  15.3 4.8 %collective-permute-start.4 = (bf16[16,1024]{1,0:T(8,128)(2,1)S(1)}, bf16[16,1024]{1,0:T(8,128)(2,1)S(1)}, u32[]{:S(2)}, u32[]{:S(2)}) collective-permute-start(bf16[16,1024]{1,0:T(8,128)(2,1)S(1)} %get-tuple-element.20.refs_0_), channel_id=1, source_target_pairs={{0,2},{2,0},{4,6},{6,4},{1,3},{3,1},{5,7},{7,5},{8,10},{10,8},{12,... | collective-permute-start | bytes 98312 | tf_op jit(solution)/shard_map/ppermute | solution.py:24
  20.1 7.1 %collective-permute-start.9 = (bf16[48,1024]{1,0:T(8,128)(2,1)S(1)}, bf16[48,1024]{1,0:T(8,128)(2,1)S(1)}, u32[]{:S(2)}, u32[]{:S(2)}) collective-permute-start(bf16[48,1024]{1,0:T(8,128)(2,1)S(1)} %pad_maximum_fusion.1.refs_4_), channel_id=1, source_target_pairs={{0,6},{2,4},{4,2},{6,0},{1,7},{3,5},{5,3},{7,1},{8,14},{10,12},{12... | collective-permute-start | bytes 294920 | tf_op jit(solution)/shard_map/ppermute | solution.py:24
  21.5 8.7 %collective-permute-start.8 = (bf16[48,1024]{1,0:T(8,128)(2,1)S(1)}, bf16[48,1024]{1,0:T(8,128)(2,1)S(1)}, u32[]{:S(2)}, u32[]{:S(2)}) collective-permute-start(bf16[48,1024]{1,0:T(8,128)(2,1)S(1)} %pad_maximum_fusion.1.refs_4_), channel_id=1, source_target_pairs={{0,4},{2,6},{4,0},{6,2},{1,5},{3,7},{5,1},{7,3},{8,12},{10,14},{12... | collective-permute-start | bytes 294920 | tf_op jit(solution)/shard_map/ppermute | solution.py:24
  22.1 8.1 %collective-permute-start.7 = (bf16[48,1024]{1,0:T(8,128)(2,1)S(1)}, bf16[48,1024]{1,0:T(8,128)(2,1)S(1)}, u32[]{:S(2)}, u32[]{:S(2)}) collective-permute-start(bf16[48,1024]{1,0:T(8,128)(2,1)S(1)} %pad_maximum_fusion.1.refs_4_), channel_id=1, source_target_pairs={{0,2},{2,0},{4,6},{6,4},{1,3},{3,1},{5,7},{7,5},{8,10},{10,8},{12,... | collective-permute-start | bytes 294920 | tf_op jit(solution)/shard_map/ppermute | solution.py:24
  30.2 10.6 %copy-start.1 = (bf16[128,1024]{1,0:T(8,128)(2,1)S(1)}, bf16[128,1024]{1,0:T(8,128)(2,1)}, u32[]{:S(2)}) copy-start(bf16[128,1024]{1,0:T(8,128)(2,1)} %query_ref.1) | copy-start | bytes 786436
  30.2 10.6 %copy-start.3 = (s32[512,1]{0,1:T(1,128)S(1)}, s32[512,1]{0,1:T(1,128)}, u32[]{:S(2)}) copy-start(s32[512,1]{0,1:T(1,128)} %param.12) | copy-start | bytes 6148
  31.2 6.4 %collective-permute-start.12 = (bf16[64,512]{1,0:T(8,128)(2,1)S(1)}, bf16[64,512]{1,0:T(8,128)(2,1)S(1)}, u32[]{:S(2)}, u32[]{:S(2)}) collective-permute-start(bf16[64,512]{1,0:T(8,128)(2,1)S(1)} %shard_map.74.refs_0_), channel_id=1, source_target_pairs={{0,6},{2,4},{4,2},{6,0},{1,7},{3,5},{5,3},{7,1},{8,14},{10,12},{12... | collective-permute-start | bytes 196616 | tf_op jit(solution)/shard_map/ppermute | solution.py:24
  33.4 5.7 %collective-permute-start.11 = (bf16[64,512]{1,0:T(8,128)(2,1)S(1)}, bf16[64,512]{1,0:T(8,128)(2,1)S(1)}, u32[]{:S(2)}, u32[]{:S(2)}) collective-permute-start(bf16[64,512]{1,0:T(8,128)(2,1)S(1)} %shard_map.74.refs_0_), channel_id=1, source_target_pairs={{0,4},{2,6},{4,0},{6,2},{1,5},{3,7},{5,1},{7,3},{8,12},{10,14},{12... | collective-permute-start | bytes 196616 | tf_op jit(solution)/shard_map/ppermute | solution.py:24
  33.4 5.7 %collective-permute-start.10 = (bf16[64,512]{1,0:T(8,128)(2,1)S(1)}, bf16[64,512]{1,0:T(8,128)(2,1)S(1)}, u32[]{:S(2)}, u32[]{:S(2)}) collective-permute-start(bf16[64,512]{1,0:T(8,128)(2,1)S(1)} %shard_map.74.refs_0_), channel_id=1, source_target_pairs={{0,2},{2,0},{4,6},{6,4},{1,3},{3,1},{5,7},{7,5},{8,10},{10,8},{12,... | collective-permute-start | bytes 196616 | tf_op jit(solution)/shard_map/ppermute | solution.py:24
  39.2 1.6 %collective-permute-start.13 = (bf16[4,64,512]{2,1,0:T(8,128)(2,1)S(1)}, bf16[4,64,512]{2,1,0:T(8,128)(2,1)S(1)}, u32[]{:S(2)}, u32[]{:S(2)}) collective-permute-start(bf16[4,64,512]{2,1,0:T(8,128)(2,1)S(1)} %pad_maximum_fusion), channel_id=1, source_target_pairs={{0,1},{1,0},{2,3},{3,2},{4,5},{5,4},{6,7},{7,6},{8,9},{9,8},{10,11... | collective-permute-start | bytes 786440 | tf_op jit(solution)/shard_map/ppermute | solution.py:24

commit v10 on v7

--- a/solution.py
+++ b/solution.py
@@ -22,6 +22,14 @@
 def swap(value, axis, offset):
     size = lax.axis_size(axis)
     return lax.ppermute(value, axis, [(i, i ^ offset) for i in range(size)])
+
+
+def seq_steps(parts):
+    return [0] + list(range(parts - 1, 0, -1))
+
+
+def spread(value):
+    return [swap(value, "seq", k) if k else value for k in seq_steps(lax.axis_size("seq"))]
 
 
 def routing(clips, cores, capacity):
@@ -75,42 +83,34 @@
 
 def ffn_kernel(capacity, cores, steps, dest_hbm, hidden_hbm, weight_hbm, residual_hbm,
                own_ref, send_ref, text_ref, dest_ref, hidden_ref, weight_ref, residual_ref,
-               packed_ref, total_ref, sems):
+               packed_ref, sems):
     clip, core = lax.axis_index("clip"), lax.axis_index("tp")
-    share = own_ref.shape[0]
-    block = hidden_hbm.shape[1] // steps
+    share, width = own_ref.shape
+    block = width // steps
+    parts = [pl.ds(i * block, block) for i in range(steps)]
     get_dest = pltpu.make_async_copy(dest_hbm, dest_ref, sems.at[steps])
     get_hidden = pltpu.make_async_copy(hidden_hbm, hidden_ref, sems.at[steps + 1])
     get_residual = pltpu.make_async_copy(residual_hbm, residual_ref, sems.at[steps + 2])
     get_weight = [
-        pltpu.make_async_copy(
-            weight_hbm.at[pl.ds(i * block, block), :],
-            weight_ref.at[pl.ds(i * block, block), :],
-            sems.at[i],
-        )
-        for i in range(steps)
+        pltpu.make_async_copy(weight_hbm.at[:, part], weight_ref.at[:, part], sems.at[i])
+        for i, part in enumerate(parts)
     ]
-    for copy in [get_dest, get_hidden] + get_weight + [get_residual]:
+    for copy in [get_dest, get_hidden] + get_weight[:-1] + [get_residual, get_weight[-1]]:
         copy.start()
     get_dest.wait()
     select = slot_select(dest_ref, clip, core, capacity, cores)
     get_hidden.wait()
     packed_ref[...] = jnp.dot(select, hidden_ref[...], preferred_element_type=F32).astype(BF16)
-    for i in range(steps):
-        part = pl.ds(i * block, block)
+    for i, part in enumerate(parts):
+        if i == steps - 1:
+            get_residual.wait()
+            text_ref[...] = jnp.dot(
+                select[:share], residual_ref[...], preferred_element_type=F32
+            ).astype(BF16)
         get_weight[i].wait()
-        product = jnp.dot(packed_ref[:, part], weight_ref[part, :], preferred_element_type=F32)
-        if i == 0:
-            total_ref[...] = product
-        elif i < steps - 1:
-            total_ref[...] += product
-        else:
-            own_ref[...] = total_ref[:share, :] + product[:share]
-            send_ref[...] = total_ref[share:, :] + product[share:]
-    get_residual.wait()
-    text_ref[...] = jnp.dot(
-        select[:share], residual_ref[...], preferred_element_type=F32
-    ).astype(BF16)
+        product = jnp.dot(packed_ref[...], weight_ref[:, part], preferred_element_type=F32)
+        own_ref[:, part] = product[:share]
+        send_ref[:, part] = product[share:]
 
 
 def ffn(dest, hidden, weight, residual, capacity, cores):
@@ -118,7 +118,7 @@
     width = weight.shape[1]
     slots = dest.shape[0] * capacity
     share = slots // cores
-    steps = math.gcd(5, depth // 128)
+    steps = max(1, width // 256)
     return pl.pallas_call(
         functools.partial(ffn_kernel, capacity, cores, steps),
         in_specs=[pl.BlockSpec(memory_space=pltpu.HBM)] * 4,
@@ -134,7 +134,6 @@
             pltpu.VMEM(weight.shape, BF16),
             pltpu.VMEM(residual.shape, BF16),
             pltpu.VMEM((slots, depth), BF16),
-            pltpu.VMEM((slots, width), F32),
             pltpu.SemaphoreType.DMA((steps + 3,)),
         ],
         compiler_params=pltpu.CompilerParams(vmem_limit_bytes=VMEM_LIMIT),
@@ -157,7 +156,7 @@
     scale = lax.rsqrt(squares / (parts * width) + EPSILON)
     totals = [0.0] * cores
     for k, text in enumerate(texts):
-        place = pl.ds(pl.multiple_of((seq ^ k) * width, width), width)
+        place = pl.ds(pl.multiple_of((seq ^ seq_steps(parts)[k]) * width, width), width)
         normed = (text[...].astype(F32) * scale * gain_ref[:, place]).astype(BF16)
         for c, weight in enumerate(weights):
             totals[c] += jnp.dot(normed, weight[place, :], preferred_element_type=F32)
@@ -190,7 +189,7 @@
 
     def columns(head):
         k, c, i = head
-        at = ((seq ^ k) * cores + (core ^ c)) * heads_here + i
+        at = ((seq ^ seq_steps(parts)[k]) * cores + (core ^ c)) * heads_here + i
         return pl.ds(pl.multiple_of(at * dim, dim), dim)
 
     def stored(head, offset):
@@ -201,7 +200,9 @@
             if g == 0:
                 found += [own[n * parts + k][:, at:at + dim] for n in range(groups)]
             else:
-                found += [others[g - 1][n * parts + k, :, at:at + dim] for n in range(groups)]
+                found += [
+                    others[n * (cores - 1) + g - 1][k, :, at:at + dim] for n in range(groups)
+                ]
         return jnp.concatenate(found, axis=0)
 
     group = 8
@@ -266,14 +267,12 @@
         route(text[edges[n]:edges[n + 1]], [some[n][0] for some in runs])
         for n in range(len(runs[0]))
     ]
-    own = []
+    own, others = [], []
     for group in groups:
         mine = jnp.concatenate([arrived[n] for n in group], axis=0)
-        texts = [mine] + [swap(mine, "seq", k) for k in range(1, parts)]
-        block = keyval(texts, gain, weights)
-        own += [block] + [swap(block, "seq", k) for k in range(1, parts)]
-    packed = jnp.stack(own)
-    others = [swap(packed, "tp", g) for g in range(1, cores)]
+        block = spread(keyval(spread(mine), gain, weights))
+        own += block
+        others += [swap(jnp.stack(block), "tp", g) for g in range(1, cores)]
     return pl.pallas_call(
         functools.partial(attend_kernel, parts, cores, heads_here, capacity, len(groups)),
         in_specs=[whole()] * (2 + len(own) + len(others)),

time: 42.8 us -> 42.7 us (level)
  starting transfers between devices: 26 us -> 24.6 us
  waiting for transfers between devices: 7.92 us -> 8.67 us
  Pallas kernels: 8.46 us -> 9.07 us
    ppermute x15 -> x16, starting transfers between devices: 21.8 us -> 20.4 us  [swap(): return lax.ppermute(value, axis, [(i, i ^ offset) for i in range(size)])]
    ppermute x15 -> x16, waiting for transfers between devices: 6.53 us -> 7.3 us  [swap(): return lax.ppermute(value, axis, [(i, i ^ offset) for i in range(size)])]
    pallas_call x1, Pallas kernels: 5.3 us -> 5.9 us  [ffn(): pl.pallas_call(functools.partial(ffn_kernel, capacity, cores, steps), in_...]
  transfers between devices with their start and end apart: 17 -> 18, of which waited for: 5 -> 6; matrix products, arithmetic and copies ran while one was open for 0% -> 0% of each run, Pallas kernels for 17% -> 18%
where the time goes in v10:
time: 42.7 us; the launch traced here: 42.6 us
  starting transfers between devices  24.6 us (58%)
  Pallas kernels  9.07 us (21%)
  waiting for transfers between devices  8.67 us (20%)
    ppermute x16, starting transfers between devices, swap(): return lax.ppermute(value, axis, [(i, i ^ offset) for i in range(size)])  20.4 us
    ppermute x16, waiting for transfers between devices, swap(): return lax.ppermute(value, axis, [(i, i ^ offset) for i in range(size)])  7.3 us
    pallas_call x1, Pallas kernels, ffn(): pl.pallas_call(functools.partial(ffn_kernel, capacity, cores, steps), in_...  5.9 us
    ppermute x2, starting transfers between devices, route(): moved = lax.ppermute(value, ('clip', 'tp'), pairs)  4.19 us
    pallas_call x2, Pallas kernels, keyval(): pl.pallas_call(functools.partial(keyval_kernel, parts, len(weights)), in_...  1.77 us
    pallas_call x1, Pallas kernels, shards(): pl.pallas_call(functools.partial(attend_kernel, parts, cores, heads_here,...  1.39 us
    ppermute x2, waiting for transfers between devices, route(): moved = lax.ppermute(value, ('clip', 'tp'), pairs)  1.37 us
  transfers between devices with their start and end apart: 18, of which 6 were waited for; matrix products, arithmetic and copies ran while one was open for 0% of the time, Pallas kernels for 18%

profile of v10, /device:TPU:0, one launch (start us, length us, event | category | flops | bytes accessed | tf_op | source)
XLA Modules:
  0.0 42.6 jit_solution(18203749312232223569)
XLA Ops:
  0.0 0.5 %collective-permute-start.5 = (bf16[4096,256]{1,0:T(8,128)(2,1)}, bf16[4096,256]{1,0:T(8,128)(2,1)S(1)}, u32[]{:S(2)}, u32[]{:S(2)}) collective-permute-start(bf16[4096,256]{1,0:T(8,128)(2,1)} %bitcast.11), channel_id=1, source_target_pairs={{0,1},{1,0},{2,3},{3,2},{4,5},{5,4},{6,7},{7,6},{8,9},{9,8},{10,11... | collective-permute-start | bytes 6291464 | tf_op jit(solution)/shard_map/ppermute | solution.py:24
  0.5 0.0 copy-start
  0.5 0.0 copy-start.2
  0.5 5.9 %shard_map.73 = (f32[64,1024]{1,0:T(8,128)S(1)}, f32[64,1024]{1,0:T(8,128)S(1)}, bf16[64,1024]{1,0:T(8,128)(2,1)S(1)}) custom-call(s32[4,128]{1,0:T(4,128)} %bitcast.24, bf16[128,5120]{1,0:T(8,128)(2,1)} %hidden_hbm.1, bf16[5120,1024]{1,0:T(8,128)(2,1)} %weight_hbm.1, bf16[128,1024]{1,0:T(8,128)(2,1)} %residual_hbm.1), custom_call_target="tpu_custom_call" | custom-call | flops 1509949440 | bytes 11796480 | tf_op jit(solution)/shard_map/pallas_call | solution.py:122
  6.4 0.1 collective-permute-start
  6.5 1.5 %collective-permute-done = f32[64,1024]{1,0:T(8,128)S(1)} collective-permute-done((f32[64,1024]{1,0:T(8,128)S(1)}, f32[64,1024]{1,0:T(8,128)S(1)}, u32[]{:S(2)}, u32[]{:S(2)}) %collective-permute-start) | collective-permute-done | bytes 262176 | tf_op jit(solution)/shard_map/ppermute | solution.py:24
  8.0 3.7 %collective-permute-start.1 = (bf16[16,1024]{1,0:T(8,128)(2,1)S(1)}, bf16[16,1024]{1,0:T(8,128)(2,1)S(1)}, u32[]{:S(2)}, u32[]{:S(2)}) collective-permute-start(bf16[16,1024]{1,0:T(8,128)(2,1)S(1)} %get-tuple-element.12), channel_id=1, source_target_pairs={{0,24},{1,25},{8,16},{9,17},{16,8},{17,9},{24,0},{25,1},{2,26},{3,... | collective-permute-start | bytes 98312 | tf_op jit(solution)/shard_map/ppermute | solution.py:56
  11.7 0.5 %collective-permute-start.9 = (bf16[32,1024]{1,0:T(8,128)(2,1)S(1)}, bf16[32,1024]{1,0:T(8,128)(2,1)S(1)}, u32[]{:S(2)}, u32[]{:S(2)}) collective-permute-start(bf16[32,1024]{1,0:T(8,128)(2,1)S(1)} %slice.14), channel_id=1, source_target_pairs={{0,8},{1,17},{8,0},{9,25},{16,24},{17,1},{24,16},{25,9},{2,10},{3,... | collective-permute-start | bytes 196616 | tf_op jit(solution)/shard_map/ppermute | solution.py:56
  12.2 1.4 %collective-permute-done.1 = bf16[16,1024]{1,0:T(8,128)(2,1)S(1)} collective-permute-done((bf16[16,1024]{1,0:T(8,128)(2,1)S(1)}, bf16[16,1024]{1,0:T(8,128)(2,1)S(1)}, u32[]{:S(2)}, u32[]{:S(2)}) %collective-permute-start.1) | collective-permute-done | bytes 32800 | tf_op jit(solution)/shard_map/ppermute | solution.py:56
  13.6 4.1 %collective-permute-start.2 = (bf16[32,1024]{1,0:T(8,128)(2,1)S(1)}, bf16[32,1024]{1,0:T(8,128)(2,1)S(1)}, u32[]{:S(2)}, u32[]{:S(2)}) collective-permute-start(bf16[32,1024]{1,0:T(8,128)(2,1)S(1)} %pad_maximum_fusion.2.refs_0_), channel_id=1, source_target_pairs={{0,6},{2,4},{4,2},{6,0},{1,7},{3,5},{5,3},{7,1},{8,14},{10,12},{12... | collective-permute-start | bytes 196616 | tf_op jit(solution)/shard_map/ppermute | solution.py:24
  17.7 0.0 collective-permute-start.3
  17.7 0.6 %collective-permute-start.4 = (bf16[32,1024]{1,0:T(8,128)(2,1)S(1)}, bf16[32,1024]{1,0:T(8,128)(2,1)S(1)}, u32[]{:S(2)}, u32[]{:S(2)}) collective-permute-start(bf16[32,1024]{1,0:T(8,128)(2,1)S(1)} %pad_maximum_fusion.2.refs_0_), channel_id=1, source_target_pairs={{0,2},{2,0},{4,6},{6,4},{1,3},{3,1},{5,7},{7,5},{8,10},{10,8},{12,... | collective-permute-start | bytes 196616 | tf_op jit(solution)/shard_map/ppermute | solution.py:24
  18.3 0.0 collective-permute-done.9.refs_0_
  18.3 3.7 %collective-permute-start.10 = (bf16[32,1024]{1,0:T(8,128)(2,1)S(1)}, bf16[32,1024]{1,0:T(8,128)(2,1)S(1)}, u32[]{:S(2)}, u32[]{:S(2)}) collective-permute-start(bf16[32,1024]{1,0:T(8,128)(2,1)S(1)} %collective-permute-done.9.refs_0_), channel_id=1, source_target_pairs={{0,6},{2,4},{4,2},{6,0},{1,7},{3,5},{5,3},{7,1},{8,14},{10,12},{12... | collective-permute-start | bytes 196616 | tf_op jit(solution)/shard_map/ppermute | solution.py:24
  22.0 0.0 collective-permute-done.2.refs_1_
  22.1 2.4 %collective-permute-start.11 = (bf16[32,1024]{1,0:T(8,128)(2,1)S(1)}, bf16[32,1024]{1,0:T(8,128)(2,1)S(1)}, u32[]{:S(2)}, u32[]{:S(2)}) collective-permute-start(bf16[32,1024]{1,0:T(8,128)(2,1)S(1)} %collective-permute-done.9.refs_0_), channel_id=1, source_target_pairs={{0,4},{2,6},{4,0},{6,2},{1,5},{3,7},{5,1},{7,3},{8,12},{10,14},{12... | collective-permute-start | bytes 196616 | tf_op jit(solution)/shard_map/ppermute | solution.py:24
  24.5 1.4 %collective-permute-done.3.refs_2_ = bf16[32,1024]{1,0:T(8,128)(2,1)S(1)} collective-permute-done((bf16[32,1024]{1,0:T(8,128)(2,1)S(1)}, bf16[32,1024]{1,0:T(8,128)(2,1)S(1)}, u32[]{:S(2)}, u32[]{:S(2)}) %collective-permute-start.3) | collective-permute-done | bytes 65568 | tf_op jit(solution)/shard_map/ppermute | solution.py:24
  25.9 0.0 collective-permute-start.12
  25.9 0.0 collective-permute-done.4.refs_3_
  25.9 0.0 collective-permute-done.5.refs_6_
  25.9 0.0 copy-done
  25.9 0.0 copy-done.2
  25.9 0.9 %shard_map.74.refs_0_ = bf16[32,512]{1,0:T(8,128)(2,1)S(1)} custom-call(bf16[32,1024]{1,0:T(8,128)(2,1)S(1)} %pad_maximum_fusion.2.refs_0_, bf16[32,1024]{1,0:T(8,128)(2,1)S(1)} %collective-permute-done.2.refs_1_, bf16[32,1024]{1,0:T(8,128)(2,1)S(1)} %collective-permute-done.3.refs_2_, bf16[32,1024]{1,0:T(8,128)(2,1)S(1)} %collective-permute-done.4.refs_3_, ...), custom_call_target="tpu_custom_call" | custom-call | flops 134217728 | bytes 4456448 | tf_op jit(solution)/shard_map/pallas_call | solution.py:236
  26.8 0.0 copy-start.1
  26.8 0.0 copy-start.3
  26.8 2.8 %collective-permute-start.6 = (bf16[32,512]{1,0:T(8,128)(2,1)S(1)}, bf16[32,512]{1,0:T(8,128)(2,1)S(1)}, u32[]{:S(2)}, u32[]{:S(2)}) collective-permute-start(bf16[32,512]{1,0:T(8,128)(2,1)S(1)} %shard_map.74.refs_0_), channel_id=1, source_target_pairs={{0,6},{2,4},{4,2},{6,0},{1,7},{3,5},{5,3},{7,1},{8,14},{10,12},{12... | collective-permute-start | bytes 98312 | tf_op jit(solution)/shard_map/ppermute | solution.py:24
  29.7 0.7 %collective-permute-start.7 = (bf16[32,512]{1,0:T(8,128)(2,1)S(1)}, bf16[32,512]{1,0:T(8,128)(2,1)S(1)}, u32[]{:S(2)}, u32[]{:S(2)}) collective-permute-start(bf16[32,512]{1,0:T(8,128)(2,1)S(1)} %shard_map.74.refs_0_), channel_id=1, source_target_pairs={{0,4},{2,6},{4,0},{6,2},{1,5},{3,7},{5,1},{7,3},{8,12},{10,14},{12... | collective-permute-start | bytes 98312 | tf_op jit(solution)/shard_map/ppermute | solution.py:24
  30.4 0.0 collective-permute-done.10.refs_1_
  30.4 0.9 %collective-permute-start.8 = (bf16[32,512]{1,0:T(8,128)(2,1)S(1)}, bf16[32,512]{1,0:T(8,128)(2,1)S(1)}, u32[]{:S(2)}, u32[]{:S(2)}) collective-permute-start(bf16[32,512]{1,0:T(8,128)(2,1)S(1)} %shard_map.74.refs_0_), channel_id=1, source_target_pairs={{0,2},{2,0},{4,6},{6,4},{1,3},{3,1},{5,7},{7,5},{8,10},{10,8},{12,... | collective-permute-start | bytes 98312 | tf_op jit(solution)/shard_map/ppermute | solution.py:24
  31.3 0.0 collective-permute-done.11.refs_2_
  31.3 0.0 collective-permute-done.12.refs_3_
  31.3 0.9 %shard_map.75.refs_4_ = bf16[32,512]{1,0:T(8,128)(2,1)S(1)} custom-call(bf16[32,1024]{1,0:T(8,128)(2,1)S(1)} %collective-permute-done.9.refs_0_, bf16[32,1024]{1,0:T(8,128)(2,1)S(1)} %collective-permute-done.10.refs_1_, bf16[32,1024]{1,0:T(8,128)(2,1)S(1)} %collective-permute-done.11.refs_2_, bf16[32,1024]{1,0:T(8,128)(2,1)S(1)} %collective-permute-done.12.refs_3_, ...), custom_call_target="tpu_custom_call" | custom-call | flops 134217728 | bytes 4456448 | tf_op jit(solution)/shard_map/pallas_call | solution.py:236
  32.2 2.8 %collective-permute-start.13 = (bf16[32,512]{1,0:T(8,128)(2,1)S(1)}, bf16[32,512]{1,0:T(8,128)(2,1)S(1)}, u32[]{:S(2)}, u32[]{:S(2)}) collective-permute-start(bf16[32,512]{1,0:T(8,128)(2,1)S(1)} %shard_map.75.refs_4_), channel_id=1, source_target_pairs={{0,6},{2,4},{4,2},{6,0},{1,7},{3,5},{5,3},{7,1},{8,14},{10,12},{12... | collective-permute-start | bytes 98312 | tf_op jit(solution)/shard_map/ppermute | solution.py:24
  34.9 0.0 collective-permute-start.14
  34.9 0.0 collective-permute-done.6.refs_1_
  35.0 1.6 %collective-permute-start.15 = (bf16[32,512]{1,0:T(8,128)(2,1)S(1)}, bf16[32,512]{1,0:T(8,128)(2,1)S(1)}, u32[]{:S(2)}, u32[]{:S(2)}) collective-permute-start(bf16[32,512]{1,0:T(8,128)(2,1)S(1)} %shard_map.75.refs_4_), channel_id=1, source_target_pairs={{0,2},{2,0},{4,6},{6,4},{1,3},{3,1},{5,7},{7,5},{8,10},{10,8},{12,... | collective-permute-start | bytes 98312 | tf_op jit(solution)/shard_map/ppermute | solution.py:24
  36.6 0.0 collective-permute-done.7.refs_2_
  36.6 0.0 collective-permute-done.8.refs_3_
  36.6 0.1 collective-permute-start.16
  36.7 1.2 %collective-permute-done.13.refs_5_ = bf16[32,512]{1,0:T(8,128)(2,1)S(1)} collective-permute-done((bf16[32,512]{1,0:T(8,128)(2,1)S(1)}, bf16[32,512]{1,0:T(8,128)(2,1)S(1)}, u32[]{:S(2)}, u32[]{:S(2)}) %collective-permute-start.13) | collective-permute-done | bytes 32800 | tf_op jit(solution)/shard_map/ppermute | solution.py:24
  37.9 1.9 %collective-permute-done.14.refs_6_ = bf16[32,512]{1,0:T(8,128)(2,1)S(1)} collective-permute-done((bf16[32,512]{1,0:T(8,128)(2,1)S(1)}, bf16[32,512]{1,0:T(8,128)(2,1)S(1)}, u32[]{:S(2)}, u32[]{:S(2)}) %collective-permute-start.14) | collective-permute-done | bytes 32800 | tf_op jit(solution)/shard_map/ppermute | solution.py:24
  39.8 0.0 collective-permute-done.15.refs_7_
  39.8 0.1 collective-permute-start.17
  39.9 0.0 collective-permute-done.16.refs_8_
  39.9 1.3 %collective-permute-done.17.refs_9_ = bf16[4,32,512]{2,1,0:T(8,128)(2,1)S(1)} collective-permute-done((bf16[4,32,512]{2,1,0:T(8,128)(2,1)S(1)}, bf16[4,32,512]{2,1,0:T(8,128)(2,1)S(1)}, u32[]{:S(2)}, u32[]{:S(2)}) %collective-permute-start.17) | collective-permute-done | bytes 131104 | tf_op jit(solution)/shard_map/ppermute | solution.py:24
  41.2 0.0 copy-done.1
  41.2 0.0 copy-done.3
  41.2 1.4 %shard_map.76 = bf16[128,1024]{1,0:T(8,128)(2,1)} custom-call(s32[4,128]{1,0:T(4,128)S(1)} %bitcast.25, bf16[128,1024]{1,0:T(8,128)(2,1)S(1)} %copy-done.1, bf16[32,512]{1,0:T(8,128)(2,1)S(1)} %shard_map.74.refs_0_, bf16[32,512]{1,0:T(8,128)(2,1)S(1)} %collective-permute-done.6.refs_1_, bf16[32,512]{1,0:T(8,128)(2,1)S(1)} %collective-permute-done.7.refs_2_, ...), custom_call_target="tpu_custom_call" | custom-call | tf_op jit(solution)/shard_map/pallas_call | solution.py:276
  (6 shorter events, 0.1 us)
Async XLA Ops:
  0.0 25.9 %collective-permute-start.5 = (bf16[4096,256]{1,0:T(8,128)(2,1)}, bf16[4096,256]{1,0:T(8,128)(2,1)S(1)}, u32[]{:S(2)}, u32[]{:S(2)}) collective-permute-start(bf16[4096,256]{1,0:T(8,128)(2,1)} %bitcast.11), channel_id=1, source_target_pairs={{0,1},{1,0},{2,3},{3,2},{4,5},{5,4},{6,7},{7,6},{8,9},{9,8},{10,11... | collective-permute-start | bytes 6291464 | tf_op jit(solution)/shard_map/ppermute | solution.py:24
  0.5 25.4 %copy-start = (bf16[4096,1,256]{2,0,1:T(8,128)(2,1)S(1)}, bf16[4096,1,256]{2,0,1:T(8,128)(2,1)}, u32[]{:S(2)}) copy-start(bf16[4096,1,256]{2,0,1:T(8,128)(2,1)} %param.11) | copy-start | bytes 6291460
  0.5 25.4 %copy-start.2 = (f32[4096]{0:T(1024)S(1)}, f32[4096]{0:T(1024)}, u32[]{:S(2)}) copy-start(f32[4096]{0:T(1024)} %param.10) | copy-start | bytes 49156
  6.4 1.6 %collective-permute-start = (f32[64,1024]{1,0:T(8,128)S(1)}, f32[64,1024]{1,0:T(8,128)S(1)}, u32[]{:S(2)}, u32[]{:S(2)}) collective-permute-start(f32[64,1024]{1,0:T(8,128)S(1)} %get-tuple-element.10), channel_id=1, source_target_pairs={{0,1},{1,0},{2,3},{3,2},{4,5},{5,4},{6,7},{7,6},{8,9},{9,8},{10,11... | collective-permute-start | bytes 786440 | tf_op jit(solution)/shard_map/ppermute | solution.py:24
  8.0 5.6 %collective-permute-start.1 = (bf16[16,1024]{1,0:T(8,128)(2,1)S(1)}, bf16[16,1024]{1,0:T(8,128)(2,1)S(1)}, u32[]{:S(2)}, u32[]{:S(2)}) collective-permute-start(bf16[16,1024]{1,0:T(8,128)(2,1)S(1)} %get-tuple-element.12), channel_id=1, source_target_pairs={{0,24},{1,25},{8,16},{9,17},{16,8},{17,9},{24,0},{25,1},{2,26},{3,... | collective-permute-start | bytes 98312 | tf_op jit(solution)/shard_map/ppermute | solution.py:56
  11.7 6.6 %collective-permute-start.9 = (bf16[32,1024]{1,0:T(8,128)(2,1)S(1)}, bf16[32,1024]{1,0:T(8,128)(2,1)S(1)}, u32[]{:S(2)}, u32[]{:S(2)}) collective-permute-start(bf16[32,1024]{1,0:T(8,128)(2,1)S(1)} %slice.14), channel_id=1, source_target_pairs={{0,8},{1,17},{8,0},{9,25},{16,24},{17,1},{24,16},{25,9},{2,10},{3,... | collective-permute-start | bytes 196616 | tf_op jit(solution)/shard_map/ppermute | solution.py:56
  13.6 8.4 %collective-permute-start.2 = (bf16[32,1024]{1,0:T(8,128)(2,1)S(1)}, bf16[32,1024]{1,0:T(8,128)(2,1)S(1)}, u32[]{:S(2)}, u32[]{:S(2)}) collective-permute-start(bf16[32,1024]{1,0:T(8,128)(2,1)S(1)} %pad_maximum_fusion.2.refs_0_), channel_id=1, source_target_pairs={{0,6},{2,4},{4,2},{6,0},{1,7},{3,5},{5,3},{7,1},{8,14},{10,12},{12... | collective-permute-start | bytes 196616 | tf_op jit(solution)/shard_map/ppermute | solution.py:24
  17.7 8.2 %collective-permute-start.3 = (bf16[32,1024]{1,0:T(8,128)(2,1)S(1)}, bf16[32,1024]{1,0:T(8,128)(2,1)S(1)}, u32[]{:S(2)}, u32[]{:S(2)}) collective-permute-start(bf16[32,1024]{1,0:T(8,128)(2,1)S(1)} %pad_maximum_fusion.2.refs_0_), channel_id=1, source_target_pairs={{0,4},{2,6},{4,0},{6,2},{1,5},{3,7},{5,1},{7,3},{8,12},{10,14},{12... | collective-permute-start | bytes 196616 | tf_op jit(solution)/shard_map/ppermute | solution.py:24
  17.7 8.2 %collective-permute-start.4 = (bf16[32,1024]{1,0:T(8,128)(2,1)S(1)}, bf16[32,1024]{1,0:T(8,128)(2,1)S(1)}, u32[]{:S(2)}, u32[]{:S(2)}) collective-permute-start(bf16[32,1024]{1,0:T(8,128)(2,1)S(1)} %pad_maximum_fusion.2.refs_0_), channel_id=1, source_target_pairs={{0,2},{2,0},{4,6},{6,4},{1,3},{3,1},{5,7},{7,5},{8,10},{10,8},{12,... | collective-permute-start | bytes 196616 | tf_op jit(solution)/shard_map/ppermute | solution.py:24
  18.3 12.1 %collective-permute-start.10 = (bf16[32,1024]{1,0:T(8,128)(2,1)S(1)}, bf16[32,1024]{1,0:T(8,128)(2,1)S(1)}, u32[]{:S(2)}, u32[]{:S(2)}) collective-permute-start(bf16[32,1024]{1,0:T(8,128)(2,1)S(1)} %collective-permute-done.9.refs_0_), channel_id=1, source_target_pairs={{0,6},{2,4},{4,2},{6,0},{1,7},{3,5},{5,3},{7,1},{8,14},{10,12},{12... | collective-permute-start | bytes 196616 | tf_op jit(solution)/shard_map/ppermute | solution.py:24
  22.1 9.2 %collective-permute-start.11 = (bf16[32,1024]{1,0:T(8,128)(2,1)S(1)}, bf16[32,1024]{1,0:T(8,128)(2,1)S(1)}, u32[]{:S(2)}, u32[]{:S(2)}) collective-permute-start(bf16[32,1024]{1,0:T(8,128)(2,1)S(1)} %collective-permute-done.9.refs_0_), channel_id=1, source_target_pairs={{0,4},{2,6},{4,0},{6,2},{1,5},{3,7},{5,1},{7,3},{8,12},{10,14},{12... | collective-permute-start | bytes 196616 | tf_op jit(solution)/shard_map/ppermute | solution.py:24
  25.9 5.4 %collective-permute-start.12 = (bf16[32,1024]{1,0:T(8,128)(2,1)S(1)}, bf16[32,1024]{1,0:T(8,128)(2,1)S(1)}, u32[]{:S(2)}, u32[]{:S(2)}) collective-permute-start(bf16[32,1024]{1,0:T(8,128)(2,1)S(1)} %collective-permute-done.9.refs_0_), channel_id=1, source_target_pairs={{0,2},{2,0},{4,6},{6,4},{1,3},{3,1},{5,7},{7,5},{8,10},{10,8},{12,... | collective-permute-start | bytes 196616 | tf_op jit(solution)/shard_map/ppermute | solution.py:24
  26.8 14.4 %copy-start.1 = (bf16[128,1024]{1,0:T(8,128)(2,1)S(1)}, bf16[128,1024]{1,0:T(8,128)(2,1)}, u32[]{:S(2)}) copy-start(bf16[128,1024]{1,0:T(8,128)(2,1)} %query_ref.1) | copy-start | bytes 786436
  26.8 14.4 %copy-start.3 = (s32[512,1]{0,1:T(1,128)S(1)}, s32[512,1]{0,1:T(1,128)}, u32[]{:S(2)}) copy-start(s32[512,1]{0,1:T(1,128)} %param.12) | copy-start | bytes 6148
  26.8 8.1 %collective-permute-start.6 = (bf16[32,512]{1,0:T(8,128)(2,1)S(1)}, bf16[32,512]{1,0:T(8,128)(2,1)S(1)}, u32[]{:S(2)}, u32[]{:S(2)}) collective-permute-start(bf16[32,512]{1,0:T(8,128)(2,1)S(1)} %shard_map.74.refs_0_), channel_id=1, source_target_pairs={{0,6},{2,4},{4,2},{6,0},{1,7},{3,5},{5,3},{7,1},{8,14},{10,12},{12... | collective-permute-start | bytes 98312 | tf_op jit(solution)/shard_map/ppermute | solution.py:24
  29.7 6.9 %collective-permute-start.7 = (bf16[32,512]{1,0:T(8,128)(2,1)S(1)}, bf16[32,512]{1,0:T(8,128)(2,1)S(1)}, u32[]{:S(2)}, u32[]{:S(2)}) collective-permute-start(bf16[32,512]{1,0:T(8,128)(2,1)S(1)} %shard_map.74.refs_0_), channel_id=1, source_target_pairs={{0,4},{2,6},{4,0},{6,2},{1,5},{3,7},{5,1},{7,3},{8,12},{10,14},{12... | collective-permute-start | bytes 98312 | tf_op jit(solution)/shard_map/ppermute | solution.py:24
  30.4 6.2 %collective-permute-start.8 = (bf16[32,512]{1,0:T(8,128)(2,1)S(1)}, bf16[32,512]{1,0:T(8,128)(2,1)S(1)}, u32[]{:S(2)}, u32[]{:S(2)}) collective-permute-start(bf16[32,512]{1,0:T(8,128)(2,1)S(1)} %shard_map.74.refs_0_), channel_id=1, source_target_pairs={{0,2},{2,0},{4,6},{6,4},{1,3},{3,1},{5,7},{7,5},{8,10},{10,8},{12,... | collective-permute-start | bytes 98312 | tf_op jit(solution)/shard_map/ppermute | solution.py:24
  32.2 5.7 %collective-permute-start.13 = (bf16[32,512]{1,0:T(8,128)(2,1)S(1)}, bf16[32,512]{1,0:T(8,128)(2,1)S(1)}, u32[]{:S(2)}, u32[]{:S(2)}) collective-permute-start(bf16[32,512]{1,0:T(8,128)(2,1)S(1)} %shard_map.75.refs_4_), channel_id=1, source_target_pairs={{0,6},{2,4},{4,2},{6,0},{1,7},{3,5},{5,3},{7,1},{8,14},{10,12},{12... | collective-permute-start | bytes 98312 | tf_op jit(solution)/shard_map/ppermute | solution.py:24
  34.9 4.8 %collective-permute-start.14 = (bf16[32,512]{1,0:T(8,128)(2,1)S(1)}, bf16[32,512]{1,0:T(8,128)(2,1)S(1)}, u32[]{:S(2)}, u32[]{:S(2)}) collective-permute-start(bf16[32,512]{1,0:T(8,128)(2,1)S(1)} %shard_map.75.refs_4_), channel_id=1, source_target_pairs={{0,4},{2,6},{4,0},{6,2},{1,5},{3,7},{5,1},{7,3},{8,12},{10,14},{12... | collective-permute-start | bytes 98312 | tf_op jit(solution)/shard_map/ppermute | solution.py:24
  35.0 4.8 %collective-permute-start.15 = (bf16[32,512]{1,0:T(8,128)(2,1)S(1)}, bf16[32,512]{1,0:T(8,128)(2,1)S(1)}, u32[]{:S(2)}, u32[]{:S(2)}) collective-permute-start(bf16[32,512]{1,0:T(8,128)(2,1)S(1)} %shard_map.75.refs_4_), channel_id=1, source_target_pairs={{0,2},{2,0},{4,6},{6,4},{1,3},{3,1},{5,7},{7,5},{8,10},{10,8},{12,... | collective-permute-start | bytes 98312 | tf_op jit(solution)/shard_map/ppermute | solution.py:24
  36.6 3.3 %collective-permute-start.16 = (bf16[4,32,512]{2,1,0:T(8,128)(2,1)S(1)}, bf16[4,32,512]{2,1,0:T(8,128)(2,1)S(1)}, u32[]{:S(2)}, u32[]{:S(2)}) collective-permute-start(bf16[4,32,512]{2,1,0:T(8,128)(2,1)S(1)} %pad_maximum_fusion), channel_id=1, source_target_pairs={{0,1},{1,0},{2,3},{3,2},{4,5},{5,4},{6,7},{7,6},{8,9},{9,8},{10,11... | collective-permute-start | bytes 393224 | tf_op jit(solution)/shard_map/ppermute | solution.py:24
  39.8 1.4 %collective-permute-start.17 = (bf16[4,32,512]{2,1,0:T(8,128)(2,1)S(1)}, bf16[4,32,512]{2,1,0:T(8,128)(2,1)S(1)}, u32[]{:S(2)}, u32[]{:S(2)}) collective-permute-start(bf16[4,32,512]{2,1,0:T(8,128)(2,1)S(1)} %pad_maximum_fusion.1), channel_id=1, source_target_pairs={{0,1},{1,0},{2,3},{3,2},{4,5},{5,4},{6,7},{7,6},{8,9},{9,8},{10,11... | collective-permute-start | bytes 393224 | tf_op jit(solution)/shard_map/ppermute | solution.py:24

commit v11 on v4

--- a/solution.py
+++ b/solution.py
@@ -24,9 +24,17 @@
     return lax.ppermute(value, axis, [(i, i ^ offset) for i in range(size)])
 
 
+def seq_steps(parts):
+    return [0] + list(range(parts - 1, 0, -1))
+
+
+def spread(value):
+    return [swap(value, "seq", k) if k else value for k in seq_steps(lax.axis_size("seq"))]
+
+
 def route_offsets(clips, cores):
     if clips == 4 and cores == 2:
-        return [0, 3, 1, 2]
+        return [3, 0, 2, 1]
     return list(range(clips))
 
 
@@ -142,7 +150,7 @@
     scale = lax.rsqrt(squares / (parts * width) + EPSILON)
     totals = [0.0] * cores
     for k, text in enumerate(texts):
-        place = pl.ds(pl.multiple_of((seq ^ k) * width, width), width)
+        place = pl.ds(pl.multiple_of((seq ^ seq_steps(parts)[k]) * width, width), width)
         normed = (text[...].astype(F32) * scale * gain_ref[:, place]).astype(BF16)
         for c, weight in enumerate(weights):
             totals[c] += jnp.dot(normed, weight[place, :], preferred_element_type=F32)
@@ -151,9 +159,14 @@
         out_ref[:, c * each:(c + 1) * each] = totals[c].astype(BF16)
 
 
-def attend_kernel(parts, cores, heads_here, capacity, groups, dest_ref, query_ref, *refs):
-    blocks, out_ref = refs[:-1], refs[-1]
-    each = parts + cores - 1
+def attend_kernel(parts, cores, heads_here, capacity, steps, counts_of, dest_ref, query_ref, *refs):
+    groups, stacks = sum(counts_of) // len(steps), len(counts_of)
+    own, refs = refs[:groups * len(steps)], refs[groups * len(steps):]
+    found_of = [
+        [stack.at[n] for count, stack in zip(counts_of, refs[g * stacks:(g + 1) * stacks]) for n in range(count)]
+        for g in range(cores - 1)
+    ]
+    done, out_ref = refs[(cores - 1) * stacks:-1], refs[-1]
     clip, seq, core = lax.axis_index("clip"), lax.axis_index("seq"), lax.axis_index("tp")
     clips = dest_ref.shape[0]
     slots = clips * capacity
@@ -169,11 +182,13 @@
         axis=0, keepdims=True,
     )
     valid = lax.broadcasted_iota(jnp.int32, (1, slots), 1) % capacity < limit
-    heads = [(k, c, i) for k in range(parts) for c in range(cores) for i in range(heads_here)]
+    heads = [
+        (k, c, i) for k in range(len(steps)) for c in range(cores) for i in range(heads_here)
+    ]
 
     def columns(head):
         k, c, i = head
-        at = ((seq ^ k) * cores + (core ^ c)) * heads_here + i
+        at = ((seq ^ steps[k]) * cores + (core ^ c)) * heads_here + i
         return pl.ds(pl.multiple_of(at * dim, dim), dim)
 
     def stored(head, offset):
@@ -181,13 +196,13 @@
         found = []
         for g in range(cores):
             at = ((c ^ g) * heads_here + i) * 2 * dim + offset
-            for first in range(0, groups * each, each):
-                if g == 0:
-                    found.append(blocks[first + k][:, at:at + dim])
-                else:
-                    found.append(blocks[first + parts + g - 1][k, :, at:at + dim])
+            for n in range(groups):
+                block = own[n * len(steps) + k] if g == 0 else found_of[g - 1][n * len(steps) + k]
+                found.append(block[:, at:at + dim])
         return jnp.concatenate(found, axis=0)
 
+    if done:
+        out_ref[...] = done[0][...]
     group = 8
     for first in range(0, len(heads), group):
         some = heads[first:first + group]
@@ -227,7 +242,7 @@
             bytes_accessed=2 * parts * width * (rows + wide),
             transcendentals=0,
         ),
-    )(*texts, gain, *weights)
+    )(*texts, gain, *[pltpu.with_memory_space_constraint(x, pltpu.VMEM) for x in weights])
 
 
 def shards(ffn_hidden, ffn_weight, residual, norm_gain, kv_weight, destination, queries):
@@ -246,24 +261,36 @@
     text = (text.astype(F32) + own).astype(BF16)
     places = clips // cores
     groups = math.gcd(2, places)
-    blocks = []
+    own = []
     for first in range(0, places, places // groups):
         arrived = [
             route(text[i * capacity:(i + 1) * capacity], i)
             for i in range(first, first + places // groups)
         ]
         arrived = jnp.concatenate(arrived, axis=0)
-        texts = [arrived] + [swap(arrived, "seq", k) for k in range(1, parts)]
-        block = keyval(texts, gain, weights)
-        block = [block] + [swap(block, "seq", k) for k in range(1, parts)]
-        blocks += block + [swap(jnp.stack(block), "tp", g) for g in range(1, cores)]
-    return pl.pallas_call(
-        functools.partial(attend_kernel, parts, cores, heads_here, capacity, groups),
-        in_specs=[whole()] * (2 + len(blocks)),
-        out_specs=whole(),
-        out_shape=jax.ShapeDtypeStruct(queries.shape, BF16),
-        compiler_params=pltpu.CompilerParams(vmem_limit_bytes=VMEM_LIMIT),
-    )(dest, queries, *blocks)
+        own.append(spread(keyval(spread(arrived), gain, weights)))
+
+    def crossed(blocks):
+        return [swap(jnp.stack(blocks), "tp", g) for g in range(1, cores)]
+
+    def attend(steps, blocks, stacks, counts_of, done):
+        return pl.pallas_call(
+            functools.partial(
+                attend_kernel, parts, cores, heads_here, capacity, steps, counts_of
+            ),
+            in_specs=[whole()] * (2 + len(blocks) + len(stacks) + len(done)),
+            out_specs=whole(),
+            out_shape=jax.ShapeDtypeStruct(queries.shape, BF16),
+            compiler_params=pltpu.CompilerParams(vmem_limit_bytes=VMEM_LIMIT),
+        )(dest, queries, *blocks, *stacks, *done)
+
+    cut = max(1, parts // 2)
+    steps = seq_steps(parts)
+    soon = [block for some in own for block in some[:cut]]
+    late = [block for some in own for block in some[cut:]]
+    soon_crossed, late_crossed = crossed(soon), crossed(late)
+    done = [attend(steps[:cut], soon, soon_crossed, [len(soon)], [])]
+    return attend(steps[cut:], late, late_crossed, [len(late)], done)
 
 
 def solution(mesh):

time: 40.1 us -> 40.9 us (1.020)
  starting transfers between devices: 25.2 us -> 25.7 us
    ppermute x16, starting transfers between devices: 20.9 us -> 21.4 us  [swap(): return lax.ppermute(value, axis, [(i, i ^ offset) for i in range(size)])]
    pallas_call x1 -> x2, Pallas kernels: 1.39 us -> 1.74 us  [attend(): pl.pallas_call(functools.partial(attend_kernel, parts, cores, heads_here,...]
  transfers between devices with their start and end apart: 18 -> 18, of which waited for: 5 -> 6; matrix products, arithmetic and copies ran while one was open for 0% -> 0% of each run, Pallas kernels for 18% -> 19%
where the time goes in v11:
time: 40.9 us; the launch traced here: 40.7 us
  starting transfers between devices  25.7 us (63%)
  Pallas kernels  8.82 us (22%)
  waiting for transfers between devices  6.04 us (15%)
    ppermute x16, starting transfers between devices, swap(): return lax.ppermute(value, axis, [(i, i ^ offset) for i in range(size)])  21.4 us
    ppermute x16, waiting for transfers between devices, swap(): return lax.ppermute(value, axis, [(i, i ^ offset) for i in range(size)])  6.03 us
    pallas_call x1, Pallas kernels, ffn(): pl.pallas_call(functools.partial(ffn_kernel, capacity, cores, steps), in_...  5.3 us
    ppermute x2, starting transfers between devices, route(): return lax.ppermute(value, ('clip', 'tp'), pairs)  4.32 us
    pallas_call x2, Pallas kernels, keyval(): pl.pallas_call(functools.partial(keyval_kernel, parts, len(weights)), in_...  1.77 us
    pallas_call x2, Pallas kernels, attend(): pl.pallas_call(functools.partial(attend_kernel, parts, cores, heads_here,...  1.74 us
  transfers between devices with their start and end apart: 18, of which 6 were waited for; matrix products, arithmetic and copies ran while one was open for 0% of the time, Pallas kernels for 19%

profile of v11, /device:TPU:0, one launch (start us, length us, event | category | flops | bytes accessed | tf_op | source)
XLA Modules:
  0.0 40.7 jit_solution(14862423044949641523)
XLA Ops:
  0.0 0.5 %collective-permute-start.5 = (bf16[4096,256]{1,0:T(8,128)(2,1)}, bf16[4096,256]{1,0:T(8,128)(2,1)S(1)}, u32[]{:S(2)}, u32[]{:S(2)}) collective-permute-start(bf16[4096,256]{1,0:T(8,128)(2,1)} %bitcast.11), channel_id=1, source_target_pairs={{0,1},{1,0},{2,3},{3,2},{4,5},{5,4},{6,7},{7,6},{8,9},{9,8},{10,11... | collective-permute-start | bytes 6291464 | tf_op jit(solution)/shard_map/ppermute | solution.py:24
  0.5 0.0 copy-start
  0.5 0.0 copy-start.2
  0.5 5.3 %shard_map.73 = (f32[64,1024]{1,0:T(8,128)S(1)}, f32[64,1024]{1,0:T(8,128)S(1)}, bf16[64,1024]{1,0:T(8,128)(2,1)S(1)}) custom-call(s32[4,128]{1,0:T(4,128)} %bitcast.24, bf16[128,5120]{1,0:T(8,128)(2,1)} %hidden_hbm.1, bf16[5120,1024]{1,0:T(8,128)(2,1)} %weight_hbm.1, bf16[128,1024]{1,0:T(8,128)(2,1)} %residual_hbm.1), custom_call_target="tpu_custom_call" | custom-call | flops 1509949440 | bytes 11796480 | tf_op jit(solution)/shard_map/pallas_call | solution.py:115
  5.8 0.1 collective-permute-start
  5.9 1.5 %collective-permute-done = f32[64,1024]{1,0:T(8,128)S(1)} collective-permute-done((f32[64,1024]{1,0:T(8,128)S(1)}, f32[64,1024]{1,0:T(8,128)S(1)}, u32[]{:S(2)}, u32[]{:S(2)}) %collective-permute-start) | collective-permute-done | bytes 262176 | tf_op jit(solution)/shard_map/ppermute | solution.py:24
  7.4 0.7 %collective-permute-start.8 = (bf16[32,1024]{1,0:T(8,128)(2,1)S(1)}, bf16[32,1024]{1,0:T(8,128)(2,1)S(1)}, u32[]{:S(2)}, u32[]{:S(2)}) collective-permute-start(bf16[32,1024]{1,0:T(8,128)(2,1)S(1)} %get-tuple-element.11), channel_id=1, source_target_pairs={{0,0},{1,9},{8,8},{9,1},{16,16},{17,25},{24,24},{25,17},{2,2},{3,1... | collective-permute-start | bytes 196616 | tf_op jit(solution)/shard_map/ppermute | solution.py:48
  8.1 3.7 %collective-permute-start.1 = (bf16[32,1024]{1,0:T(8,128)(2,1)S(1)}, bf16[32,1024]{1,0:T(8,128)(2,1)S(1)}, u32[]{:S(2)}, u32[]{:S(2)}) collective-permute-start(bf16[32,1024]{1,0:T(8,128)(2,1)S(1)} %get-tuple-element.12), channel_id=1, source_target_pairs={{0,24},{1,17},{8,16},{9,25},{16,8},{17,1},{24,0},{25,9},{2,26},{3,... | collective-permute-start | bytes 196616 | tf_op jit(solution)/shard_map/ppermute | solution.py:48
  11.8 0.0 collective-permute-done.8.refs_0_
  11.8 2.6 %collective-permute-start.10 = (bf16[32,1024]{1,0:T(8,128)(2,1)S(1)}, bf16[32,1024]{1,0:T(8,128)(2,1)S(1)}, u32[]{:S(2)}, u32[]{:S(2)}) collective-permute-start(bf16[32,1024]{1,0:T(8,128)(2,1)S(1)} %collective-permute-done.8.refs_0_), channel_id=1, source_target_pairs={{0,4},{2,6},{4,0},{6,2},{1,5},{3,7},{5,1},{7,3},{8,12},{10,14},{12... | collective-permute-start | bytes 196616 | tf_op jit(solution)/shard_map/ppermute | solution.py:24
  14.3 1.6 %collective-permute-start.11 = (bf16[32,1024]{1,0:T(8,128)(2,1)S(1)}, bf16[32,1024]{1,0:T(8,128)(2,1)S(1)}, u32[]{:S(2)}, u32[]{:S(2)}) collective-permute-start(bf16[32,1024]{1,0:T(8,128)(2,1)S(1)} %collective-permute-done.8.refs_0_), channel_id=1, source_target_pairs={{0,2},{2,0},{4,6},{6,4},{1,3},{3,1},{5,7},{7,5},{8,10},{10,8},{12,... | collective-permute-start | bytes 196616 | tf_op jit(solution)/shard_map/ppermute | solution.py:24
  15.9 0.2 collective-permute-start.9
  16.2 0.0 collective-permute-done.1.refs_0_
  16.2 3.6 %collective-permute-start.2 = (bf16[32,1024]{1,0:T(8,128)(2,1)S(1)}, bf16[32,1024]{1,0:T(8,128)(2,1)S(1)}, u32[]{:S(2)}, u32[]{:S(2)}) collective-permute-start(bf16[32,1024]{1,0:T(8,128)(2,1)S(1)} %collective-permute-done.1.refs_0_), channel_id=1, source_target_pairs={{0,6},{2,4},{4,2},{6,0},{1,7},{3,5},{5,3},{7,1},{8,14},{10,12},{12... | collective-permute-start | bytes 196616 | tf_op jit(solution)/shard_map/ppermute | solution.py:24
  19.8 0.0 collective-permute-done.10.refs_2_
  19.8 0.0 collective-permute-start.3
  19.8 0.0 collective-permute-done.11.refs_3_
  19.8 1.9 %collective-permute-start.4 = (bf16[32,1024]{1,0:T(8,128)(2,1)S(1)}, bf16[32,1024]{1,0:T(8,128)(2,1)S(1)}, u32[]{:S(2)}, u32[]{:S(2)}) collective-permute-start(bf16[32,1024]{1,0:T(8,128)(2,1)S(1)} %collective-permute-done.1.refs_0_), channel_id=1, source_target_pairs={{0,2},{2,0},{4,6},{6,4},{1,3},{3,1},{5,7},{7,5},{8,10},{10,8},{12,... | collective-permute-start | bytes 196616 | tf_op jit(solution)/shard_map/ppermute | solution.py:24
  21.7 0.4 collective-permute-done.9.refs_1_
  22.1 0.0 collective-permute-done.5.refs_6_
  22.1 0.0 copy-done
  22.1 0.0 copy-done.2
  22.1 0.9 %shard_map.75.refs_2_ = bf16[32,512]{1,0:T(8,128)(2,1)S(1)} custom-call(bf16[32,1024]{1,0:T(8,128)(2,1)S(1)} %collective-permute-done.8.refs_0_, bf16[32,1024]{1,0:T(8,128)(2,1)S(1)} %collective-permute-done.9.refs_1_, bf16[32,1024]{1,0:T(8,128)(2,1)S(1)} %collective-permute-done.10.refs_2_, bf16[32,1024]{1,0:T(8,128)(2,1)S(1)} %collective-permute-done.11.refs_3_, ...), custom_call_target="tpu_custom_call" | custom-call | flops 134217728 | bytes 4456448 | tf_op jit(solution)/shard_map/pallas_call | solution.py:234
  23.0 0.0 copy-start.1
  23.0 0.0 copy-start.3
  23.0 2.1 %collective-permute-start.16 = (bf16[32,512]{1,0:T(8,128)(2,1)S(1)}, bf16[32,512]{1,0:T(8,128)(2,1)S(1)}, u32[]{:S(2)}, u32[]{:S(2)}) collective-permute-start(bf16[32,512]{1,0:T(8,128)(2,1)S(1)} %shard_map.75.refs_2_), channel_id=1, source_target_pairs={{0,6},{2,4},{4,2},{6,0},{1,7},{3,5},{5,3},{7,1},{8,14},{10,12},{12... | collective-permute-start | bytes 98312 | tf_op jit(solution)/shard_map/ppermute | solution.py:24
  25.1 0.0 collective-permute-done.2.refs_1_
  25.2 1.5 %collective-permute-done.3.refs_2_ = bf16[32,1024]{1,0:T(8,128)(2,1)S(1)} collective-permute-done((bf16[32,1024]{1,0:T(8,128)(2,1)S(1)}, bf16[32,1024]{1,0:T(8,128)(2,1)S(1)}, u32[]{:S(2)}, u32[]{:S(2)}) %collective-permute-start.3) | collective-permute-done | bytes 65568 | tf_op jit(solution)/shard_map/ppermute | solution.py:24
  26.6 0.0 collective-permute-done.4.refs_3_
  26.6 0.9 %shard_map.74.refs_0_ = bf16[32,512]{1,0:T(8,128)(2,1)S(1)} custom-call(bf16[32,1024]{1,0:T(8,128)(2,1)S(1)} %collective-permute-done.1.refs_0_, bf16[32,1024]{1,0:T(8,128)(2,1)S(1)} %collective-permute-done.2.refs_1_, bf16[32,1024]{1,0:T(8,128)(2,1)S(1)} %collective-permute-done.3.refs_2_, bf16[32,1024]{1,0:T(8,128)(2,1)S(1)} %collective-permute-done.4.refs_3_, ...), custom_call_target="tpu_custom_call" | custom-call | flops 134217728 | bytes 4456448 | tf_op jit(solution)/shard_map/pallas_call | solution.py:234
  27.5 3.1 %collective-permute-start.15 = (bf16[32,512]{1,0:T(8,128)(2,1)S(1)}, bf16[32,512]{1,0:T(8,128)(2,1)S(1)}, u32[]{:S(2)}, u32[]{:S(2)}) collective-permute-start(bf16[32,512]{1,0:T(8,128)(2,1)S(1)} %shard_map.74.refs_0_), channel_id=1, source_target_pairs={{0,6},{2,4},{4,2},{6,0},{1,7},{3,5},{5,3},{7,1},{8,14},{10,12},{12... | collective-permute-start | bytes 98312 | tf_op jit(solution)/shard_map/ppermute | solution.py:24
  30.6 0.0 collective-permute-start.12
  30.6 1.3 %collective-permute-start.13 = (bf16[32,512]{1,0:T(8,128)(2,1)S(1)}, bf16[32,512]{1,0:T(8,128)(2,1)S(1)}, u32[]{:S(2)}, u32[]{:S(2)}) collective-permute-start(bf16[32,512]{1,0:T(8,128)(2,1)S(1)} %shard_map.75.refs_2_), channel_id=1, source_target_pairs={{0,2},{2,0},{4,6},{6,4},{1,3},{3,1},{5,7},{7,5},{8,10},{10,8},{12,... | collective-permute-start | bytes 98312 | tf_op jit(solution)/shard_map/ppermute | solution.py:24
  31.9 1.6 %collective-permute-start.6 = (bf16[32,512]{1,0:T(8,128)(2,1)S(1)}, bf16[32,512]{1,0:T(8,128)(2,1)S(1)}, u32[]{:S(2)}, u32[]{:S(2)}) collective-permute-start(bf16[32,512]{1,0:T(8,128)(2,1)S(1)} %shard_map.74.refs_0_), channel_id=1, source_target_pairs={{0,4},{2,6},{4,0},{6,2},{1,5},{3,7},{5,1},{7,3},{8,12},{10,14},{12... | collective-permute-start | bytes 98312 | tf_op jit(solution)/shard_map/ppermute | solution.py:24
  33.5 0.0 collective-permute-done.16.refs_3_
  33.5 2.0 %collective-permute-start.7 = (bf16[32,512]{1,0:T(8,128)(2,1)S(1)}, bf16[32,512]{1,0:T(8,128)(2,1)S(1)}, u32[]{:S(2)}, u32[]{:S(2)}) collective-permute-start(bf16[32,512]{1,0:T(8,128)(2,1)S(1)} %shard_map.74.refs_0_), channel_id=1, source_target_pairs={{0,2},{2,0},{4,6},{6,4},{1,3},{3,1},{5,7},{7,5},{8,10},{10,8},{12,... | collective-permute-start | bytes 98312 | tf_op jit(solution)/shard_map/ppermute | solution.py:24
  35.5 0.0 collective-permute-done.15.refs_1_
  35.6 0.5 %collective-permute-start.17 = (bf16[4,32,512]{2,1,0:T(8,128)(2,1)S(1)}, bf16[4,32,512]{2,1,0:T(8,128)(2,1)S(1)}, u32[]{:S(2)}, u32[]{:S(2)}) collective-permute-start(bf16[4,32,512]{2,1,0:T(8,128)(2,1)S(1)} %pad_maximum_fusion.1), channel_id=1, source_target_pairs={{0,1},{1,0},{2,3},{3,2},{4,5},{5,4},{6,7},{7,6},{8,9},{9,8},{10,11... | collective-permute-start | bytes 393224 | tf_op jit(solution)/shard_map/ppermute | solution.py:24
  36.1 0.0 collective-permute-done.12.refs_2_
  36.1 0.0 collective-permute-done.13.refs_3_
  36.1 0.6 %collective-permute-done.6.refs_0_ = bf16[32,512]{1,0:T(8,128)(2,1)S(1)} collective-permute-done((bf16[32,512]{1,0:T(8,128)(2,1)S(1)}, bf16[32,512]{1,0:T(8,128)(2,1)S(1)}, u32[]{:S(2)}, u32[]{:S(2)}) %collective-permute-start.6) | collective-permute-done | bytes 32800 | tf_op jit(solution)/shard_map/ppermute | solution.py:24
  36.7 1.3 %collective-permute-done.7.refs_1_ = bf16[32,512]{1,0:T(8,128)(2,1)S(1)} collective-permute-done((bf16[32,512]{1,0:T(8,128)(2,1)S(1)}, bf16[32,512]{1,0:T(8,128)(2,1)S(1)}, u32[]{:S(2)}, u32[]{:S(2)}) %collective-permute-start.7) | collective-permute-done | bytes 32800 | tf_op jit(solution)/shard_map/ppermute | solution.py:24
  38.1 0.2 collective-permute-start.14
  38.3 0.0 collective-permute-done.17.refs_4_
  38.3 0.0 copy-done.1
  38.3 0.0 copy-done.3
  38.3 0.5 %shard_map.76.refs_5_ = bf16[128,1024]{1,0:T(8,128)(2,1)S(1)} custom-call(s32[4,128]{1,0:T(4,128)S(1)} %bitcast.25, bf16[128,1024]{1,0:T(8,128)(2,1)S(1)} %copy-done.1, bf16[32,512]{1,0:T(8,128)(2,1)S(1)} %shard_map.74.refs_0_, bf16[32,512]{1,0:T(8,128)(2,1)S(1)} %collective-permute-done.15.refs_1_, bf16[32,512]{1,0:T(8,128)(2,1)S(1)} %shard_map.75.refs_2_, ...), custom_call_target="tpu_custom_call" | custom-call | tf_op jit(solution)/shard_map/pallas_call | solution.py:277
  38.8 0.7 %collective-permute-done.14.refs_4_ = bf16[4,32,512]{2,1,0:T(8,128)(2,1)S(1)} collective-permute-done((bf16[4,32,512]{2,1,0:T(8,128)(2,1)S(1)}, bf16[4,32,512]{2,1,0:T(8,128)(2,1)S(1)}, u32[]{:S(2)}, u32[]{:S(2)}) %collective-permute-start.14) | collective-permute-done | bytes 131104 | tf_op jit(solution)/shard_map/ppermute | solution.py:24
  39.5 1.2 %shard_map.77 = bf16[128,1024]{1,0:T(8,128)(2,1)} custom-call(s32[4,128]{1,0:T(4,128)S(1)} %bitcast.26, bf16[128,1024]{1,0:T(8,128)(2,1)S(1)} %copy-done.1, bf16[32,512]{1,0:T(8,128)(2,1)S(1)} %collective-permute-done.6.refs_0_, bf16[32,512]{1,0:T(8,128)(2,1)S(1)} %collective-permute-done.7.refs_1_, bf16[32,512]{1,0:T(8,128)(2,1)S(1)} %collective-permute-done.12.refs_2_, ...), custom_call_target="tpu_custom_call" | custom-call | tf_op jit(solution)/shard_map/pallas_call | solution.py:277
  (4 shorter events, 0.1 us)
Async XLA Ops:
  0.0 22.1 %collective-permute-start.5 = (bf16[4096,256]{1,0:T(8,128)(2,1)}, bf16[4096,256]{1,0:T(8,128)(2,1)S(1)}, u32[]{:S(2)}, u32[]{:S(2)}) collective-permute-start(bf16[4096,256]{1,0:T(8,128)(2,1)} %bitcast.11), channel_id=1, source_target_pairs={{0,1},{1,0},{2,3},{3,2},{4,5},{5,4},{6,7},{7,6},{8,9},{9,8},{10,11... | collective-permute-start | bytes 6291464 | tf_op jit(solution)/shard_map/ppermute | solution.py:24
  0.5 21.6 %copy-start = (bf16[4096,1,256]{2,0,1:T(8,128)(2,1)S(1)}, bf16[4096,1,256]{2,0,1:T(8,128)(2,1)}, u32[]{:S(2)}) copy-start(bf16[4096,1,256]{2,0,1:T(8,128)(2,1)} %param.11) | copy-start | bytes 6291460
  0.5 21.6 %copy-start.2 = (f32[4096]{0:T(1024)S(1)}, f32[4096]{0:T(1024)}, u32[]{:S(2)}) copy-start(f32[4096]{0:T(1024)} %param.10) | copy-start | bytes 49156
  5.8 1.6 %collective-permute-start = (f32[64,1024]{1,0:T(8,128)S(1)}, f32[64,1024]{1,0:T(8,128)S(1)}, u32[]{:S(2)}, u32[]{:S(2)}) collective-permute-start(f32[64,1024]{1,0:T(8,128)S(1)} %get-tuple-element.10), channel_id=1, source_target_pairs={{0,1},{1,0},{2,3},{3,2},{4,5},{5,4},{6,7},{7,6},{8,9},{9,8},{10,11... | collective-permute-start | bytes 786440 | tf_op jit(solution)/shard_map/ppermute | solution.py:24
  7.4 4.3 %collective-permute-start.8 = (bf16[32,1024]{1,0:T(8,128)(2,1)S(1)}, bf16[32,1024]{1,0:T(8,128)(2,1)S(1)}, u32[]{:S(2)}, u32[]{:S(2)}) collective-permute-start(bf16[32,1024]{1,0:T(8,128)(2,1)S(1)} %get-tuple-element.11), channel_id=1, source_target_pairs={{0,0},{1,9},{8,8},{9,1},{16,16},{17,25},{24,24},{25,17},{2,2},{3,1... | collective-permute-start | bytes 196616 | tf_op jit(solution)/shard_map/ppermute | solution.py:48
  8.1 8.0 %collective-permute-start.1 = (bf16[32,1024]{1,0:T(8,128)(2,1)S(1)}, bf16[32,1024]{1,0:T(8,128)(2,1)S(1)}, u32[]{:S(2)}, u32[]{:S(2)}) collective-permute-start(bf16[32,1024]{1,0:T(8,128)(2,1)S(1)} %get-tuple-element.12), channel_id=1, source_target_pairs={{0,24},{1,17},{8,16},{9,25},{16,8},{17,1},{24,0},{25,9},{2,26},{3,... | collective-permute-start | bytes 196616 | tf_op jit(solution)/shard_map/ppermute | solution.py:48
  11.8 8.0 %collective-permute-start.10 = (bf16[32,1024]{1,0:T(8,128)(2,1)S(1)}, bf16[32,1024]{1,0:T(8,128)(2,1)S(1)}, u32[]{:S(2)}, u32[]{:S(2)}) collective-permute-start(bf16[32,1024]{1,0:T(8,128)(2,1)S(1)} %collective-permute-done.8.refs_0_), channel_id=1, source_target_pairs={{0,4},{2,6},{4,0},{6,2},{1,5},{3,7},{5,1},{7,3},{8,12},{10,14},{12... | collective-permute-start | bytes 196616 | tf_op jit(solution)/shard_map/ppermute | solution.py:24
  14.3 5.4 %collective-permute-start.11 = (bf16[32,1024]{1,0:T(8,128)(2,1)S(1)}, bf16[32,1024]{1,0:T(8,128)(2,1)S(1)}, u32[]{:S(2)}, u32[]{:S(2)}) collective-permute-start(bf16[32,1024]{1,0:T(8,128)(2,1)S(1)} %collective-permute-done.8.refs_0_), channel_id=1, source_target_pairs={{0,2},{2,0},{4,6},{6,4},{1,3},{3,1},{5,7},{7,5},{8,10},{10,8},{12,... | collective-permute-start | bytes 196616 | tf_op jit(solution)/shard_map/ppermute | solution.py:24
  15.9 6.2 %collective-permute-start.9 = (bf16[32,1024]{1,0:T(8,128)(2,1)S(1)}, bf16[32,1024]{1,0:T(8,128)(2,1)S(1)}, u32[]{:S(2)}, u32[]{:S(2)}) collective-permute-start(bf16[32,1024]{1,0:T(8,128)(2,1)S(1)} %collective-permute-done.8.refs_0_), channel_id=1, source_target_pairs={{0,6},{2,4},{4,2},{6,0},{1,7},{3,5},{5,3},{7,1},{8,14},{10,12},{12... | collective-permute-start | bytes 196616 | tf_op jit(solution)/shard_map/ppermute | solution.py:24
  16.2 9.0 %collective-permute-start.2 = (bf16[32,1024]{1,0:T(8,128)(2,1)S(1)}, bf16[32,1024]{1,0:T(8,128)(2,1)S(1)}, u32[]{:S(2)}, u32[]{:S(2)}) collective-permute-start(bf16[32,1024]{1,0:T(8,128)(2,1)S(1)} %collective-permute-done.1.refs_0_), channel_id=1, source_target_pairs={{0,6},{2,4},{4,2},{6,0},{1,7},{3,5},{5,3},{7,1},{8,14},{10,12},{12... | collective-permute-start | bytes 196616 | tf_op jit(solution)/shard_map/ppermute | solution.py:24
  19.8 6.9 %collective-permute-start.3 = (bf16[32,1024]{1,0:T(8,128)(2,1)S(1)}, bf16[32,1024]{1,0:T(8,128)(2,1)S(1)}, u32[]{:S(2)}, u32[]{:S(2)}) collective-permute-start(bf16[32,1024]{1,0:T(8,128)(2,1)S(1)} %collective-permute-done.1.refs_0_), channel_id=1, source_target_pairs={{0,4},{2,6},{4,0},{6,2},{1,5},{3,7},{5,1},{7,3},{8,12},{10,14},{12... | collective-permute-start | bytes 196616 | tf_op jit(solution)/shard_map/ppermute | solution.py:24
  19.8 6.9 %collective-permute-start.4 = (bf16[32,1024]{1,0:T(8,128)(2,1)S(1)}, bf16[32,1024]{1,0:T(8,128)(2,1)S(1)}, u32[]{:S(2)}, u32[]{:S(2)}) collective-permute-start(bf16[32,1024]{1,0:T(8,128)(2,1)S(1)} %collective-permute-done.1.refs_0_), channel_id=1, source_target_pairs={{0,2},{2,0},{4,6},{6,4},{1,3},{3,1},{5,7},{7,5},{8,10},{10,8},{12,... | collective-permute-start | bytes 196616 | tf_op jit(solution)/shard_map/ppermute | solution.py:24
  23.0 15.3 %copy-start.1 = (bf16[128,1024]{1,0:T(8,128)(2,1)S(1)}, bf16[128,1024]{1,0:T(8,128)(2,1)}, u32[]{:S(2)}) copy-start(bf16[128,1024]{1,0:T(8,128)(2,1)} %query_ref.3) | copy-start | bytes 786436
  23.0 15.3 %copy-start.3 = (s32[512,1]{0,1:T(1,128)S(1)}, s32[512,1]{0,1:T(1,128)}, u32[]{:S(2)}) copy-start(s32[512,1]{0,1:T(1,128)} %param.12) | copy-start | bytes 6148
  23.0 10.5 %collective-permute-start.16 = (bf16[32,512]{1,0:T(8,128)(2,1)S(1)}, bf16[32,512]{1,0:T(8,128)(2,1)S(1)}, u32[]{:S(2)}, u32[]{:S(2)}) collective-permute-start(bf16[32,512]{1,0:T(8,128)(2,1)S(1)} %shard_map.75.refs_2_), channel_id=1, source_target_pairs={{0,6},{2,4},{4,2},{6,0},{1,7},{3,5},{5,3},{7,1},{8,14},{10,12},{12... | collective-permute-start | bytes 98312 | tf_op jit(solution)/shard_map/ppermute | solution.py:24
  27.5 8.0 %collective-permute-start.15 = (bf16[32,512]{1,0:T(8,128)(2,1)S(1)}, bf16[32,512]{1,0:T(8,128)(2,1)S(1)}, u32[]{:S(2)}, u32[]{:S(2)}) collective-permute-start(bf16[32,512]{1,0:T(8,128)(2,1)S(1)} %shard_map.74.refs_0_), channel_id=1, source_target_pairs={{0,6},{2,4},{4,2},{6,0},{1,7},{3,5},{5,3},{7,1},{8,14},{10,12},{12... | collective-permute-start | bytes 98312 | tf_op jit(solution)/shard_map/ppermute | solution.py:24
  30.6 5.5 %collective-permute-start.12 = (bf16[32,512]{1,0:T(8,128)(2,1)S(1)}, bf16[32,512]{1,0:T(8,128)(2,1)S(1)}, u32[]{:S(2)}, u32[]{:S(2)}) collective-permute-start(bf16[32,512]{1,0:T(8,128)(2,1)S(1)} %shard_map.75.refs_2_), channel_id=1, source_target_pairs={{0,4},{2,6},{4,0},{6,2},{1,5},{3,7},{5,1},{7,3},{8,12},{10,14},{12... | collective-permute-start | bytes 98312 | tf_op jit(solution)/shard_map/ppermute | solution.py:24
  30.6 5.5 %collective-permute-start.13 = (bf16[32,512]{1,0:T(8,128)(2,1)S(1)}, bf16[32,512]{1,0:T(8,128)(2,1)S(1)}, u32[]{:S(2)}, u32[]{:S(2)}) collective-permute-start(bf16[32,512]{1,0:T(8,128)(2,1)S(1)} %shard_map.75.refs_2_), channel_id=1, source_target_pairs={{0,2},{2,0},{4,6},{6,4},{1,3},{3,1},{5,7},{7,5},{8,10},{10,8},{12,... | collective-permute-start | bytes 98312 | tf_op jit(solution)/shard_map/ppermute | solution.py:24
  31.9 4.8 %collective-permute-start.6 = (bf16[32,512]{1,0:T(8,128)(2,1)S(1)}, bf16[32,512]{1,0:T(8,128)(2,1)S(1)}, u32[]{:S(2)}, u32[]{:S(2)}) collective-permute-start(bf16[32,512]{1,0:T(8,128)(2,1)S(1)} %shard_map.74.refs_0_), channel_id=1, source_target_pairs={{0,4},{2,6},{4,0},{6,2},{1,5},{3,7},{5,1},{7,3},{8,12},{10,14},{12... | collective-permute-start | bytes 98312 | tf_op jit(solution)/shard_map/ppermute | solution.py:24
  33.5 4.6 %collective-permute-start.7 = (bf16[32,512]{1,0:T(8,128)(2,1)S(1)}, bf16[32,512]{1,0:T(8,128)(2,1)S(1)}, u32[]{:S(2)}, u32[]{:S(2)}) collective-permute-start(bf16[32,512]{1,0:T(8,128)(2,1)S(1)} %shard_map.74.refs_0_), channel_id=1, source_target_pairs={{0,2},{2,0},{4,6},{6,4},{1,3},{3,1},{5,7},{7,5},{8,10},{10,8},{12,... | collective-permute-start | bytes 98312 | tf_op jit(solution)/shard_map/ppermute | solution.py:24
  35.6 2.7 %collective-permute-start.17 = (bf16[4,32,512]{2,1,0:T(8,128)(2,1)S(1)}, bf16[4,32,512]{2,1,0:T(8,128)(2,1)S(1)}, u32[]{:S(2)}, u32[]{:S(2)}) collective-permute-start(bf16[4,32,512]{2,1,0:T(8,128)(2,1)S(1)} %pad_maximum_fusion.1), channel_id=1, source_target_pairs={{0,1},{1,0},{2,3},{3,2},{4,5},{5,4},{6,7},{7,6},{8,9},{9,8},{10,11... | collective-permute-start | bytes 393224 | tf_op jit(solution)/shard_map/ppermute | solution.py:24
  38.1 1.4 %collective-permute-start.14 = (bf16[4,32,512]{2,1,0:T(8,128)(2,1)S(1)}, bf16[4,32,512]{2,1,0:T(8,128)(2,1)S(1)}, u32[]{:S(2)}, u32[]{:S(2)}) collective-permute-start(bf16[4,32,512]{2,1,0:T(8,128)(2,1)S(1)} %pad_maximum_fusion), channel_id=1, source_target_pairs={{0,1},{1,0},{2,3},{3,2},{4,5},{5,4},{6,7},{7,6},{8,9},{9,8},{10,11... | collective-permute-start | bytes 393224 | tf_op jit(solution)/shard_map/ppermute | solution.py:24

commit v12 on v4

--- a/solution.py
+++ b/solution.py
@@ -22,6 +22,14 @@
 def swap(value, axis, offset):
     size = lax.axis_size(axis)
     return lax.ppermute(value, axis, [(i, i ^ offset) for i in range(size)])
+
+
+def relayed(value):
+    found = {0: value}
+    for k in sorted(range(1, lax.axis_size("seq")), key=lambda k: (bin(k).count("1"), -k)):
+        low = k & -k
+        found[k] = swap(found[k ^ low], "seq", low)
+    return [found[k] for k in range(len(found))]
 
 
 def route_offsets(clips, cores):
@@ -227,7 +235,7 @@
             bytes_accessed=2 * parts * width * (rows + wide),
             transcendentals=0,
         ),
-    )(*texts, gain, *weights)
+    )(*texts, gain, *[pltpu.with_memory_space_constraint(x, pltpu.VMEM) for x in weights])
 
 
 def shards(ffn_hidden, ffn_weight, residual, norm_gain, kv_weight, destination, queries):
@@ -253,8 +261,7 @@
             for i in range(first, first + places // groups)
         ]
         arrived = jnp.concatenate(arrived, axis=0)
-        texts = [arrived] + [swap(arrived, "seq", k) for k in range(1, parts)]
-        block = keyval(texts, gain, weights)
+        block = keyval(relayed(arrived), gain, weights)
         block = [block] + [swap(block, "seq", k) for k in range(1, parts)]
         blocks += block + [swap(jnp.stack(block), "tp", g) for g in range(1, cores)]
     return pl.pallas_call(

time: 40.1 us -> 40.7 us (1.015)
  waiting for transfers between devices: 6.1 us -> 7.58 us
  starting transfers between devices: 25.2 us -> 24.3 us
    ppermute x16, waiting for transfers between devices: 6.09 us -> 7.58 us  [swap(): return lax.ppermute(value, axis, [(i, i ^ offset) for i in range(size)])]
    ppermute x16, starting transfers between devices: 20.9 us -> 20 us  [swap(): return lax.ppermute(value, axis, [(i, i ^ offset) for i in range(size)])]
  transfers between devices with their start and end apart: 18 -> 18, of which waited for: 5 -> 6; matrix products, arithmetic and copies ran while one was open for 0% -> 0% of each run, Pallas kernels for 18% -> 17%
where the time goes in v12:
time: 40.7 us; the launch traced here: 40.5 us
  starting transfers between devices  24.3 us (60%)
  Pallas kernels  8.47 us (21%)
  waiting for transfers between devices  7.58 us (19%)
    ppermute x16, starting transfers between devices, swap(): return lax.ppermute(value, axis, [(i, i ^ offset) for i in range(size)])  20 us
    ppermute x16, waiting for transfers between devices, swap(): return lax.ppermute(value, axis, [(i, i ^ offset) for i in range(size)])  7.58 us
    pallas_call x1, Pallas kernels, ffn(): pl.pallas_call(functools.partial(ffn_kernel, capacity, cores, steps), in_...  5.3 us
    ppermute x2, starting transfers between devices, route(): return lax.ppermute(value, ('clip', 'tp'), pairs)  4.32 us
    pallas_call x2, Pallas kernels, keyval(): pl.pallas_call(functools.partial(keyval_kernel, parts, len(weights)), in_...  1.78 us
    pallas_call x1, Pallas kernels, shards(): pl.pallas_call(functools.partial(attend_kernel, parts, cores, heads_here,...  1.39 us
  transfers between devices with their start and end apart: 18, of which 6 were waited for; matrix products, arithmetic and copies ran while one was open for 0% of the time, Pallas kernels for 17%

profile of v12, /device:TPU:0, one launch (start us, length us, event | category | flops | bytes accessed | tf_op | source)
XLA Modules:
  0.0 40.5 jit_solution(6833213142831191907)
XLA Ops:
  0.0 0.5 %collective-permute-start.5 = (bf16[4096,256]{1,0:T(8,128)(2,1)}, bf16[4096,256]{1,0:T(8,128)(2,1)S(1)}, u32[]{:S(2)}, u32[]{:S(2)}) collective-permute-start(bf16[4096,256]{1,0:T(8,128)(2,1)} %bitcast.11), channel_id=1, source_target_pairs={{0,1},{1,0},{2,3},{3,2},{4,5},{5,4},{6,7},{7,6},{8,9},{9,8},{10,11... | collective-permute-start | bytes 6291464 | tf_op jit(solution)/shard_map/ppermute | solution.py:24
  0.5 0.0 copy-start
  0.5 0.0 copy-start.2
  0.5 5.3 %shard_map.73 = (f32[64,1024]{1,0:T(8,128)S(1)}, f32[64,1024]{1,0:T(8,128)S(1)}, bf16[64,1024]{1,0:T(8,128)(2,1)S(1)}) custom-call(s32[4,128]{1,0:T(4,128)} %bitcast.24, bf16[128,5120]{1,0:T(8,128)(2,1)} %hidden_hbm.1, bf16[5120,1024]{1,0:T(8,128)(2,1)} %weight_hbm.1, bf16[128,1024]{1,0:T(8,128)(2,1)} %residual_hbm.1), custom_call_target="tpu_custom_call" | custom-call | flops 1509949440 | bytes 11796480 | tf_op jit(solution)/shard_map/pallas_call | solution.py:115
  5.8 0.1 collective-permute-start
  5.9 1.5 %collective-permute-done = f32[64,1024]{1,0:T(8,128)S(1)} collective-permute-done((f32[64,1024]{1,0:T(8,128)S(1)}, f32[64,1024]{1,0:T(8,128)S(1)}, u32[]{:S(2)}, u32[]{:S(2)}) %collective-permute-start) | collective-permute-done | bytes 262176 | tf_op jit(solution)/shard_map/ppermute | solution.py:24
  7.4 0.7 %collective-permute-start.1 = (bf16[32,1024]{1,0:T(8,128)(2,1)S(1)}, bf16[32,1024]{1,0:T(8,128)(2,1)S(1)}, u32[]{:S(2)}, u32[]{:S(2)}) collective-permute-start(bf16[32,1024]{1,0:T(8,128)(2,1)S(1)} %get-tuple-element.12), channel_id=1, source_target_pairs={{0,0},{1,9},{8,8},{9,1},{16,16},{17,25},{24,24},{25,17},{2,2},{3,1... | collective-permute-start | bytes 196616 | tf_op jit(solution)/shard_map/ppermute | solution.py:48
  8.1 3.7 %collective-permute-start.10 = (bf16[32,1024]{1,0:T(8,128)(2,1)S(1)}, bf16[32,1024]{1,0:T(8,128)(2,1)S(1)}, u32[]{:S(2)}, u32[]{:S(2)}) collective-permute-start(bf16[32,1024]{1,0:T(8,128)(2,1)S(1)} %get-tuple-element.11), channel_id=1, source_target_pairs={{0,24},{1,17},{8,16},{9,25},{16,8},{17,1},{24,0},{25,9},{2,26},{3,... | collective-permute-start | bytes 196616 | tf_op jit(solution)/shard_map/ppermute | solution.py:48
  11.8 0.0 collective-permute-done.1.refs_0_
  11.8 2.6 %collective-permute-start.3 = (bf16[32,1024]{1,0:T(8,128)(2,1)S(1)}, bf16[32,1024]{1,0:T(8,128)(2,1)S(1)}, u32[]{:S(2)}, u32[]{:S(2)}) collective-permute-start(bf16[32,1024]{1,0:T(8,128)(2,1)S(1)} %collective-permute-done.1.refs_0_), channel_id=1, source_target_pairs={{0,4},{2,6},{4,0},{6,2},{1,5},{3,7},{5,1},{7,3},{8,12},{10,14},{12... | collective-permute-start | bytes 196616 | tf_op jit(solution)/shard_map/ppermute | solution.py:24
  14.3 0.0 collective-permute-done.10.refs_0_
  14.3 2.8 %collective-permute-start.12 = (bf16[32,1024]{1,0:T(8,128)(2,1)S(1)}, bf16[32,1024]{1,0:T(8,128)(2,1)S(1)}, u32[]{:S(2)}, u32[]{:S(2)}) collective-permute-start(bf16[32,1024]{1,0:T(8,128)(2,1)S(1)} %collective-permute-done.10.refs_0_), channel_id=1, source_target_pairs={{0,4},{2,6},{4,0},{6,2},{1,5},{3,7},{5,1},{7,3},{8,12},{10,14},{12... | collective-permute-start | bytes 196616 | tf_op jit(solution)/shard_map/ppermute | solution.py:24
  17.2 1.6 %collective-permute-start.2 = (bf16[32,1024]{1,0:T(8,128)(2,1)S(1)}, bf16[32,1024]{1,0:T(8,128)(2,1)S(1)}, u32[]{:S(2)}, u32[]{:S(2)}) collective-permute-start(bf16[32,1024]{1,0:T(8,128)(2,1)S(1)} %collective-permute-done.1.refs_0_), channel_id=1, source_target_pairs={{0,2},{2,0},{4,6},{6,4},{1,3},{3,1},{5,7},{7,5},{8,10},{10,8},{12,... | collective-permute-start | bytes 196616 | tf_op jit(solution)/shard_map/ppermute | solution.py:24
  18.8 0.0 collective-permute-done.3.refs_2_
  18.8 0.5 %collective-permute-start.4 = (bf16[32,1024]{1,0:T(8,128)(2,1)S(1)}, bf16[32,1024]{1,0:T(8,128)(2,1)S(1)}, u32[]{:S(2)}, u32[]{:S(2)}) collective-permute-start(bf16[32,1024]{1,0:T(8,128)(2,1)S(1)} %collective-permute-done.3.refs_2_), channel_id=1, source_target_pairs={{0,2},{2,0},{4,6},{6,4},{1,3},{3,1},{5,7},{7,5},{8,10},{10,8},{12,... | collective-permute-start | bytes 196616 | tf_op jit(solution)/shard_map/ppermute | solution.py:24
  19.2 1.6 %collective-permute-start.11 = (bf16[32,1024]{1,0:T(8,128)(2,1)S(1)}, bf16[32,1024]{1,0:T(8,128)(2,1)S(1)}, u32[]{:S(2)}, u32[]{:S(2)}) collective-permute-start(bf16[32,1024]{1,0:T(8,128)(2,1)S(1)} %collective-permute-done.10.refs_0_), channel_id=1, source_target_pairs={{0,2},{2,0},{4,6},{6,4},{1,3},{3,1},{5,7},{7,5},{8,10},{10,8},{12,... | collective-permute-start | bytes 196616 | tf_op jit(solution)/shard_map/ppermute | solution.py:24
  20.8 0.3 collective-permute-done.12.refs_2_
  21.1 1.3 %collective-permute-start.13 = (bf16[32,1024]{1,0:T(8,128)(2,1)S(1)}, bf16[32,1024]{1,0:T(8,128)(2,1)S(1)}, u32[]{:S(2)}, u32[]{:S(2)}) collective-permute-start(bf16[32,1024]{1,0:T(8,128)(2,1)S(1)} %collective-permute-done.12.refs_2_), channel_id=1, source_target_pairs={{0,2},{2,0},{4,6},{6,4},{1,3},{3,1},{5,7},{7,5},{8,10},{10,8},{12,... | collective-permute-start | bytes 196616 | tf_op jit(solution)/shard_map/ppermute | solution.py:24
  22.4 0.0 collective-permute-done.2.refs_1_
  22.4 0.7 %collective-permute-done.4.refs_3_ = bf16[32,1024]{1,0:T(8,128)(2,1)S(1)} collective-permute-done((bf16[32,1024]{1,0:T(8,128)(2,1)S(1)}, bf16[32,1024]{1,0:T(8,128)(2,1)S(1)}, u32[]{:S(2)}, u32[]{:S(2)}) %collective-permute-start.4) | collective-permute-done | bytes 65568 | tf_op jit(solution)/shard_map/ppermute | solution.py:24
  23.1 0.0 collective-permute-done.5.refs_6_
  23.1 0.0 copy-done
  23.1 0.0 copy-done.2
  23.1 0.9 %shard_map.74.refs_0_ = bf16[32,512]{1,0:T(8,128)(2,1)S(1)} custom-call(bf16[32,1024]{1,0:T(8,128)(2,1)S(1)} %collective-permute-done.1.refs_0_, bf16[32,1024]{1,0:T(8,128)(2,1)S(1)} %collective-permute-done.2.refs_1_, bf16[32,1024]{1,0:T(8,128)(2,1)S(1)} %collective-permute-done.3.refs_2_, bf16[32,1024]{1,0:T(8,128)(2,1)S(1)} %collective-permute-done.4.refs_3_, ...), custom_call_target="tpu_custom_call" | custom-call | flops 134217728 | bytes 4456448 | tf_op jit(solution)/shard_map/pallas_call | solution.py:227
  24.0 0.0 copy-start.1
  24.0 0.0 copy-start.3
  24.0 3.6 %collective-permute-start.8 = (bf16[32,512]{1,0:T(8,128)(2,1)S(1)}, bf16[32,512]{1,0:T(8,128)(2,1)S(1)}, u32[]{:S(2)}, u32[]{:S(2)}) collective-permute-start(bf16[32,512]{1,0:T(8,128)(2,1)S(1)} %shard_map.74.refs_0_), channel_id=1, source_target_pairs={{0,6},{2,4},{4,2},{6,0},{1,7},{3,5},{5,3},{7,1},{8,14},{10,12},{12... | collective-permute-start | bytes 98312 | tf_op jit(solution)/shard_map/ppermute | solution.py:24
  27.6 0.0 collective-permute-start.7
  27.6 0.9 %collective-permute-start.6 = (bf16[32,512]{1,0:T(8,128)(2,1)S(1)}, bf16[32,512]{1,0:T(8,128)(2,1)S(1)}, u32[]{:S(2)}, u32[]{:S(2)}) collective-permute-start(bf16[32,512]{1,0:T(8,128)(2,1)S(1)} %shard_map.74.refs_0_), channel_id=1, source_target_pairs={{0,2},{2,0},{4,6},{6,4},{1,3},{3,1},{5,7},{7,5},{8,10},{10,8},{12,... | collective-permute-start | bytes 98312 | tf_op jit(solution)/shard_map/ppermute | solution.py:24
  28.5 0.0 collective-permute-done.11.refs_1_
  28.5 0.0 collective-permute-done.13.refs_3_
  28.5 0.9 %shard_map.75.refs_5_ = bf16[32,512]{1,0:T(8,128)(2,1)S(1)} custom-call(bf16[32,1024]{1,0:T(8,128)(2,1)S(1)} %collective-permute-done.10.refs_0_, bf16[32,1024]{1,0:T(8,128)(2,1)S(1)} %collective-permute-done.11.refs_1_, bf16[32,1024]{1,0:T(8,128)(2,1)S(1)} %collective-permute-done.12.refs_2_, bf16[32,1024]{1,0:T(8,128)(2,1)S(1)} %collective-permute-done.13.refs_3_, ...), custom_call_target="tpu_custom_call" | custom-call | flops 134217728 | bytes 4456448 | tf_op jit(solution)/shard_map/pallas_call | solution.py:227
  29.4 3.5 %collective-permute-start.16 = (bf16[32,512]{1,0:T(8,128)(2,1)S(1)}, bf16[32,512]{1,0:T(8,128)(2,1)S(1)}, u32[]{:S(2)}, u32[]{:S(2)}) collective-permute-start(bf16[32,512]{1,0:T(8,128)(2,1)S(1)} %shard_map.75.refs_5_), channel_id=1, source_target_pairs={{0,6},{2,4},{4,2},{6,0},{1,7},{3,5},{5,3},{7,1},{8,14},{10,12},{12... | collective-permute-start | bytes 98312 | tf_op jit(solution)/shard_map/ppermute | solution.py:24
  32.9 0.0 collective-permute-start.15
  32.9 0.0 collective-permute-done.8.refs_3_
  32.9 0.9 %collective-permute-start.14 = (bf16[32,512]{1,0:T(8,128)(2,1)S(1)}, bf16[32,512]{1,0:T(8,128)(2,1)S(1)}, u32[]{:S(2)}, u32[]{:S(2)}) collective-permute-start(bf16[32,512]{1,0:T(8,128)(2,1)S(1)} %shard_map.75.refs_5_), channel_id=1, source_target_pairs={{0,2},{2,0},{4,6},{6,4},{1,3},{3,1},{5,7},{7,5},{8,10},{10,8},{12,... | collective-permute-start | bytes 98312 | tf_op jit(solution)/shard_map/ppermute | solution.py:24
  33.8 0.0 collective-permute-done.7.refs_2_
  33.8 0.0 collective-permute-done.6.refs_1_
  33.8 0.1 collective-permute-start.9
  33.9 1.4 %collective-permute-done.16.refs_8_ = bf16[32,512]{1,0:T(8,128)(2,1)S(1)} collective-permute-done((bf16[32,512]{1,0:T(8,128)(2,1)S(1)}, bf16[32,512]{1,0:T(8,128)(2,1)S(1)}, u32[]{:S(2)}, u32[]{:S(2)}) %collective-permute-start.16) | collective-permute-done | bytes 32800 | tf_op jit(solution)/shard_map/ppermute | solution.py:24
  35.4 2.3 %collective-permute-done.15.refs_7_ = bf16[32,512]{1,0:T(8,128)(2,1)S(1)} collective-permute-done((bf16[32,512]{1,0:T(8,128)(2,1)S(1)}, bf16[32,512]{1,0:T(8,128)(2,1)S(1)}, u32[]{:S(2)}, u32[]{:S(2)}) %collective-permute-start.15) | collective-permute-done | bytes 32800 | tf_op jit(solution)/shard_map/ppermute | solution.py:24
  37.7 0.0 collective-permute-done.14.refs_6_
  37.7 0.1 collective-permute-start.17
  37.8 0.0 collective-permute-done.9.refs_4_
  37.8 1.3 %collective-permute-done.17.refs_9_ = bf16[4,32,512]{2,1,0:T(8,128)(2,1)S(1)} collective-permute-done((bf16[4,32,512]{2,1,0:T(8,128)(2,1)S(1)}, bf16[4,32,512]{2,1,0:T(8,128)(2,1)S(1)}, u32[]{:S(2)}, u32[]{:S(2)}) %collective-permute-start.17) | collective-permute-done | bytes 131104 | tf_op jit(solution)/shard_map/ppermute | solution.py:24
  39.1 0.0 copy-done.1
  39.1 0.0 copy-done.3
  39.1 1.4 %shard_map.76 = bf16[128,1024]{1,0:T(8,128)(2,1)} custom-call(s32[4,128]{1,0:T(4,128)S(1)} %bitcast.25, bf16[128,1024]{1,0:T(8,128)(2,1)S(1)} %copy-done.1, bf16[32,512]{1,0:T(8,128)(2,1)S(1)} %shard_map.74.refs_0_, bf16[32,512]{1,0:T(8,128)(2,1)S(1)} %collective-permute-done.6.refs_1_, bf16[32,512]{1,0:T(8,128)(2,1)S(1)} %collective-permute-done.7.refs_2_, ...), custom_call_target="tpu_custom_call" | custom-call | tf_op jit(solution)/shard_map/pallas_call | solution.py:267
  (4 shorter events, 0.1 us)
Async XLA Ops:
  0.0 23.1 %collective-permute-start.5 = (bf16[4096,256]{1,0:T(8,128)(2,1)}, bf16[4096,256]{1,0:T(8,128)(2,1)S(1)}, u32[]{:S(2)}, u32[]{:S(2)}) collective-permute-start(bf16[4096,256]{1,0:T(8,128)(2,1)} %bitcast.11), channel_id=1, source_target_pairs={{0,1},{1,0},{2,3},{3,2},{4,5},{5,4},{6,7},{7,6},{8,9},{9,8},{10,11... | collective-permute-start | bytes 6291464 | tf_op jit(solution)/shard_map/ppermute | solution.py:24
  0.5 22.7 %copy-start = (bf16[4096,1,256]{2,0,1:T(8,128)(2,1)S(1)}, bf16[4096,1,256]{2,0,1:T(8,128)(2,1)}, u32[]{:S(2)}) copy-start(bf16[4096,1,256]{2,0,1:T(8,128)(2,1)} %param.11) | copy-start | bytes 6291460
  0.5 22.7 %copy-start.2 = (f32[4096]{0:T(1024)S(1)}, f32[4096]{0:T(1024)}, u32[]{:S(2)}) copy-start(f32[4096]{0:T(1024)} %param.10) | copy-start | bytes 49156
  5.8 1.6 %collective-permute-start = (f32[64,1024]{1,0:T(8,128)S(1)}, f32[64,1024]{1,0:T(8,128)S(1)}, u32[]{:S(2)}, u32[]{:S(2)}) collective-permute-start(f32[64,1024]{1,0:T(8,128)S(1)} %get-tuple-element.10), channel_id=1, source_target_pairs={{0,1},{1,0},{2,3},{3,2},{4,5},{5,4},{6,7},{7,6},{8,9},{9,8},{10,11... | collective-permute-start | bytes 786440 | tf_op jit(solution)/shard_map/ppermute | solution.py:24
  7.4 4.3 %collective-permute-start.1 = (bf16[32,1024]{1,0:T(8,128)(2,1)S(1)}, bf16[32,1024]{1,0:T(8,128)(2,1)S(1)}, u32[]{:S(2)}, u32[]{:S(2)}) collective-permute-start(bf16[32,1024]{1,0:T(8,128)(2,1)S(1)} %get-tuple-element.12), channel_id=1, source_target_pairs={{0,0},{1,9},{8,8},{9,1},{16,16},{17,25},{24,24},{25,17},{2,2},{3,1... | collective-permute-start | bytes 196616 | tf_op jit(solution)/shard_map/ppermute | solution.py:48
  8.1 6.2 %collective-permute-start.10 = (bf16[32,1024]{1,0:T(8,128)(2,1)S(1)}, bf16[32,1024]{1,0:T(8,128)(2,1)S(1)}, u32[]{:S(2)}, u32[]{:S(2)}) collective-permute-start(bf16[32,1024]{1,0:T(8,128)(2,1)S(1)} %get-tuple-element.11), channel_id=1, source_target_pairs={{0,24},{1,17},{8,16},{9,25},{16,8},{17,1},{24,0},{25,9},{2,26},{3,... | collective-permute-start | bytes 196616 | tf_op jit(solution)/shard_map/ppermute | solution.py:48
  11.8 7.0 %collective-permute-start.3 = (bf16[32,1024]{1,0:T(8,128)(2,1)S(1)}, bf16[32,1024]{1,0:T(8,128)(2,1)S(1)}, u32[]{:S(2)}, u32[]{:S(2)}) collective-permute-start(bf16[32,1024]{1,0:T(8,128)(2,1)S(1)} %collective-permute-done.1.refs_0_), channel_id=1, source_target_pairs={{0,4},{2,6},{4,0},{6,2},{1,5},{3,7},{5,1},{7,3},{8,12},{10,14},{12... | collective-permute-start | bytes 196616 | tf_op jit(solution)/shard_map/ppermute | solution.py:24
  14.3 6.7 %collective-permute-start.12 = (bf16[32,1024]{1,0:T(8,128)(2,1)S(1)}, bf16[32,1024]{1,0:T(8,128)(2,1)S(1)}, u32[]{:S(2)}, u32[]{:S(2)}) collective-permute-start(bf16[32,1024]{1,0:T(8,128)(2,1)S(1)} %collective-permute-done.10.refs_0_), channel_id=1, source_target_pairs={{0,4},{2,6},{4,0},{6,2},{1,5},{3,7},{5,1},{7,3},{8,12},{10,14},{12... | collective-permute-start | bytes 196616 | tf_op jit(solution)/shard_map/ppermute | solution.py:24
  17.2 5.2 %collective-permute-start.2 = (bf16[32,1024]{1,0:T(8,128)(2,1)S(1)}, bf16[32,1024]{1,0:T(8,128)(2,1)S(1)}, u32[]{:S(2)}, u32[]{:S(2)}) collective-permute-start(bf16[32,1024]{1,0:T(8,128)(2,1)S(1)} %collective-permute-done.1.refs_0_), channel_id=1, source_target_pairs={{0,2},{2,0},{4,6},{6,4},{1,3},{3,1},{5,7},{7,5},{8,10},{10,8},{12,... | collective-permute-start | bytes 196616 | tf_op jit(solution)/shard_map/ppermute | solution.py:24
  18.8 4.3 %collective-permute-start.4 = (bf16[32,1024]{1,0:T(8,128)(2,1)S(1)}, bf16[32,1024]{1,0:T(8,128)(2,1)S(1)}, u32[]{:S(2)}, u32[]{:S(2)}) collective-permute-start(bf16[32,1024]{1,0:T(8,128)(2,1)S(1)} %collective-permute-done.3.refs_2_), channel_id=1, source_target_pairs={{0,2},{2,0},{4,6},{6,4},{1,3},{3,1},{5,7},{7,5},{8,10},{10,8},{12,... | collective-permute-start | bytes 196616 | tf_op jit(solution)/shard_map/ppermute | solution.py:24
  19.2 9.2 %collective-permute-start.11 = (bf16[32,1024]{1,0:T(8,128)(2,1)S(1)}, bf16[32,1024]{1,0:T(8,128)(2,1)S(1)}, u32[]{:S(2)}, u32[]{:S(2)}) collective-permute-start(bf16[32,1024]{1,0:T(8,128)(2,1)S(1)} %collective-permute-done.10.refs_0_), channel_id=1, source_target_pairs={{0,2},{2,0},{4,6},{6,4},{1,3},{3,1},{5,7},{7,5},{8,10},{10,8},{12,... | collective-permute-start | bytes 196616 | tf_op jit(solution)/shard_map/ppermute | solution.py:24
  21.1 7.4 %collective-permute-start.13 = (bf16[32,1024]{1,0:T(8,128)(2,1)S(1)}, bf16[32,1024]{1,0:T(8,128)(2,1)S(1)}, u32[]{:S(2)}, u32[]{:S(2)}) collective-permute-start(bf16[32,1024]{1,0:T(8,128)(2,1)S(1)} %collective-permute-done.12.refs_2_), channel_id=1, source_target_pairs={{0,2},{2,0},{4,6},{6,4},{1,3},{3,1},{5,7},{7,5},{8,10},{10,8},{12,... | collective-permute-start | bytes 196616 | tf_op jit(solution)/shard_map/ppermute | solution.py:24
  24.0 15.1 %copy-start.1 = (bf16[128,1024]{1,0:T(8,128)(2,1)S(1)}, bf16[128,1024]{1,0:T(8,128)(2,1)}, u32[]{:S(2)}) copy-start(bf16[128,1024]{1,0:T(8,128)(2,1)} %query_ref.1) | copy-start | bytes 786436
  24.0 15.1 %copy-start.3 = (s32[512,1]{0,1:T(1,128)S(1)}, s32[512,1]{0,1:T(1,128)}, u32[]{:S(2)}) copy-start(s32[512,1]{0,1:T(1,128)} %param.12) | copy-start | bytes 6148
  24.0 8.9 %collective-permute-start.8 = (bf16[32,512]{1,0:T(8,128)(2,1)S(1)}, bf16[32,512]{1,0:T(8,128)(2,1)S(1)}, u32[]{:S(2)}, u32[]{:S(2)}) collective-permute-start(bf16[32,512]{1,0:T(8,128)(2,1)S(1)} %shard_map.74.refs_0_), channel_id=1, source_target_pairs={{0,6},{2,4},{4,2},{6,0},{1,7},{3,5},{5,3},{7,1},{8,14},{10,12},{12... | collective-permute-start | bytes 98312 | tf_op jit(solution)/shard_map/ppermute | solution.py:24
  27.6 6.2 %collective-permute-start.7 = (bf16[32,512]{1,0:T(8,128)(2,1)S(1)}, bf16[32,512]{1,0:T(8,128)(2,1)S(1)}, u32[]{:S(2)}, u32[]{:S(2)}) collective-permute-start(bf16[32,512]{1,0:T(8,128)(2,1)S(1)} %shard_map.74.refs_0_), channel_id=1, source_target_pairs={{0,4},{2,6},{4,0},{6,2},{1,5},{3,7},{5,1},{7,3},{8,12},{10,14},{12... | collective-permute-start | bytes 98312 | tf_op jit(solution)/shard_map/ppermute | solution.py:24
  27.6 6.2 %collective-permute-start.6 = (bf16[32,512]{1,0:T(8,128)(2,1)S(1)}, bf16[32,512]{1,0:T(8,128)(2,1)S(1)}, u32[]{:S(2)}, u32[]{:S(2)}) collective-permute-start(bf16[32,512]{1,0:T(8,128)(2,1)S(1)} %shard_map.74.refs_0_), channel_id=1, source_target_pairs={{0,2},{2,0},{4,6},{6,4},{1,3},{3,1},{5,7},{7,5},{8,10},{10,8},{12,... | collective-permute-start | bytes 98312 | tf_op jit(solution)/shard_map/ppermute | solution.py:24
  29.4 6.0 %collective-permute-start.16 = (bf16[32,512]{1,0:T(8,128)(2,1)S(1)}, bf16[32,512]{1,0:T(8,128)(2,1)S(1)}, u32[]{:S(2)}, u32[]{:S(2)}) collective-permute-start(bf16[32,512]{1,0:T(8,128)(2,1)S(1)} %shard_map.75.refs_5_), channel_id=1, source_target_pairs={{0,6},{2,4},{4,2},{6,0},{1,7},{3,5},{5,3},{7,1},{8,14},{10,12},{12... | collective-permute-start | bytes 98312 | tf_op jit(solution)/shard_map/ppermute | solution.py:24
  32.9 4.8 %collective-permute-start.15 = (bf16[32,512]{1,0:T(8,128)(2,1)S(1)}, bf16[32,512]{1,0:T(8,128)(2,1)S(1)}, u32[]{:S(2)}, u32[]{:S(2)}) collective-permute-start(bf16[32,512]{1,0:T(8,128)(2,1)S(1)} %shard_map.75.refs_5_), channel_id=1, source_target_pairs={{0,4},{2,6},{4,0},{6,2},{1,5},{3,7},{5,1},{7,3},{8,12},{10,14},{12... | collective-permute-start | bytes 98312 | tf_op jit(solution)/shard_map/ppermute | solution.py:24
  32.9 4.8 %collective-permute-start.14 = (bf16[32,512]{1,0:T(8,128)(2,1)S(1)}, bf16[32,512]{1,0:T(8,128)(2,1)S(1)}, u32[]{:S(2)}, u32[]{:S(2)}) collective-permute-start(bf16[32,512]{1,0:T(8,128)(2,1)S(1)} %shard_map.75.refs_5_), channel_id=1, source_target_pairs={{0,2},{2,0},{4,6},{6,4},{1,3},{3,1},{5,7},{7,5},{8,10},{10,8},{12,... | collective-permute-start | bytes 98312 | tf_op jit(solution)/shard_map/ppermute | solution.py:24
  33.8 4.0 %collective-permute-start.9 = (bf16[4,32,512]{2,1,0:T(8,128)(2,1)S(1)}, bf16[4,32,512]{2,1,0:T(8,128)(2,1)S(1)}, u32[]{:S(2)}, u32[]{:S(2)}) collective-permute-start(bf16[4,32,512]{2,1,0:T(8,128)(2,1)S(1)} %pad_maximum_fusion), channel_id=1, source_target_pairs={{0,1},{1,0},{2,3},{3,2},{4,5},{5,4},{6,7},{7,6},{8,9},{9,8},{10,11... | collective-permute-start | bytes 393224 | tf_op jit(solution)/shard_map/ppermute | solution.py:24
  37.7 1.4 %collective-permute-start.17 = (bf16[4,32,512]{2,1,0:T(8,128)(2,1)S(1)}, bf16[4,32,512]{2,1,0:T(8,128)(2,1)S(1)}, u32[]{:S(2)}, u32[]{:S(2)}) collective-permute-start(bf16[4,32,512]{2,1,0:T(8,128)(2,1)S(1)} %pad_maximum_fusion.1), channel_id=1, source_target_pairs={{0,1},{1,0},{2,3},{3,2},{4,5},{5,4},{6,7},{7,6},{8,9},{9,8},{10,11... | collective-permute-start | bytes 393224 | tf_op jit(solution)/shard_map/ppermute | solution.py:24

commit v13 on v9

--- a/solution.py
+++ b/solution.py
@@ -22,6 +22,14 @@
 def swap(value, axis, offset):
     size = lax.axis_size(axis)
     return lax.ppermute(value, axis, [(i, i ^ offset) for i in range(size)])
+
+
+def relayed(value):
+    found = {0: value}
+    for k in sorted(range(1, lax.axis_size("seq")), key=lambda k: (bin(k).count("1"), -k)):
+        low = k & -k
+        found[k] = swap(found[k ^ low], "seq", low)
+    return [found[k] for k in range(len(found))]
 
 
 def routing(clips, cores, capacity):
@@ -31,7 +39,7 @@
             [(0, 0, half), (3, 0, half), (1, 0, capacity)],
             [(0, half, half), (3, half, half), (2, 0, capacity)],
         ]
-        return runs, [[0], [1, 2]]
+        return runs, [[0, 1], [2]]
     each = clips // cores
     runs = [[(t * each + i, 0, capacity) for i in range(each)] for t in range(cores)]
     return runs, [list(range(each))]
@@ -277,8 +285,7 @@
     texts = []
     for group in groups:
         mine = jnp.concatenate([arrived[n] for n in group], axis=0)
-        mine, texts = lax.optimization_barrier((mine, texts))
-        texts.append([mine] + [swap(mine, "seq", k) for k in range(1, parts)])
+        texts.append(relayed(mine))
     block = keyval(texts, gain, weights)
     own = [block] + [swap(block, "seq", k) for k in range(1, parts)]
     packed = jnp.stack(own)

time: 42.3 us -> 39.8 us (0.941)
  waiting for transfers between devices: 16.3 us -> 12 us
  starting transfers between devices: 18.1 us -> 19.8 us
    ppermute x12, waiting for transfers between devices: 16.3 us -> 10.6 us  [swap(): return lax.ppermute(value, axis, [(i, i ^ offset) for i in range(size)])]
    ppermute x12, starting transfers between devices: 13.9 us -> 15.6 us  [swap(): return lax.ppermute(value, axis, [(i, i ^ offset) for i in range(size)])]
    ppermute x2, waiting for transfers between devices: 0.01 us -> 1.38 us  [route(): moved = lax.ppermute(value, ('clip', 'tp'), pairs)]
where the time goes in v13:
time: 39.8 us; the launch traced here: 39.7 us
  starting transfers between devices  19.8 us (50%)
  waiting for transfers between devices  12 us (30%)
  Pallas kernels  7.69 us (19%)
    ppermute x12, starting transfers between devices, swap(): return lax.ppermute(value, axis, [(i, i ^ offset) for i in range(size)])  15.6 us
    ppermute x12, waiting for transfers between devices, swap(): return lax.ppermute(value, axis, [(i, i ^ offset) for i in range(size)])  10.6 us
    pallas_call x1, Pallas kernels, ffn(): pl.pallas_call(functools.partial(ffn_kernel, capacity, cores, edges), in_...  5.36 us
    ppermute x2, starting transfers between devices, route(): moved = lax.ppermute(value, ('clip', 'tp'), pairs)  4.19 us
    pallas_call x1, Pallas kernels, shards(): pl.pallas_call(functools.partial(attend_kernel, parts, cores, heads_here,...  1.39 us
    ppermute x2, waiting for transfers between devices, route(): moved = lax.ppermute(value, ('clip', 'tp'), pairs)  1.38 us
    pallas_call x1, Pallas kernels, keyval(): pl.pallas_call(functools.partial(keyval_kernel, parts, groups), in_specs=...  0.94 us
  transfers between devices with their start and end apart: 14, of which 8 were waited for; matrix products, arithmetic and copies ran while one was open for 0% of the time, Pallas kernels for 13%

profile of v13, /device:TPU:0, one launch (start us, length us, event | category | flops | bytes accessed | tf_op | source)
XLA Modules:
  0.0 39.7 jit_solution(1603230433804228826)
XLA Ops:
  0.0 0.5 %collective-permute-start = (bf16[4096,256]{1,0:T(8,128)(2,1)}, bf16[4096,256]{1,0:T(8,128)(2,1)S(1)}, u32[]{:S(2)}, u32[]{:S(2)}) collective-permute-start(bf16[4096,256]{1,0:T(8,128)(2,1)} %bitcast.7), channel_id=1, source_target_pairs={{0,1},{1,0},{2,3},{3,2},{4,5},{5,4},{6,7},{7,6},{8,9},{9,8},{10,11... | collective-permute-start | bytes 6291464 | tf_op jit(solution)/shard_map/ppermute | solution.py:24
  0.5 0.0 copy-start
  0.5 0.0 copy-start.2
  0.5 5.4 %shard_map.73 = (f32[64,1024]{1,0:T(8,128)S(1)}, f32[64,1024]{1,0:T(8,128)S(1)}, bf16[64,1024]{1,0:T(8,128)(2,1)S(1)}) custom-call(s32[4,128]{1,0:T(4,128)} %bitcast.14, bf16[128,5120]{1,0:T(8,128)(2,1)} %hidden_hbm.1, bf16[5120,1024]{1,0:T(8,128)(2,1)} %weight_hbm.1, bf16[128,1024]{1,0:T(8,128)(2,1)} %residual_hbm.1), custom_call_target="tpu_custom_call" | custom-call | flops 1509949440 | bytes 11796480 | tf_op jit(solution)/shard_map/pallas_call | solution.py:128
  5.8 0.1 collective-permute-start.1
  5.9 0.0 collective-permute-done.refs_10_
  6.0 1.5 %collective-permute-done.1 = f32[64,1024]{1,0:T(8,128)S(1)} collective-permute-done((f32[64,1024]{1,0:T(8,128)S(1)}, f32[64,1024]{1,0:T(8,128)S(1)}, u32[]{:S(2)}, u32[]{:S(2)}) %collective-permute-start.1) | collective-permute-done | bytes 262176 | tf_op jit(solution)/shard_map/ppermute | solution.py:24
  7.5 3.7 %collective-permute-start.2 = (bf16[16,1024]{1,0:T(8,128)(2,1)S(1)}, bf16[16,1024]{1,0:T(8,128)(2,1)S(1)}, u32[]{:S(2)}, u32[]{:S(2)}) collective-permute-start(bf16[16,1024]{1,0:T(8,128)(2,1)S(1)} %get-tuple-element.18), channel_id=1, source_target_pairs={{0,24},{1,25},{8,16},{9,17},{16,8},{17,9},{24,0},{25,1},{2,26},{3,... | collective-permute-start | bytes 98312 | tf_op jit(solution)/shard_map/ppermute | solution.py:56
  11.1 0.5 %collective-permute-start.6 = (bf16[32,1024]{1,0:T(8,128)(2,1)S(1)}, bf16[32,1024]{1,0:T(8,128)(2,1)S(1)}, u32[]{:S(2)}, u32[]{:S(2)}) collective-permute-start(bf16[32,1024]{1,0:T(8,128)(2,1)S(1)} %slice.14), channel_id=1, source_target_pairs={{0,8},{1,17},{8,0},{9,25},{16,24},{17,1},{24,16},{25,9},{2,10},{3,... | collective-permute-start | bytes 196616 | tf_op jit(solution)/shard_map/ppermute | solution.py:56
  11.7 1.4 %collective-permute-done.2 = bf16[16,1024]{1,0:T(8,128)(2,1)S(1)} collective-permute-done((bf16[16,1024]{1,0:T(8,128)(2,1)S(1)}, bf16[16,1024]{1,0:T(8,128)(2,1)S(1)}, u32[]{:S(2)}, u32[]{:S(2)}) %collective-permute-start.2) | collective-permute-done | bytes 32800 | tf_op jit(solution)/shard_map/ppermute | solution.py:56
  13.1 3.0 %collective-permute-start.4 = (bf16[32,1024]{1,0:T(8,128)(2,1)S(1)}, bf16[32,1024]{1,0:T(8,128)(2,1)S(1)}, u32[]{:S(2)}, u32[]{:S(2)}) collective-permute-start(bf16[32,1024]{1,0:T(8,128)(2,1)S(1)} %pad_maximum_fusion.1.refs_0_), channel_id=1, source_target_pairs={{0,4},{2,6},{4,0},{6,2},{1,5},{3,7},{5,1},{7,3},{8,12},{10,14},{12... | collective-permute-start | bytes 196616 | tf_op jit(solution)/shard_map/ppermute | solution.py:24
  16.1 0.0 collective-permute-done.6.refs_4_
  16.1 1.9 %collective-permute-start.8 = (bf16[32,1024]{1,0:T(8,128)(2,1)S(1)}, bf16[32,1024]{1,0:T(8,128)(2,1)S(1)}, u32[]{:S(2)}, u32[]{:S(2)}) collective-permute-start(bf16[32,1024]{1,0:T(8,128)(2,1)S(1)} %collective-permute-done.6.refs_4_), channel_id=1, source_target_pairs={{0,4},{2,6},{4,0},{6,2},{1,5},{3,7},{5,1},{7,3},{8,12},{10,14},{12... | collective-permute-start | bytes 196616 | tf_op jit(solution)/shard_map/ppermute | solution.py:24
  18.0 1.6 %collective-permute-start.3 = (bf16[32,1024]{1,0:T(8,128)(2,1)S(1)}, bf16[32,1024]{1,0:T(8,128)(2,1)S(1)}, u32[]{:S(2)}, u32[]{:S(2)}) collective-permute-start(bf16[32,1024]{1,0:T(8,128)(2,1)S(1)} %pad_maximum_fusion.1.refs_0_), channel_id=1, source_target_pairs={{0,2},{2,0},{4,6},{6,4},{1,3},{3,1},{5,7},{7,5},{8,10},{10,8},{12,... | collective-permute-start | bytes 196616 | tf_op jit(solution)/shard_map/ppermute | solution.py:24
  19.6 0.5 %collective-permute-start.7 = (bf16[32,1024]{1,0:T(8,128)(2,1)S(1)}, bf16[32,1024]{1,0:T(8,128)(2,1)S(1)}, u32[]{:S(2)}, u32[]{:S(2)}) collective-permute-start(bf16[32,1024]{1,0:T(8,128)(2,1)S(1)} %collective-permute-done.6.refs_4_), channel_id=1, source_target_pairs={{0,2},{2,0},{4,6},{6,4},{1,3},{3,1},{5,7},{7,5},{8,10},{10,8},{12,... | collective-permute-start | bytes 196616 | tf_op jit(solution)/shard_map/ppermute | solution.py:24
  20.0 0.0 collective-permute-done.4.refs_2_
  20.0 1.9 %collective-permute-start.5 = (bf16[32,1024]{1,0:T(8,128)(2,1)S(1)}, bf16[32,1024]{1,0:T(8,128)(2,1)S(1)}, u32[]{:S(2)}, u32[]{:S(2)}) collective-permute-start(bf16[32,1024]{1,0:T(8,128)(2,1)S(1)} %collective-permute-done.4.refs_2_), channel_id=1, source_target_pairs={{0,2},{2,0},{4,6},{6,4},{1,3},{3,1},{5,7},{7,5},{8,10},{10,8},{12,... | collective-permute-start | bytes 196616 | tf_op jit(solution)/shard_map/ppermute | solution.py:24
  22.0 0.0 collective-permute-done.8.refs_6_
  22.0 1.6 %collective-permute-start.9 = (bf16[32,1024]{1,0:T(8,128)(2,1)S(1)}, bf16[32,1024]{1,0:T(8,128)(2,1)S(1)}, u32[]{:S(2)}, u32[]{:S(2)}) collective-permute-start(bf16[32,1024]{1,0:T(8,128)(2,1)S(1)} %collective-permute-done.8.refs_6_), channel_id=1, source_target_pairs={{0,2},{2,0},{4,6},{6,4},{1,3},{3,1},{5,7},{7,5},{8,10},{10,8},{12,... | collective-permute-start | bytes 196616 | tf_op jit(solution)/shard_map/ppermute | solution.py:24
  23.6 0.0 collective-permute-done.3.refs_1_
  23.6 1.0 %collective-permute-done.7.refs_5_ = bf16[32,1024]{1,0:T(8,128)(2,1)S(1)} collective-permute-done((bf16[32,1024]{1,0:T(8,128)(2,1)S(1)}, bf16[32,1024]{1,0:T(8,128)(2,1)S(1)}, u32[]{:S(2)}, u32[]{:S(2)}) %collective-permute-start.7) | collective-permute-done | bytes 65568 | tf_op jit(solution)/shard_map/ppermute | solution.py:24
  24.6 1.0 %collective-permute-done.5.refs_3_ = bf16[32,1024]{1,0:T(8,128)(2,1)S(1)} collective-permute-done((bf16[32,1024]{1,0:T(8,128)(2,1)S(1)}, bf16[32,1024]{1,0:T(8,128)(2,1)S(1)}, u32[]{:S(2)}, u32[]{:S(2)}) %collective-permute-start.5) | collective-permute-done | bytes 65568 | tf_op jit(solution)/shard_map/ppermute | solution.py:24
  25.7 0.7 %collective-permute-done.9.refs_7_ = bf16[32,1024]{1,0:T(8,128)(2,1)S(1)} collective-permute-done((bf16[32,1024]{1,0:T(8,128)(2,1)S(1)}, bf16[32,1024]{1,0:T(8,128)(2,1)S(1)}, u32[]{:S(2)}, u32[]{:S(2)}) %collective-permute-start.9) | collective-permute-done | bytes 65568 | tf_op jit(solution)/shard_map/ppermute | solution.py:24
  26.4 0.0 copy-done
  26.4 0.0 copy-done.2
  26.4 0.0 copy-start.1
  26.4 0.0 copy-start.3
  26.4 0.9 %shard_map.74.refs_0_ = bf16[64,512]{1,0:T(8,128)(2,1)S(1)} custom-call(bf16[32,1024]{1,0:T(8,128)(2,1)S(1)} %pad_maximum_fusion.1.refs_0_, bf16[32,1024]{1,0:T(8,128)(2,1)S(1)} %collective-permute-done.3.refs_1_, bf16[32,1024]{1,0:T(8,128)(2,1)S(1)} %collective-permute-done.4.refs_2_, bf16[32,1024]{1,0:T(8,128)(2,1)S(1)} %collective-permute-done.5.refs_3_, ...), custom_call_target="tpu_custom_call" | custom-call | flops 268435456 | bytes 4718592 | tf_op jit(solution)/shard_map/pallas_call | solution.py:246
  27.3 3.6 %collective-permute-start.12 = (bf16[64,512]{1,0:T(8,128)(2,1)S(1)}, bf16[64,512]{1,0:T(8,128)(2,1)S(1)}, u32[]{:S(2)}, u32[]{:S(2)}) collective-permute-start(bf16[64,512]{1,0:T(8,128)(2,1)S(1)} %shard_map.74.refs_0_), channel_id=1, source_target_pairs={{0,6},{2,4},{4,2},{6,0},{1,7},{3,5},{5,3},{7,1},{8,14},{10,12},{12... | collective-permute-start | bytes 196616 | tf_op jit(solution)/shard_map/ppermute | solution.py:24
  30.9 0.0 collective-permute-start.11
  30.9 0.8 %collective-permute-start.10 = (bf16[64,512]{1,0:T(8,128)(2,1)S(1)}, bf16[64,512]{1,0:T(8,128)(2,1)S(1)}, u32[]{:S(2)}, u32[]{:S(2)}) collective-permute-start(bf16[64,512]{1,0:T(8,128)(2,1)S(1)} %shard_map.74.refs_0_), channel_id=1, source_target_pairs={{0,2},{2,0},{4,6},{6,4},{1,3},{3,1},{5,7},{7,5},{8,10},{10,8},{12,... | collective-permute-start | bytes 196616 | tf_op jit(solution)/shard_map/ppermute | solution.py:24
  31.8 1.8 %collective-permute-done.12.refs_3_ = bf16[64,512]{1,0:T(8,128)(2,1)S(1)} collective-permute-done((bf16[64,512]{1,0:T(8,128)(2,1)S(1)}, bf16[64,512]{1,0:T(8,128)(2,1)S(1)}, u32[]{:S(2)}, u32[]{:S(2)}) %collective-permute-start.12) | collective-permute-done | bytes 65568 | tf_op jit(solution)/shard_map/ppermute | solution.py:24
  33.5 3.1 %collective-permute-done.11.refs_2_ = bf16[64,512]{1,0:T(8,128)(2,1)S(1)} collective-permute-done((bf16[64,512]{1,0:T(8,128)(2,1)S(1)}, bf16[64,512]{1,0:T(8,128)(2,1)S(1)}, u32[]{:S(2)}, u32[]{:S(2)}) %collective-permute-start.11) | collective-permute-done | bytes 65568 | tf_op jit(solution)/shard_map/ppermute | solution.py:24
  36.7 0.0 collective-permute-done.10.refs_1_
  36.7 0.1 collective-permute-start.13
  36.8 1.5 %collective-permute-done.13.refs_4_ = bf16[4,64,512]{2,1,0:T(8,128)(2,1)S(1)} collective-permute-done((bf16[4,64,512]{2,1,0:T(8,128)(2,1)S(1)}, bf16[4,64,512]{2,1,0:T(8,128)(2,1)S(1)}, u32[]{:S(2)}, u32[]{:S(2)}) %collective-permute-start.13) | collective-permute-done | bytes 262176 | tf_op jit(solution)/shard_map/ppermute | solution.py:24
  38.3 0.0 copy-done.1
  38.3 0.0 copy-done.3
  38.3 1.4 %shard_map.75 = bf16[128,1024]{1,0:T(8,128)(2,1)} custom-call(s32[4,128]{1,0:T(4,128)S(1)} %bitcast.15, bf16[128,1024]{1,0:T(8,128)(2,1)S(1)} %copy-done.1, bf16[64,512]{1,0:T(8,128)(2,1)S(1)} %shard_map.74.refs_0_, bf16[64,512]{1,0:T(8,128)(2,1)S(1)} %collective-permute-done.10.refs_1_, bf16[64,512]{1,0:T(8,128)(2,1)S(1)} %collective-permute-done.11.refs_2_, ...), custom_call_target="tpu_custom_call" | custom-call | tf_op jit(solution)/shard_map/pallas_call | solution.py:293
  (5 shorter events, 0.1 us)
Async XLA Ops:
  0.0 6.0 %collective-permute-start = (bf16[4096,256]{1,0:T(8,128)(2,1)}, bf16[4096,256]{1,0:T(8,128)(2,1)S(1)}, u32[]{:S(2)}, u32[]{:S(2)}) collective-permute-start(bf16[4096,256]{1,0:T(8,128)(2,1)} %bitcast.7), channel_id=1, source_target_pairs={{0,1},{1,0},{2,3},{3,2},{4,5},{5,4},{6,7},{7,6},{8,9},{9,8},{10,11... | collective-permute-start | bytes 6291464 | tf_op jit(solution)/shard_map/ppermute | solution.py:24
  0.5 25.9 %copy-start = (bf16[4096,1,256]{2,0,1:T(8,128)(2,1)S(1)}, bf16[4096,1,256]{2,0,1:T(8,128)(2,1)}, u32[]{:S(2)}) copy-start(bf16[4096,1,256]{2,0,1:T(8,128)(2,1)} %param.11) | copy-start | bytes 6291460
  0.5 25.9 %copy-start.2 = (f32[4096]{0:T(1024)S(1)}, f32[4096]{0:T(1024)}, u32[]{:S(2)}) copy-start(f32[4096]{0:T(1024)} %param.10) | copy-start | bytes 49156
  5.8 1.6 %collective-permute-start.1 = (f32[64,1024]{1,0:T(8,128)S(1)}, f32[64,1024]{1,0:T(8,128)S(1)}, u32[]{:S(2)}, u32[]{:S(2)}) collective-permute-start(f32[64,1024]{1,0:T(8,128)S(1)} %get-tuple-element.14), channel_id=1, source_target_pairs={{0,1},{1,0},{2,3},{3,2},{4,5},{5,4},{6,7},{7,6},{8,9},{9,8},{10,11... | collective-permute-start | bytes 786440 | tf_op jit(solution)/shard_map/ppermute | solution.py:24
  7.5 5.6 %collective-permute-start.2 = (bf16[16,1024]{1,0:T(8,128)(2,1)S(1)}, bf16[16,1024]{1,0:T(8,128)(2,1)S(1)}, u32[]{:S(2)}, u32[]{:S(2)}) collective-permute-start(bf16[16,1024]{1,0:T(8,128)(2,1)S(1)} %get-tuple-element.18), channel_id=1, source_target_pairs={{0,24},{1,25},{8,16},{9,17},{16,8},{17,9},{24,0},{25,1},{2,26},{3,... | collective-permute-start | bytes 98312 | tf_op jit(solution)/shard_map/ppermute | solution.py:56
  11.1 5.0 %collective-permute-start.6 = (bf16[32,1024]{1,0:T(8,128)(2,1)S(1)}, bf16[32,1024]{1,0:T(8,128)(2,1)S(1)}, u32[]{:S(2)}, u32[]{:S(2)}) collective-permute-start(bf16[32,1024]{1,0:T(8,128)(2,1)S(1)} %slice.14), channel_id=1, source_target_pairs={{0,8},{1,17},{8,0},{9,25},{16,24},{17,1},{24,16},{25,9},{2,10},{3,... | collective-permute-start | bytes 196616 | tf_op jit(solution)/shard_map/ppermute | solution.py:56
  13.1 7.0 %collective-permute-start.4 = (bf16[32,1024]{1,0:T(8,128)(2,1)S(1)}, bf16[32,1024]{1,0:T(8,128)(2,1)S(1)}, u32[]{:S(2)}, u32[]{:S(2)}) collective-permute-start(bf16[32,1024]{1,0:T(8,128)(2,1)S(1)} %pad_maximum_fusion.1.refs_0_), channel_id=1, source_target_pairs={{0,4},{2,6},{4,0},{6,2},{1,5},{3,7},{5,1},{7,3},{8,12},{10,14},{12... | collective-permute-start | bytes 196616 | tf_op jit(solution)/shard_map/ppermute | solution.py:24
  16.1 5.9 %collective-permute-start.8 = (bf16[32,1024]{1,0:T(8,128)(2,1)S(1)}, bf16[32,1024]{1,0:T(8,128)(2,1)S(1)}, u32[]{:S(2)}, u32[]{:S(2)}) collective-permute-start(bf16[32,1024]{1,0:T(8,128)(2,1)S(1)} %collective-permute-done.6.refs_4_), channel_id=1, source_target_pairs={{0,4},{2,6},{4,0},{6,2},{1,5},{3,7},{5,1},{7,3},{8,12},{10,14},{12... | collective-permute-start | bytes 196616 | tf_op jit(solution)/shard_map/ppermute | solution.py:24
  18.0 5.6 %collective-permute-start.3 = (bf16[32,1024]{1,0:T(8,128)(2,1)S(1)}, bf16[32,1024]{1,0:T(8,128)(2,1)S(1)}, u32[]{:S(2)}, u32[]{:S(2)}) collective-permute-start(bf16[32,1024]{1,0:T(8,128)(2,1)S(1)} %pad_maximum_fusion.1.refs_0_), channel_id=1, source_target_pairs={{0,2},{2,0},{4,6},{6,4},{1,3},{3,1},{5,7},{7,5},{8,10},{10,8},{12,... | collective-permute-start | bytes 196616 | tf_op jit(solution)/shard_map/ppermute | solution.py:24
  19.6 5.0 %collective-permute-start.7 = (bf16[32,1024]{1,0:T(8,128)(2,1)S(1)}, bf16[32,1024]{1,0:T(8,128)(2,1)S(1)}, u32[]{:S(2)}, u32[]{:S(2)}) collective-permute-start(bf16[32,1024]{1,0:T(8,128)(2,1)S(1)} %collective-permute-done.6.refs_4_), channel_id=1, source_target_pairs={{0,2},{2,0},{4,6},{6,4},{1,3},{3,1},{5,7},{7,5},{8,10},{10,8},{12,... | collective-permute-start | bytes 196616 | tf_op jit(solution)/shard_map/ppermute | solution.py:24
  20.0 5.6 %collective-permute-start.5 = (bf16[32,1024]{1,0:T(8,128)(2,1)S(1)}, bf16[32,1024]{1,0:T(8,128)(2,1)S(1)}, u32[]{:S(2)}, u32[]{:S(2)}) collective-permute-start(bf16[32,1024]{1,0:T(8,128)(2,1)S(1)} %collective-permute-done.4.refs_2_), channel_id=1, source_target_pairs={{0,2},{2,0},{4,6},{6,4},{1,3},{3,1},{5,7},{7,5},{8,10},{10,8},{12,... | collective-permute-start | bytes 196616 | tf_op jit(solution)/shard_map/ppermute | solution.py:24
  22.0 4.4 %collective-permute-start.9 = (bf16[32,1024]{1,0:T(8,128)(2,1)S(1)}, bf16[32,1024]{1,0:T(8,128)(2,1)S(1)}, u32[]{:S(2)}, u32[]{:S(2)}) collective-permute-start(bf16[32,1024]{1,0:T(8,128)(2,1)S(1)} %collective-permute-done.8.refs_6_), channel_id=1, source_target_pairs={{0,2},{2,0},{4,6},{6,4},{1,3},{3,1},{5,7},{7,5},{8,10},{10,8},{12,... | collective-permute-start | bytes 196616 | tf_op jit(solution)/shard_map/ppermute | solution.py:24
  26.4 11.9 %copy-start.1 = (bf16[128,1024]{1,0:T(8,128)(2,1)S(1)}, bf16[128,1024]{1,0:T(8,128)(2,1)}, u32[]{:S(2)}) copy-start(bf16[128,1024]{1,0:T(8,128)(2,1)} %query_ref.1) | copy-start | bytes 786436
  26.4 11.9 %copy-start.3 = (s32[512,1]{0,1:T(1,128)S(1)}, s32[512,1]{0,1:T(1,128)}, u32[]{:S(2)}) copy-start(s32[512,1]{0,1:T(1,128)} %param.12) | copy-start | bytes 6148
  27.3 6.2 %collective-permute-start.12 = (bf16[64,512]{1,0:T(8,128)(2,1)S(1)}, bf16[64,512]{1,0:T(8,128)(2,1)S(1)}, u32[]{:S(2)}, u32[]{:S(2)}) collective-permute-start(bf16[64,512]{1,0:T(8,128)(2,1)S(1)} %shard_map.74.refs_0_), channel_id=1, source_target_pairs={{0,6},{2,4},{4,2},{6,0},{1,7},{3,5},{5,3},{7,1},{8,14},{10,12},{12... | collective-permute-start | bytes 196616 | tf_op jit(solution)/shard_map/ppermute | solution.py:24
  30.9 5.7 %collective-permute-start.11 = (bf16[64,512]{1,0:T(8,128)(2,1)S(1)}, bf16[64,512]{1,0:T(8,128)(2,1)S(1)}, u32[]{:S(2)}, u32[]{:S(2)}) collective-permute-start(bf16[64,512]{1,0:T(8,128)(2,1)S(1)} %shard_map.74.refs_0_), channel_id=1, source_target_pairs={{0,4},{2,6},{4,0},{6,2},{1,5},{3,7},{5,1},{7,3},{8,12},{10,14},{12... | collective-permute-start | bytes 196616 | tf_op jit(solution)/shard_map/ppermute | solution.py:24
  30.9 5.7 %collective-permute-start.10 = (bf16[64,512]{1,0:T(8,128)(2,1)S(1)}, bf16[64,512]{1,0:T(8,128)(2,1)S(1)}, u32[]{:S(2)}, u32[]{:S(2)}) collective-permute-start(bf16[64,512]{1,0:T(8,128)(2,1)S(1)} %shard_map.74.refs_0_), channel_id=1, source_target_pairs={{0,2},{2,0},{4,6},{6,4},{1,3},{3,1},{5,7},{7,5},{8,10},{10,8},{12,... | collective-permute-start | bytes 196616 | tf_op jit(solution)/shard_map/ppermute | solution.py:24
  36.7 1.6 %collective-permute-start.13 = (bf16[4,64,512]{2,1,0:T(8,128)(2,1)S(1)}, bf16[4,64,512]{2,1,0:T(8,128)(2,1)S(1)}, u32[]{:S(2)}, u32[]{:S(2)}) collective-permute-start(bf16[4,64,512]{2,1,0:T(8,128)(2,1)S(1)} %pad_maximum_fusion), channel_id=1, source_target_pairs={{0,1},{1,0},{2,3},{3,2},{4,5},{5,4},{6,7},{7,6},{8,9},{9,8},{10,11... | collective-permute-start | bytes 786440 | tf_op jit(solution)/shard_map/ppermute | solution.py:24

commit v14 on v13

--- a/solution.py
+++ b/solution.py
@@ -34,12 +34,8 @@
 
 def routing(clips, cores, capacity):
     if clips == 4 and cores == 2:
-        half = capacity // 2
-        runs = [
-            [(0, 0, half), (3, 0, half), (1, 0, capacity)],
-            [(0, half, half), (3, half, half), (2, 0, capacity)],
-        ]
-        return runs, [[0, 1], [2]]
+        runs = [[(1, 0, capacity), (0, 0, capacity)], [(2, 0, capacity), (3, 0, capacity)]]
+        return runs, [[0], [1]]
     each = clips // cores
     runs = [[(t * each + i, 0, capacity) for i in range(each)] for t in range(cores)]
     return runs, [list(range(each))]
@@ -124,7 +120,7 @@
     slots = dest.shape[0] * capacity
     share = slots // cores
     unit = depth // 20
-    edges = [0, 5 * unit, 10 * unit, 15 * unit, 19 * unit, depth] if unit % 128 == 0 else [0, depth]
+    edges = [0, 6 * unit, 12 * unit, 18 * unit, depth] if unit % 128 == 0 else [0, depth]
     return pl.pallas_call(
         functools.partial(ffn_kernel, capacity, cores, edges),
         in_specs=[pl.BlockSpec(memory_space=pltpu.HBM)] * 4,
@@ -278,9 +274,11 @@
     text = (text.astype(F32) + own).astype(BF16)
     runs, groups = routing(clips, cores, capacity)
     edges = [sum(run[2] for run in runs[0][:n]) for n in range(len(runs[0]) + 1)]
+    pieces = lax.optimization_barrier(
+        [text[edges[n]:edges[n + 1]] for n in range(len(runs[0]))]
+    )
     arrived = [
-        route(text[edges[n]:edges[n + 1]], [some[n][0] for some in runs])
-        for n in range(len(runs[0]))
+        route(piece, [some[n][0] for some in runs]) for n, piece in enumerate(pieces)
     ]
     texts = []
     for group in groups:

time: 39.8 us -> 42.3 us (1.063)
  starting transfers between devices: 19.8 us -> 16.7 us
  local copies, waits for them, and re-layouts: 0.03 us -> 2.95 us
  waiting for transfers between devices: 12 us -> 14.6 us
    unnamed x8 -> x12, local copies, waits for them, and re-layouts: 0.01 us -> 2.94 us
    ppermute x12, starting transfers between devices: 15.6 us -> 13.2 us  [swap(): return lax.ppermute(value, axis, [(i, i ^ offset) for i in range(size)])]
    ppermute x12, waiting for transfers between devices: 10.6 us -> 13 us  [swap(): return lax.ppermute(value, axis, [(i, i ^ offset) for i in range(size)])]
    ppermute x2, starting transfers between devices: 4.19 us -> 3.51 us  [route(): moved = lax.ppermute(value, ('clip', 'tp'), pairs)]
  transfers between devices with their start and end apart: 14 -> 14, of which waited for: 8 -> 11; matrix products, arithmetic and copies ran while one was open for 0% -> 0% of each run, Pallas kernels for 13% -> 13%
where the time goes in v14:
time: 42.3 us; the launch traced here: 42.1 us
  starting transfers between devices  16.7 us (39%)
  waiting for transfers between devices  14.6 us (35%)
  Pallas kernels  7.66 us (18%)
  local copies, waits for them, and re-layouts  2.95 us (7%)
    ppermute x12, starting transfers between devices, swap(): return lax.ppermute(value, axis, [(i, i ^ offset) for i in range(size)])  13.2 us
    ppermute x12, waiting for transfers between devices, swap(): return lax.ppermute(value, axis, [(i, i ^ offset) for i in range(size)])  13 us
    pallas_call x1, Pallas kernels, ffn(): pl.pallas_call(functools.partial(ffn_kernel, capacity, cores, edges), in_...  5.33 us
    ppermute x2, starting transfers between devices, route(): moved = lax.ppermute(value, ('clip', 'tp'), pairs)  3.51 us
    unnamed x12, local copies, waits for them, and re-layouts  2.94 us
    ppermute x2, waiting for transfers between devices, route(): moved = lax.ppermute(value, ('clip', 'tp'), pairs)  1.58 us
    pallas_call x1, Pallas kernels, shards(): pl.pallas_call(functools.partial(attend_kernel, parts, cores, heads_here,...  1.39 us
    pallas_call x1, Pallas kernels, keyval(): pl.pallas_call(functools.partial(keyval_kernel, parts, groups), in_specs=...  0.94 us
  transfers between devices with their start and end apart: 14, of which 11 were waited for; matrix products, arithmetic and copies ran while one was open for 0% of the time, Pallas kernels for 13%

profile of v14, /device:TPU:0, one launch (start us, length us, event | category | flops | bytes accessed | tf_op | source)
XLA Modules:
  0.0 42.1 jit_solution(802457326153345256)
XLA Ops:
  0.0 0.5 %collective-permute-start = (bf16[4096,256]{1,0:T(8,128)(2,1)}, bf16[4096,256]{1,0:T(8,128)(2,1)S(1)}, u32[]{:S(2)}, u32[]{:S(2)}) collective-permute-start(bf16[4096,256]{1,0:T(8,128)(2,1)} %bitcast.7), channel_id=1, source_target_pairs={{0,1},{1,0},{2,3},{3,2},{4,5},{5,4},{6,7},{7,6},{8,9},{9,8},{10,11... | collective-permute-start | bytes 6291464 | tf_op jit(solution)/shard_map/ppermute | solution.py:24
  0.5 0.0 copy-start
  0.5 0.0 copy-start.4
  0.5 5.3 %shard_map.73 = (f32[64,1024]{1,0:T(8,128)S(1)}, f32[64,1024]{1,0:T(8,128)S(1)}, bf16[64,1024]{1,0:T(8,128)(2,1)S(1)}) custom-call(s32[4,128]{1,0:T(4,128)} %bitcast.14, bf16[128,5120]{1,0:T(8,128)(2,1)} %hidden_hbm.1, bf16[5120,1024]{1,0:T(8,128)(2,1)} %weight_hbm.1, bf16[128,1024]{1,0:T(8,128)(2,1)} %residual_hbm.1), custom_call_target="tpu_custom_call" | custom-call | flops 1509949440 | bytes 11796480 | tf_op jit(solution)/shard_map/pallas_call | solution.py:124
  5.8 0.1 collective-permute-start.1
  5.9 0.0 collective-permute-done.refs_10_
  5.9 0.0 copy-start.1
  5.9 1.3 %copy-done.1 = bf16[4096,256]{1,0:T(8,128)(2,1)} copy-done((bf16[4096,256]{1,0:T(8,128)(2,1)}, bf16[4096,256]{1,0:T(8,128)(2,1)S(1)}, u32[]{:S(2)}) %copy-start.1) | copy-done | bytes 2097176
  7.3 0.1 collective-permute-done.1
  7.5 2.9 %collective-permute-start.2 = (bf16[32,1024]{1,0:T(8,128)(2,1)S(1)}, bf16[32,1024]{1,0:T(8,128)(2,1)S(1)}, u32[]{:S(2)}, u32[]{:S(2)}) collective-permute-start(bf16[32,1024]{1,0:T(8,128)(2,1)S(1)} %get-tuple-element.17), channel_id=1, source_target_pairs={{0,8},{1,17},{8,0},{9,25},{16,24},{17,1},{24,16},{25,9},{2,10},{3,... | collective-permute-start | bytes 196616 | tf_op jit(solution)/shard_map/ppermute | solution.py:52
  10.3 0.7 %collective-permute-start.6 = (bf16[32,1024]{1,0:T(8,128)(2,1)S(1)}, bf16[32,1024]{1,0:T(8,128)(2,1)S(1)}, u32[]{:S(2)}, u32[]{:S(2)}) collective-permute-start(bf16[32,1024]{1,0:T(8,128)(2,1)S(1)} %get-tuple-element.18), channel_id=1, source_target_pairs={{1,25},{9,17},{17,9},{25,1},{3,27},{11,19},{19,11},{27,3},{5,29},{... | collective-permute-start | bytes 196616 | tf_op jit(solution)/shard_map/ppermute | solution.py:52
  11.0 1.6 %collective-permute-done.2.refs_0_ = bf16[32,1024]{1,0:T(8,128)(2,1)S(1)} collective-permute-done((bf16[32,1024]{1,0:T(8,128)(2,1)S(1)}, bf16[32,1024]{1,0:T(8,128)(2,1)S(1)}, u32[]{:S(2)}, u32[]{:S(2)}) %collective-permute-start.2) | collective-permute-done | bytes 65568 | tf_op jit(solution)/shard_map/ppermute | solution.py:52
  12.6 3.1 %collective-permute-start.4 = (bf16[32,1024]{1,0:T(8,128)(2,1)S(1)}, bf16[32,1024]{1,0:T(8,128)(2,1)S(1)}, u32[]{:S(2)}, u32[]{:S(2)}) collective-permute-start(bf16[32,1024]{1,0:T(8,128)(2,1)S(1)} %collective-permute-done.2.refs_0_), channel_id=1, source_target_pairs={{0,4},{2,6},{4,0},{6,2},{1,5},{3,7},{5,1},{7,3},{8,12},{10,14},{12... | collective-permute-start | bytes 196616 | tf_op jit(solution)/shard_map/ppermute | solution.py:24
  15.7 0.0 collective-permute-done.6
  15.7 0.1 collective-permute-start.8
  15.8 1.9 %collective-permute-start.7 = (bf16[32,1024]{1,0:T(8,128)(2,1)S(1)}, bf16[32,1024]{1,0:T(8,128)(2,1)S(1)}, u32[]{:S(2)}, u32[]{:S(2)}) collective-permute-start(bf16[32,1024]{1,0:T(8,128)(2,1)S(1)} %broadcast_select_fusion.refs_4_), channel_id=1, source_target_pairs={{0,2},{2,0},{4,6},{6,4},{1,3},{3,1},{5,7},{7,5},{8,10},{10,8},{12,... | collective-permute-start | bytes 196616 | tf_op jit(solution)/shard_map/ppermute | solution.py:24
  17.7 0.2 collective-permute-start.3
  17.9 1.9 %collective-permute-done.4.refs_2_ = bf16[32,1024]{1,0:T(8,128)(2,1)S(1)} collective-permute-done((bf16[32,1024]{1,0:T(8,128)(2,1)S(1)}, bf16[32,1024]{1,0:T(8,128)(2,1)S(1)}, u32[]{:S(2)}, u32[]{:S(2)}) %collective-permute-start.4) | collective-permute-done | bytes 65568 | tf_op jit(solution)/shard_map/ppermute | solution.py:24
  19.8 1.8 %collective-permute-start.5 = (bf16[32,1024]{1,0:T(8,128)(2,1)S(1)}, bf16[32,1024]{1,0:T(8,128)(2,1)S(1)}, u32[]{:S(2)}, u32[]{:S(2)}) collective-permute-start(bf16[32,1024]{1,0:T(8,128)(2,1)S(1)} %collective-permute-done.4.refs_2_), channel_id=1, source_target_pairs={{0,2},{2,0},{4,6},{6,4},{1,3},{3,1},{5,7},{7,5},{8,10},{10,8},{12,... | collective-permute-start | bytes 196616 | tf_op jit(solution)/shard_map/ppermute | solution.py:24
  21.6 0.9 %collective-permute-done.8.refs_6_ = bf16[32,1024]{1,0:T(8,128)(2,1)S(1)} collective-permute-done((bf16[32,1024]{1,0:T(8,128)(2,1)S(1)}, bf16[32,1024]{1,0:T(8,128)(2,1)S(1)}, u32[]{:S(2)}, u32[]{:S(2)}) %collective-permute-start.8) | collective-permute-done | bytes 65568 | tf_op jit(solution)/shard_map/ppermute | solution.py:24
  22.5 0.7 %collective-permute-start.9 = (bf16[32,1024]{1,0:T(8,128)(2,1)S(1)}, bf16[32,1024]{1,0:T(8,128)(2,1)S(1)}, u32[]{:S(2)}, u32[]{:S(2)}) collective-permute-start(bf16[32,1024]{1,0:T(8,128)(2,1)S(1)} %collective-permute-done.8.refs_6_), channel_id=1, source_target_pairs={{0,2},{2,0},{4,6},{6,4},{1,3},{3,1},{5,7},{7,5},{8,10},{10,8},{12,... | collective-permute-start | bytes 196616 | tf_op jit(solution)/shard_map/ppermute | solution.py:24
  23.2 0.3 collective-permute-done.3.refs_1_
  23.5 0.0 collective-permute-done.7.refs_5_
  23.5 1.4 %collective-permute-done.5.refs_3_ = bf16[32,1024]{1,0:T(8,128)(2,1)S(1)} collective-permute-done((bf16[32,1024]{1,0:T(8,128)(2,1)S(1)}, bf16[32,1024]{1,0:T(8,128)(2,1)S(1)}, u32[]{:S(2)}, u32[]{:S(2)}) %collective-permute-start.5) | collective-permute-done | bytes 65568 | tf_op jit(solution)/shard_map/ppermute | solution.py:24
  24.9 1.9 %collective-permute-done.9.refs_7_ = bf16[32,1024]{1,0:T(8,128)(2,1)S(1)} collective-permute-done((bf16[32,1024]{1,0:T(8,128)(2,1)S(1)}, bf16[32,1024]{1,0:T(8,128)(2,1)S(1)}, u32[]{:S(2)}, u32[]{:S(2)}) %collective-permute-start.9) | collective-permute-done | bytes 65568 | tf_op jit(solution)/shard_map/ppermute | solution.py:24
  26.8 0.0 copy-done
  26.8 0.0 copy-done.4
  26.8 0.0 copy-start.2
  26.8 1.6 %copy-done.2 = bf16[4096,256]{1,0:T(8,128)(2,1)S(1)} copy-done((bf16[4096,256]{1,0:T(8,128)(2,1)S(1)}, bf16[4096,256]{1,0:T(8,128)(2,1)}, u32[]{:S(2)}) %copy-start.2) | copy-done | bytes 2097176
  28.4 0.0 copy-start.3
  28.4 0.0 copy-start.5
  28.4 0.9 %shard_map.74.refs_0_ = bf16[64,512]{1,0:T(8,128)(2,1)S(1)} custom-call(bf16[32,1024]{1,0:T(8,128)(2,1)S(1)} %collective-permute-done.2.refs_0_, bf16[32,1024]{1,0:T(8,128)(2,1)S(1)} %collective-permute-done.3.refs_1_, bf16[32,1024]{1,0:T(8,128)(2,1)S(1)} %collective-permute-done.4.refs_2_, bf16[32,1024]{1,0:T(8,128)(2,1)S(1)} %collective-permute-done.5.refs_3_, ...), custom_call_target="tpu_custom_call" | custom-call | flops 268435456 | bytes 4718592 | tf_op jit(solution)/shard_map/pallas_call | solution.py:242
  29.3 4.1 %collective-permute-start.12 = (bf16[64,512]{1,0:T(8,128)(2,1)S(1)}, bf16[64,512]{1,0:T(8,128)(2,1)S(1)}, u32[]{:S(2)}, u32[]{:S(2)}) collective-permute-start(bf16[64,512]{1,0:T(8,128)(2,1)S(1)} %shard_map.74.refs_0_), channel_id=1, source_target_pairs={{0,6},{2,4},{4,2},{6,0},{1,7},{3,5},{5,3},{7,1},{8,14},{10,12},{12... | collective-permute-start | bytes 196616 | tf_op jit(solution)/shard_map/ppermute | solution.py:24
  33.5 0.0 collective-permute-start.11
  33.5 0.6 %collective-permute-start.10 = (bf16[64,512]{1,0:T(8,128)(2,1)S(1)}, bf16[64,512]{1,0:T(8,128)(2,1)S(1)}, u32[]{:S(2)}, u32[]{:S(2)}) collective-permute-start(bf16[64,512]{1,0:T(8,128)(2,1)S(1)} %shard_map.74.refs_0_), channel_id=1, source_target_pairs={{0,2},{2,0},{4,6},{6,4},{1,3},{3,1},{5,7},{7,5},{8,10},{10,8},{12,... | collective-permute-start | bytes 196616 | tf_op jit(solution)/shard_map/ppermute | solution.py:24
  34.1 2.4 %collective-permute-done.12.refs_3_ = bf16[64,512]{1,0:T(8,128)(2,1)S(1)} collective-permute-done((bf16[64,512]{1,0:T(8,128)(2,1)S(1)}, bf16[64,512]{1,0:T(8,128)(2,1)S(1)}, u32[]{:S(2)}, u32[]{:S(2)}) %collective-permute-start.12) | collective-permute-done | bytes 65568 | tf_op jit(solution)/shard_map/ppermute | solution.py:24
  36.5 2.3 %collective-permute-done.11.refs_2_ = bf16[64,512]{1,0:T(8,128)(2,1)S(1)} collective-permute-done((bf16[64,512]{1,0:T(8,128)(2,1)S(1)}, bf16[64,512]{1,0:T(8,128)(2,1)S(1)}, u32[]{:S(2)}, u32[]{:S(2)}) %collective-permute-start.11) | collective-permute-done | bytes 65568 | tf_op jit(solution)/shard_map/ppermute | solution.py:24
  38.7 0.3 collective-permute-done.10.refs_1_
  39.1 0.1 collective-permute-start.13
  39.2 1.5 %collective-permute-done.13.refs_4_ = bf16[4,64,512]{2,1,0:T(8,128)(2,1)S(1)} collective-permute-done((bf16[4,64,512]{2,1,0:T(8,128)(2,1)S(1)}, bf16[4,64,512]{2,1,0:T(8,128)(2,1)S(1)}, u32[]{:S(2)}, u32[]{:S(2)}) %collective-permute-start.13) | collective-permute-done | bytes 262176 | tf_op jit(solution)/shard_map/ppermute | solution.py:24
  40.7 0.0 copy-done.3
  40.7 0.0 copy-done.5
  40.7 1.4 %shard_map.75 = bf16[128,1024]{1,0:T(8,128)(2,1)} custom-call(s32[4,128]{1,0:T(4,128)S(1)} %bitcast.15, bf16[128,1024]{1,0:T(8,128)(2,1)S(1)} %copy-done.3, bf16[64,512]{1,0:T(8,128)(2,1)S(1)} %shard_map.74.refs_0_, bf16[64,512]{1,0:T(8,128)(2,1)S(1)} %collective-permute-done.10.refs_1_, bf16[64,512]{1,0:T(8,128)(2,1)S(1)} %collective-permute-done.11.refs_2_, ...), custom_call_target="tpu_custom_call" | custom-call | tf_op jit(solution)/shard_map/pallas_call | solution.py:291
  (4 shorter events, 0.1 us)
Async XLA Ops:
  0.0 5.9 %collective-permute-start = (bf16[4096,256]{1,0:T(8,128)(2,1)}, bf16[4096,256]{1,0:T(8,128)(2,1)S(1)}, u32[]{:S(2)}, u32[]{:S(2)}) collective-permute-start(bf16[4096,256]{1,0:T(8,128)(2,1)} %bitcast.7), channel_id=1, source_target_pairs={{0,1},{1,0},{2,3},{3,2},{4,5},{5,4},{6,7},{7,6},{8,9},{9,8},{10,11... | collective-permute-start | bytes 6291464 | tf_op jit(solution)/shard_map/ppermute | solution.py:24
  0.5 26.3 %copy-start = (bf16[4096,1,256]{2,0,1:T(8,128)(2,1)S(1)}, bf16[4096,1,256]{2,0,1:T(8,128)(2,1)}, u32[]{:S(2)}) copy-start(bf16[4096,1,256]{2,0,1:T(8,128)(2,1)} %param.11) | copy-start | bytes 6291460
  0.5 26.3 %copy-start.4 = (f32[4096]{0:T(1024)S(1)}, f32[4096]{0:T(1024)}, u32[]{:S(2)}) copy-start(f32[4096]{0:T(1024)} %param.10) | copy-start | bytes 49156
  5.8 1.6 %collective-permute-start.1 = (f32[64,1024]{1,0:T(8,128)S(1)}, f32[64,1024]{1,0:T(8,128)S(1)}, u32[]{:S(2)}, u32[]{:S(2)}) collective-permute-start(f32[64,1024]{1,0:T(8,128)S(1)} %get-tuple-element.16), channel_id=1, source_target_pairs={{0,1},{1,0},{2,3},{3,2},{4,5},{5,4},{6,7},{7,6},{8,9},{9,8},{10,11... | collective-permute-start | bytes 786440 | tf_op jit(solution)/shard_map/ppermute | solution.py:24
  5.9 1.3 %copy-start.1 = (bf16[4096,256]{1,0:T(8,128)(2,1)}, bf16[4096,256]{1,0:T(8,128)(2,1)S(1)}, u32[]{:S(2)}) copy-start(bf16[4096,256]{1,0:T(8,128)(2,1)S(1)} %collective-permute-done.refs_10_) | copy-start | bytes 6291460
  7.5 5.1 %collective-permute-start.2 = (bf16[32,1024]{1,0:T(8,128)(2,1)S(1)}, bf16[32,1024]{1,0:T(8,128)(2,1)S(1)}, u32[]{:S(2)}, u32[]{:S(2)}) collective-permute-start(bf16[32,1024]{1,0:T(8,128)(2,1)S(1)} %get-tuple-element.17), channel_id=1, source_target_pairs={{0,8},{1,17},{8,0},{9,25},{16,24},{17,1},{24,16},{25,9},{2,10},{3,... | collective-permute-start | bytes 196616 | tf_op jit(solution)/shard_map/ppermute | solution.py:52
  10.3 5.4 %collective-permute-start.6 = (bf16[32,1024]{1,0:T(8,128)(2,1)S(1)}, bf16[32,1024]{1,0:T(8,128)(2,1)S(1)}, u32[]{:S(2)}, u32[]{:S(2)}) collective-permute-start(bf16[32,1024]{1,0:T(8,128)(2,1)S(1)} %get-tuple-element.18), channel_id=1, source_target_pairs={{1,25},{9,17},{17,9},{25,1},{3,27},{11,19},{19,11},{27,3},{5,29},{... | collective-permute-start | bytes 196616 | tf_op jit(solution)/shard_map/ppermute | solution.py:52
  12.6 7.2 %collective-permute-start.4 = (bf16[32,1024]{1,0:T(8,128)(2,1)S(1)}, bf16[32,1024]{1,0:T(8,128)(2,1)S(1)}, u32[]{:S(2)}, u32[]{:S(2)}) collective-permute-start(bf16[32,1024]{1,0:T(8,128)(2,1)S(1)} %collective-permute-done.2.refs_0_), channel_id=1, source_target_pairs={{0,4},{2,6},{4,0},{6,2},{1,5},{3,7},{5,1},{7,3},{8,12},{10,14},{12... | collective-permute-start | bytes 196616 | tf_op jit(solution)/shard_map/ppermute | solution.py:24
  15.7 6.8 %collective-permute-start.8 = (bf16[32,1024]{1,0:T(8,128)(2,1)S(1)}, bf16[32,1024]{1,0:T(8,128)(2,1)S(1)}, u32[]{:S(2)}, u32[]{:S(2)}) collective-permute-start(bf16[32,1024]{1,0:T(8,128)(2,1)S(1)} %broadcast_select_fusion.refs_4_), channel_id=1, source_target_pairs={{0,4},{2,6},{4,0},{6,2},{1,5},{3,7},{5,1},{7,3},{8,12},{10,14},{12... | collective-permute-start | bytes 196616 | tf_op jit(solution)/shard_map/ppermute | solution.py:24
  15.8 7.7 %collective-permute-start.7 = (bf16[32,1024]{1,0:T(8,128)(2,1)S(1)}, bf16[32,1024]{1,0:T(8,128)(2,1)S(1)}, u32[]{:S(2)}, u32[]{:S(2)}) collective-permute-start(bf16[32,1024]{1,0:T(8,128)(2,1)S(1)} %broadcast_select_fusion.refs_4_), channel_id=1, source_target_pairs={{0,2},{2,0},{4,6},{6,4},{1,3},{3,1},{5,7},{7,5},{8,10},{10,8},{12,... | collective-permute-start | bytes 196616 | tf_op jit(solution)/shard_map/ppermute | solution.py:24
  17.7 5.8 %collective-permute-start.3 = (bf16[32,1024]{1,0:T(8,128)(2,1)S(1)}, bf16[32,1024]{1,0:T(8,128)(2,1)S(1)}, u32[]{:S(2)}, u32[]{:S(2)}) collective-permute-start(bf16[32,1024]{1,0:T(8,128)(2,1)S(1)} %collective-permute-done.2.refs_0_), channel_id=1, source_target_pairs={{0,2},{2,0},{4,6},{6,4},{1,3},{3,1},{5,7},{7,5},{8,10},{10,8},{12,... | collective-permute-start | bytes 196616 | tf_op jit(solution)/shard_map/ppermute | solution.py:24
  19.8 5.1 %collective-permute-start.5 = (bf16[32,1024]{1,0:T(8,128)(2,1)S(1)}, bf16[32,1024]{1,0:T(8,128)(2,1)S(1)}, u32[]{:S(2)}, u32[]{:S(2)}) collective-permute-start(bf16[32,1024]{1,0:T(8,128)(2,1)S(1)} %collective-permute-done.4.refs_2_), channel_id=1, source_target_pairs={{0,2},{2,0},{4,6},{6,4},{1,3},{3,1},{5,7},{7,5},{8,10},{10,8},{12,... | collective-permute-start | bytes 196616 | tf_op jit(solution)/shard_map/ppermute | solution.py:24
  22.5 4.3 %collective-permute-start.9 = (bf16[32,1024]{1,0:T(8,128)(2,1)S(1)}, bf16[32,1024]{1,0:T(8,128)(2,1)S(1)}, u32[]{:S(2)}, u32[]{:S(2)}) collective-permute-start(bf16[32,1024]{1,0:T(8,128)(2,1)S(1)} %collective-permute-done.8.refs_6_), channel_id=1, source_target_pairs={{0,2},{2,0},{4,6},{6,4},{1,3},{3,1},{5,7},{7,5},{8,10},{10,8},{12,... | collective-permute-start | bytes 196616 | tf_op jit(solution)/shard_map/ppermute | solution.py:24
  26.8 1.6 %copy-start.2 = (bf16[4096,256]{1,0:T(8,128)(2,1)S(1)}, bf16[4096,256]{1,0:T(8,128)(2,1)}, u32[]{:S(2)}) copy-start(bf16[4096,256]{1,0:T(8,128)(2,1)} %copy-done.1) | copy-start | bytes 6291460
  28.4 12.4 %copy-start.3 = (bf16[128,1024]{1,0:T(8,128)(2,1)S(1)}, bf16[128,1024]{1,0:T(8,128)(2,1)}, u32[]{:S(2)}) copy-start(bf16[128,1024]{1,0:T(8,128)(2,1)} %query_ref.1) | copy-start | bytes 786436
  28.4 12.4 %copy-start.5 = (s32[512,1]{0,1:T(1,128)S(1)}, s32[512,1]{0,1:T(1,128)}, u32[]{:S(2)}) copy-start(s32[512,1]{0,1:T(1,128)} %param.12) | copy-start | bytes 6148
  29.3 7.2 %collective-permute-start.12 = (bf16[64,512]{1,0:T(8,128)(2,1)S(1)}, bf16[64,512]{1,0:T(8,128)(2,1)S(1)}, u32[]{:S(2)}, u32[]{:S(2)}) collective-permute-start(bf16[64,512]{1,0:T(8,128)(2,1)S(1)} %shard_map.74.refs_0_), channel_id=1, source_target_pairs={{0,6},{2,4},{4,2},{6,0},{1,7},{3,5},{5,3},{7,1},{8,14},{10,12},{12... | collective-permute-start | bytes 196616 | tf_op jit(solution)/shard_map/ppermute | solution.py:24
  33.5 5.3 %collective-permute-start.11 = (bf16[64,512]{1,0:T(8,128)(2,1)S(1)}, bf16[64,512]{1,0:T(8,128)(2,1)S(1)}, u32[]{:S(2)}, u32[]{:S(2)}) collective-permute-start(bf16[64,512]{1,0:T(8,128)(2,1)S(1)} %shard_map.74.refs_0_), channel_id=1, source_target_pairs={{0,4},{2,6},{4,0},{6,2},{1,5},{3,7},{5,1},{7,3},{8,12},{10,14},{12... | collective-permute-start | bytes 196616 | tf_op jit(solution)/shard_map/ppermute | solution.py:24
  33.5 5.6 %collective-permute-start.10 = (bf16[64,512]{1,0:T(8,128)(2,1)S(1)}, bf16[64,512]{1,0:T(8,128)(2,1)S(1)}, u32[]{:S(2)}, u32[]{:S(2)}) collective-permute-start(bf16[64,512]{1,0:T(8,128)(2,1)S(1)} %shard_map.74.refs_0_), channel_id=1, source_target_pairs={{0,2},{2,0},{4,6},{6,4},{1,3},{3,1},{5,7},{7,5},{8,10},{10,8},{12,... | collective-permute-start | bytes 196616 | tf_op jit(solution)/shard_map/ppermute | solution.py:24
  39.1 1.6 %collective-permute-start.13 = (bf16[4,64,512]{2,1,0:T(8,128)(2,1)S(1)}, bf16[4,64,512]{2,1,0:T(8,128)(2,1)S(1)}, u32[]{:S(2)}, u32[]{:S(2)}) collective-permute-start(bf16[4,64,512]{2,1,0:T(8,128)(2,1)S(1)} %pad_maximum_fusion), channel_id=1, source_target_pairs={{0,1},{1,0},{2,3},{3,2},{4,5},{5,4},{6,7},{7,6},{8,9},{9,8},{10,11... | collective-permute-start | bytes 786440 | tf_op jit(solution)/shard_map/ppermute | solution.py:24

commit v15 on v14

--- a/solution.py
+++ b/solution.py
@@ -268,7 +268,7 @@
     weight = kv_weight.reshape(kv_weight.shape[0], heads_here * kv_weight.shape[2])
     weights = [swap(weight, "tp", g) for g in range(1, cores)]
     own, send, text = ffn(dest, ffn_hidden, ffn_weight, residual, capacity, cores)
-    weights, own = lax.optimization_barrier(([weight] + weights, own))
+    weights = [weight] + weights
     for g in range(1, cores):
         own = own + swap(send[(g - 1) * share:g * share], "tp", g)
     text = (text.astype(F32) + own).astype(BF16)

time: 42.3 us -> 42.4 us (level)
  local copies, waits for them, and re-layouts: 2.95 us -> 0.03 us
  waiting for transfers between devices: 14.6 us -> 16.3 us
  Pallas kernels: 7.66 us -> 9.29 us
    unnamed x12 -> x8, local copies, waits for them, and re-layouts: 2.94 us -> 0.02 us
    ppermute x12, waiting for transfers between devices: 13 us -> 14.7 us  [swap(): return lax.ppermute(value, axis, [(i, i ^ offset) for i in range(size)])]
    pallas_call x1, Pallas kernels: 0.94 us -> 2.57 us  [keyval(): pl.pallas_call(functools.partial(keyval_kernel, parts, groups), in_specs=...]
  transfers between devices with their start and end apart: 14 -> 14, of which waited for: 11 -> 10; matrix products, arithmetic and copies ran while one was open for 0% -> 0% of each run, Pallas kernels for 13% -> 13%
where the time goes in v15:
time: 42.4 us; the launch traced here: 42.2 us
  starting transfers between devices  16.4 us (39%)
  waiting for transfers between devices  16.3 us (38%)
  Pallas kernels  9.29 us (22%)
    ppermute x12, waiting for transfers between devices, swap(): return lax.ppermute(value, axis, [(i, i ^ offset) for i in range(size)])  14.7 us
    ppermute x12, starting transfers between devices, swap(): return lax.ppermute(value, axis, [(i, i ^ offset) for i in range(size)])  13.1 us
    pallas_call x1, Pallas kernels, ffn(): pl.pallas_call(functools.partial(ffn_kernel, capacity, cores, edges), in_...  5.33 us
    ppermute x2, starting transfers between devices, route(): moved = lax.ppermute(value, ('clip', 'tp'), pairs)  3.34 us
    pallas_call x1, Pallas kernels, keyval(): pl.pallas_call(functools.partial(keyval_kernel, parts, groups), in_specs=...  2.57 us
    ppermute x2, waiting for transfers between devices, route(): moved = lax.ppermute(value, ('clip', 'tp'), pairs)  1.58 us
    pallas_call x1, Pallas kernels, shards(): pl.pallas_call(functools.partial(attend_kernel, parts, cores, heads_here,...  1.39 us
  transfers between devices with their start and end apart: 14, of which 10 were waited for; matrix products, arithmetic and copies ran while one was open for 0% of the time, Pallas kernels for 13%

profile of v15, /device:TPU:0, one launch (start us, length us, event | category | flops | bytes accessed | tf_op | source)
XLA Modules:
  0.0 42.2 jit_solution(3037643656392912975)
XLA Ops:
  0.0 0.5 %collective-permute-start.9 = (bf16[4096,256]{1,0:T(8,128)(2,1)}, bf16[4096,256]{1,0:T(8,128)(2,1)}, u32[]{:S(2)}, u32[]{:S(2)}) collective-permute-start(bf16[4096,256]{1,0:T(8,128)(2,1)} %bitcast.7), channel_id=1, source_target_pairs={{0,1},{1,0},{2,3},{3,2},{4,5},{5,4},{6,7},{7,6},{8,9},{9,8},{10,11... | collective-permute-start | bytes 6291464 | tf_op jit(solution)/shard_map/ppermute | solution.py:24
  0.5 0.0 copy-start
  0.5 0.0 copy-start.2
  0.5 5.3 %shard_map.73 = (f32[64,1024]{1,0:T(8,128)S(1)}, f32[64,1024]{1,0:T(8,128)S(1)}, bf16[64,1024]{1,0:T(8,128)(2,1)S(1)}) custom-call(s32[4,128]{1,0:T(4,128)} %bitcast.14, bf16[128,5120]{1,0:T(8,128)(2,1)} %hidden_hbm.1, bf16[5120,1024]{1,0:T(8,128)(2,1)} %weight_hbm.1, bf16[128,1024]{1,0:T(8,128)(2,1)} %residual_hbm.1), custom_call_target="tpu_custom_call" | custom-call | flops 1509949440 | bytes 11796480 | tf_op jit(solution)/shard_map/pallas_call | solution.py:124
  5.8 0.1 collective-permute-start
  5.9 1.5 %collective-permute-done = f32[64,1024]{1,0:T(8,128)S(1)} collective-permute-done((f32[64,1024]{1,0:T(8,128)S(1)}, f32[64,1024]{1,0:T(8,128)S(1)}, u32[]{:S(2)}, u32[]{:S(2)}) %collective-permute-start) | collective-permute-done | bytes 262176 | tf_op jit(solution)/shard_map/ppermute | solution.py:24
  7.5 2.7 %collective-permute-start.1 = (bf16[32,1024]{1,0:T(8,128)(2,1)S(1)}, bf16[32,1024]{1,0:T(8,128)(2,1)S(1)}, u32[]{:S(2)}, u32[]{:S(2)}) collective-permute-start(bf16[32,1024]{1,0:T(8,128)(2,1)S(1)} %get-tuple-element.13), channel_id=1, source_target_pairs={{0,8},{1,17},{8,0},{9,25},{16,24},{17,1},{24,16},{25,9},{2,10},{3,... | collective-permute-start | bytes 196616 | tf_op jit(solution)/shard_map/ppermute | solution.py:52
  10.2 0.7 %collective-permute-start.5 = (bf16[32,1024]{1,0:T(8,128)(2,1)S(1)}, bf16[32,1024]{1,0:T(8,128)(2,1)S(1)}, u32[]{:S(2)}, u32[]{:S(2)}) collective-permute-start(bf16[32,1024]{1,0:T(8,128)(2,1)S(1)} %get-tuple-element.14), channel_id=1, source_target_pairs={{1,25},{9,17},{17,9},{25,1},{3,27},{11,19},{19,11},{27,3},{5,29},{... | collective-permute-start | bytes 196616 | tf_op jit(solution)/shard_map/ppermute | solution.py:52
  10.8 1.6 %collective-permute-done.1.refs_0_ = bf16[32,1024]{1,0:T(8,128)(2,1)S(1)} collective-permute-done((bf16[32,1024]{1,0:T(8,128)(2,1)S(1)}, bf16[32,1024]{1,0:T(8,128)(2,1)S(1)}, u32[]{:S(2)}, u32[]{:S(2)}) %collective-permute-start.1) | collective-permute-done | bytes 65568 | tf_op jit(solution)/shard_map/ppermute | solution.py:52
  12.4 3.1 %collective-permute-start.3 = (bf16[32,1024]{1,0:T(8,128)(2,1)S(1)}, bf16[32,1024]{1,0:T(8,128)(2,1)S(1)}, u32[]{:S(2)}, u32[]{:S(2)}) collective-permute-start(bf16[32,1024]{1,0:T(8,128)(2,1)S(1)} %collective-permute-done.1.refs_0_), channel_id=1, source_target_pairs={{0,4},{2,6},{4,0},{6,2},{1,5},{3,7},{5,1},{7,3},{8,12},{10,14},{12... | collective-permute-start | bytes 196616 | tf_op jit(solution)/shard_map/ppermute | solution.py:24
  15.5 0.0 collective-permute-done.5
  15.5 0.1 collective-permute-start.7
  15.6 1.9 %collective-permute-start.6 = (bf16[32,1024]{1,0:T(8,128)(2,1)S(1)}, bf16[32,1024]{1,0:T(8,128)(2,1)S(1)}, u32[]{:S(2)}, u32[]{:S(2)}) collective-permute-start(bf16[32,1024]{1,0:T(8,128)(2,1)S(1)} %broadcast_select_fusion.refs_4_), channel_id=1, source_target_pairs={{0,2},{2,0},{4,6},{6,4},{1,3},{3,1},{5,7},{7,5},{8,10},{10,8},{12,... | collective-permute-start | bytes 196616 | tf_op jit(solution)/shard_map/ppermute | solution.py:24
  17.5 0.2 collective-permute-start.2
  17.7 2.1 %collective-permute-done.3.refs_2_ = bf16[32,1024]{1,0:T(8,128)(2,1)S(1)} collective-permute-done((bf16[32,1024]{1,0:T(8,128)(2,1)S(1)}, bf16[32,1024]{1,0:T(8,128)(2,1)S(1)}, u32[]{:S(2)}, u32[]{:S(2)}) %collective-permute-start.3) | collective-permute-done | bytes 65568 | tf_op jit(solution)/shard_map/ppermute | solution.py:24
  19.8 1.9 %collective-permute-start.4 = (bf16[32,1024]{1,0:T(8,128)(2,1)S(1)}, bf16[32,1024]{1,0:T(8,128)(2,1)S(1)}, u32[]{:S(2)}, u32[]{:S(2)}) collective-permute-start(bf16[32,1024]{1,0:T(8,128)(2,1)S(1)} %collective-permute-done.3.refs_2_), channel_id=1, source_target_pairs={{0,2},{2,0},{4,6},{6,4},{1,3},{3,1},{5,7},{7,5},{8,10},{10,8},{12,... | collective-permute-start | bytes 196616 | tf_op jit(solution)/shard_map/ppermute | solution.py:24
  21.8 0.9 %collective-permute-done.7.refs_6_ = bf16[32,1024]{1,0:T(8,128)(2,1)S(1)} collective-permute-done((bf16[32,1024]{1,0:T(8,128)(2,1)S(1)}, bf16[32,1024]{1,0:T(8,128)(2,1)S(1)}, u32[]{:S(2)}, u32[]{:S(2)}) %collective-permute-start.7) | collective-permute-done | bytes 65568 | tf_op jit(solution)/shard_map/ppermute | solution.py:24
  22.7 0.6 %collective-permute-start.8 = (bf16[32,1024]{1,0:T(8,128)(2,1)S(1)}, bf16[32,1024]{1,0:T(8,128)(2,1)S(1)}, u32[]{:S(2)}, u32[]{:S(2)}) collective-permute-start(bf16[32,1024]{1,0:T(8,128)(2,1)S(1)} %collective-permute-done.7.refs_6_), channel_id=1, source_target_pairs={{0,2},{2,0},{4,6},{6,4},{1,3},{3,1},{5,7},{7,5},{8,10},{10,8},{12,... | collective-permute-start | bytes 196616 | tf_op jit(solution)/shard_map/ppermute | solution.py:24
  23.2 0.0 collective-permute-done.2.refs_1_
  23.3 0.0 collective-permute-done.6.refs_5_
  23.3 1.6 %collective-permute-done.4.refs_3_ = bf16[32,1024]{1,0:T(8,128)(2,1)S(1)} collective-permute-done((bf16[32,1024]{1,0:T(8,128)(2,1)S(1)}, bf16[32,1024]{1,0:T(8,128)(2,1)S(1)}, u32[]{:S(2)}, u32[]{:S(2)}) %collective-permute-start.4) | collective-permute-done | bytes 65568 | tf_op jit(solution)/shard_map/ppermute | solution.py:24
  24.8 2.1 %collective-permute-done.8.refs_7_ = bf16[32,1024]{1,0:T(8,128)(2,1)S(1)} collective-permute-done((bf16[32,1024]{1,0:T(8,128)(2,1)S(1)}, bf16[32,1024]{1,0:T(8,128)(2,1)S(1)}, u32[]{:S(2)}, u32[]{:S(2)}) %collective-permute-start.8) | collective-permute-done | bytes 65568 | tf_op jit(solution)/shard_map/ppermute | solution.py:24
  26.9 0.0 collective-permute-done.9.refs_10_
  26.9 0.0 copy-done
  26.9 0.0 copy-done.2
  26.9 0.0 copy-start.1
  27.0 0.0 copy-start.3
  27.0 2.6 %shard_map.74.refs_0_ = bf16[64,512]{1,0:T(8,128)(2,1)S(1)} custom-call(bf16[32,1024]{1,0:T(8,128)(2,1)S(1)} %collective-permute-done.1.refs_0_, bf16[32,1024]{1,0:T(8,128)(2,1)S(1)} %collective-permute-done.2.refs_1_, bf16[32,1024]{1,0:T(8,128)(2,1)S(1)} %collective-permute-done.3.refs_2_, bf16[32,1024]{1,0:T(8,128)(2,1)S(1)} %collective-permute-done.4.refs_3_, ...), custom_call_target="tpu_custom_call" | custom-call | flops 268435456 | bytes 4718592 | tf_op jit(solution)/shard_map/pallas_call | solution.py:242
  29.5 4.0 %collective-permute-start.12 = (bf16[64,512]{1,0:T(8,128)(2,1)S(1)}, bf16[64,512]{1,0:T(8,128)(2,1)S(1)}, u32[]{:S(2)}, u32[]{:S(2)}) collective-permute-start(bf16[64,512]{1,0:T(8,128)(2,1)S(1)} %shard_map.74.refs_0_), channel_id=1, source_target_pairs={{0,6},{2,4},{4,2},{6,0},{1,7},{3,5},{5,3},{7,1},{8,14},{10,12},{12... | collective-permute-start | bytes 196616 | tf_op jit(solution)/shard_map/ppermute | solution.py:24
  33.6 0.0 collective-permute-start.11
  33.6 0.6 %collective-permute-start.10 = (bf16[64,512]{1,0:T(8,128)(2,1)S(1)}, bf16[64,512]{1,0:T(8,128)(2,1)S(1)}, u32[]{:S(2)}, u32[]{:S(2)}) collective-permute-start(bf16[64,512]{1,0:T(8,128)(2,1)S(1)} %shard_map.74.refs_0_), channel_id=1, source_target_pairs={{0,2},{2,0},{4,6},{6,4},{1,3},{3,1},{5,7},{7,5},{8,10},{10,8},{12,... | collective-permute-start | bytes 196616 | tf_op jit(solution)/shard_map/ppermute | solution.py:24
  34.2 2.4 %collective-permute-done.12.refs_3_ = bf16[64,512]{1,0:T(8,128)(2,1)S(1)} collective-permute-done((bf16[64,512]{1,0:T(8,128)(2,1)S(1)}, bf16[64,512]{1,0:T(8,128)(2,1)S(1)}, u32[]{:S(2)}, u32[]{:S(2)}) %collective-permute-start.12) | collective-permute-done | bytes 65568 | tf_op jit(solution)/shard_map/ppermute | solution.py:24
  36.6 2.3 %collective-permute-done.11.refs_2_ = bf16[64,512]{1,0:T(8,128)(2,1)S(1)} collective-permute-done((bf16[64,512]{1,0:T(8,128)(2,1)S(1)}, bf16[64,512]{1,0:T(8,128)(2,1)S(1)}, u32[]{:S(2)}, u32[]{:S(2)}) %collective-permute-start.11) | collective-permute-done | bytes 65568 | tf_op jit(solution)/shard_map/ppermute | solution.py:24
  38.9 0.4 collective-permute-done.10.refs_1_
  39.2 0.1 collective-permute-start.13
  39.3 1.5 %collective-permute-done.13.refs_4_ = bf16[4,64,512]{2,1,0:T(8,128)(2,1)S(1)} collective-permute-done((bf16[4,64,512]{2,1,0:T(8,128)(2,1)S(1)}, bf16[4,64,512]{2,1,0:T(8,128)(2,1)S(1)}, u32[]{:S(2)}, u32[]{:S(2)}) %collective-permute-start.13) | collective-permute-done | bytes 262176 | tf_op jit(solution)/shard_map/ppermute | solution.py:24
  40.8 0.0 copy-done.1
  40.9 0.0 copy-done.3
  40.9 1.4 %shard_map.75 = bf16[128,1024]{1,0:T(8,128)(2,1)} custom-call(s32[4,128]{1,0:T(4,128)S(1)} %bitcast.15, bf16[128,1024]{1,0:T(8,128)(2,1)S(1)} %copy-done.1, bf16[64,512]{1,0:T(8,128)(2,1)S(1)} %shard_map.74.refs_0_, bf16[64,512]{1,0:T(8,128)(2,1)S(1)} %collective-permute-done.10.refs_1_, bf16[64,512]{1,0:T(8,128)(2,1)S(1)} %collective-permute-done.11.refs_2_, ...), custom_call_target="tpu_custom_call" | custom-call | tf_op jit(solution)/shard_map/pallas_call | solution.py:291
  (4 shorter events, 0.1 us)
Async XLA Ops:
  0.0 26.9 %collective-permute-start.9 = (bf16[4096,256]{1,0:T(8,128)(2,1)}, bf16[4096,256]{1,0:T(8,128)(2,1)}, u32[]{:S(2)}, u32[]{:S(2)}) collective-permute-start(bf16[4096,256]{1,0:T(8,128)(2,1)} %bitcast.7), channel_id=1, source_target_pairs={{0,1},{1,0},{2,3},{3,2},{4,5},{5,4},{6,7},{7,6},{8,9},{9,8},{10,11... | collective-permute-start | bytes 6291464 | tf_op jit(solution)/shard_map/ppermute | solution.py:24
  0.5 26.5 %copy-start = (bf16[4096,1,256]{2,0,1:T(8,128)(2,1)S(1)}, bf16[4096,1,256]{2,0,1:T(8,128)(2,1)}, u32[]{:S(2)}) copy-start(bf16[4096,1,256]{2,0,1:T(8,128)(2,1)} %param.11) | copy-start | bytes 6291460
  0.5 26.5 %copy-start.2 = (f32[4096]{0:T(1024)S(1)}, f32[4096]{0:T(1024)}, u32[]{:S(2)}) copy-start(f32[4096]{0:T(1024)} %param.10) | copy-start | bytes 49156
  5.8 1.6 %collective-permute-start = (f32[64,1024]{1,0:T(8,128)S(1)}, f32[64,1024]{1,0:T(8,128)S(1)}, u32[]{:S(2)}, u32[]{:S(2)}) collective-permute-start(f32[64,1024]{1,0:T(8,128)S(1)} %get-tuple-element.12), channel_id=1, source_target_pairs={{0,1},{1,0},{2,3},{3,2},{4,5},{5,4},{6,7},{7,6},{8,9},{9,8},{10,11... | collective-permute-start | bytes 786440 | tf_op jit(solution)/shard_map/ppermute | solution.py:24
  7.5 4.9 %collective-permute-start.1 = (bf16[32,1024]{1,0:T(8,128)(2,1)S(1)}, bf16[32,1024]{1,0:T(8,128)(2,1)S(1)}, u32[]{:S(2)}, u32[]{:S(2)}) collective-permute-start(bf16[32,1024]{1,0:T(8,128)(2,1)S(1)} %get-tuple-element.13), channel_id=1, source_target_pairs={{0,8},{1,17},{8,0},{9,25},{16,24},{17,1},{24,16},{25,9},{2,10},{3,... | collective-permute-start | bytes 196616 | tf_op jit(solution)/shard_map/ppermute | solution.py:52
  10.2 5.4 %collective-permute-start.5 = (bf16[32,1024]{1,0:T(8,128)(2,1)S(1)}, bf16[32,1024]{1,0:T(8,128)(2,1)S(1)}, u32[]{:S(2)}, u32[]{:S(2)}) collective-permute-start(bf16[32,1024]{1,0:T(8,128)(2,1)S(1)} %get-tuple-element.14), channel_id=1, source_target_pairs={{1,25},{9,17},{17,9},{25,1},{3,27},{11,19},{19,11},{27,3},{5,29},{... | collective-permute-start | bytes 196616 | tf_op jit(solution)/shard_map/ppermute | solution.py:52
  12.4 7.4 %collective-permute-start.3 = (bf16[32,1024]{1,0:T(8,128)(2,1)S(1)}, bf16[32,1024]{1,0:T(8,128)(2,1)S(1)}, u32[]{:S(2)}, u32[]{:S(2)}) collective-permute-start(bf16[32,1024]{1,0:T(8,128)(2,1)S(1)} %collective-permute-done.1.refs_0_), channel_id=1, source_target_pairs={{0,4},{2,6},{4,0},{6,2},{1,5},{3,7},{5,1},{7,3},{8,12},{10,14},{12... | collective-permute-start | bytes 196616 | tf_op jit(solution)/shard_map/ppermute | solution.py:24
  15.5 7.1 %collective-permute-start.7 = (bf16[32,1024]{1,0:T(8,128)(2,1)S(1)}, bf16[32,1024]{1,0:T(8,128)(2,1)S(1)}, u32[]{:S(2)}, u32[]{:S(2)}) collective-permute-start(bf16[32,1024]{1,0:T(8,128)(2,1)S(1)} %broadcast_select_fusion.refs_4_), channel_id=1, source_target_pairs={{0,4},{2,6},{4,0},{6,2},{1,5},{3,7},{5,1},{7,3},{8,12},{10,14},{12... | collective-permute-start | bytes 196616 | tf_op jit(solution)/shard_map/ppermute | solution.py:24
  15.6 7.6 %collective-permute-start.6 = (bf16[32,1024]{1,0:T(8,128)(2,1)S(1)}, bf16[32,1024]{1,0:T(8,128)(2,1)S(1)}, u32[]{:S(2)}, u32[]{:S(2)}) collective-permute-start(bf16[32,1024]{1,0:T(8,128)(2,1)S(1)} %broadcast_select_fusion.refs_4_), channel_id=1, source_target_pairs={{0,2},{2,0},{4,6},{6,4},{1,3},{3,1},{5,7},{7,5},{8,10},{10,8},{12,... | collective-permute-start | bytes 196616 | tf_op jit(solution)/shard_map/ppermute | solution.py:24
  17.5 5.7 %collective-permute-start.2 = (bf16[32,1024]{1,0:T(8,128)(2,1)S(1)}, bf16[32,1024]{1,0:T(8,128)(2,1)S(1)}, u32[]{:S(2)}, u32[]{:S(2)}) collective-permute-start(bf16[32,1024]{1,0:T(8,128)(2,1)S(1)} %collective-permute-done.1.refs_0_), channel_id=1, source_target_pairs={{0,2},{2,0},{4,6},{6,4},{1,3},{3,1},{5,7},{7,5},{8,10},{10,8},{12,... | collective-permute-start | bytes 196616 | tf_op jit(solution)/shard_map/ppermute | solution.py:24
  19.8 5.0 %collective-permute-start.4 = (bf16[32,1024]{1,0:T(8,128)(2,1)S(1)}, bf16[32,1024]{1,0:T(8,128)(2,1)S(1)}, u32[]{:S(2)}, u32[]{:S(2)}) collective-permute-start(bf16[32,1024]{1,0:T(8,128)(2,1)S(1)} %collective-permute-done.3.refs_2_), channel_id=1, source_target_pairs={{0,2},{2,0},{4,6},{6,4},{1,3},{3,1},{5,7},{7,5},{8,10},{10,8},{12,... | collective-permute-start | bytes 196616 | tf_op jit(solution)/shard_map/ppermute | solution.py:24
  22.7 4.3 %collective-permute-start.8 = (bf16[32,1024]{1,0:T(8,128)(2,1)S(1)}, bf16[32,1024]{1,0:T(8,128)(2,1)S(1)}, u32[]{:S(2)}, u32[]{:S(2)}) collective-permute-start(bf16[32,1024]{1,0:T(8,128)(2,1)S(1)} %collective-permute-done.7.refs_6_), channel_id=1, source_target_pairs={{0,2},{2,0},{4,6},{6,4},{1,3},{3,1},{5,7},{7,5},{8,10},{10,8},{12,... | collective-permute-start | bytes 196616 | tf_op jit(solution)/shard_map/ppermute | solution.py:24
  26.9 13.9 %copy-start.1 = (bf16[128,1024]{1,0:T(8,128)(2,1)S(1)}, bf16[128,1024]{1,0:T(8,128)(2,1)}, u32[]{:S(2)}) copy-start(bf16[128,1024]{1,0:T(8,128)(2,1)} %query_ref.1) | copy-start | bytes 786436
  27.0 13.9 %copy-start.3 = (s32[512,1]{0,1:T(1,128)S(1)}, s32[512,1]{0,1:T(1,128)}, u32[]{:S(2)}) copy-start(s32[512,1]{0,1:T(1,128)} %param.12) | copy-start | bytes 6148
  29.5 7.0 %collective-permute-start.12 = (bf16[64,512]{1,0:T(8,128)(2,1)S(1)}, bf16[64,512]{1,0:T(8,128)(2,1)S(1)}, u32[]{:S(2)}, u32[]{:S(2)}) collective-permute-start(bf16[64,512]{1,0:T(8,128)(2,1)S(1)} %shard_map.74.refs_0_), channel_id=1, source_target_pairs={{0,6},{2,4},{4,2},{6,0},{1,7},{3,5},{5,3},{7,1},{8,14},{10,12},{12... | collective-permute-start | bytes 196616 | tf_op jit(solution)/shard_map/ppermute | solution.py:24
  33.6 5.3 %collective-permute-start.11 = (bf16[64,512]{1,0:T(8,128)(2,1)S(1)}, bf16[64,512]{1,0:T(8,128)(2,1)S(1)}, u32[]{:S(2)}, u32[]{:S(2)}) collective-permute-start(bf16[64,512]{1,0:T(8,128)(2,1)S(1)} %shard_map.74.refs_0_), channel_id=1, source_target_pairs={{0,4},{2,6},{4,0},{6,2},{1,5},{3,7},{5,1},{7,3},{8,12},{10,14},{12... | collective-permute-start | bytes 196616 | tf_op jit(solution)/shard_map/ppermute | solution.py:24
  33.6 5.6 %collective-permute-start.10 = (bf16[64,512]{1,0:T(8,128)(2,1)S(1)}, bf16[64,512]{1,0:T(8,128)(2,1)S(1)}, u32[]{:S(2)}, u32[]{:S(2)}) collective-permute-start(bf16[64,512]{1,0:T(8,128)(2,1)S(1)} %shard_map.74.refs_0_), channel_id=1, source_target_pairs={{0,2},{2,0},{4,6},{6,4},{1,3},{3,1},{5,7},{7,5},{8,10},{10,8},{12,... | collective-permute-start | bytes 196616 | tf_op jit(solution)/shard_map/ppermute | solution.py:24
  39.2 1.6 %collective-permute-start.13 = (bf16[4,64,512]{2,1,0:T(8,128)(2,1)S(1)}, bf16[4,64,512]{2,1,0:T(8,128)(2,1)S(1)}, u32[]{:S(2)}, u32[]{:S(2)}) collective-permute-start(bf16[4,64,512]{2,1,0:T(8,128)(2,1)S(1)} %pad_maximum_fusion), channel_id=1, source_target_pairs={{0,1},{1,0},{2,3},{3,2},{4,5},{5,4},{6,7},{7,6},{8,9},{9,8},{10,11... | collective-permute-start | bytes 786440 | tf_op jit(solution)/shard_map/ppermute | solution.py:24

commit v16 on v13

--- a/solution.py
+++ b/solution.py
@@ -176,8 +176,9 @@
         out_ref[:, c * each:(c + 1) * each] = totals[c].astype(BF16)
 
 
-def attend_kernel(parts, cores, heads_here, capacity, dest_ref, query_ref, *refs):
-    own, others, out_ref = refs[:parts], refs[parts:-1], refs[-1]
+def attend_kernel(parts, cores, heads_here, capacity, steps, dest_ref, query_ref, *refs):
+    own, refs = refs[:len(steps)], refs[len(steps):]
+    others, done, out_ref = refs[:cores - 1], refs[cores - 1:-1], refs[-1]
     clip, seq, core = lax.axis_index("clip"), lax.axis_index("seq"), lax.axis_index("tp")
     clips = dest_ref.shape[0]
     slots = clips * capacity
@@ -196,11 +197,13 @@
             at += count
     here = lax.broadcasted_iota(jnp.int32, lane.shape, 0) == source
     valid = jnp.sum(jnp.where(here & (rank < counts), 1, 0), axis=0, keepdims=True) > 0
-    heads = [(k, c, i) for k in range(parts) for c in range(cores) for i in range(heads_here)]
+    heads = [
+        (k, c, i) for k in range(len(steps)) for c in range(cores) for i in range(heads_here)
+    ]
 
     def columns(head):
         k, c, i = head
-        at = ((seq ^ k) * cores + (core ^ c)) * heads_here + i
+        at = ((seq ^ steps[k]) * cores + (core ^ c)) * heads_here + i
         return pl.ds(pl.multiple_of(at * dim, dim), dim)
 
     def stored(head, offset):
@@ -214,6 +217,8 @@
                 found.append(others[g - 1][k, :, at:at + dim])
         return jnp.concatenate(found, axis=0)
 
+    if done:
+        out_ref[...] = done[0][...]
     group = 8
     for first in range(0, len(heads), group):
         some = heads[first:first + group]
@@ -288,15 +293,22 @@
         texts.append(relayed(mine))
     block = keyval(texts, gain, weights)
     own = [block] + [swap(block, "seq", k) for k in range(1, parts)]
-    packed = jnp.stack(own)
-    others = [swap(packed, "tp", g) for g in range(1, cores)]
-    return pl.pallas_call(
-        functools.partial(attend_kernel, parts, cores, heads_here, capacity),
-        in_specs=[whole()] * (2 + len(own) + len(others)),
-        out_specs=whole(),
-        out_shape=jax.ShapeDtypeStruct(queries.shape, BF16),
-        compiler_params=pltpu.CompilerParams(vmem_limit_bytes=VMEM_LIMIT),
-    )(dest, queries, *own, *others)
+
+    def attend(steps, done):
+        some = [own[k] for k in steps]
+        others = [swap(jnp.stack(some), "tp", g) for g in range(1, cores)]
+        return pl.pallas_call(
+            functools.partial(attend_kernel, parts, cores, heads_here, capacity, steps),
+            in_specs=[whole()] * (2 + len(some) + len(others) + len(done)),
+            out_specs=whole(),
+            out_shape=jax.ShapeDtypeStruct(queries.shape, BF16),
+            compiler_params=pltpu.CompilerParams(vmem_limit_bytes=VMEM_LIMIT),
+        )(dest, queries, *some, *others, *done)
+
+    order = [0] + list(range(parts - 1, 0, -1))
+    cut = max(1, parts // 2)
+    output = attend(order[:cut], [])
+    return attend(order[:cut - 1:-1], [output]) if order[cut:] else output
 
 
 def solution(mesh):

time: 39.8 us -> 39.5 us (level)
  waiting for transfers between devices: 12 us -> 11.2 us
    ppermute x12 -> x13, waiting for transfers between devices: 10.6 us -> 9.81 us  [swap(): return lax.ppermute(value, axis, [(i, i ^ offset) for i in range(size)])]
    pallas_call x1 -> x2, Pallas kernels: 1.39 us -> 1.74 us  [attend(): pl.pallas_call(functools.partial(attend_kernel, parts, cores, heads_here,...]
    ppermute x12 -> x13, starting transfers between devices: 15.6 us -> 15.7 us  [swap(): return lax.ppermute(value, axis, [(i, i ^ offset) for i in range(size)])]
  transfers between devices with their start and end apart: 14 -> 15, of which waited for: 8 -> 8; matrix products, arithmetic and copies ran while one was open for 0% -> 0% of each run, Pallas kernels for 13% -> 15%
where the time goes in v16:
time: 39.5 us; the launch traced here: 39.3 us
  starting transfers between devices  19.9 us (50%)
  waiting for transfers between devices  11.2 us (28%)
  Pallas kernels  8.04 us (20%)
    ppermute x13, starting transfers between devices, swap(): return lax.ppermute(value, axis, [(i, i ^ offset) for i in range(size)])  15.7 us
    ppermute x13, waiting for transfers between devices, swap(): return lax.ppermute(value, axis, [(i, i ^ offset) for i in range(size)])  9.81 us
    pallas_call x1, Pallas kernels, ffn(): pl.pallas_call(functools.partial(ffn_kernel, capacity, cores, edges), in_...  5.36 us
    ppermute x2, starting transfers between devices, route(): moved = lax.ppermute(value, ('clip', 'tp'), pairs)  4.19 us
    pallas_call x2, Pallas kernels, attend(): pl.pallas_call(functools.partial(attend_kernel, parts, cores, heads_here,...  1.74 us
    ppermute x2, waiting for transfers between devices, route(): moved = lax.ppermute(value, ('clip', 'tp'), pairs)  1.38 us
    pallas_call x1, Pallas kernels, keyval(): pl.pallas_call(functools.partial(keyval_kernel, parts, groups), in_specs=...  0.94 us
  transfers between devices with their start and end apart: 15, of which 8 were waited for; matrix products, arithmetic and copies ran while one was open for 0% of the time, Pallas kernels for 15%

profile of v16, /device:TPU:0, one launch (start us, length us, event | category | flops | bytes accessed | tf_op | source)
XLA Modules:
  0.0 39.3 jit_solution(782551247808518462)
XLA Ops:
  0.0 0.5 %collective-permute-start = (bf16[4096,256]{1,0:T(8,128)(2,1)}, bf16[4096,256]{1,0:T(8,128)(2,1)S(1)}, u32[]{:S(2)}, u32[]{:S(2)}) collective-permute-start(bf16[4096,256]{1,0:T(8,128)(2,1)} %bitcast.7), channel_id=1, source_target_pairs={{0,1},{1,0},{2,3},{3,2},{4,5},{5,4},{6,7},{7,6},{8,9},{9,8},{10,11... | collective-permute-start | bytes 6291464 | tf_op jit(solution)/shard_map/ppermute | solution.py:24
  0.5 0.0 copy-start
  0.5 0.0 copy-start.3
  0.5 5.4 %shard_map.73 = (f32[64,1024]{1,0:T(8,128)S(1)}, f32[64,1024]{1,0:T(8,128)S(1)}, bf16[64,1024]{1,0:T(8,128)(2,1)S(1)}) custom-call(s32[4,128]{1,0:T(4,128)} %bitcast.13, bf16[128,5120]{1,0:T(8,128)(2,1)} %hidden_hbm.1, bf16[5120,1024]{1,0:T(8,128)(2,1)} %weight_hbm.1, bf16[128,1024]{1,0:T(8,128)(2,1)} %residual_hbm.1), custom_call_target="tpu_custom_call" | custom-call | flops 1509949440 | bytes 11796480 | tf_op jit(solution)/shard_map/pallas_call | solution.py:128
  5.8 0.1 collective-permute-start.1
  5.9 0.0 collective-permute-done.refs_10_
  6.0 1.5 %collective-permute-done.1 = f32[64,1024]{1,0:T(8,128)S(1)} collective-permute-done((f32[64,1024]{1,0:T(8,128)S(1)}, f32[64,1024]{1,0:T(8,128)S(1)}, u32[]{:S(2)}, u32[]{:S(2)}) %collective-permute-start.1) | collective-permute-done | bytes 262176 | tf_op jit(solution)/shard_map/ppermute | solution.py:24
  7.5 3.7 %collective-permute-start.2 = (bf16[16,1024]{1,0:T(8,128)(2,1)S(1)}, bf16[16,1024]{1,0:T(8,128)(2,1)S(1)}, u32[]{:S(2)}, u32[]{:S(2)}) collective-permute-start(bf16[16,1024]{1,0:T(8,128)(2,1)S(1)} %get-tuple-element.18), channel_id=1, source_target_pairs={{0,24},{1,25},{8,16},{9,17},{16,8},{17,9},{24,0},{25,1},{2,26},{3,... | collective-permute-start | bytes 98312 | tf_op jit(solution)/shard_map/ppermute | solution.py:56
  11.2 0.5 %collective-permute-start.6 = (bf16[32,1024]{1,0:T(8,128)(2,1)S(1)}, bf16[32,1024]{1,0:T(8,128)(2,1)S(1)}, u32[]{:S(2)}, u32[]{:S(2)}) collective-permute-start(bf16[32,1024]{1,0:T(8,128)(2,1)S(1)} %slice.14), channel_id=1, source_target_pairs={{0,8},{1,17},{8,0},{9,25},{16,24},{17,1},{24,16},{25,9},{2,10},{3,... | collective-permute-start | bytes 196616 | tf_op jit(solution)/shard_map/ppermute | solution.py:56
  11.7 1.4 %collective-permute-done.2 = bf16[16,1024]{1,0:T(8,128)(2,1)S(1)} collective-permute-done((bf16[16,1024]{1,0:T(8,128)(2,1)S(1)}, bf16[16,1024]{1,0:T(8,128)(2,1)S(1)}, u32[]{:S(2)}, u32[]{:S(2)}) %collective-permute-start.2) | collective-permute-done | bytes 32800 | tf_op jit(solution)/shard_map/ppermute | solution.py:56
  13.1 3.0 %collective-permute-start.4 = (bf16[32,1024]{1,0:T(8,128)(2,1)S(1)}, bf16[32,1024]{1,0:T(8,128)(2,1)S(1)}, u32[]{:S(2)}, u32[]{:S(2)}) collective-permute-start(bf16[32,1024]{1,0:T(8,128)(2,1)S(1)} %pad_maximum_fusion.2.refs_0_), channel_id=1, source_target_pairs={{0,4},{2,6},{4,0},{6,2},{1,5},{3,7},{5,1},{7,3},{8,12},{10,14},{12... | collective-permute-start | bytes 196616 | tf_op jit(solution)/shard_map/ppermute | solution.py:24
  16.1 0.0 collective-permute-done.6.refs_4_
  16.1 1.9 %collective-permute-start.8 = (bf16[32,1024]{1,0:T(8,128)(2,1)S(1)}, bf16[32,1024]{1,0:T(8,128)(2,1)S(1)}, u32[]{:S(2)}, u32[]{:S(2)}) collective-permute-start(bf16[32,1024]{1,0:T(8,128)(2,1)S(1)} %collective-permute-done.6.refs_4_), channel_id=1, source_target_pairs={{0,4},{2,6},{4,0},{6,2},{1,5},{3,7},{5,1},{7,3},{8,12},{10,14},{12... | collective-permute-start | bytes 196616 | tf_op jit(solution)/shard_map/ppermute | solution.py:24
  18.0 1.6 %collective-permute-start.3 = (bf16[32,1024]{1,0:T(8,128)(2,1)S(1)}, bf16[32,1024]{1,0:T(8,128)(2,1)S(1)}, u32[]{:S(2)}, u32[]{:S(2)}) collective-permute-start(bf16[32,1024]{1,0:T(8,128)(2,1)S(1)} %pad_maximum_fusion.2.refs_0_), channel_id=1, source_target_pairs={{0,2},{2,0},{4,6},{6,4},{1,3},{3,1},{5,7},{7,5},{8,10},{10,8},{12,... | collective-permute-start | bytes 196616 | tf_op jit(solution)/shard_map/ppermute | solution.py:24
  19.6 0.5 %collective-permute-start.7 = (bf16[32,1024]{1,0:T(8,128)(2,1)S(1)}, bf16[32,1024]{1,0:T(8,128)(2,1)S(1)}, u32[]{:S(2)}, u32[]{:S(2)}) collective-permute-start(bf16[32,1024]{1,0:T(8,128)(2,1)S(1)} %collective-permute-done.6.refs_4_), channel_id=1, source_target_pairs={{0,2},{2,0},{4,6},{6,4},{1,3},{3,1},{5,7},{7,5},{8,10},{10,8},{12,... | collective-permute-start | bytes 196616 | tf_op jit(solution)/shard_map/ppermute | solution.py:24
  20.0 0.0 collective-permute-done.4.refs_2_
  20.0 1.9 %collective-permute-start.5 = (bf16[32,1024]{1,0:T(8,128)(2,1)S(1)}, bf16[32,1024]{1,0:T(8,128)(2,1)S(1)}, u32[]{:S(2)}, u32[]{:S(2)}) collective-permute-start(bf16[32,1024]{1,0:T(8,128)(2,1)S(1)} %collective-permute-done.4.refs_2_), channel_id=1, source_target_pairs={{0,2},{2,0},{4,6},{6,4},{1,3},{3,1},{5,7},{7,5},{8,10},{10,8},{12,... | collective-permute-start | bytes 196616 | tf_op jit(solution)/shard_map/ppermute | solution.py:24
  22.0 0.0 collective-permute-done.8.refs_6_
  22.0 1.6 %collective-permute-start.9 = (bf16[32,1024]{1,0:T(8,128)(2,1)S(1)}, bf16[32,1024]{1,0:T(8,128)(2,1)S(1)}, u32[]{:S(2)}, u32[]{:S(2)}) collective-permute-start(bf16[32,1024]{1,0:T(8,128)(2,1)S(1)} %collective-permute-done.8.refs_6_), channel_id=1, source_target_pairs={{0,2},{2,0},{4,6},{6,4},{1,3},{3,1},{5,7},{7,5},{8,10},{10,8},{12,... | collective-permute-start | bytes 196616 | tf_op jit(solution)/shard_map/ppermute | solution.py:24
  23.6 0.0 collective-permute-done.3.refs_1_
  23.6 1.0 %collective-permute-done.7.refs_5_ = bf16[32,1024]{1,0:T(8,128)(2,1)S(1)} collective-permute-done((bf16[32,1024]{1,0:T(8,128)(2,1)S(1)}, bf16[32,1024]{1,0:T(8,128)(2,1)S(1)}, u32[]{:S(2)}, u32[]{:S(2)}) %collective-permute-start.7) | collective-permute-done | bytes 65568 | tf_op jit(solution)/shard_map/ppermute | solution.py:24
  24.6 1.0 %collective-permute-done.5.refs_3_ = bf16[32,1024]{1,0:T(8,128)(2,1)S(1)} collective-permute-done((bf16[32,1024]{1,0:T(8,128)(2,1)S(1)}, bf16[32,1024]{1,0:T(8,128)(2,1)S(1)}, u32[]{:S(2)}, u32[]{:S(2)}) %collective-permute-start.5) | collective-permute-done | bytes 65568 | tf_op jit(solution)/shard_map/ppermute | solution.py:24
  25.7 0.7 %collective-permute-done.9.refs_7_ = bf16[32,1024]{1,0:T(8,128)(2,1)S(1)} collective-permute-done((bf16[32,1024]{1,0:T(8,128)(2,1)S(1)}, bf16[32,1024]{1,0:T(8,128)(2,1)S(1)}, u32[]{:S(2)}, u32[]{:S(2)}) %collective-permute-start.9) | collective-permute-done | bytes 65568 | tf_op jit(solution)/shard_map/ppermute | solution.py:24
  26.4 0.0 copy-done
  26.4 0.0 copy-done.3
  26.4 0.0 copy-start.1
  26.4 0.0 copy-start.2
  26.4 0.9 %shard_map.74.refs_0_ = bf16[64,512]{1,0:T(8,128)(2,1)S(1)} custom-call(bf16[32,1024]{1,0:T(8,128)(2,1)S(1)} %pad_maximum_fusion.2.refs_0_, bf16[32,1024]{1,0:T(8,128)(2,1)S(1)} %collective-permute-done.3.refs_1_, bf16[32,1024]{1,0:T(8,128)(2,1)S(1)} %collective-permute-done.4.refs_2_, bf16[32,1024]{1,0:T(8,128)(2,1)S(1)} %collective-permute-done.5.refs_3_, ...), custom_call_target="tpu_custom_call" | custom-call | flops 268435456 | bytes 4718592 | tf_op jit(solution)/shard_map/pallas_call | solution.py:251
  27.3 3.6 %collective-permute-start.13 = (bf16[64,512]{1,0:T(8,128)(2,1)S(1)}, bf16[64,512]{1,0:T(8,128)(2,1)S(1)}, u32[]{:S(2)}, u32[]{:S(2)}) collective-permute-start(bf16[64,512]{1,0:T(8,128)(2,1)S(1)} %shard_map.74.refs_0_), channel_id=1, source_target_pairs={{0,6},{2,4},{4,2},{6,0},{1,7},{3,5},{5,3},{7,1},{8,14},{10,12},{12... | collective-permute-start | bytes 196616 | tf_op jit(solution)/shard_map/ppermute | solution.py:24
  30.9 0.0 collective-permute-start.11
  30.9 0.8 %collective-permute-start.10 = (bf16[64,512]{1,0:T(8,128)(2,1)S(1)}, bf16[64,512]{1,0:T(8,128)(2,1)S(1)}, u32[]{:S(2)}, u32[]{:S(2)}) collective-permute-start(bf16[64,512]{1,0:T(8,128)(2,1)S(1)} %shard_map.74.refs_0_), channel_id=1, source_target_pairs={{0,2},{2,0},{4,6},{6,4},{1,3},{3,1},{5,7},{7,5},{8,10},{10,8},{12,... | collective-permute-start | bytes 196616 | tf_op jit(solution)/shard_map/ppermute | solution.py:24
  31.8 1.8 %collective-permute-done.13.refs_1_ = bf16[64,512]{1,0:T(8,128)(2,1)S(1)} collective-permute-done((bf16[64,512]{1,0:T(8,128)(2,1)S(1)}, bf16[64,512]{1,0:T(8,128)(2,1)S(1)}, u32[]{:S(2)}, u32[]{:S(2)}) %collective-permute-start.13) | collective-permute-done | bytes 65568 | tf_op jit(solution)/shard_map/ppermute | solution.py:24
  33.6 0.1 collective-permute-start.14
  33.6 3.0 %collective-permute-done.11.refs_1_ = bf16[64,512]{1,0:T(8,128)(2,1)S(1)} collective-permute-done((bf16[64,512]{1,0:T(8,128)(2,1)S(1)}, bf16[64,512]{1,0:T(8,128)(2,1)S(1)}, u32[]{:S(2)}, u32[]{:S(2)}) %collective-permute-start.11) | collective-permute-done | bytes 65568 | tf_op jit(solution)/shard_map/ppermute | solution.py:24
  36.7 0.0 collective-permute-done.10.refs_0_
  36.7 0.1 collective-permute-start.12
  36.8 0.0 collective-permute-done.14.refs_2_
  36.8 0.0 copy-done.1
  36.8 0.0 copy-done.2
  36.8 0.5 %shard_map.75.refs_3_ = bf16[128,1024]{1,0:T(8,128)(2,1)S(1)} custom-call(s32[4,128]{1,0:T(4,128)S(1)} %bitcast.14, bf16[128,1024]{1,0:T(8,128)(2,1)S(1)} %copy-done.1, bf16[64,512]{1,0:T(8,128)(2,1)S(1)} %shard_map.74.refs_0_, bf16[64,512]{1,0:T(8,128)(2,1)S(1)} %collective-permute-done.13.refs_1_, bf16[2,64,512]{2,1,0:T(8,128)(2,1)S(1)} %collective-permute-done.14.refs_2_), custom_call_target="tpu_custom_call" | custom-call | tf_op jit(solution)/shard_map/pallas_call | solution.py:300
  37.3 0.8 %collective-permute-done.12.refs_2_ = bf16[2,64,512]{2,1,0:T(8,128)(2,1)S(1)} collective-permute-done((bf16[2,64,512]{2,1,0:T(8,128)(2,1)S(1)}, bf16[2,64,512]{2,1,0:T(8,128)(2,1)S(1)}, u32[]{:S(2)}, u32[]{:S(2)}) %collective-permute-start.12) | collective-permute-done | bytes 131104 | tf_op jit(solution)/shard_map/ppermute | solution.py:24
  38.1 1.2 %shard_map.76 = bf16[128,1024]{1,0:T(8,128)(2,1)} custom-call(s32[4,128]{1,0:T(4,128)S(1)} %bitcast.15, bf16[128,1024]{1,0:T(8,128)(2,1)S(1)} %copy-done.1, bf16[64,512]{1,0:T(8,128)(2,1)S(1)} %collective-permute-done.10.refs_0_, bf16[64,512]{1,0:T(8,128)(2,1)S(1)} %collective-permute-done.11.refs_1_, ...), custom_call_target="tpu_custom_call" | custom-call | tf_op jit(solution)/shard_map/pallas_call | solution.py:300
  (6 shorter events, 0.1 us)
Async XLA Ops:
  0.0 6.0 %collective-permute-start = (bf16[4096,256]{1,0:T(8,128)(2,1)}, bf16[4096,256]{1,0:T(8,128)(2,1)S(1)}, u32[]{:S(2)}, u32[]{:S(2)}) collective-permute-start(bf16[4096,256]{1,0:T(8,128)(2,1)} %bitcast.7), channel_id=1, source_target_pairs={{0,1},{1,0},{2,3},{3,2},{4,5},{5,4},{6,7},{7,6},{8,9},{9,8},{10,11... | collective-permute-start | bytes 6291464 | tf_op jit(solution)/shard_map/ppermute | solution.py:24
  0.5 25.9 %copy-start = (bf16[4096,1,256]{2,0,1:T(8,128)(2,1)S(1)}, bf16[4096,1,256]{2,0,1:T(8,128)(2,1)}, u32[]{:S(2)}) copy-start(bf16[4096,1,256]{2,0,1:T(8,128)(2,1)} %param.11) | copy-start | bytes 6291460
  0.5 25.9 %copy-start.3 = (f32[4096]{0:T(1024)S(1)}, f32[4096]{0:T(1024)}, u32[]{:S(2)}) copy-start(f32[4096]{0:T(1024)} %param.10) | copy-start | bytes 49156
  5.8 1.6 %collective-permute-start.1 = (f32[64,1024]{1,0:T(8,128)S(1)}, f32[64,1024]{1,0:T(8,128)S(1)}, u32[]{:S(2)}, u32[]{:S(2)}) collective-permute-start(f32[64,1024]{1,0:T(8,128)S(1)} %get-tuple-element.14), channel_id=1, source_target_pairs={{0,1},{1,0},{2,3},{3,2},{4,5},{5,4},{6,7},{7,6},{8,9},{9,8},{10,11... | collective-permute-start | bytes 786440 | tf_op jit(solution)/shard_map/ppermute | solution.py:24
  7.5 5.6 %collective-permute-start.2 = (bf16[16,1024]{1,0:T(8,128)(2,1)S(1)}, bf16[16,1024]{1,0:T(8,128)(2,1)S(1)}, u32[]{:S(2)}, u32[]{:S(2)}) collective-permute-start(bf16[16,1024]{1,0:T(8,128)(2,1)S(1)} %get-tuple-element.18), channel_id=1, source_target_pairs={{0,24},{1,25},{8,16},{9,17},{16,8},{17,9},{24,0},{25,1},{2,26},{3,... | collective-permute-start | bytes 98312 | tf_op jit(solution)/shard_map/ppermute | solution.py:56
  11.2 5.0 %collective-permute-start.6 = (bf16[32,1024]{1,0:T(8,128)(2,1)S(1)}, bf16[32,1024]{1,0:T(8,128)(2,1)S(1)}, u32[]{:S(2)}, u32[]{:S(2)}) collective-permute-start(bf16[32,1024]{1,0:T(8,128)(2,1)S(1)} %slice.14), channel_id=1, source_target_pairs={{0,8},{1,17},{8,0},{9,25},{16,24},{17,1},{24,16},{25,9},{2,10},{3,... | collective-permute-start | bytes 196616 | tf_op jit(solution)/shard_map/ppermute | solution.py:56
  13.1 7.0 %collective-permute-start.4 = (bf16[32,1024]{1,0:T(8,128)(2,1)S(1)}, bf16[32,1024]{1,0:T(8,128)(2,1)S(1)}, u32[]{:S(2)}, u32[]{:S(2)}) collective-permute-start(bf16[32,1024]{1,0:T(8,128)(2,1)S(1)} %pad_maximum_fusion.2.refs_0_), channel_id=1, source_target_pairs={{0,4},{2,6},{4,0},{6,2},{1,5},{3,7},{5,1},{7,3},{8,12},{10,14},{12... | collective-permute-start | bytes 196616 | tf_op jit(solution)/shard_map/ppermute | solution.py:24
  16.1 5.9 %collective-permute-start.8 = (bf16[32,1024]{1,0:T(8,128)(2,1)S(1)}, bf16[32,1024]{1,0:T(8,128)(2,1)S(1)}, u32[]{:S(2)}, u32[]{:S(2)}) collective-permute-start(bf16[32,1024]{1,0:T(8,128)(2,1)S(1)} %collective-permute-done.6.refs_4_), channel_id=1, source_target_pairs={{0,4},{2,6},{4,0},{6,2},{1,5},{3,7},{5,1},{7,3},{8,12},{10,14},{12... | collective-permute-start | bytes 196616 | tf_op jit(solution)/shard_map/ppermute | solution.py:24
  18.0 5.6 %collective-permute-start.3 = (bf16[32,1024]{1,0:T(8,128)(2,1)S(1)}, bf16[32,1024]{1,0:T(8,128)(2,1)S(1)}, u32[]{:S(2)}, u32[]{:S(2)}) collective-permute-start(bf16[32,1024]{1,0:T(8,128)(2,1)S(1)} %pad_maximum_fusion.2.refs_0_), channel_id=1, source_target_pairs={{0,2},{2,0},{4,6},{6,4},{1,3},{3,1},{5,7},{7,5},{8,10},{10,8},{12,... | collective-permute-start | bytes 196616 | tf_op jit(solution)/shard_map/ppermute | solution.py:24
  19.6 5.0 %collective-permute-start.7 = (bf16[32,1024]{1,0:T(8,128)(2,1)S(1)}, bf16[32,1024]{1,0:T(8,128)(2,1)S(1)}, u32[]{:S(2)}, u32[]{:S(2)}) collective-permute-start(bf16[32,1024]{1,0:T(8,128)(2,1)S(1)} %collective-permute-done.6.refs_4_), channel_id=1, source_target_pairs={{0,2},{2,0},{4,6},{6,4},{1,3},{3,1},{5,7},{7,5},{8,10},{10,8},{12,... | collective-permute-start | bytes 196616 | tf_op jit(solution)/shard_map/ppermute | solution.py:24
  20.0 5.6 %collective-permute-start.5 = (bf16[32,1024]{1,0:T(8,128)(2,1)S(1)}, bf16[32,1024]{1,0:T(8,128)(2,1)S(1)}, u32[]{:S(2)}, u32[]{:S(2)}) collective-permute-start(bf16[32,1024]{1,0:T(8,128)(2,1)S(1)} %collective-permute-done.4.refs_2_), channel_id=1, source_target_pairs={{0,2},{2,0},{4,6},{6,4},{1,3},{3,1},{5,7},{7,5},{8,10},{10,8},{12,... | collective-permute-start | bytes 196616 | tf_op jit(solution)/shard_map/ppermute | solution.py:24
  22.0 4.4 %collective-permute-start.9 = (bf16[32,1024]{1,0:T(8,128)(2,1)S(1)}, bf16[32,1024]{1,0:T(8,128)(2,1)S(1)}, u32[]{:S(2)}, u32[]{:S(2)}) collective-permute-start(bf16[32,1024]{1,0:T(8,128)(2,1)S(1)} %collective-permute-done.8.refs_6_), channel_id=1, source_target_pairs={{0,2},{2,0},{4,6},{6,4},{1,3},{3,1},{5,7},{7,5},{8,10},{10,8},{12,... | collective-permute-start | bytes 196616 | tf_op jit(solution)/shard_map/ppermute | solution.py:24
  26.4 10.4 %copy-start.1 = (bf16[128,1024]{1,0:T(8,128)(2,1)S(1)}, bf16[128,1024]{1,0:T(8,128)(2,1)}, u32[]{:S(2)}) copy-start(bf16[128,1024]{1,0:T(8,128)(2,1)} %query_ref.3) | copy-start | bytes 786436
  26.4 10.4 %copy-start.2 = (s32[512,1]{0,1:T(1,128)S(1)}, s32[512,1]{0,1:T(1,128)}, u32[]{:S(2)}) copy-start(s32[512,1]{0,1:T(1,128)} %param.12) | copy-start | bytes 6148
  27.3 6.2 %collective-permute-start.13 = (bf16[64,512]{1,0:T(8,128)(2,1)S(1)}, bf16[64,512]{1,0:T(8,128)(2,1)S(1)}, u32[]{:S(2)}, u32[]{:S(2)}) collective-permute-start(bf16[64,512]{1,0:T(8,128)(2,1)S(1)} %shard_map.74.refs_0_), channel_id=1, source_target_pairs={{0,6},{2,4},{4,2},{6,0},{1,7},{3,5},{5,3},{7,1},{8,14},{10,12},{12... | collective-permute-start | bytes 196616 | tf_op jit(solution)/shard_map/ppermute | solution.py:24
  30.9 5.7 %collective-permute-start.11 = (bf16[64,512]{1,0:T(8,128)(2,1)S(1)}, bf16[64,512]{1,0:T(8,128)(2,1)S(1)}, u32[]{:S(2)}, u32[]{:S(2)}) collective-permute-start(bf16[64,512]{1,0:T(8,128)(2,1)S(1)} %shard_map.74.refs_0_), channel_id=1, source_target_pairs={{0,4},{2,6},{4,0},{6,2},{1,5},{3,7},{5,1},{7,3},{8,12},{10,14},{12... | collective-permute-start | bytes 196616 | tf_op jit(solution)/shard_map/ppermute | solution.py:24
  30.9 5.7 %collective-permute-start.10 = (bf16[64,512]{1,0:T(8,128)(2,1)S(1)}, bf16[64,512]{1,0:T(8,128)(2,1)S(1)}, u32[]{:S(2)}, u32[]{:S(2)}) collective-permute-start(bf16[64,512]{1,0:T(8,128)(2,1)S(1)} %shard_map.74.refs_0_), channel_id=1, source_target_pairs={{0,2},{2,0},{4,6},{6,4},{1,3},{3,1},{5,7},{7,5},{8,10},{10,8},{12,... | collective-permute-start | bytes 196616 | tf_op jit(solution)/shard_map/ppermute | solution.py:24
  33.6 3.2 %collective-permute-start.14 = (bf16[2,64,512]{2,1,0:T(8,128)(2,1)S(1)}, bf16[2,64,512]{2,1,0:T(8,128)(2,1)S(1)}, u32[]{:S(2)}, u32[]{:S(2)}) collective-permute-start(bf16[2,64,512]{2,1,0:T(8,128)(2,1)S(1)} %pad_maximum_fusion.1), channel_id=1, source_target_pairs={{0,1},{1,0},{2,3},{3,2},{4,5},{5,4},{6,7},{7,6},{8,9},{9,8},{10,11... | collective-permute-start | bytes 393224 | tf_op jit(solution)/shard_map/ppermute | solution.py:24
  36.7 1.4 %collective-permute-start.12 = (bf16[2,64,512]{2,1,0:T(8,128)(2,1)S(1)}, bf16[2,64,512]{2,1,0:T(8,128)(2,1)S(1)}, u32[]{:S(2)}, u32[]{:S(2)}) collective-permute-start(bf16[2,64,512]{2,1,0:T(8,128)(2,1)S(1)} %pad_maximum_fusion), channel_id=1, source_target_pairs={{0,1},{1,0},{2,3},{3,2},{4,5},{5,4},{6,7},{7,6},{8,9},{9,8},{10,11... | collective-permute-start | bytes 393224 | tf_op jit(solution)/shard_map/ppermute | solution.py:24

commit v17 on v16

--- a/solution.py
+++ b/solution.py
@@ -305,10 +305,10 @@
             compiler_params=pltpu.CompilerParams(vmem_limit_bytes=VMEM_LIMIT),
         )(dest, queries, *some, *others, *done)
 
-    order = [0] + list(range(parts - 1, 0, -1))
-    cut = max(1, parts // 2)
-    output = attend(order[:cut], [])
-    return attend(order[:cut - 1:-1], [output]) if order[cut:] else output
+    soon = sorted({0, parts // 2})
+    late = [k for k in range(parts) if k not in soon]
+    output = attend(soon, [])
+    return attend(late, [output]) if late else output
 
 
 def solution(mesh):

time: 39.5 us -> 39.7 us (level)
  waiting for transfers between devices: 11.2 us -> 11.6 us
    ppermute x13, waiting for transfers between devices: 9.81 us -> 10.3 us  [swap(): return lax.ppermute(value, axis, [(i, i ^ offset) for i in range(size)])]
where the time goes in v17:
time: 39.7 us; the launch traced here: 39.5 us
  starting transfers between devices  19.6 us (49%)
  waiting for transfers between devices  11.6 us (29%)
  Pallas kernels  8.04 us (20%)
    ppermute x13, starting transfers between devices, swap(): return lax.ppermute(value, axis, [(i, i ^ offset) for i in range(size)])  15.4 us
    ppermute x13, waiting for transfers between devices, swap(): return lax.ppermute(value, axis, [(i, i ^ offset) for i in range(size)])  10.3 us
    pallas_call x1, Pallas kernels, ffn(): pl.pallas_call(functools.partial(ffn_kernel, capacity, cores, edges), in_...  5.36 us
    ppermute x2, starting transfers between devices, route(): moved = lax.ppermute(value, ('clip', 'tp'), pairs)  4.19 us
    pallas_call x2, Pallas kernels, attend(): pl.pallas_call(functools.partial(attend_kernel, parts, cores, heads_here,...  1.74 us
    ppermute x2, waiting for transfers between devices, route(): moved = lax.ppermute(value, ('clip', 'tp'), pairs)  1.38 us
    pallas_call x1, Pallas kernels, keyval(): pl.pallas_call(functools.partial(keyval_kernel, parts, groups), in_specs=...  0.94 us
  transfers between devices with their start and end apart: 15, of which 8 were waited for; matrix products, arithmetic and copies ran while one was open for 0% of the time, Pallas kernels for 15%

profile of v17, /device:TPU:0, one launch (start us, length us, event | category | flops | bytes accessed | tf_op | source)
XLA Modules:
  0.0 39.5 jit_solution(14211559793420820204)
XLA Ops:
  0.0 0.5 %collective-permute-start = (bf16[4096,256]{1,0:T(8,128)(2,1)}, bf16[4096,256]{1,0:T(8,128)(2,1)S(1)}, u32[]{:S(2)}, u32[]{:S(2)}) collective-permute-start(bf16[4096,256]{1,0:T(8,128)(2,1)} %bitcast.7), channel_id=1, source_target_pairs={{0,1},{1,0},{2,3},{3,2},{4,5},{5,4},{6,7},{7,6},{8,9},{9,8},{10,11... | collective-permute-start | bytes 6291464 | tf_op jit(solution)/shard_map/ppermute | solution.py:24
  0.5 0.0 copy-start
  0.5 0.0 copy-start.3
  0.5 5.4 %shard_map.73 = (f32[64,1024]{1,0:T(8,128)S(1)}, f32[64,1024]{1,0:T(8,128)S(1)}, bf16[64,1024]{1,0:T(8,128)(2,1)S(1)}) custom-call(s32[4,128]{1,0:T(4,128)} %bitcast.13, bf16[128,5120]{1,0:T(8,128)(2,1)} %hidden_hbm.1, bf16[5120,1024]{1,0:T(8,128)(2,1)} %weight_hbm.1, bf16[128,1024]{1,0:T(8,128)(2,1)} %residual_hbm.1), custom_call_target="tpu_custom_call" | custom-call | flops 1509949440 | bytes 11796480 | tf_op jit(solution)/shard_map/pallas_call | solution.py:128
  5.8 0.1 collective-permute-start.1
  5.9 0.0 collective-permute-done.refs_10_
  6.0 1.5 %collective-permute-done.1 = f32[64,1024]{1,0:T(8,128)S(1)} collective-permute-done((f32[64,1024]{1,0:T(8,128)S(1)}, f32[64,1024]{1,0:T(8,128)S(1)}, u32[]{:S(2)}, u32[]{:S(2)}) %collective-permute-start.1) | collective-permute-done | bytes 262176 | tf_op jit(solution)/shard_map/ppermute | solution.py:24
  7.5 3.7 %collective-permute-start.2 = (bf16[16,1024]{1,0:T(8,128)(2,1)S(1)}, bf16[16,1024]{1,0:T(8,128)(2,1)S(1)}, u32[]{:S(2)}, u32[]{:S(2)}) collective-permute-start(bf16[16,1024]{1,0:T(8,128)(2,1)S(1)} %get-tuple-element.18), channel_id=1, source_target_pairs={{0,24},{1,25},{8,16},{9,17},{16,8},{17,9},{24,0},{25,1},{2,26},{3,... | collective-permute-start | bytes 98312 | tf_op jit(solution)/shard_map/ppermute | solution.py:56
  11.2 0.5 %collective-permute-start.6 = (bf16[32,1024]{1,0:T(8,128)(2,1)S(1)}, bf16[32,1024]{1,0:T(8,128)(2,1)S(1)}, u32[]{:S(2)}, u32[]{:S(2)}) collective-permute-start(bf16[32,1024]{1,0:T(8,128)(2,1)S(1)} %slice.14), channel_id=1, source_target_pairs={{0,8},{1,17},{8,0},{9,25},{16,24},{17,1},{24,16},{25,9},{2,10},{3,... | collective-permute-start | bytes 196616 | tf_op jit(solution)/shard_map/ppermute | solution.py:56
  11.7 1.4 %collective-permute-done.2 = bf16[16,1024]{1,0:T(8,128)(2,1)S(1)} collective-permute-done((bf16[16,1024]{1,0:T(8,128)(2,1)S(1)}, bf16[16,1024]{1,0:T(8,128)(2,1)S(1)}, u32[]{:S(2)}, u32[]{:S(2)}) %collective-permute-start.2) | collective-permute-done | bytes 32800 | tf_op jit(solution)/shard_map/ppermute | solution.py:56
  13.1 3.0 %collective-permute-start.4 = (bf16[32,1024]{1,0:T(8,128)(2,1)S(1)}, bf16[32,1024]{1,0:T(8,128)(2,1)S(1)}, u32[]{:S(2)}, u32[]{:S(2)}) collective-permute-start(bf16[32,1024]{1,0:T(8,128)(2,1)S(1)} %pad_maximum_fusion.2.refs_0_), channel_id=1, source_target_pairs={{0,4},{2,6},{4,0},{6,2},{1,5},{3,7},{5,1},{7,3},{8,12},{10,14},{12... | collective-permute-start | bytes 196616 | tf_op jit(solution)/shard_map/ppermute | solution.py:24
  16.1 0.0 collective-permute-done.6.refs_4_
  16.1 1.9 %collective-permute-start.8 = (bf16[32,1024]{1,0:T(8,128)(2,1)S(1)}, bf16[32,1024]{1,0:T(8,128)(2,1)S(1)}, u32[]{:S(2)}, u32[]{:S(2)}) collective-permute-start(bf16[32,1024]{1,0:T(8,128)(2,1)S(1)} %collective-permute-done.6.refs_4_), channel_id=1, source_target_pairs={{0,4},{2,6},{4,0},{6,2},{1,5},{3,7},{5,1},{7,3},{8,12},{10,14},{12... | collective-permute-start | bytes 196616 | tf_op jit(solution)/shard_map/ppermute | solution.py:24
  18.0 1.6 %collective-permute-start.3 = (bf16[32,1024]{1,0:T(8,128)(2,1)S(1)}, bf16[32,1024]{1,0:T(8,128)(2,1)S(1)}, u32[]{:S(2)}, u32[]{:S(2)}) collective-permute-start(bf16[32,1024]{1,0:T(8,128)(2,1)S(1)} %pad_maximum_fusion.2.refs_0_), channel_id=1, source_target_pairs={{0,2},{2,0},{4,6},{6,4},{1,3},{3,1},{5,7},{7,5},{8,10},{10,8},{12,... | collective-permute-start | bytes 196616 | tf_op jit(solution)/shard_map/ppermute | solution.py:24
  19.6 0.5 %collective-permute-start.7 = (bf16[32,1024]{1,0:T(8,128)(2,1)S(1)}, bf16[32,1024]{1,0:T(8,128)(2,1)S(1)}, u32[]{:S(2)}, u32[]{:S(2)}) collective-permute-start(bf16[32,1024]{1,0:T(8,128)(2,1)S(1)} %collective-permute-done.6.refs_4_), channel_id=1, source_target_pairs={{0,2},{2,0},{4,6},{6,4},{1,3},{3,1},{5,7},{7,5},{8,10},{10,8},{12,... | collective-permute-start | bytes 196616 | tf_op jit(solution)/shard_map/ppermute | solution.py:24
  20.0 0.0 collective-permute-done.4.refs_2_
  20.0 1.9 %collective-permute-start.5 = (bf16[32,1024]{1,0:T(8,128)(2,1)S(1)}, bf16[32,1024]{1,0:T(8,128)(2,1)S(1)}, u32[]{:S(2)}, u32[]{:S(2)}) collective-permute-start(bf16[32,1024]{1,0:T(8,128)(2,1)S(1)} %collective-permute-done.4.refs_2_), channel_id=1, source_target_pairs={{0,2},{2,0},{4,6},{6,4},{1,3},{3,1},{5,7},{7,5},{8,10},{10,8},{12,... | collective-permute-start | bytes 196616 | tf_op jit(solution)/shard_map/ppermute | solution.py:24
  22.0 0.0 collective-permute-done.8.refs_6_
  22.0 1.6 %collective-permute-start.9 = (bf16[32,1024]{1,0:T(8,128)(2,1)S(1)}, bf16[32,1024]{1,0:T(8,128)(2,1)S(1)}, u32[]{:S(2)}, u32[]{:S(2)}) collective-permute-start(bf16[32,1024]{1,0:T(8,128)(2,1)S(1)} %collective-permute-done.8.refs_6_), channel_id=1, source_target_pairs={{0,2},{2,0},{4,6},{6,4},{1,3},{3,1},{5,7},{7,5},{8,10},{10,8},{12,... | collective-permute-start | bytes 196616 | tf_op jit(solution)/shard_map/ppermute | solution.py:24
  23.6 0.0 collective-permute-done.3.refs_1_
  23.6 1.0 %collective-permute-done.7.refs_5_ = bf16[32,1024]{1,0:T(8,128)(2,1)S(1)} collective-permute-done((bf16[32,1024]{1,0:T(8,128)(2,1)S(1)}, bf16[32,1024]{1,0:T(8,128)(2,1)S(1)}, u32[]{:S(2)}, u32[]{:S(2)}) %collective-permute-start.7) | collective-permute-done | bytes 65568 | tf_op jit(solution)/shard_map/ppermute | solution.py:24
  24.6 1.0 %collective-permute-done.5.refs_3_ = bf16[32,1024]{1,0:T(8,128)(2,1)S(1)} collective-permute-done((bf16[32,1024]{1,0:T(8,128)(2,1)S(1)}, bf16[32,1024]{1,0:T(8,128)(2,1)S(1)}, u32[]{:S(2)}, u32[]{:S(2)}) %collective-permute-start.5) | collective-permute-done | bytes 65568 | tf_op jit(solution)/shard_map/ppermute | solution.py:24
  25.7 0.7 %collective-permute-done.9.refs_7_ = bf16[32,1024]{1,0:T(8,128)(2,1)S(1)} collective-permute-done((bf16[32,1024]{1,0:T(8,128)(2,1)S(1)}, bf16[32,1024]{1,0:T(8,128)(2,1)S(1)}, u32[]{:S(2)}, u32[]{:S(2)}) %collective-permute-start.9) | collective-permute-done | bytes 65568 | tf_op jit(solution)/shard_map/ppermute | solution.py:24
  26.4 0.0 copy-done
  26.4 0.0 copy-done.3
  26.4 0.0 copy-start.1
  26.4 0.0 copy-start.2
  26.4 0.9 %shard_map.74.refs_0_ = bf16[64,512]{1,0:T(8,128)(2,1)S(1)} custom-call(bf16[32,1024]{1,0:T(8,128)(2,1)S(1)} %pad_maximum_fusion.2.refs_0_, bf16[32,1024]{1,0:T(8,128)(2,1)S(1)} %collective-permute-done.3.refs_1_, bf16[32,1024]{1,0:T(8,128)(2,1)S(1)} %collective-permute-done.4.refs_2_, bf16[32,1024]{1,0:T(8,128)(2,1)S(1)} %collective-permute-done.5.refs_3_, ...), custom_call_target="tpu_custom_call" | custom-call | flops 268435456 | bytes 4718592 | tf_op jit(solution)/shard_map/pallas_call | solution.py:251
  27.3 3.5 %collective-permute-start.13 = (bf16[64,512]{1,0:T(8,128)(2,1)S(1)}, bf16[64,512]{1,0:T(8,128)(2,1)S(1)}, u32[]{:S(2)}, u32[]{:S(2)}) collective-permute-start(bf16[64,512]{1,0:T(8,128)(2,1)S(1)} %shard_map.74.refs_0_), channel_id=1, source_target_pairs={{0,4},{2,6},{4,0},{6,2},{1,5},{3,7},{5,1},{7,3},{8,12},{10,14},{12... | collective-permute-start | bytes 196616 | tf_op jit(solution)/shard_map/ppermute | solution.py:24
  30.8 0.5 %collective-permute-start.11 = (bf16[64,512]{1,0:T(8,128)(2,1)S(1)}, bf16[64,512]{1,0:T(8,128)(2,1)S(1)}, u32[]{:S(2)}, u32[]{:S(2)}) collective-permute-start(bf16[64,512]{1,0:T(8,128)(2,1)S(1)} %shard_map.74.refs_0_), channel_id=1, source_target_pairs={{0,6},{2,4},{4,2},{6,0},{1,7},{3,5},{5,3},{7,1},{8,14},{10,12},{12... | collective-permute-start | bytes 196616 | tf_op jit(solution)/shard_map/ppermute | solution.py:24
  31.3 0.2 collective-permute-start.10
  31.5 2.9 %collective-permute-done.13.refs_1_ = bf16[64,512]{1,0:T(8,128)(2,1)S(1)} collective-permute-done((bf16[64,512]{1,0:T(8,128)(2,1)S(1)}, bf16[64,512]{1,0:T(8,128)(2,1)S(1)}, u32[]{:S(2)}, u32[]{:S(2)}) %collective-permute-start.13) | collective-permute-done | bytes 65568 | tf_op jit(solution)/shard_map/ppermute | solution.py:24
  34.5 0.1 collective-permute-start.14
  34.5 2.3 %collective-permute-done.11.refs_1_ = bf16[64,512]{1,0:T(8,128)(2,1)S(1)} collective-permute-done((bf16[64,512]{1,0:T(8,128)(2,1)S(1)}, bf16[64,512]{1,0:T(8,128)(2,1)S(1)}, u32[]{:S(2)}, u32[]{:S(2)}) %collective-permute-start.11) | collective-permute-done | bytes 65568 | tf_op jit(solution)/shard_map/ppermute | solution.py:24
  36.9 0.0 collective-permute-done.10.refs_0_
  36.9 0.1 collective-permute-start.12
  37.0 0.0 collective-permute-done.14.refs_2_
  37.0 0.0 copy-done.1
  37.0 0.0 copy-done.2
  37.0 0.5 %shard_map.75.refs_3_ = bf16[128,1024]{1,0:T(8,128)(2,1)S(1)} custom-call(s32[4,128]{1,0:T(4,128)S(1)} %bitcast.14, bf16[128,1024]{1,0:T(8,128)(2,1)S(1)} %copy-done.1, bf16[64,512]{1,0:T(8,128)(2,1)S(1)} %shard_map.74.refs_0_, bf16[64,512]{1,0:T(8,128)(2,1)S(1)} %collective-permute-done.13.refs_1_, bf16[2,64,512]{2,1,0:T(8,128)(2,1)S(1)} %collective-permute-done.14.refs_2_), custom_call_target="tpu_custom_call" | custom-call | tf_op jit(solution)/shard_map/pallas_call | solution.py:300
  37.5 0.8 %collective-permute-done.12.refs_2_ = bf16[2,64,512]{2,1,0:T(8,128)(2,1)S(1)} collective-permute-done((bf16[2,64,512]{2,1,0:T(8,128)(2,1)S(1)}, bf16[2,64,512]{2,1,0:T(8,128)(2,1)S(1)}, u32[]{:S(2)}, u32[]{:S(2)}) %collective-permute-start.12) | collective-permute-done | bytes 131104 | tf_op jit(solution)/shard_map/ppermute | solution.py:24
  38.3 1.2 %shard_map.76 = bf16[128,1024]{1,0:T(8,128)(2,1)} custom-call(s32[4,128]{1,0:T(4,128)S(1)} %bitcast.15, bf16[128,1024]{1,0:T(8,128)(2,1)S(1)} %copy-done.1, bf16[64,512]{1,0:T(8,128)(2,1)S(1)} %collective-permute-done.10.refs_0_, bf16[64,512]{1,0:T(8,128)(2,1)S(1)} %collective-permute-done.11.refs_1_, ...), custom_call_target="tpu_custom_call" | custom-call | tf_op jit(solution)/shard_map/pallas_call | solution.py:300
  (6 shorter events, 0.1 us)
Async XLA Ops:
  0.0 6.0 %collective-permute-start = (bf16[4096,256]{1,0:T(8,128)(2,1)}, bf16[4096,256]{1,0:T(8,128)(2,1)S(1)}, u32[]{:S(2)}, u32[]{:S(2)}) collective-permute-start(bf16[4096,256]{1,0:T(8,128)(2,1)} %bitcast.7), channel_id=1, source_target_pairs={{0,1},{1,0},{2,3},{3,2},{4,5},{5,4},{6,7},{7,6},{8,9},{9,8},{10,11... | collective-permute-start | bytes 6291464 | tf_op jit(solution)/shard_map/ppermute | solution.py:24
  0.5 25.9 %copy-start = (bf16[4096,1,256]{2,0,1:T(8,128)(2,1)S(1)}, bf16[4096,1,256]{2,0,1:T(8,128)(2,1)}, u32[]{:S(2)}) copy-start(bf16[4096,1,256]{2,0,1:T(8,128)(2,1)} %param.11) | copy-start | bytes 6291460
  0.5 25.9 %copy-start.3 = (f32[4096]{0:T(1024)S(1)}, f32[4096]{0:T(1024)}, u32[]{:S(2)}) copy-start(f32[4096]{0:T(1024)} %param.10) | copy-start | bytes 49156
  5.8 1.6 %collective-permute-start.1 = (f32[64,1024]{1,0:T(8,128)S(1)}, f32[64,1024]{1,0:T(8,128)S(1)}, u32[]{:S(2)}, u32[]{:S(2)}) collective-permute-start(f32[64,1024]{1,0:T(8,128)S(1)} %get-tuple-element.14), channel_id=1, source_target_pairs={{0,1},{1,0},{2,3},{3,2},{4,5},{5,4},{6,7},{7,6},{8,9},{9,8},{10,11... | collective-permute-start | bytes 786440 | tf_op jit(solution)/shard_map/ppermute | solution.py:24
  7.5 5.6 %collective-permute-start.2 = (bf16[16,1024]{1,0:T(8,128)(2,1)S(1)}, bf16[16,1024]{1,0:T(8,128)(2,1)S(1)}, u32[]{:S(2)}, u32[]{:S(2)}) collective-permute-start(bf16[16,1024]{1,0:T(8,128)(2,1)S(1)} %get-tuple-element.18), channel_id=1, source_target_pairs={{0,24},{1,25},{8,16},{9,17},{16,8},{17,9},{24,0},{25,1},{2,26},{3,... | collective-permute-start | bytes 98312 | tf_op jit(solution)/shard_map/ppermute | solution.py:56
  11.2 5.0 %collective-permute-start.6 = (bf16[32,1024]{1,0:T(8,128)(2,1)S(1)}, bf16[32,1024]{1,0:T(8,128)(2,1)S(1)}, u32[]{:S(2)}, u32[]{:S(2)}) collective-permute-start(bf16[32,1024]{1,0:T(8,128)(2,1)S(1)} %slice.14), channel_id=1, source_target_pairs={{0,8},{1,17},{8,0},{9,25},{16,24},{17,1},{24,16},{25,9},{2,10},{3,... | collective-permute-start | bytes 196616 | tf_op jit(solution)/shard_map/ppermute | solution.py:56
  13.1 7.0 %collective-permute-start.4 = (bf16[32,1024]{1,0:T(8,128)(2,1)S(1)}, bf16[32,1024]{1,0:T(8,128)(2,1)S(1)}, u32[]{:S(2)}, u32[]{:S(2)}) collective-permute-start(bf16[32,1024]{1,0:T(8,128)(2,1)S(1)} %pad_maximum_fusion.2.refs_0_), channel_id=1, source_target_pairs={{0,4},{2,6},{4,0},{6,2},{1,5},{3,7},{5,1},{7,3},{8,12},{10,14},{12... | collective-permute-start | bytes 196616 | tf_op jit(solution)/shard_map/ppermute | solution.py:24
  16.1 5.9 %collective-permute-start.8 = (bf16[32,1024]{1,0:T(8,128)(2,1)S(1)}, bf16[32,1024]{1,0:T(8,128)(2,1)S(1)}, u32[]{:S(2)}, u32[]{:S(2)}) collective-permute-start(bf16[32,1024]{1,0:T(8,128)(2,1)S(1)} %collective-permute-done.6.refs_4_), channel_id=1, source_target_pairs={{0,4},{2,6},{4,0},{6,2},{1,5},{3,7},{5,1},{7,3},{8,12},{10,14},{12... | collective-permute-start | bytes 196616 | tf_op jit(solution)/shard_map/ppermute | solution.py:24
  18.0 5.6 %collective-permute-start.3 = (bf16[32,1024]{1,0:T(8,128)(2,1)S(1)}, bf16[32,1024]{1,0:T(8,128)(2,1)S(1)}, u32[]{:S(2)}, u32[]{:S(2)}) collective-permute-start(bf16[32,1024]{1,0:T(8,128)(2,1)S(1)} %pad_maximum_fusion.2.refs_0_), channel_id=1, source_target_pairs={{0,2},{2,0},{4,6},{6,4},{1,3},{3,1},{5,7},{7,5},{8,10},{10,8},{12,... | collective-permute-start | bytes 196616 | tf_op jit(solution)/shard_map/ppermute | solution.py:24
  19.6 5.0 %collective-permute-start.7 = (bf16[32,1024]{1,0:T(8,128)(2,1)S(1)}, bf16[32,1024]{1,0:T(8,128)(2,1)S(1)}, u32[]{:S(2)}, u32[]{:S(2)}) collective-permute-start(bf16[32,1024]{1,0:T(8,128)(2,1)S(1)} %collective-permute-done.6.refs_4_), channel_id=1, source_target_pairs={{0,2},{2,0},{4,6},{6,4},{1,3},{3,1},{5,7},{7,5},{8,10},{10,8},{12,... | collective-permute-start | bytes 196616 | tf_op jit(solution)/shard_map/ppermute | solution.py:24
  20.0 5.6 %collective-permute-start.5 = (bf16[32,1024]{1,0:T(8,128)(2,1)S(1)}, bf16[32,1024]{1,0:T(8,128)(2,1)S(1)}, u32[]{:S(2)}, u32[]{:S(2)}) collective-permute-start(bf16[32,1024]{1,0:T(8,128)(2,1)S(1)} %collective-permute-done.4.refs_2_), channel_id=1, source_target_pairs={{0,2},{2,0},{4,6},{6,4},{1,3},{3,1},{5,7},{7,5},{8,10},{10,8},{12,... | collective-permute-start | bytes 196616 | tf_op jit(solution)/shard_map/ppermute | solution.py:24
  22.0 4.4 %collective-permute-start.9 = (bf16[32,1024]{1,0:T(8,128)(2,1)S(1)}, bf16[32,1024]{1,0:T(8,128)(2,1)S(1)}, u32[]{:S(2)}, u32[]{:S(2)}) collective-permute-start(bf16[32,1024]{1,0:T(8,128)(2,1)S(1)} %collective-permute-done.8.refs_6_), channel_id=1, source_target_pairs={{0,2},{2,0},{4,6},{6,4},{1,3},{3,1},{5,7},{7,5},{8,10},{10,8},{12,... | collective-permute-start | bytes 196616 | tf_op jit(solution)/shard_map/ppermute | solution.py:24
  26.4 10.6 %copy-start.1 = (bf16[128,1024]{1,0:T(8,128)(2,1)S(1)}, bf16[128,1024]{1,0:T(8,128)(2,1)}, u32[]{:S(2)}) copy-start(bf16[128,1024]{1,0:T(8,128)(2,1)} %query_ref.3) | copy-start | bytes 786436
  26.4 10.6 %copy-start.2 = (s32[512,1]{0,1:T(1,128)S(1)}, s32[512,1]{0,1:T(1,128)}, u32[]{:S(2)}) copy-start(s32[512,1]{0,1:T(1,128)} %param.12) | copy-start | bytes 6148
  27.3 7.1 %collective-permute-start.13 = (bf16[64,512]{1,0:T(8,128)(2,1)S(1)}, bf16[64,512]{1,0:T(8,128)(2,1)S(1)}, u32[]{:S(2)}, u32[]{:S(2)}) collective-permute-start(bf16[64,512]{1,0:T(8,128)(2,1)S(1)} %shard_map.74.refs_0_), channel_id=1, source_target_pairs={{0,4},{2,6},{4,0},{6,2},{1,5},{3,7},{5,1},{7,3},{8,12},{10,14},{12... | collective-permute-start | bytes 196616 | tf_op jit(solution)/shard_map/ppermute | solution.py:24
  30.8 6.1 %collective-permute-start.11 = (bf16[64,512]{1,0:T(8,128)(2,1)S(1)}, bf16[64,512]{1,0:T(8,128)(2,1)S(1)}, u32[]{:S(2)}, u32[]{:S(2)}) collective-permute-start(bf16[64,512]{1,0:T(8,128)(2,1)S(1)} %shard_map.74.refs_0_), channel_id=1, source_target_pairs={{0,6},{2,4},{4,2},{6,0},{1,7},{3,5},{5,3},{7,1},{8,14},{10,12},{12... | collective-permute-start | bytes 196616 | tf_op jit(solution)/shard_map/ppermute | solution.py:24
  31.3 5.6 %collective-permute-start.10 = (bf16[64,512]{1,0:T(8,128)(2,1)S(1)}, bf16[64,512]{1,0:T(8,128)(2,1)S(1)}, u32[]{:S(2)}, u32[]{:S(2)}) collective-permute-start(bf16[64,512]{1,0:T(8,128)(2,1)S(1)} %shard_map.74.refs_0_), channel_id=1, source_target_pairs={{0,2},{2,0},{4,6},{6,4},{1,3},{3,1},{5,7},{7,5},{8,10},{10,8},{12,... | collective-permute-start | bytes 196616 | tf_op jit(solution)/shard_map/ppermute | solution.py:24
  34.5 2.5 %collective-permute-start.14 = (bf16[2,64,512]{2,1,0:T(8,128)(2,1)S(1)}, bf16[2,64,512]{2,1,0:T(8,128)(2,1)S(1)}, u32[]{:S(2)}, u32[]{:S(2)}) collective-permute-start(bf16[2,64,512]{2,1,0:T(8,128)(2,1)S(1)} %pad_maximum_fusion.1), channel_id=1, source_target_pairs={{0,1},{1,0},{2,3},{3,2},{4,5},{5,4},{6,7},{7,6},{8,9},{9,8},{10,11... | collective-permute-start | bytes 393224 | tf_op jit(solution)/shard_map/ppermute | solution.py:24
  36.9 1.4 %collective-permute-start.12 = (bf16[2,64,512]{2,1,0:T(8,128)(2,1)S(1)}, bf16[2,64,512]{2,1,0:T(8,128)(2,1)S(1)}, u32[]{:S(2)}, u32[]{:S(2)}) collective-permute-start(bf16[2,64,512]{2,1,0:T(8,128)(2,1)S(1)} %pad_maximum_fusion), channel_id=1, source_target_pairs={{0,1},{1,0},{2,3},{3,2},{4,5},{5,4},{6,7},{7,6},{8,9},{9,8},{10,11... | collective-permute-start | bytes 393224 | tf_op jit(solution)/shard_map/ppermute | solution.py:24
